TPU v7x, 32 devices: a whole 2x2x4 slice. The times are simulated.
32 devices in a mesh: dev: 32 (over z, y, x, core).
Axes of the slice: x: 2, y: 2, z: 4, core: 2. Of those that a mesh axis runs over, the one named last changes fastest.
Arguments:
- patches: bfloat16 [64, 256, 588], P('dev'), may hold values from -6 to 6
- masked: int32 [64, 16], P('dev'), may hold values from 0 to 255, as said below
- slot_used: int32 [64], P('dev'), may hold values from 0 to 1, as said below
- stem: float32 [5831040], P('dev')
- stem_moment: float32 [5831040], P('dev'), may hold values from -8.940697e-08 to 8.940697e-08
- stem_second: float32 [5831040], P('dev'), may hold values from 3.4414446e-18 to 1.37657785e-17
- stem_teacher: float32 [5831040], P('dev')
- layers: float32 [2, 1771776], P(None, 'dev')
- layer_moment: float32 [2, 1771776], P(None, 'dev'), may hold values from -8.940697e-08 to 8.940697e-08
- layer_second: float32 [2, 1771776], P(None, 'dev'), may hold values from 3.4414446e-18 to 1.37657785e-17
- layer_teacher: float32 [2, 1771776], P(None, 'dev')
- protos: float32 [65536, 256], P('dev'), may hold values from -0.4375 to 0.4375
- proto_moment: float32 [65536, 256], P('dev'), may hold values from -8.940697e-08 to 8.940697e-08
- proto_second: float32 [65536, 256], P('dev'), may hold values from 3.4414446e-18 to 1.37657785e-17
- proto_teacher: float32 [65536, 256], P('dev'), may hold values from -0.4375 to 0.4375
- centre: float32 [65536], replicated, may hold values from -0.078125 to 0.078125
Outputs:
- loss_sum: float32 [], replicated
- image_count: float32 [], replicated
- clip_norm: float32 [], replicated
- new_centre: float32 [65536], replicated
- stem_moment_out: float32 [5831040], P('dev')
- stem_second_out: float32 [5831040], P('dev')
- stem_out: float32 [5831040], P('dev')
- stem_copy: bfloat16 [5831040], P('dev')
- stem_teacher_out: float32 [5831040], P('dev')
- layer_moment_out: float32 [2, 1771776], P(None, 'dev')
- layer_second_out: float32 [2, 1771776], P(None, 'dev')
- layers_out: float32 [2, 1771776], P(None, 'dev')
- layer_copy: bfloat16 [2, 1771776], P(None, 'dev')
- layer_teacher_out: float32 [2, 1771776], P(None, 'dev')
- proto_moment_out: float32 [65536, 256], P('dev')
- proto_second_out: float32 [65536, 256], P('dev')
- protos_out: float32 [65536, 256], P('dev')
- proto_copy: bfloat16 [65536, 256], P('dev')
- proto_teacher_out: float32 [65536, 256], P('dev')
Inputs may be any that keep to these rules, and one draw needn't show every extreme that they name: `masked`: each row names 16 different patch positions. `slot_used`: the first of every device's 2 slots is 1.
All inputs are finite; a program needn't handle non-finite values.
Results may differ from a plain program's by a relative error of at most 0.0075.
The roundings to bfloat16 on the way count: a program that leaves them out, or rounds other values in their place, can miss the bound.
Values may be sent and summed in bfloat16 or wider, within the bound.
No kernel may reach another device: no remote copies, remote signals or barrier semaphores. Data moves between devices by JAX's collectives and lax.ppermute only.
A program may use at most 448 MiB of HBM per device.

v0:
```python
import jax
import jax.numpy as jnp
from jax import lax
from jax.sharding import PartitionSpec as P

D = 384
HEADS = 6
HEAD_DIM = 64
FF = 1536
HID = 2048
BOT = 256
PIX = 588
PATCHES = 256
LAYERS = 2
STEP = 10
SEQ = 257


tau_student = 0.1
tau_teacher = 0.04
clip_limit = 0.003
learn_rate = 0.03
beta_one = 0.9
beta_two = 0.999
adam_eps = 1e-08
decay_rate = 0.04
teacher_keep = 0.8
centre_keep = 0.9
narrow = jnp.bfloat16
single = jnp.float32


def layer_shapes():
    return ((D, 3 * D), (D, D), (D, FF), (FF, D), (6, D))


def stem_shapes():
    return ((PIX, D), (SEQ, D), (4, D), (D, HID), (HID, HID), (HID, BOT))


def cut_flat(flat_row, shape_list):
    pieces = []
    offset = 0
    for shape_pair in shape_list:
        length = shape_pair[0] * shape_pair[1]
        pieces.append(flat_row[offset : offset + length].reshape(shape_pair))
        offset = offset + length
    return pieces


def pack_flat(grad_list, total_length):
    joined = jnp.concatenate([grad_item.reshape(-1) for grad_item in grad_list])
    return jnp.concatenate([joined, jnp.zeros((total_length - joined.shape[0],), single)])


def contract(form, left_arg, right_arg):
    return jnp.einsum(form, left_arg, right_arg, preferred_element_type=single)


def layer_norm(values, gain_row, bias_row):
    centred = values - jnp.mean(values, axis=-1, keepdims=True)
    spread = jnp.mean(centred * centred, axis=-1, keepdims=True)
    return centred * lax.rsqrt(spread + 1e-06) * gain_row + bias_row


def unit_rows(values):
    return values * lax.rsqrt(jnp.sum(values * values, axis=-1, keepdims=True) + 1e-06)


def gelu_back(pre_act, grad_act):
    return jax.vjp(jax.nn.gelu, pre_act)[1](grad_act)[0]


def block_forward(stream, weights):
    w_qkv, w_proj, w_up, w_down, vectors = weights
    vectors = vectors.astype(single)
    batch_size = stream.shape[0]
    normed = layer_norm(stream, vectors[0], vectors[1]).astype(narrow)
    packed = (
        contract("bsd,de->bse", normed, w_qkv)
        .astype(narrow)
        .reshape(batch_size, SEQ, 3, HEADS, HEAD_DIM)
    )
    scores = contract("bqhe,bkhe->bhqk", packed[:, :, 0], packed[:, :, 1]) * HEAD_DIM ** (-0.5)
    top_score = jnp.max(scores, axis=-1, keepdims=True)
    exp_terms = jnp.exp(scores - top_score)
    totals = jnp.sum(exp_terms, axis=-1, keepdims=True)
    log_total = top_score + jnp.log(totals)
    mixed = contract("bhqk,bkhe->bqhe", (exp_terms / totals).astype(narrow), packed[:, :, 2])
    mixed = mixed.astype(narrow).reshape(batch_size, SEQ, D)
    attn_out = contract("bsd,de->bse", mixed, w_proj)
    middle = stream + vectors[2] * attn_out
    normed_two = layer_norm(middle, vectors[3], vectors[4]).astype(narrow)
    pre_act = contract("bsd,df->bsf", normed_two, w_up)
    hidden = jax.nn.gelu(pre_act).astype(narrow)
    mlp_out = contract("bsf,fd->bsd", hidden, w_down)
    saved = (
        stream,
        normed,
        packed,
        log_total,
        mixed,
        attn_out,
        middle,
        normed_two,
        pre_act,
        hidden,
        mlp_out,
    )
    return (middle + vectors[5] * mlp_out, saved)


def block_backward(grad_out, weights, saved):
    w_qkv, w_proj, w_up, w_down, vectors = weights
    vectors = vectors.astype(single)
    (
        stream,
        normed,
        packed,
        log_total,
        mixed,
        attn_out,
        middle,
        normed_two,
        pre_act,
        hidden,
        mlp_out,
    ) = saved
    batch_size = stream.shape[0]
    score_scale = HEAD_DIM ** (-0.5)
    grad_ls_two = jnp.sum(grad_out * mlp_out, axis=(0, 1))
    grad_mlp = (grad_out * vectors[5]).astype(narrow)
    grad_down = contract("bsf,bsd->fd", hidden, grad_mlp)
    grad_pre = gelu_back(pre_act, contract("bsd,fd->bsf", grad_mlp, w_down)).astype(narrow)
    grad_up = contract("bsd,bsf->df", normed_two, grad_pre)
    grad_normed_two = contract("bsf,df->bsd", grad_pre, w_up)
    grad_mid, grad_gain_two, grad_bias_two = jax.vjp(layer_norm, middle, vectors[3], vectors[4])[1](
        grad_normed_two
    )
    grad_mid = grad_mid + grad_out
    grad_ls_one = jnp.sum(grad_mid * attn_out, axis=(0, 1))
    grad_attn = (grad_mid * vectors[2]).astype(narrow)
    grad_proj = contract("bsd,bse->de", mixed, grad_attn)
    grad_mixed = (
        contract("bse,de->bsd", grad_attn, w_proj)
        .astype(narrow)
        .reshape(batch_size, SEQ, HEADS, HEAD_DIM)
    )
    query_rows = packed[:, :, 0]
    key_rows = packed[:, :, 1]
    value_rows = packed[:, :, 2]
    probs = jnp.exp(contract("bqhe,bkhe->bhqk", query_rows, key_rows) * score_scale - log_total)
    grad_probs = contract("bqhe,bkhe->bhqk", grad_mixed, value_rows)
    grad_values = contract("bhqk,bqhe->bkhe", probs.astype(narrow), grad_mixed)
    grad_scores = probs * (grad_probs - jnp.sum(probs * grad_probs, axis=-1, keepdims=True))
    grad_raw = (grad_scores * score_scale).astype(narrow)
    grad_queries = contract("bhqk,bkhe->bqhe", grad_raw, key_rows)
    grad_keys = contract("bhqk,bqhe->bkhe", grad_raw, query_rows)
    grad_packed = (
        jnp.stack([grad_queries, grad_keys, grad_values], axis=2)
        .astype(narrow)
        .reshape(batch_size, SEQ, 3 * D)
    )
    grad_qkv = contract("bsd,bse->de", normed, grad_packed)
    grad_normed = contract("bse,de->bsd", grad_packed, w_qkv)
    grad_in, grad_gain_one, grad_bias_one = jax.vjp(layer_norm, stream, vectors[0], vectors[1])[1](
        grad_normed
    )
    grad_vectors = jnp.stack(
        [grad_gain_one, grad_bias_one, grad_ls_one, grad_gain_two, grad_bias_two, grad_ls_two]
    )
    return (grad_in + grad_mid, (grad_qkv, grad_proj, grad_up, grad_down, grad_vectors))


def embed(stem_parts, image_rows, masked_here, student):
    patch_w, position, extras, w_first, w_second, w_third = stem_parts
    extras = extras.astype(single)
    embedded = contract("gpc,cd->gpd", image_rows, patch_w)
    if student:
        embedded = jnp.where(masked_here[:, :, None], extras[1], embedded)
    cls_rows = jnp.broadcast_to(extras[0], (image_rows.shape[0], 1, D))
    return jnp.concatenate([cls_rows, embedded], axis=1) + position.astype(single)


def embed_backward(grad_stream, image_rows, masked_here):
    grad_cls = jnp.sum(grad_stream[:, 0], axis=0)
    grad_position = jnp.sum(grad_stream, axis=0)
    grad_patch_rows = grad_stream[:, 1:]
    grad_mask_token = jnp.sum(jnp.where(masked_here[:, :, None], grad_patch_rows, 0.0), axis=(0, 1))
    grad_embedded = jnp.where(masked_here[:, :, None], 0.0, grad_patch_rows).astype(narrow)
    grad_patch_w = contract("gpc,gpd->cd", image_rows, grad_embedded)
    return (grad_patch_w, grad_position, grad_cls, grad_mask_token)


def head_forward(stem_parts, proto_rows, stream, row_index):
    patch_w, position, extras, w_first, w_second, w_third = stem_parts
    extras = extras.astype(single)
    chosen = jnp.take_along_axis(stream, row_index[:, :, None], axis=1)
    normed = layer_norm(chosen, extras[2], extras[3]).astype(narrow)
    pre_one = contract("grd,dh->grh", normed, w_first)
    hidden_one = jax.nn.gelu(pre_one).astype(narrow)
    pre_two = contract("grh,hk->grk", hidden_one, w_second)
    hidden_two = jax.nn.gelu(pre_two).astype(narrow)
    bottleneck = contract("grh,hb->grb", hidden_two, w_third)
    unit_z = unit_rows(bottleneck).astype(narrow)
    unit_protos = unit_rows(proto_rows.astype(single)).astype(narrow)
    logits = contract("grb,kb->grk", unit_z, unit_protos)
    return (
        logits,
        (chosen, normed, pre_one, hidden_one, pre_two, hidden_two, bottleneck, unit_z, unit_protos),
    )


def head_backward(grad_logits, stem_parts, saved, row_index, stream_shape):
    patch_w, position, extras, w_first, w_second, w_third = stem_parts
    extras = extras.astype(single)
    chosen, normed, pre_one, hidden_one, pre_two, hidden_two, bottleneck, unit_z, unit_protos = (
        saved
    )
    grad_rounded = grad_logits.astype(narrow)
    grad_unit_z = contract("grk,kb->grb", grad_rounded, unit_protos)
    grad_unit_protos = contract("grk,grb->kb", grad_rounded, unit_z)
    grad_bottle = jax.vjp(unit_rows, bottleneck)[1](grad_unit_z)[0].astype(narrow)
    grad_third = contract("grh,grb->hb", hidden_two, grad_bottle)
    grad_pre_two = gelu_back(pre_two, contract("grb,hb->grh", grad_bottle, w_third)).astype(narrow)
    grad_second = contract("grh,grk->hk", hidden_one, grad_pre_two)
    grad_pre_one = gelu_back(pre_one, contract("grk,hk->grh", grad_pre_two, w_second)).astype(
        narrow
    )
    grad_first = contract("grd,grh->dh", normed, grad_pre_one)
    grad_normed = contract("grh,dh->grd", grad_pre_one, w_first)
    grad_chosen, grad_gain, grad_bias = jax.vjp(layer_norm, chosen, extras[2], extras[3])[1](
        grad_normed
    )
    image_index = jnp.arange(row_index.shape[0], dtype=jnp.int32)[:, None]
    grad_stream = jnp.zeros(stream_shape, single).at[image_index, row_index].add(grad_chosen)
    return (
        grad_stream,
        (grad_first, grad_second, grad_third),
        grad_gain,
        grad_bias,
        grad_unit_protos,
    )


def adam_update(weight, moment, second, grad, teacher):
    new_moment = beta_one * moment + (1.0 - beta_one) * grad
    new_second = beta_two * second + (1.0 - beta_two) * grad * grad
    direction = (
        new_moment
        / (1.0 - beta_one**STEP)
        / (jnp.sqrt(new_second / (1.0 - beta_two**STEP)) + adam_eps)
    )
    new_weight = weight - learn_rate * (direction + decay_rate * weight)
    return (
        new_moment,
        new_second,
        new_weight,
        new_weight.astype(narrow),
        teacher_keep * teacher + (1.0 - teacher_keep) * new_weight,
    )


def local(
    patches,
    masked,
    slot_used,
    stem,
    stem_moment,
    stem_second,
    stem_teacher,
    layers,
    layer_moment,
    layer_second,
    layer_teacher,
    protos,
    proto_moment,
    proto_second,
    proto_teacher,
    centre,
):
    images_here = patches.shape[0]
    row_index = jnp.concatenate([jnp.zeros((images_here, 1), jnp.int32), masked + 1], axis=1)
    masked_here = jnp.any(
        masked[:, :, None] == jnp.arange(PATCHES, dtype=jnp.int32)[None, None, :], axis=1
    )
    kept = slot_used.astype(single)
    teacher_flat, teacher_protos = (
        lax.all_gather(stem_teacher.astype(narrow), "dev", axis=0, tiled=True),
        lax.all_gather(proto_teacher.astype(narrow), "dev", axis=0, tiled=True),
    )
    teacher_parts = cut_flat(teacher_flat, stem_shapes())
    stream = embed(teacher_parts, patches, masked_here, False)
    for layer_index in range(LAYERS):
        teacher_layer = lax.all_gather(
            layer_teacher[layer_index].astype(narrow), "dev", axis=0, tiled=True
        )
        stream = block_forward(stream, cut_flat(teacher_layer, layer_shapes()))[0]
    teacher_logits = head_forward(teacher_parts, teacher_protos, stream, row_index)[0]
    teacher_probs = jax.nn.softmax((teacher_logits - centre) / tau_teacher, axis=-1)
    centre_terms = jnp.sum(kept[:, None] * teacher_logits[:, 0], axis=0)
    student_flat, student_protos = (
        lax.all_gather(stem.astype(narrow), "dev", axis=0, tiled=True),
        lax.all_gather(protos.astype(narrow), "dev", axis=0, tiled=True),
    )
    student_parts = cut_flat(student_flat, stem_shapes())
    stream = embed(student_parts, patches, masked_here, True)
    saved_layers = []
    gathered_layers = []
    for layer_index in range(LAYERS):
        layer_flat = lax.all_gather(layers[layer_index].astype(narrow), "dev", axis=0, tiled=True)
        gathered_layers.append(layer_flat)
        stream, saved = block_forward(stream, cut_flat(layer_flat, layer_shapes()))
        saved_layers.append(saved)
    logits, head_saved = head_forward(student_parts, student_protos, stream, row_index)

    def loss_piece(logit_rows):
        log_probs = jax.nn.log_softmax(logit_rows / tau_student, axis=-1)
        cross = -jnp.sum(teacher_probs * log_probs, axis=-1)
        return jnp.sum(kept * (cross[:, 0] + jnp.mean(cross[:, 1:], axis=1)))

    loss_local, loss_puller = jax.vjp(loss_piece, logits)
    grad_logits = loss_puller(jnp.float32(1.0))[0]
    count_local = jnp.sum(kept)
    loss_total, count_total, centre_total = lax.psum((loss_local, count_local, centre_terms), "dev")
    back_flat, back_protos = (
        lax.all_gather(stem.astype(narrow), "dev", axis=0, tiled=True),
        lax.all_gather(protos.astype(narrow), "dev", axis=0, tiled=True),
    )
    back_parts = cut_flat(back_flat, stem_shapes())
    grad_stream, head_grads, grad_gain, grad_bias, grad_unit_protos = head_backward(
        grad_logits, back_parts, head_saved, row_index, stream.shape
    )
    layer_grads = []
    for layer_index in reversed(range(LAYERS)):
        weight_flat = lax.all_gather(layers[layer_index].astype(narrow), "dev", axis=0, tiled=True)
        grad_stream, block_grads = block_backward(
            grad_stream, cut_flat(weight_flat, layer_shapes()), saved_layers[layer_index]
        )
        layer_grads.insert(
            0,
            lax.psum_scatter(
                pack_flat(block_grads, weight_flat.shape[0]), "dev", scatter_dimension=0, tiled=True
            ),
        )
    grad_patch_w, grad_position, grad_cls, grad_mask_token = embed_backward(
        grad_stream, patches, masked_here
    )
    grad_extras = jnp.stack([grad_cls, grad_mask_token, grad_gain, grad_bias])
    stem_flat_grad = pack_flat(
        (grad_patch_w, grad_position, grad_extras) + head_grads, back_flat.shape[0]
    )
    stem_grad, proto_row_grad = (
        lax.psum_scatter(stem_flat_grad, "dev", scatter_dimension=0, tiled=True),
        lax.psum_scatter(grad_unit_protos, "dev", scatter_dimension=0, tiled=True),
    )
    own_protos = lax.optimization_barrier(protos.astype(narrow)).astype(single)
    proto_grad = jax.vjp(unit_rows, own_protos)[1](proto_row_grad)[0]
    layer_grad = jnp.stack(layer_grads)
    square_local = (
        jnp.sum(stem_grad * stem_grad)
        + jnp.sum(layer_grad * layer_grad)
        + jnp.sum(proto_grad * proto_grad)
    )
    square_total = lax.psum(square_local, "dev")
    grad_norm = jnp.sqrt(square_total) / count_total
    factor = jnp.minimum(1.0, clip_limit / (grad_norm + 1e-06)) / count_total
    new_centre = centre_keep * centre + (1.0 - centre_keep) * centre_total / count_total
    stem_set = adam_update(stem, stem_moment, stem_second, stem_grad * factor, stem_teacher)
    layer_set = adam_update(layers, layer_moment, layer_second, layer_grad * factor, layer_teacher)
    proto_set = adam_update(protos, proto_moment, proto_second, proto_grad * factor, proto_teacher)
    return (
        loss_total,
        count_total,
        grad_norm,
        new_centre,
        stem_set[0],
        stem_set[1],
        stem_set[2],
        stem_set[3],
        stem_set[4],
        layer_set[0],
        layer_set[1],
        layer_set[2],
        layer_set[3],
        layer_set[4],
        proto_set[0],
        proto_set[1],
        proto_set[2],
        proto_set[3],
        proto_set[4],
    )


def solution(mesh):
    placed = (
        P("dev", None, None),
        P("dev", None),
        P("dev"),
        P("dev"),
        P("dev"),
        P("dev"),
        P("dev"),
        P(None, "dev"),
        P(None, "dev"),
        P(None, "dev"),
        P(None, "dev"),
        P("dev", None),
        P("dev", None),
        P("dev", None),
        P("dev", None),
        P(),
    )
    return jax.shard_map(
        local,
        mesh=mesh,
        in_specs=placed,
        out_specs=(
            P(),
            P(),
            P(),
            P(),
            P("dev"),
            P("dev"),
            P("dev"),
            P("dev"),
            P("dev"),
            P(None, "dev"),
            P(None, "dev"),
            P(None, "dev"),
            P(None, "dev"),
            P(None, "dev"),
            P("dev", None),
            P("dev", None),
            P("dev", None),
            P("dev", None),
            P("dev", None),
        ),
        check_vma=False,
    )
```

profile of v0, /device:TPU:8, one launch (start us, length us, event | category | flops | bytes accessed | tf_op | source)
XLA Modules:
  0.0 3021.6 jit_solution(17143308680115971054)
XLA Ops:
  63.6 549.5 %all-reduce.20.cloned.1.call-done = (bf16[5831040]{0:T(1024)(128)(2,1)}, bf16[1771776]{0:T(1024)(128)(2,1)}, bf16[1771776]{0:T(1024)(128)(2,1)}, bf16[5831040]{0...) async-done(((bf16[5831040]{0:T(1024)(128)(2,1)}, bf16[1771776]{0:T(1024)(128)(2,1)}, bf16[1771776]{0:T(1024)(128)(2,1)}, ...) | async-done | bytes 37498384
  650.6 34.4 %reshape.907 = bf16[1,1771776]{1,0:T(2,128)(2,1)S(1)} reshape(bf16[1771776]{0:T(1024)(128)(2,1)} %get-tuple-element.91) | data formatting | bytes 7087104
  687.8 15.0 slice_reduce_fusion.11
  724.8 28.2 slice_reduce_fusion.7
  759.5 34.4 %reshape.909 = bf16[1,1771776]{1,0:T(2,128)(2,1)S(1)} reshape(bf16[1771776]{0:T(1024)(128)(2,1)} %get-tuple-element.92) | data formatting | bytes 7087104
  796.9 15.8 slice_reduce_fusion.10
  843.2 27.7 slice_reduce_fusion.5
  890.6 34.4 %reshape.913 = bf16[1,1771776]{1,0:T(2,128)(2,1)S(1)} reshape(bf16[1771776]{0:T(1024)(128)(2,1)} %get-tuple-element.94) | data formatting | bytes 7087104
  928.0 14.9 slice_reduce_fusion.9
  957.3 27.7 slice_reduce_fusion.3
  991.8 34.4 %reshape.915 = bf16[1,1771776]{1,0:T(2,128)(2,1)S(1)} reshape(bf16[1771776]{0:T(1024)(128)(2,1)} %get-tuple-element.95) | data formatting | bytes 7087104
  1029.2 15.7 slice_reduce_fusion.8
  1066.5 27.6 slice_reduce_fusion.1
  1174.9 16.1 fusion.317
  1195.7 16.3 fusion.16
  1237.5 31.2 %multiply_reduce_fusion.35 = (f32[2,17]{1,0:T(2,128)S(1)}, f32[2,17,256]{2,1,0:T(8,128)S(1)}) fusion(f32[2,17,256]{2,1,0:T(8,128)S(1)} %get-tuple-element.162, bf16[2,17,65536]{2,1,0:T(8,128)(2,1)} %multiply_convert_fusion, bf16[65536,256]{1,0:T(8,128)(2,1)} %all-gather.9.cloned.1.call-done, f32[65536]{0:T(1024)S(1)} %copy-done.90), kind=kOutput, calls=%fused_computation.365 | convolution fusion | flops 1191199744 | bytes 38342792 | tf_op jit(solution)/shard_map/grk,kb->grb/dot_general | solution.py:57
  1418.1 14.3 copy.306
  1489.8 27.8 dynamic-update-slice.19
  1517.7 142.0 %dynamic-update-slice.20 = f32[5831040]{0:T(1024)} dynamic-update-slice(f32[5831040]{0:T(1024)} %dynamic-update-slice.19, f32[4194304]{0:T(1024)} %bitcast.256, s32[]{} %constant.319) | dynamic-update-slice | bytes 33554436
  1659.7 17.9 dynamic-update-slice.21
  1677.7 28.1 convolution_bitcast_fusion
  1707.4 528.5 %all-reduce.18.cloned.1.call-done = (f32[5831040]{0:T(1024)}, f32[1771776]{0:T(1024)}, f32[1771776]{0:T(1024)}, f32[65536]{0:T(1024)}) async-done(((f32[5831040]{0:T(1024)}, f32[1771776]{0:T(1024)}, f32[1771776]{0:T(1024)}, f32[65536]{0:T(1024)}), (f32[5831040]{0:T(1024)}, f32[1771776]{0:T(1024)}, f32[1771776]{0:T(1024)}, f32[65536]{0:T(1024)})) %all-reduce.18.cloned.1.call-update) | async-done | bytes 37760528
  2243.0 697.9 %reduce-scatter.2.cloned.1.call-done = f32[2048,256]{1,0:T(8,128)} async-done(((f32[65536,256]{1,0:T(8,128)}), f32[2048,256]{1,0:T(8,128)}) %reduce-scatter.2.cloned.1.call-update) | async-done | bytes 2097168 | tf_op jit(solution)/shard_map/reduce_scatter | solution.py:355
  2945.5 47.1 %all-reduce.12 = (f32[]{:T(128)}, f32[]{:T(128)}, f32[]{:T(128)}) all-reduce(f32[]{:T(128)} %get-tuple-element.80, f32[]{:T(128)} %get-tuple-element.79, f32[]{:T(128)S(6)} %add.539), channel_id=1, replica_groups=mesh['dev'=32] {'dev'}, use_global_device_ids=true, to_apply=%region_40.42 | all-reduce | flops 3 | bytes 24 | tf_op jit(solution)/shard_map/psum | solution.py:325
  (751 shorter events, 572.2 us)
Async XLA Ops:
  7.2 703.7 %copy-start = (bf16[2,256,588]{1,0,2:T(2,128)(2,1)S(1)}, bf16[2,256,588]{1,0,2:T(2,128)(2,1)}, u32[]{:S(2)}) copy-start(bf16[2,256,588]{1,0,2:T(2,128)(2,1)} %param.18) | copy-start | bytes 1806340
  7.2 605.9 %all-reduce.20.cloned.1.call-start = ((), (), s32[]{:S(2)}) async-start(), calls=%async_computation.5 | async-start | bytes 75014144
  55.8 1094.3 %all-gather.7.cloned.1.call-start = ((), (), s32[]{:S(2)}) async-start(), calls=%async_computation.1 | async-start | bytes 34603008 | tf_op jit(solution)/shard_map/all_gather | solution.py:290
  58.5 1104.2 %all-gather.9.cloned.1.call-start = ((), (), s32[]{:S(2)}) async-start(), calls=%async_computation.2 | async-start | bytes 34603008 | tf_op jit(solution)/shard_map/all_gather | solution.py:304
  61.2 2174.7 %all-reduce.18.cloned.1.call-start = ((), (), s32[]{:S(2)}) async-start(), calls=%async_computation.4 | async-start | bytes 75538432
  63.5 1078.0 %copy-start.139 = (pred[2,17]{1,0:T(4,128)(4,1)}, pred[2,17]{1,0:T(4,128)(4,1)S(1)}, u32[]{:S(2)}) copy-start(pred[2,17]{1,0:T(4,128)(4,1)S(1)} %and_bitcast_fusion) | copy-start | bytes 106
  63.6 647.9 %copy-start.176 = (pred[2,256]{1,0:T(4,128)(4,1)}, pred[2,256]{1,0:T(4,128)(4,1)S(1)}, u32[]{:S(2)}) copy-start(pred[2,256]{1,0:T(4,128)(4,1)S(1)} %fusion.245) | copy-start | bytes 1540
  710.8 430.6 %copy-start.126 = (f32[384]{0:T(512)}, f32[384]{0:T(512)S(1)}, u32[]{:S(2)}) copy-start(f32[384]{0:T(512)S(1)} %get-tuple-element.127) | copy-start | bytes 4612
  713.5 338.7 %copy-start.5 = (f32[2,257,384]{2,1,0:T(8,128)}, f32[2,257,384]{2,1,0:T(8,128)S(1)}, u32[]{:S(2)}) copy-start(f32[2,257,384]{2,1,0:T(8,128)S(1)} %get-tuple-element.123) | copy-start | bytes 2368516
  944.8 107.4 %copy-start.145 = (f32[384]{0:T(512)}, f32[384]{0:T(512)S(1)}, u32[]{:S(2)}) copy-start(f32[384]{0:T(512)S(1)} %get-tuple-element.77) | copy-start | bytes 4612
  944.8 109.2 %copy-start.142 = (f32[384]{0:T(512)}, f32[384]{0:T(512)S(1)}, u32[]{:S(2)}) copy-start(f32[384]{0:T(512)S(1)} %get-tuple-element.74) | copy-start | bytes 4612
  944.8 109.2 %copy-start.188 = (f32[384]{0:T(512)}, f32[384]{0:T(512)S(1)}, u32[]{:S(2)}) copy-start(f32[384]{0:T(512)S(1)} %get-tuple-element.78) | copy-start | bytes 4612
  944.8 110.3 %copy-start.197 = (f32[384]{0:T(512)}, f32[384]{0:T(512)S(1)}, u32[]{:S(2)}) copy-start(f32[384]{0:T(512)S(1)} %get-tuple-element.73) | copy-start | bytes 4612
  949.3 101.5 %copy-start.33 = (bf16[2,257,1152]{1,2,0:T(8,128)(2,1)}, bf16[2,257,1152]{1,2,0:T(8,128)(2,1)S(1)}, u32[]{:S(2)}) copy-start(bf16[2,257,1152]{1,2,0:T(8,128)(2,1)S(1)} %copy.238) | copy-start | bytes 3552772
  957.3 94.9 %copy-start.64 = (bf16[384,384,1]{1,0,2:T(8,128)(2,1)}, bf16[384,384,1]{1,0,2:T(8,128)(2,1)S(1)}, u32[]{:S(2)}) copy-start(bf16[384,384,1]{1,0,2:T(8,128)(2,1)S(1)} %reshape.939) | copy-start | bytes 884740
  1048.9 58.4 %copy-start.150 = (f32[384]{0:T(512)}, f32[384]{0:T(512)S(1)}, u32[]{:S(2)}) copy-start(f32[384]{0:T(512)S(1)} %get-tuple-element.68) | copy-start | bytes 4612
  1048.9 59.5 %copy-start.202 = (f32[384]{0:T(512)}, f32[384]{0:T(512)S(1)}, u32[]{:S(2)}) copy-start(f32[384]{0:T(512)S(1)} %get-tuple-element.67) | copy-start | bytes 4612
  1107.0 178.6 %copy-start.119 = (f32[2,257]{1,0:T(2,128)}, f32[2,257]{1,0:T(2,128)S(1)}, u32[]{:S(2)}) copy-start(f32[2,257]{1,0:T(2,128)S(1)} %broadcast_multiply_fusion) | copy-start | bytes 6172
  1148.4 120.5 %copy-start.87 = (f32[2,17,2048]{2,1,0:T(8,128)}, f32[2,17,2048]{2,1,0:T(8,128)S(1)}, u32[]{:S(2)}) copy-start(f32[2,17,2048]{2,1,0:T(8,128)S(1)} %fusion.292) | copy-start | bytes 835588
  1517.7 142.0 %copy-start.31 = (f32[256,2,8,128]{3,1,2,0:T(2,128)S(1)}, f32[256,2,8,128]{3,1,2,0:T(2,128)}, u32[]{:S(2)}) copy-start(f32[256,2,8,128]{3,1,2,0:T(2,128)} %copy.307) | copy-start | bytes 6291460
  1677.7 1263.2 %reduce-scatter.2.cloned.1.call-start = ((), (), s32[]{:S(2)}) async-start(), calls=%async_computation.3 | async-start | bytes 69206016 | tf_op jit(solution)/shard_map/reduce_scatter | solution.py:355
  1705.8 1235.0 %copy-start.11 = (bf16[2048,256]{1,0:T(8,128)(2,1)S(1)}, bf16[2048,256]{1,0:T(8,128)(2,1)}, u32[]{:S(2)}) copy-start(bf16[2048,256]{1,0:T(8,128)(2,1)} %convert_element_type.325) | copy-start | bytes 3145732
  2241.7 752.3 %copy-start.23 = (f32[65536]{0:T(1024)S(1)}, f32[65536]{0:T(1024)}, u32[]{:S(2)}) copy-start(f32[65536]{0:T(1024)} %param.33) | copy-start | bytes 786436
  2243.0 754.1 %copy-start.61 = (f32[182220]{0:T(1024)S(1)}, f32[182220]{0:T(1024)}, u32[]{:S(2)}) copy-start(f32[182220]{0:T(1024)} %param.24) | copy-start | bytes 2186644
  (196 other events, 1175.2 us)
Sparse Core Ops, SparseCore 0:
  55.9 557.1 all-reduce.19
  616.9 192.8 all-gather.6
  813.1 193.0 all-gather.8
  1677.8 558.1 all-reduce.17
  2238.1 702.7 reduce-scatter.1
where the time goes:
time: 3050 us; the launch traced here: 3020 us
  waiting for transfers between devices  1780 us (58%)
  local copies, waits for them, and re-layouts  786 us (26%)
  matrix products  259 us (8%)
  other arithmetic  130 us (4%)
  blocking collectives  47.1 us (2%)
    unnamed x7, waiting for transfers between devices  1080 us
    reduce_scatter x1, waiting for transfers between devices, local(): lax.psum_scatter(grad_unit_protos, 'dev', scatter_dimension=0, tiled=True)  698 us
    unnamed x464, local copies, waits for them, and re-layouts  412 us
    dot_general x64, matrix products, contract(): return jnp.einsum(form, left_arg, right_arg, preferred_element_type=single)  259 us
    slice x34, local copies, waits for them, and re-layouts, cut_flat(): pieces.append(flat_row[offset:offset + length].reshape(shape_pair))  244 us
  transfers between devices with their start and end apart: 5, of which 3 were waited for; matrix products, arithmetic and copies ran while one was open for 19% of the time, Pallas kernels for 0%

commit v1 on v0

--- a/solution.py
+++ b/solution.py
@@ -261,7 +261,7 @@
     )
 
 
-def local(
+def spread_local(
     patches,
     masked,
     slot_used,
@@ -392,7 +392,429 @@
     )
 
 
+GROUP = 16
+ROW = HID
+MATRIX_ROWS = D * 3 + D + FF + FF
+EMBED_ROWS = PIX + SEQ + 4
+EMBED_FLAT = EMBED_ROWS * D
+HEAD_ROWS = D + HID + BOT
+BITS = ("b", "a", "y", "x", "c")
+MASKS = {"c": 1, "x": 2, "y": 4, "a": 8, "b": 24}
+
+
+def head_bounds(count, stem_piece):
+    bounds = [-(-(stem_piece * device - EMBED_FLAT) // (ROW * GROUP)) * GROUP for device in range(count + 1)]
+    bounds[0] = -(-EMBED_FLAT // (ROW * GROUP)) * -GROUP
+    bounds[-1] = HEAD_ROWS
+    return bounds
+
+
+def fits(count, stem_piece, layer_piece):
+    if count != 1 << len(BITS) or MATRIX_ROWS % (3 * count):
+        return False
+    bounds = head_bounds(count, stem_piece)
+    sizes = [bounds[i + 1] - bounds[i] for i in range(count)]
+    return (
+        min(sizes) > GROUP
+        and bounds[1] <= 0
+        and stem_piece < EMBED_FLAT <= 2 * stem_piece
+        and D in bounds
+        and D + HID in bounds
+        and stem_piece * count == EMBED_FLAT + HEAD_ROWS * ROW
+    )
+
+
+def pairs(count, mask):
+    return [(i, i ^ mask) for i in range(count)]
+
+
+def bit_flags(me):
+    return {name: (me >> (len(BITS) - 1 - place)) & 1 for place, name in enumerate(BITS)}
+
+
+def cube_gather(parts, orders):
+    count = 1 << len(BITS)
+    flags = bit_flags(lax.axis_index("dev"))
+    held = [part[None] for part in parts]
+    for turn in range(len(BITS)):
+        got = [
+            lax.ppermute(h, "dev", pairs(count, MASKS[order[turn]])) for h, order in zip(held, orders)
+        ]
+        held = [
+            jnp.where(
+                flags[order[turn]] == 1,
+                jnp.concatenate([g, h], axis=0),
+                jnp.concatenate([h, g], axis=0),
+            )
+            for h, g, order in zip(held, got, orders)
+        ]
+    return held
+
+
+def cube_scatter(parts, orders, axes):
+    count = 1 << len(BITS)
+    flags = bit_flags(lax.axis_index("dev"))
+    held = list(parts)
+    names = [list(a) for a in axes]
+    for turn in range(len(BITS)):
+        sent, kept = [], []
+        for h, order, name in zip(held, orders, names):
+            place = name.index(order[turn])
+            low = lax.index_in_dim(h, 0, place, keepdims=False)
+            high = lax.index_in_dim(h, 1, place, keepdims=False)
+            flag = flags[order[turn]] == 1
+            sent.append(jnp.where(flag, low, high))
+            kept.append(jnp.where(flag, high, low))
+            name.pop(place)
+        got = [
+            lax.ppermute(s, "dev", pairs(count, MASKS[order[turn]])) for s, order in zip(sent, orders)
+        ]
+        held = [
+            (k.astype(single) + g.astype(single)).astype(k.dtype) for k, g in zip(kept, got)
+        ]
+    return held
+
+
+def cube_sum(values):
+    for name in "cxyab":
+        values = values + lax.ppermute(values, "dev", pairs(1 << len(BITS), MASKS[name]))
+    return values
+
+
+def split_bits(array):
+    return array.reshape((2,) * len(BITS) + array.shape[1:])
+
+
+def scatter_rows(array, cuts, axis):
+    points = [0, cuts[0], cuts[0] + cuts[1], array.shape[axis]]
+    parts = [
+        split_bits(lax.slice_in_dim(array, points[i], points[i + 1], axis=axis)) for i in range(3)
+    ]
+    done = cube_scatter(parts, ("cxyba", "cyxba", "cbaxy"), (BITS,) * 3)
+    return jnp.concatenate(done, axis=axis - 1)
+
+
+def step_pairs(count, step):
+    return [(i, i + step) for i in range(count) if 0 <= i + step < count]
+
+
+def close_local(
+    patches,
+    masked,
+    slot_used,
+    stem,
+    stem_moment,
+    stem_second,
+    stem_teacher,
+    layers,
+    layer_moment,
+    layer_second,
+    layer_teacher,
+    protos,
+    proto_moment,
+    proto_second,
+    proto_teacher,
+    centre,
+):
+    count = 1 << len(BITS)
+    me = lax.axis_index("dev")
+    images_here = patches.shape[0]
+    rows_here = images_here * 17
+    stem_piece = stem.shape[0]
+    layer_piece = layers.shape[1]
+    block_rows = MATRIX_ROWS // count
+    block = block_rows * D
+    tail = layer_piece * count - MATRIX_ROWS * D
+    drift = layer_piece - block
+    bounds = head_bounds(count, stem_piece)
+    sizes = [bounds[i + 1] - bounds[i] for i in range(count)]
+    slot = max(sizes)
+    starts = [b * ROW + EMBED_FLAT - stem_piece * i for i, b in enumerate(bounds[:-1])]
+    first_w2 = bounds.index(D)
+    first_w3 = bounds.index(D + HID)
+    row_index = jnp.concatenate([jnp.zeros((images_here, 1), jnp.int32), masked + 1], axis=1)
+    masked_here = jnp.any(
+        masked[:, :, None] == jnp.arange(PATCHES, dtype=jnp.int32)[None, None, :], axis=1
+    )
+    kept = slot_used.astype(single)
+
+    own_layers = jnp.stack([layer_teacher, layers]).astype(narrow).reshape(2 * LAYERS, layer_piece)
+    own_tail = own_layers[:, layer_piece - tail :]
+    before = lax.ppermute(own_tail, "dev", step_pairs(count, 1))
+    joined = jnp.concatenate([before, own_layers], axis=1)
+    layer_blocks = lax.dynamic_slice(joined, (0, tail - drift * me), (2 * LAYERS, block)).reshape(
+        2 * LAYERS, block_rows, D
+    )
+    gathered = lax.all_gather(layer_blocks, "dev", axis=0)
+    head_span = GROUP * ROW
+    own_stems = jnp.stack([stem_teacher, stem]).astype(narrow)
+    after = lax.ppermute(own_stems[:, :head_span], "dev", step_pairs(count, -1))
+    start_here = jnp.array(starts, jnp.int32)[me]
+    front = -min(starts) + (starts[0] % 128)
+    joined = jnp.concatenate(
+        [
+            jnp.zeros((2, front), narrow),
+            own_stems,
+            after,
+            jnp.zeros((2, slot * ROW), narrow),
+        ],
+        axis=1,
+    )
+    head_blocks = lax.dynamic_slice(joined, (0, front + start_here), (2, slot * ROW)).reshape(
+        2, slot, ROW
+    )
+    gathered_head = lax.all_gather(head_blocks, "dev", axis=0)
+    vectors_flat = lax.ppermute(own_tail, "dev", [(count - 1, 0)]).reshape(1, 2 * LAYERS * tail)
+    seed = jnp.concatenate([own_stems.reshape(1, -1), vectors_flat], axis=1)
+    spread = seed
+    reached = [0, 1]
+    for name in "baxy":
+        moves = [(i, i ^ MASKS[name]) for i in reached]
+        got = lax.ppermute(spread, "dev", moves)
+        targets = [t for s, t in moves]
+        is_target = jnp.array([i in targets for i in range(count)])[me]
+        spread = jnp.where(is_target, got, spread)
+        reached = reached + targets
+    other = lax.ppermute(spread, "dev", pairs(count, 1))
+    is_even = me % 2 == 0
+    even = jnp.where(is_even, spread, other)[0]
+    odd = jnp.where(is_even, other, spread)[0]
+    rest = EMBED_FLAT - stem_piece
+    embed_flat = [
+        jnp.concatenate([even[m * stem_piece : (m + 1) * stem_piece], odd[m * stem_piece : m * stem_piece + rest]])
+        for m in range(2)
+    ]
+    vectors_all = even[2 * stem_piece :].reshape(2, LAYERS, 6, D)
+
+    def layer_weights(model, layer_index):
+        flat = gathered[:, model * LAYERS + layer_index].reshape(MATRIX_ROWS, D)
+        return (
+            flat[: 3 * D].reshape(D, 3 * D),
+            flat[3 * D : 4 * D],
+            flat[4 * D : 4 * D + FF].reshape(D, FF),
+            flat[4 * D + FF :],
+            vectors_all[model, layer_index],
+        )
+
+    def head_weights(model):
+        one = gathered_head[:, model]
+        w_one = one[1:first_w2].reshape((first_w2 - 1) * slot, ROW)
+        w_two = one[first_w2:first_w3].reshape((first_w3 - first_w2) * slot, ROW)
+        w_three = jnp.concatenate([one[i, : sizes[i]] for i in range(first_w3, count)]).reshape(HID, BOT)
+        return (w_one, w_two, w_three)
+
+    def pad_columns(values, first, last, origin):
+        pieces = []
+        for i in range(first, last):
+            low, high = bounds[i] - origin, bounds[i + 1] - origin
+            if low < 0:
+                pieces.append(jnp.zeros(values.shape[:-1] + (-low,), values.dtype))
+            pieces.append(values[..., max(low, 0) : high])
+            pieces.append(jnp.zeros(values.shape[:-1] + (slot - sizes[i],), values.dtype))
+        return jnp.concatenate([p for p in pieces if p.shape[-1]], axis=-1)
+
+    def cut_columns(values, first, last, origin):
+        pieces = []
+        for i in range(first, last):
+            low, high = bounds[i] - origin, bounds[i + 1] - origin
+            at = (i - first) * slot
+            pieces.append(values[..., at + max(-low, 0) : at + sizes[i]])
+        return jnp.concatenate(pieces, axis=-1)
+
+    def embed_parts(model):
+        patch_w = embed_flat[model][: PIX * D].reshape(PIX, D)
+        position = embed_flat[model][PIX * D : (PIX + SEQ) * D].reshape(SEQ, D)
+        extras = embed_flat[model][(PIX + SEQ) * D :].reshape(4, D)
+        return (patch_w, position, extras, None, None, None)
+
+    def head_up(stream, extras, weights):
+        w_one, w_two, w_three = weights
+        chosen = jnp.take_along_axis(stream, row_index[:, :, None], axis=1).reshape(rows_here, D)
+        normed = layer_norm(chosen, extras[2].astype(single), extras[3].astype(single)).astype(narrow)
+        normed_wide = pad_columns(normed, 1, first_w2, 0)
+        pre_one = contract("rd,dh->rh", normed_wide, w_one)
+        hidden_one = jax.nn.gelu(pre_one).astype(narrow)
+        hidden_wide = pad_columns(hidden_one, first_w2, first_w3, D)
+        pre_two = contract("rh,hk->rk", hidden_wide, w_two)
+        hidden_two = jax.nn.gelu(pre_two).astype(narrow)
+        bottleneck = contract("rh,hb->rb", hidden_two, w_three)
+        unit_z = unit_rows(bottleneck).astype(narrow)
+        return unit_z, (chosen, normed_wide, pre_one, hidden_wide, pre_two, hidden_two, bottleneck)
+
+    student_parts = embed_parts(1)
+    stream = embed(student_parts, patches, masked_here, True)
+    saved_layers = []
+    student_layers = []
+    for layer_index in range(LAYERS):
+        weights = layer_weights(1, layer_index)
+        student_layers.append(weights)
+        stream, saved = block_forward(stream, weights)
+        saved_layers.append(saved)
+    teacher_parts = embed_parts(0)
+    teacher_stream = embed(teacher_parts, patches, masked_here, False)
+    for layer_index in range(LAYERS):
+        teacher_stream = block_forward(teacher_stream, layer_weights(0, layer_index))[0]
+    student_head = head_weights(1)
+    teacher_z, _ = head_up(teacher_stream, teacher_parts[2], head_weights(0))
+    student_z, head_saved = head_up(stream, student_parts[2], student_head)
+
+    all_rows = count * rows_here
+    kept_row = jnp.broadcast_to(kept[:, None], (images_here, 17)).reshape(1, rows_here)
+    all_kept = cube_gather([kept_row], ("xyabc",))[0].reshape(all_rows)
+    z_all = cube_gather([jnp.stack([teacher_z, student_z])], ("xyabc",))[0]
+    teacher_z_all = z_all[:, 0].reshape(all_rows, BOT)
+    student_z_all = z_all[:, 1].reshape(all_rows, BOT)
+    own_student = lax.optimization_barrier(protos.astype(narrow)).astype(single)
+    own_teacher = lax.optimization_barrier(proto_teacher.astype(narrow)).astype(single)
+    unit_student = unit_rows(own_student).astype(narrow)
+    unit_teacher = unit_rows(own_teacher).astype(narrow)
+    protos_here = protos.shape[0]
+    own_centre = lax.dynamic_slice(centre, (me * protos_here,), (protos_here,))
+    teacher_logits = contract("rb,kb->rk", teacher_z_all, unit_teacher)
+    logits = contract("rb,kb->rk", student_z_all, unit_student)
+    teacher_exp = jnp.exp((teacher_logits - own_centre) / tau_teacher)
+    student_exp = jnp.exp(logits / tau_student)
+    sums = jnp.stack(
+        [
+            jnp.sum(teacher_exp, axis=1),
+            jnp.sum(student_exp, axis=1),
+            jnp.sum(teacher_exp * logits, axis=1),
+        ]
+    )
+    sums = cube_sum(sums)
+    is_class = (jnp.arange(all_rows) % 17) == 0
+    row_weight = all_kept * jnp.where(is_class, 1.0, 1.0 / 16.0)
+    cross = jnp.log(sums[1]) - sums[2] / (sums[0] * tau_student)
+    loss_total = jnp.sum(row_weight * cross)
+    count_total = jnp.sum(jnp.where(is_class, all_kept, 0.0))
+    centre_sum = jnp.sum(
+        jnp.where(is_class, all_kept, 0.0)[:, None] * teacher_logits, axis=0
+    )
+    own_new_centre = centre_keep * own_centre + (1.0 - centre_keep) * centre_sum / count_total
+    new_centre = cube_gather([own_new_centre.reshape(1, protos_here)], ("cxyab",))[0].reshape(-1)
+    scale = row_weight / tau_student
+    grad_logits = (
+        student_exp * (scale / sums[1])[:, None] - teacher_exp * (scale / sums[0])[:, None]
+    ).astype(narrow)
+    z_partial = contract("rk,kb->rb", grad_logits, unit_student)
+    proto_unit_grad = contract("rk,rb->kb", grad_logits, student_z_all)
+    proto_grad = jax.vjp(unit_rows, own_student)[1](proto_unit_grad)[0]
+    grad_unit_z = cube_scatter(
+        [split_bits(z_partial.reshape(count, rows_here, BOT))], ("cbayx",), ("cbayx",)
+    )[0]
+
+    chosen, normed_wide, pre_one, hidden_wide, pre_two, hidden_two, bottleneck = head_saved
+    w_one, w_two, w_three = student_head
+    grad_bottle = jax.vjp(unit_rows, bottleneck)[1](grad_unit_z)[0].astype(narrow)
+    grad_third = contract("rh,rb->hb", hidden_two, grad_bottle)
+    grad_pre_two = gelu_back(pre_two, contract("rb,hb->rh", grad_bottle, w_three)).astype(narrow)
+    grad_second = contract("rh,rk->hk", hidden_wide, grad_pre_two)
+    grad_hidden = cut_columns(contract("rk,hk->rh", grad_pre_two, w_two), first_w2, first_w3, D)
+    grad_pre_one = gelu_back(pre_one, grad_hidden).astype(narrow)
+    grad_first = contract("rd,rh->dh", normed_wide, grad_pre_one)
+    grad_normed = cut_columns(contract("rh,dh->rd", grad_pre_one, w_one), 1, first_w2, 0)
+    extras = student_parts[2].astype(single)
+    grad_chosen, grad_gain, grad_bias = jax.vjp(layer_norm, chosen, extras[2], extras[3])[1](
+        grad_normed
+    )
+    third_rows = grad_third.reshape(BOT, ROW).astype(narrow)
+    third_pieces = []
+    for i in range(first_w3, count):
+        at = bounds[i] - (D + HID)
+        third_pieces.append(third_rows[at : at + sizes[i]])
+        third_pieces.append(jnp.zeros((slot - sizes[i], ROW), narrow))
+    head_grads = jnp.concatenate(
+        [
+            jnp.zeros((slot, ROW), narrow),
+            grad_first.astype(narrow),
+            grad_second.astype(narrow),
+        ]
+        + third_pieces
+    ).reshape(count, slot, ROW)
+    head_block_grad = scatter_rows(head_grads, (768, 768), 2).astype(single)
+    image_index = jnp.arange(images_here, dtype=jnp.int32)[:, None]
+    grad_stream = (
+        jnp.zeros(stream.shape, single)
+        .at[image_index, row_index]
+        .add(grad_chosen.reshape(images_here, 17, D))
+    )
+
+    layer_block_grads = [None] * LAYERS
+    vector_grads = [None] * LAYERS
+    for layer_index in reversed(range(LAYERS)):
+        grad_stream, grads = block_backward(
+            grad_stream, student_layers[layer_index], saved_layers[layer_index]
+        )
+        grad_qkv, grad_proj, grad_up, grad_down, vector_grads[layer_index] = grads
+        flat = jnp.concatenate(
+            [
+                grad_qkv.astype(narrow).reshape(3 * D, D),
+                grad_proj.astype(narrow),
+                grad_up.astype(narrow).reshape(FF, D),
+                grad_down.astype(narrow),
+            ]
+        ).reshape(count, block_rows, D)
+        layer_block_grads[layer_index] = scatter_rows(flat, (64, 48), 1).astype(single)
+    grad_patch_w, grad_position, grad_cls, grad_mask_token = embed_backward(
+        grad_stream, patches, masked_here
+    )
+    small = jnp.concatenate(
+        [
+            grad_patch_w,
+            grad_position,
+            jnp.stack([grad_cls, grad_mask_token, grad_gain, grad_bias]),
+        ]
+        + vector_grads
+    )
+    small_rows = -(-small.shape[0] // count)
+    small = jnp.pad(small, ((0, small_rows * count - small.shape[0]), (0, 0)))
+    small_block = cube_scatter(
+        [split_bits(small.reshape(count, small_rows, D))], ("cxyba",), (BITS,)
+    )[0]
+    layer_block = jnp.stack(layer_block_grads)
+
+    square_local = (
+        jnp.sum(head_block_grad * head_block_grad)
+        + jnp.sum(layer_block * layer_block)
+        + jnp.sum(small_block * small_block)
+        + jnp.sum(proto_grad * proto_grad)
+    )
+    square_total = cube_sum(square_local.reshape(1, 1))[0, 0]
+    small_all = cube_gather([small_block], ("cxyab",))[0].reshape(small_rows * count, D)
+    embed_grad = small_all[:EMBED_ROWS].reshape(-1)
+    vector_grad = small_all[EMBED_ROWS : EMBED_ROWS + 6 * LAYERS].reshape(LAYERS, 6 * D)
+
+    layer_block = layer_block.reshape(LAYERS, block)
+    behind = lax.ppermute(layer_block[:, :tail], "dev", step_pairs(count, -1))
+    behind = jnp.where(me == count - 1, vector_grad, behind)
+    layer_grad = lax.dynamic_slice(
+        jnp.concatenate([layer_block, behind], axis=1), (0, drift * me), (LAYERS, layer_piece)
+    )
+    last_rows = lax.dynamic_slice(
+        head_block_grad, (jnp.array(sizes, jnp.int32)[me] - GROUP, 0), (GROUP, ROW)
+    )
+    previous = lax.ppermute(last_rows, "dev", step_pairs(count, 1))
+    joined = jnp.concatenate(
+        [previous.reshape(-1), head_block_grad.reshape(-1), jnp.zeros((head_span,), single)]
+    )
+    stem_grad = lax.dynamic_slice(joined, (head_span - start_here,), (stem_piece,))
+    second_part = jnp.concatenate([embed_grad[stem_piece:], stem_grad[rest:]])
+    stem_grad = jnp.where(
+        me == 0, embed_grad[:stem_piece], jnp.where(me == 1, second_part, stem_grad)
+    )
+
+    grad_norm = jnp.sqrt(square_total) / count_total
+    factor = jnp.minimum(1.0, clip_limit / (grad_norm + 1e-06)) / count_total
+    stem_set = adam_update(stem, stem_moment, stem_second, stem_grad * factor, stem_teacher)
+    layer_set = adam_update(layers, layer_moment, layer_second, layer_grad * factor, layer_teacher)
+    proto_set = adam_update(protos, proto_moment, proto_second, proto_grad * factor, proto_teacher)
+    return (loss_total, count_total, grad_norm, new_centre) + stem_set + layer_set + proto_set
+
+
 def solution(mesh):
+    count = mesh.shape["dev"]
+    stem_length = -(-(EMBED_FLAT + HEAD_ROWS * ROW) // count) * count
+    close = fits(count, stem_length // count, (MATRIX_ROWS + 6) * D // count)
     placed = (
         P("dev", None, None),
         P("dev", None),
@@ -412,7 +834,7 @@
         P(),
     )
     return jax.shard_map(
-        local,
+        close_local if close else spread_local,
         mesh=mesh,
         in_specs=placed,
         out_specs=(

time: 3050 us -> 1180 us (0.39)
  waiting for transfers between devices: 1780 us -> 369 us
  local copies, waits for them, and re-layouts: 786 us -> 308 us
  starting transfers between devices: 0.42 us -> 101 us
  matrix products: 259 us -> 182 us
  blocking collectives: 47.1 us -> 0 us
  other arithmetic: 130 us -> 168 us
    unnamed x7 -> x2, waiting for transfers between devices: 1080 us -> 0.03 us
    reduce_scatter x1 -> x0, waiting for transfers between devices: 698 us -> none  [local(): lax.psum_scatter(grad_unit_protos, 'dev', scatter_dimension=0, tiled=True)]
    unnamed x464 -> x503, local copies, waits for them, and re-layouts: 412 us -> 69.6 us
    ppermute x0 -> x95, waiting for transfers between devices: none -> 311 us  [the longest x55 197 us: cube_scatter(): lax.ppermute(s, 'dev', pairs(count, MASKS[order[turn]]))]
    slice x40 -> x63, local copies, waits for them, and re-layouts: 250 us -> 102 us  [the longest x1 17.1 us: close_local(): even[m * stem_piece:(m + 1) * stem_piece]]
    ppermute x0 -> x95, starting transfers between devices: none -> 101 us  [the longest x55 44.2 us: cube_scatter(): lax.ppermute(s, 'dev', pairs(count, MASKS[order[turn]]))]
    dot_general x64, matrix products: 259 us -> 182 us  [contract(): return jnp.einsum(form, left_arg, right_arg, preferred_element_type=single)]
    all_gather x2, waiting for transfers between devices: 0.01 us -> 57.2 us  [the longest x1 29.2 us: close_local(): gathered_head = lax.all_gather(head_blocks, 'dev', axis=0)]
  transfers between devices with their start and end apart: 5 -> 97, of which waited for: 3 -> 58; matrix products, arithmetic and copies ran while one was open for 19% -> 37% of each run, Pallas kernels for 0% -> 0%
where the time goes in v1:
time: 1180 us; the launch traced here: 1160 us
  waiting for transfers between devices  369 us (31%)
  local copies, waits for them, and re-layouts  308 us (26%)
  matrix products  182 us (15%)
  other arithmetic  168 us (14%)
  starting transfers between devices  101 us (9%)
  between operations  30.7 us (3%)
    ppermute x55, waiting for transfers between devices, cube_scatter(): lax.ppermute(s, 'dev', pairs(count, MASKS[order[turn]]))  197 us
    dot_general x64, matrix products, contract(): return jnp.einsum(form, left_arg, right_arg, preferred_element_type=single)  182 us
    unnamed x503, local copies, waits for them, and re-layouts  69.6 us
    ppermute x4, waiting for transfers between devices, close_local(): got = lax.ppermute(spread, 'dev', moves)  57.8 us
    ppermute x55, starting transfers between devices, cube_scatter(): lax.ppermute(s, 'dev', pairs(count, MASKS[order[turn]]))  44.2 us
    ppermute x20, waiting for transfers between devices, cube_gather(): lax.ppermute(h, 'dev', pairs(count, MASKS[order[turn]]))  43.8 us
    all_gather x1, waiting for transfers between devices, close_local(): gathered_head = lax.all_gather(head_blocks, 'dev', axis=0)  29.2 us
    all_gather x1, waiting for transfers between devices, close_local(): gathered = lax.all_gather(layer_blocks, 'dev', axis=0)  28 us
  transfers between devices with their start and end apart: 97, of which 58 were waited for; matrix products, arithmetic and copies ran while one was open for 37% of the time, Pallas kernels for 0%

profile of v1, /device:TPU:8, one launch (start us, length us, event | category | flops | bytes accessed | tf_op | source)
XLA Modules:
  0.0 1157.8 jit_solution(14566314511081011464)
XLA Ops:
  38.9 9.3 broadcast_select_fusion
  71.8 32.9 %collective-permute-done.7 = bf16[1,373656]{1,0:T(2,128)(2,1)} collective-permute-done((bf16[1,373656]{1,0:T(2,128)(2,1)}, bf16[1,373656]{1,0:T(2,128)(2,1)}, u32[]{:S(2)}, u32[]{:S(2)}) %collective-permute-start.7) | collective-permute-done | bytes 747344 | tf_op jit(solution)/shard_map/ppermute | solution.py:573
  113.5 12.4 %dynamic-update-slice.8 = bf16[2,413260]{1,0:T(2,128)(2,1)} dynamic-update-slice(bf16[2,413260]{1,0:T(2,128)(2,1)} %constant_dynamic-update-slice_fusion, bf16[2,182220]{1,0:T(2,128)(2,1)S(1)} %copy-done.29, s32[]{} %constant.406, s32[]{} %constant.433) | dynamic-update-slice | bytes 1457764
  126.9 14.0 %collective-permute-done.8 = bf16[1,373656]{1,0:T(2,128)(2,1)} collective-permute-done((bf16[1,373656]{1,0:T(2,128)(2,1)S(1)}, bf16[1,373656]{1,0:T(2,128)(2,1)}, u32[]{:S(2)}, u32[]{:S(2)}) %collective-permute-start.8) | collective-permute-done | bytes 747344 | tf_op jit(solution)/shard_map/ppermute | solution.py:573
  154.1 14.6 %dynamic-update-slice.10 = bf16[2,413260]{1,0:T(2,128)(2,1)} dynamic-update-slice(bf16[2,413260]{1,0:T(2,128)(2,1)} %dynamic-update-slice.9, bf16[2,196608]{1,0:T(2,128)(2,1)S(1)} %broadcast_in_dim.105, s32[]{} %constant.406, s32[]{} %constant.435) | dynamic-update-slice | bytes 1572868 | tf_op jit(solution)/shard_map/concatenate | solution.py:554
  168.7 10.9 collective-permute-done.9
  203.1 17.1 %slice_reduce_fusion.1 = (bf16[182220]{0:T(1024)(128)(2,1)}, bf16[182220]{0:T(1024)(128)(2,1)S(1)}) fusion(bf16[1,373656]{1,0:T(2,128)(2,1)S(1)} %copy-done.48), kind=kLoop, calls=%fused_computation.312 | loop fusion | bytes 1457760 | tf_op jit(solution)/shard_map/slice | solution.py:584
  230.0 28.0 %all-gather.3.cloned.1.call-done = bf16[32,4,144,384]{3,2,0,1:T(8,128)(2,1)} async-done(((bf16[1,4,144,384]{3,2,0,1:T(8,128)(2,1)}), bf16[32,4,144,384]{3,2,0,1:T(8,128)(2,1)}) %all-gather.3.cloned.1.call-update) | async-done | bytes 14155792 | tf_op jit(solution)/shard_map/all_gather | solution.py:548
  269.9 9.7 fusion.385
  383.4 29.2 %all-gather.5.cloned.1.call-done = bf16[32,2,96,2048]{3,2,0,1:T(8,128)(2,1)} async-done(((bf16[1,2,96,2048]{3,2,0,1:T(8,128)(2,1)}), bf16[32,2,96,2048]{3,2,0,1:T(8,128)(2,1)}) %all-gather.5.cloned.1.call-update) | async-done | bytes 25165840 | tf_op jit(solution)/shard_map/all_gather | solution.py:566
  421.2 9.9 slice_bitcast_fusion.1
  437.7 10.0 fusion.383
  481.4 10.4 collective-permute-done.16
  555.0 11.6 collective-permute-done.24
  653.0 10.3 fusion.129
  663.2 10.3 fusion.126
  718.7 10.2 fusion.135
  728.9 10.3 fusion.132
  783.4 9.1 concatenate.694
  876.0 8.7 collective-permute-done.65
  964.2 18.7 %collective-permute-done.91 = f32[8,27,384]{2,1,0:T(8,128)S(1)} collective-permute-done((f32[8,27,384]{2,1,0:T(8,128)S(1)}, f32[8,27,384]{2,1,0:T(8,128)S(1)}, u32[]{:S(2)}, u32[]{:S(2)}) %collective-permute-start.91) | collective-permute-done | bytes 331808 | tf_op jit(solution)/shard_map/ppermute | solution.py:441
  985.0 21.6 %collective-permute-done.39 = bf16[2,2,2,96,512]{4,3,2,1,0:T(8,128)(2,1)S(1)} collective-permute-done((bf16[2,2,2,96,512]{4,3,2,1,0:T(8,128)(2,1)S(1)}, bf16[2,2,2,96,512]{4,3,2,1,0:T(8,128)(2,1)S(1)}, u32[]{:S(2)}, u32[]{:S(2)}) %collective-permute-start.39) | collective-permute-done | bytes 786464 | tf_op jit(solution)/shard_map/ppermute | solution.py:470
  1032.1 13.0 %collective-permute-done.41 = bf16[2,96,512]{2,1,0:T(8,128)(2,1)S(1)} collective-permute-done((bf16[2,96,512]{2,1,0:T(8,128)(2,1)}, bf16[2,96,512]{2,1,0:T(8,128)(2,1)S(1)}, u32[]{:S(2)}, u32[]{:S(2)}) %collective-permute-start.41) | collective-permute-done | bytes 196640 | tf_op jit(solution)/shard_map/ppermute | solution.py:470
  1064.8 13.9 %collective-permute-done.36 = bf16[2,96,768]{2,1,0:T(8,128)(2,1)S(1)} collective-permute-done((bf16[2,96,768]{2,1,0:T(8,128)(2,1)S(1)}, bf16[2,96,768]{2,1,0:T(8,128)(2,1)S(1)}, u32[]{:S(2)}, u32[]{:S(2)}) %collective-permute-start.36) | collective-permute-done | bytes 294944 | tf_op jit(solution)/shard_map/ppermute | solution.py:470
  (1194 shorter events, 781.1 us)
Async XLA Ops:
  7.2 250.7 %all-gather.3.cloned.1.call-start = ((), (), s32[]{:S(2)}) async-start(), calls=%async_computation | async-start | bytes 14598144 | tf_op jit(solution)/shard_map/all_gather | solution.py:548
  25.6 122.0 %collective-permute-start.11 = (bf16[4,2304]{1,0:T(4,128)(2,1)}, bf16[4,2304]{1,0:T(4,128)(2,1)}, u32[]{:S(2)}, u32[]{:S(2)}) collective-permute-start(bf16[4,2304]{1,0:T(4,128)(2,1)} %slice.1287), channel_id=1, source_target_pairs={{0,1},{1,2},{2,3},{3,4},{4,5},{5,6},{6,7},{7,8},{8,9},{9,10},{10,1... | collective-permute-start | bytes 55304 | tf_op jit(solution)/shard_map/ppermute | solution.py:543
  27.7 122.2 %collective-permute-start.12 = (bf16[2,32768]{1,0:T(2,128)(2,1)S(1)}, bf16[2,32768]{1,0:T(2,128)(2,1)S(1)}, u32[]{:S(2)}, u32[]{:S(2)}) collective-permute-start(bf16[2,32768]{1,0:T(2,128)(2,1)S(1)} %slice.1328), channel_id=1, source_target_pairs={{1,0},{2,1},{3,2},{4,3},{5,4},{6,5},{7,6},{8,7},{9,8},{10,9},{11,1... | collective-permute-start | bytes 393224 | tf_op jit(solution)/shard_map/ppermute | solution.py:551
  33.3 92.6 %collective-permute-start = (f32[1,1,34]{2,1,0:T(1,128)S(1)}, f32[1,1,34]{2,1,0:T(1,128)S(1)}, u32[]{:S(2)}, u32[]{:S(2)}) collective-permute-start(f32[1,1,34]{2,1,0:T(1,128)S(1)} %broadcast_in_dim_reshape.6), channel_id=1, source_target_pairs={{0,2},{1,3},{2,0},{3,1},{4,6},{5,7},{6,4},{7,5},{8,10},{9,11},{10,... | collective-permute-start | bytes 416 | tf_op jit(solution)/shard_map/ppermute | solution.py:441
  48.3 56.4 %collective-permute-start.7 = (bf16[1,373656]{1,0:T(2,128)(2,1)}, bf16[1,373656]{1,0:T(2,128)(2,1)}, u32[]{:S(2)}, u32[]{:S(2)}) collective-permute-start(bf16[1,373656]{1,0:T(2,128)(2,1)} %broadcast_select_fusion), channel_id=1, source_target_pairs={{0,8},{1,9},{24,16},{25,17}} | collective-permute-start | bytes 2241944 | tf_op jit(solution)/shard_map/ppermute | solution.py:573
  109.1 31.8 %collective-permute-start.8 = (bf16[1,373656]{1,0:T(2,128)(2,1)S(1)}, bf16[1,373656]{1,0:T(2,128)(2,1)}, u32[]{:S(2)}, u32[]{:S(2)}) collective-permute-start(bf16[1,373656]{1,0:T(2,128)(2,1)S(1)} %broadcast_select_fusion.1), channel_id=1, source_target_pairs={{0,2},{1,3},{24,26},{25,27},{8,10},{9,11},{16,18},{17,19}} | collective-permute-start | bytes 2241944 | tf_op jit(solution)/shard_map/ppermute | solution.py:573
  126.4 338.0 %collective-permute-start.1 = (f32[2,1,34]{2,1,0:T(1,128)}, f32[2,1,34]{2,1,0:T(1,128)}, u32[]{:S(2)}, u32[]{:S(2)}) collective-permute-start(f32[2,1,34]{2,1,0:T(1,128)} %broadcast_select_fusion.13), channel_id=1, source_target_pairs={{0,4},{1,5},{2,6},{3,7},{4,0},{5,1},{6,2},{7,3},{8,12},{9,13},{10,... | collective-permute-start | bytes 824 | tf_op jit(solution)/shard_map/ppermute | solution.py:441
  145.2 34.3 %collective-permute-start.9 = (bf16[1,373656]{1,0:T(2,128)(2,1)S(1)}, bf16[1,373656]{1,0:T(2,128)(2,1)}, u32[]{:S(2)}, u32[]{:S(2)}) collective-permute-start(bf16[1,373656]{1,0:T(2,128)(2,1)S(1)} %broadcast_select_fusion.2), channel_id=1, source_target_pairs={{0,4},{1,5},{24,28},{25,29},{8,12},{9,13},{16,20},{17,21},{2,6},{3... | collective-permute-start | bytes 2241944 | tf_op jit(solution)/shard_map/ppermute | solution.py:573
  149.8 262.8 %all-gather.5.cloned.1.call-start = ((), (), s32[]{:S(2)}) async-start(), calls=%async_computation.1 | async-start | bytes 25952256 | tf_op jit(solution)/shard_map/all_gather | solution.py:566
  544.5 29.0 %collective-permute-start.86 = (f32[8,1,2048]{2,1,0:T(1,128)}, f32[8,1,2048]{2,1,0:T(1,128)}, u32[]{:S(2)}, u32[]{:S(2)}) collective-permute-start(f32[8,1,2048]{2,1,0:T(1,128)} %copy.499), channel_id=1, source_target_pairs={{0,8},{1,9},{2,10},{3,11},{4,12},{5,13},{6,14},{7,15},{8,0},{9,1},... | collective-permute-start | bytes 196616 | tf_op jit(solution)/shard_map/ppermute | solution.py:441
  760.1 196.0 %collective-permute-start.38 = (bf16[2,2,2,2,96,512]{5,4,3,2,1,0:T(8,128)(2,1)}, bf16[2,2,2,2,96,512]{5,4,3,2,1,0:T(8,128)(2,1)}, u32[]{:S(2)}, u32[]{:S(2)}) collective-permute-start(bf16[2,2,2,2,96,512]{5,4,3,2,1,0:T(8,128)(2,1)} %fusion.115), channel_id=1, source_target_pairs={{0,1},{1,0},{2,3},{3,2},{4,5},{5,4},{6,7},{7,6},{8,9},{9,8},{10,11... | collective-permute-start | bytes 4718600 | tf_op jit(solution)/shard_map/ppermute | solution.py:470
  763.9 243.1 %collective-permute-start.33 = (bf16[2,2,2,2,96,768]{5,4,3,2,1,0:T(8,128)(2,1)}, bf16[2,2,2,2,96,768]{5,4,3,2,1,0:T(8,128)(2,1)}, u32[]{:S(2)}, u32[]{:S(2)}) collective-permute-start(bf16[2,2,2,2,96,768]{5,4,3,2,1,0:T(8,128)(2,1)} %get-tuple-element.219), channel_id=1, source_target_pairs={{0,1},{1,0},{2,3},{3,2},{4,5},{5,4},{6,7},{7,6},{8,9},{9,8},{10,11... | collective-permute-start | bytes 7077896 | tf_op jit(solution)/shard_map/ppermute | solution.py:470
  767.6 34.5 %collective-permute-start.68 = (bf16[2,2,2,2,32,384]{5,4,2,3,1,0:T(8,128)(2,1)}, bf16[2,2,2,2,32,384]{5,4,2,3,1,0:T(8,128)(2,1)}, u32[]{:S(2)}, u32[]{:S(2)}) collective-permute-start(bf16[2,2,2,2,32,384]{5,4,2,3,1,0:T(8,128)(2,1)} %select_bitcast_fusion.11), channel_id=1, source_target_pairs={{0,1},{1,0},{2,3},{3,2},{4,5},{5,4},{6,7},{7,6},{8,9},{9,8},{10,11... | collective-permute-start | bytes 1179656 | tf_op jit(solution)/shard_map/ppermute | solution.py:470
  769.5 35.2 %collective-permute-start.63 = (bf16[2,2,2,2,48,384]{5,4,1,0,3,2:T(8,128)(2,1)}, bf16[2,2,2,2,48,384]{5,4,1,0,3,2:T(8,128)(2,1)}, u32[]{:S(2)}, u32[]{:S(2)}) collective-permute-start(bf16[2,2,2,2,48,384]{5,4,1,0,3,2:T(8,128)(2,1)} %select_bitcast_fusion.7), channel_id=1, source_target_pairs={{0,1},{1,0},{2,3},{3,2},{4,5},{5,4},{6,7},{7,6},{8,9},{9,8},{10,11... | collective-permute-start | bytes 1769480 | tf_op jit(solution)/shard_map/ppermute | solution.py:470
  771.4 81.5 %collective-permute-start.58 = (bf16[2,2,2,2,64,384]{5,4,1,0,2,3:T(8,128)(2,1)}, bf16[2,2,2,2,64,384]{5,4,1,0,2,3:T(8,128)(2,1)}, u32[]{:S(2)}, u32[]{:S(2)}) collective-permute-start(bf16[2,2,2,2,64,384]{5,4,1,0,2,3:T(8,128)(2,1)} %select_bitcast_fusion.4), channel_id=1, source_target_pairs={{0,1},{1,0},{2,3},{3,2},{4,5},{5,4},{6,7},{7,6},{8,9},{9,8},{10,11... | collective-permute-start | bytes 2359304 | tf_op jit(solution)/shard_map/ppermute | solution.py:470
  825.2 30.2 %collective-permute-start.43 = (bf16[2,2,2,2,64,384]{5,4,1,0,2,3:T(8,128)(2,1)S(1)}, bf16[2,2,2,2,64,384]{5,4,1,0,2,3:T(8,128)(2,1)S(1)}, u32[]{:S(2)}, u32[]{:S(2)}) collective-permute-start(bf16[2,2,2,2,64,384]{5,4,1,0,2,3:T(8,128)(2,1)S(1)} %select_bitcast_fusion.5), channel_id=1, source_target_pairs={{0,1},{1,0},{2,3},{3,2},{4,5},{5,4},{6,7},{7,6},{8,9},{9,8},{10,11... | collective-permute-start | bytes 2359304 | tf_op jit(solution)/shard_map/ppermute | solution.py:470
  852.8 159.8 %collective-permute-start.28 = (bf16[2,2,2,2,96,768]{5,4,1,0,2,3:T(8,128)(2,1)S(1)}, bf16[2,2,2,2,96,768]{5,4,1,0,2,3:T(8,128)(2,1)S(1)}, u32[]{:S(2)}, u32[]{:S(2)}) collective-permute-start(bf16[2,2,2,2,96,768]{5,4,1,0,2,3:T(8,128)(2,1)S(1)} %select_bitcast_fusion.1), channel_id=1, source_target_pairs={{0,1},{1,0},{2,3},{3,2},{4,5},{5,4},{6,7},{7,6},{8,9},{9,8},{10,11... | collective-permute-start | bytes 7077896 | tf_op jit(solution)/shard_map/ppermute | solution.py:470
  868.7 48.7 %collective-permute-start.59 = (bf16[2,2,2,64,384]{4,3,1,0,2:T(8,128)(2,1)S(1)}, bf16[2,2,2,64,384]{4,3,1,0,2:T(8,128)(2,1)S(1)}, u32[]{:S(2)}, u32[]{:S(2)}) collective-permute-start(bf16[2,2,2,64,384]{4,3,1,0,2:T(8,128)(2,1)S(1)} %select_bitcast_fusion.12), channel_id=1, source_target_pairs={{0,2},{1,3},{2,0},{3,1},{4,6},{5,7},{6,4},{7,5},{8,10},{9,11},{10,... | collective-permute-start | bytes 1179656 | tf_op jit(solution)/shard_map/ppermute | solution.py:470
  958.2 48.4 %collective-permute-start.39 = (bf16[2,2,2,96,512]{4,3,2,1,0:T(8,128)(2,1)S(1)}, bf16[2,2,2,96,512]{4,3,2,1,0:T(8,128)(2,1)S(1)}, u32[]{:S(2)}, u32[]{:S(2)}) collective-permute-start(bf16[2,2,2,96,512]{4,3,2,1,0:T(8,128)(2,1)S(1)} %select_bitcast_fusion.6), channel_id=1, source_target_pairs={{0,24},{1,25},{2,26},{3,27},{4,28},{5,29},{6,30},{7,31},{8,16},{9,... | collective-permute-start | bytes 2359304 | tf_op jit(solution)/shard_map/ppermute | solution.py:470
  961.3 63.6 %collective-permute-start.94 = (f32[2,2304]{1,0:T(2,128)}, f32[2,2304]{1,0:T(2,128)}, u32[]{:S(2)}, u32[]{:S(2)}) collective-permute-start(f32[2,2304]{1,0:T(2,128)} %slice.1552), channel_id=1, source_target_pairs={{1,0},{2,1},{3,2},{4,3},{5,4},{6,5},{7,6},{8,7},{9,8},{10,9},{11,1... | collective-permute-start | bytes 55304 | tf_op jit(solution)/shard_map/ppermute | solution.py:788
  983.3 36.6 %collective-permute-start.92 = (f32[16,27,384]{2,0,1:T(8,128)S(1)}, f32[16,27,384]{2,0,1:T(8,128)S(1)}, u32[]{:S(2)}, u32[]{:S(2)}) collective-permute-start(f32[16,27,384]{2,0,1:T(8,128)S(1)} %copy.500), channel_id=1, source_target_pairs={{0,24},{1,25},{2,26},{3,27},{4,28},{5,29},{6,30},{7,31},{8,16},{9,... | collective-permute-start | bytes 1990664 | tf_op jit(solution)/shard_map/ppermute | solution.py:441
  1011.9 34.6 %collective-permute-start.34 = (bf16[2,2,2,96,768]{4,3,2,1,0:T(8,128)(2,1)}, bf16[2,2,2,96,768]{4,3,2,1,0:T(8,128)(2,1)}, u32[]{:S(2)}, u32[]{:S(2)}) collective-permute-start(bf16[2,2,2,96,768]{4,3,2,1,0:T(8,128)(2,1)} %fusion.149), channel_id=1, source_target_pairs={{0,4},{1,5},{2,6},{3,7},{4,0},{5,1},{6,2},{7,3},{8,12},{9,13},{10,... | collective-permute-start | bytes 3538952 | tf_op jit(solution)/shard_map/ppermute | solution.py:470
  1015.1 34.0 %collective-permute-start.29 = (bf16[2,2,2,96,768]{4,3,1,0,2:T(8,128)(2,1)}, bf16[2,2,2,96,768]{4,3,1,0,2:T(8,128)(2,1)}, u32[]{:S(2)}, u32[]{:S(2)}) collective-permute-start(bf16[2,2,2,96,768]{4,3,1,0,2:T(8,128)(2,1)} %select_bitcast_fusion.2), channel_id=1, source_target_pairs={{0,2},{1,3},{2,0},{3,1},{4,6},{5,7},{6,4},{7,5},{8,10},{9,11},{10,... | collective-permute-start | bytes 3538952 | tf_op jit(solution)/shard_map/ppermute | solution.py:470
  1094.8 48.4 %collective-permute-start.93 = (f32[16,2048]{1,0:T(8,128)}, f32[16,2048]{1,0:T(8,128)}, u32[]{:S(2)}, u32[]{:S(2)}) collective-permute-start(f32[16,2048]{1,0:T(8,128)} %constant_dynamic-slice_fusion), channel_id=1, source_target_pairs={{0,1},{1,2},{2,3},{3,4},{4,5},{5,6},{6,7},{7,8},{8,9},{9,10},{10,1... | collective-permute-start | bytes 393224 | tf_op jit(solution)/shard_map/ppermute | solution.py:796
  (314 other events, 4120.1 us)
Sparse Core Ops, SparseCore 0:
  149.9 107.9 all-gather.2
  260.8 151.8 all-gather.4

commit v2 on v1

--- a/solution.py
+++ b/solution.py
@@ -1,6 +1,8 @@
 import jax
 import jax.numpy as jnp
 from jax import lax
+from jax.experimental import pallas as pl
+from jax.experimental.pallas import tpu as pltpu
 from jax.sharding import PartitionSpec as P
 
 D = 384
@@ -399,7 +401,7 @@
 EMBED_FLAT = EMBED_ROWS * D
 HEAD_ROWS = D + HID + BOT
 BITS = ("b", "a", "y", "x", "c")
-MASKS = {"c": 1, "x": 2, "y": 4, "a": 8, "b": 24}
+MASKS = {"c": 1, "x": 2, "y": 4, "a": 8, "b": 24, "g": 8}
 
 
 def head_bounds(count, stem_piece):
@@ -429,25 +431,22 @@
 
 
 def bit_flags(me):
-    return {name: (me >> (len(BITS) - 1 - place)) & 1 for place, name in enumerate(BITS)}
-
-
-def cube_gather(parts, orders):
+    flags = {name: (me >> (len(BITS) - 1 - place)) & 1 for place, name in enumerate(BITS)}
+    flags["g"] = flags["a"] ^ flags["b"]
+    return flags
+
+
+def cube_gather(part, order):
     count = 1 << len(BITS)
     flags = bit_flags(lax.axis_index("dev"))
-    held = [part[None] for part in parts]
-    for turn in range(len(BITS)):
-        got = [
-            lax.ppermute(h, "dev", pairs(count, MASKS[order[turn]])) for h, order in zip(held, orders)
-        ]
-        held = [
-            jnp.where(
-                flags[order[turn]] == 1,
-                jnp.concatenate([g, h], axis=0),
-                jnp.concatenate([h, g], axis=0),
-            )
-            for h, g, order in zip(held, got, orders)
-        ]
+    held = part[None]
+    for name in order:
+        got = lax.ppermute(held, "dev", pairs(count, MASKS[name]))
+        held = jnp.where(
+            flags[name] == 1,
+            jnp.concatenate([got, held], axis=0),
+            jnp.concatenate([held, got], axis=0),
+        )
     return held
 
 
@@ -456,22 +455,21 @@
     flags = bit_flags(lax.axis_index("dev"))
     held = list(parts)
     names = [list(a) for a in axes]
-    for turn in range(len(BITS)):
+    for turn in range(len(orders[0])):
         sent, kept = [], []
         for h, order, name in zip(held, orders, names):
             place = name.index(order[turn])
             low = lax.index_in_dim(h, 0, place, keepdims=False)
             high = lax.index_in_dim(h, 1, place, keepdims=False)
             flag = flags[order[turn]] == 1
-            sent.append(jnp.where(flag, low, high))
+            out = jnp.where(flag, low, high)
+            sent.append(out if order[turn] == "c" else out.astype(narrow))
             kept.append(jnp.where(flag, high, low))
             name.pop(place)
         got = [
             lax.ppermute(s, "dev", pairs(count, MASKS[order[turn]])) for s, order in zip(sent, orders)
         ]
-        held = [
-            (k.astype(single) + g.astype(single)).astype(k.dtype) for k, g in zip(kept, got)
-        ]
+        held = [k + g.astype(single) for k, g in zip(kept, got)]
     return held
 
 
@@ -485,17 +483,145 @@
     return array.reshape((2,) * len(BITS) + array.shape[1:])
 
 
-def scatter_rows(array, cuts, axis):
-    points = [0, cuts[0], cuts[0] + cuts[1], array.shape[axis]]
-    parts = [
-        split_bits(lax.slice_in_dim(array, points[i], points[i + 1], axis=axis)) for i in range(3)
-    ]
-    done = cube_scatter(parts, ("cxyba", "cyxba", "cbaxy"), (BITS,) * 3)
-    return jnp.concatenate(done, axis=axis - 1)
+def scatter_rows(array):
+    half = array.shape[1] // 2
+    done = cube_scatter(
+        [split_bits(array[:, :half]), split_bits(array[:, half:])], ("cxyba", "cyxba"), (BITS, BITS)
+    )
+    return jnp.concatenate(done, axis=0)
 
 
 def step_pairs(count, step):
     return [(i, i + step) for i in range(count) if 0 <= i + step < count]
+
+
+def lane_rows(length):
+    return -(-length // 1024) * 8
+
+
+def as_lanes(flat):
+    rows = lane_rows(flat.shape[-1])
+    gap = rows * 128 - flat.shape[-1]
+    padded = jnp.pad(flat, [(0, 0)] * (flat.ndim - 1) + [(0, gap)])
+    return padded.reshape(flat.shape[:-1] + (rows, 128))
+
+
+def shifted(line_ref, row, lane, first, rows, stride):
+    spots = lax.broadcasted_iota(jnp.int32, (rows, 128), 1)
+    turn = lax.rem(128 - lane, 128)
+    here = pltpu.roll(line_ref[pl.ds(row + first, rows, stride=stride), :], turn, 1)
+    there = pltpu.roll(line_ref[pl.ds(row + first + 1, rows, stride=stride), :], turn, 1)
+    return jnp.where(spots < 128 - lane, here, there)
+
+
+def blocks_kernel(
+    shape,
+    place_ref,
+    stem_ref,
+    after_ref,
+    layer_ref,
+    before_ref,
+    head_ref,
+    block_ref,
+    embed_ref,
+    vector_ref,
+    line_ref,
+    flat_ref,
+):
+    front, stem_piece, layer_piece, tail = shape
+    stem_lines = stem_ref.shape[1]
+    end_row, end_lane = stem_piece // 128, stem_piece % 128
+    after_lines = after_ref.shape[1]
+    slot = head_ref.shape[1]
+    for model in range(2):
+        line_ref[pl.ds(0, front), :] = jnp.zeros((front, 128), single)
+        line_ref[pl.ds(front, end_row), :] = stem_ref[model, pl.ds(0, end_row), :]
+        turned = pltpu.roll(after_ref[model], end_lane, 1)
+        spots = lax.broadcasted_iota(jnp.int32, (after_lines, 128), 1)
+        line_ref[pl.ds(front + end_row, after_lines), :] = turned
+        line_ref[pl.ds(front + end_row + after_lines, 128), :] = jnp.zeros((128, 128), single)
+        lower = pltpu.roll(turned, 1, 0)
+        first_line = jnp.broadcast_to(stem_ref[model, pl.ds(end_row, 1), :], (after_lines, 128))
+        number = lax.broadcasted_iota(jnp.int32, (after_lines, 128), 0)
+        lower = jnp.where(number == 0, first_line, lower)
+        line_ref[pl.ds(front + end_row, after_lines), :] = jnp.where(spots < end_lane, lower, turned)
+        per_row = ROW // 128
+        for chunk in range(per_row):
+            head_ref[model, :, pl.ds(chunk * 128, 128)] = shifted(
+                line_ref, place_ref[0], place_ref[1], chunk, slot, per_row
+            ).astype(narrow)
+        for chunk in range(D // 128):
+            embed_ref[model, :, pl.ds(chunk * 128, 128)] = shifted(
+                line_ref, place_ref[2], place_ref[3], chunk, embed_ref.shape[1], D // 128
+            ).astype(narrow)
+    tail_lines = tail // 128
+    layer_lines = layer_ref.shape[1]
+    vector_at = tail + layer_piece - tail
+    for part in range(layer_ref.shape[0]):
+        flat_ref[pl.ds(0, tail_lines), :] = before_ref[part]
+        flat_ref[pl.ds(tail_lines, layer_lines), :] = layer_ref[part]
+        for chunk in range(D // 128):
+            block_ref[part, :, pl.ds(chunk * 128, 128)] = shifted(
+                flat_ref, place_ref[4], place_ref[5], chunk, block_ref.shape[1], D // 128
+            ).astype(narrow)
+            vector_ref[part, :, pl.ds(chunk * 128, 128)] = shifted(
+                flat_ref, vector_at // 128, vector_at % 128, chunk, 8, D // 128
+            ).astype(narrow)
+
+
+def own_blocks(place, stems, after, layer_rows, before, shape, slot, block_rows, embed_rows):
+    front, stem_piece, layer_piece, tail = shape
+    lines = front + stem_piece // 128 + after.shape[1] + slot * ROW // 128
+    flats = tail // 128 + layer_rows.shape[1] + 48
+    return pl.pallas_call(
+        lambda *refs: blocks_kernel(shape, *refs),
+        out_shape=[
+            jax.ShapeDtypeStruct((2, slot, ROW), narrow),
+            jax.ShapeDtypeStruct((2 * LAYERS, block_rows, D), narrow),
+            jax.ShapeDtypeStruct((2, embed_rows, D), narrow),
+            jax.ShapeDtypeStruct((2 * LAYERS, 8, D), narrow),
+        ],
+        in_specs=[pl.BlockSpec(memory_space=pltpu.SMEM)] + [pl.BlockSpec(memory_space=pltpu.VMEM)] * 4,
+        out_specs=[pl.BlockSpec(memory_space=pltpu.VMEM)] * 4,
+        scratch_shapes=[pltpu.VMEM((lines, 128), single), pltpu.VMEM((flats, 128), single)],
+        compiler_params=pltpu.CompilerParams(vmem_limit_bytes=40 << 20),
+    )(place, stems, after, layer_rows, before)
+
+
+def shards_kernel(place_ref, head_ref, previous_ref, block_ref, behind_ref, stem_ref, layer_ref, line_ref, flat_ref):
+    per_row = ROW // 128
+    extra = previous_ref.shape[0]
+    slot = head_ref.shape[0]
+    for chunk in range(per_row):
+        spot = pl.ds(chunk * 128, 128)
+        line_ref[pl.ds(chunk, extra, stride=per_row), :] = previous_ref[:, spot]
+        line_ref[pl.ds(extra * per_row + chunk, slot, stride=per_row), :] = head_ref[:, spot]
+    stem_ref[...] = shifted(line_ref, place_ref[0], place_ref[1], 0, stem_ref.shape[0], 1)
+    per_row = D // 128
+    rows = block_ref.shape[1]
+    for part in range(block_ref.shape[0]):
+        for chunk in range(per_row):
+            spot = pl.ds(chunk * 128, 128)
+            flat_ref[pl.ds(chunk, rows, stride=per_row), :] = block_ref[part, :, spot]
+            flat_ref[pl.ds(rows * per_row + chunk, 6, stride=per_row), :] = behind_ref[part, pl.ds(0, 6), spot]
+        layer_ref[part] = shifted(flat_ref, place_ref[2], place_ref[3], 0, layer_ref.shape[1], 1)
+
+
+def own_shards(place, head_grad, previous, block_grad, behind, stem_lines, layer_lines):
+    per_row = ROW // 128
+    lines = (head_grad.shape[0] + previous.shape[0]) * per_row + 256
+    flats = max(block_grad.shape[1] * 3 + 18, layer_lines + 18) + 16
+    return pl.pallas_call(
+        shards_kernel,
+        out_shape=[
+            jax.ShapeDtypeStruct((stem_lines, 128), single),
+            jax.ShapeDtypeStruct((block_grad.shape[0], layer_lines, 128), single),
+        ],
+        in_specs=[pl.BlockSpec(memory_space=pltpu.SMEM)] + [pl.BlockSpec(memory_space=pltpu.VMEM)] * 4,
+        out_specs=[pl.BlockSpec(memory_space=pltpu.VMEM)] * 2,
+        scratch_shapes=[pltpu.VMEM((lines, 128), single), pltpu.VMEM((flats, 128), single)],
+        compiler_params=pltpu.CompilerParams(vmem_limit_bytes=40 << 20),
+    )(place, head_grad, previous, block_grad, behind)
 
 
 def close_local(
@@ -517,7 +643,11 @@
     centre,
 ):
     count = 1 << len(BITS)
+    half = count // 2
     me = lax.axis_index("dev")
+    across = MASKS["b"]
+    student_side = me >= half
+    groups = [list(range(half)), [i ^ across for i in range(half)]]
     images_here = patches.shape[0]
     rows_here = images_here * 17
     stem_piece = stem.shape[0]
@@ -538,56 +668,84 @@
     )
     kept = slot_used.astype(single)
 
-    own_layers = jnp.stack([layer_teacher, layers]).astype(narrow).reshape(2 * LAYERS, layer_piece)
-    own_tail = own_layers[:, layer_piece - tail :]
+    front = 16
+    early_rows = -(-stem_piece // D)
+    late_start = early_rows * D - stem_piece
+    embed_rows = -(-early_rows // 16) * 16
+    own_layers = jnp.concatenate([layer_teacher, layers])
+    own_tail = own_layers[:, layer_piece - tail :].reshape(2 * LAYERS, tail // 128, 128)
     before = lax.ppermute(own_tail, "dev", step_pairs(count, 1))
-    joined = jnp.concatenate([before, own_layers], axis=1)
-    layer_blocks = lax.dynamic_slice(joined, (0, tail - drift * me), (2 * LAYERS, block)).reshape(
-        2 * LAYERS, block_rows, D
-    )
-    gathered = lax.all_gather(layer_blocks, "dev", axis=0)
     head_span = GROUP * ROW
-    own_stems = jnp.stack([stem_teacher, stem]).astype(narrow)
-    after = lax.ppermute(own_stems[:, :head_span], "dev", step_pairs(count, -1))
+    stems = jnp.stack([as_lanes(stem_teacher), as_lanes(stem)])
+    after = lax.ppermute(stems[:, : head_span // 128], "dev", step_pairs(count, -1))
     start_here = jnp.array(starts, jnp.int32)[me]
-    front = -min(starts) + (starts[0] % 128)
-    joined = jnp.concatenate(
-        [
-            jnp.zeros((2, front), narrow),
-            own_stems,
-            after,
-            jnp.zeros((2, slot * ROW), narrow),
-        ],
-        axis=1,
-    )
-    head_blocks = lax.dynamic_slice(joined, (0, front + start_here), (2, slot * ROW)).reshape(
-        2, slot, ROW
-    )
-    gathered_head = lax.all_gather(head_blocks, "dev", axis=0)
-    vectors_flat = lax.ppermute(own_tail, "dev", [(count - 1, 0)]).reshape(1, 2 * LAYERS * tail)
-    seed = jnp.concatenate([own_stems.reshape(1, -1), vectors_flat], axis=1)
-    spread = seed
-    reached = [0, 1]
-    for name in "baxy":
-        moves = [(i, i ^ MASKS[name]) for i in reached]
-        got = lax.ppermute(spread, "dev", moves)
-        targets = [t for s, t in moves]
-        is_target = jnp.array([i in targets for i in range(count)])[me]
-        spread = jnp.where(is_target, got, spread)
-        reached = reached + targets
+    head_at = start_here + front * 128
+    embed_at = front * 128 + jnp.where(me == 0, 0, late_start)
+    block_at = tail - drift * me
+    place = jnp.stack(
+        [head_at // 128, head_at % 128, embed_at // 128, embed_at % 128, block_at // 128, block_at % 128]
+    ).astype(jnp.int32)
+    head_blocks, layer_blocks, embed_blocks, vector_blocks = own_blocks(
+        place,
+        stems,
+        after,
+        as_lanes(own_layers),
+        before,
+        (front, stem_piece, layer_piece, tail),
+        slot,
+        block_rows,
+        embed_rows,
+    )
+
+    other_layers = lax.ppermute(layer_blocks, "dev", pairs(count, across))
+    both_layers = jnp.where(
+        student_side,
+        jnp.stack([other_layers, layer_blocks]),
+        jnp.stack([layer_blocks, other_layers]),
+    )
+    gathered = lax.all_gather(both_layers, "dev", axis=0, axis_index_groups=groups)
+    head_out = jnp.where(student_side, head_blocks[0], head_blocks[1])
+    head_keep = jnp.where(student_side, head_blocks[1], head_blocks[0])
+    head_got = lax.ppermute(head_out, "dev", pairs(count, across))
+    both_head = jnp.where(
+        student_side, jnp.stack([head_got, head_keep]), jnp.stack([head_keep, head_got])
+    )
+    gathered_head = lax.all_gather(both_head, "dev", axis=0, axis_index_groups=groups)
+
+    vectors = lax.ppermute(vector_blocks, "dev", [(count - 1, 0)])
+    seed = jnp.concatenate([embed_blocks.reshape(2 * embed_rows, D), vectors.reshape(8 * 2 * LAYERS, D)])
+    third = -(-seed.shape[0] // 48) * 16
+    spread_parts = []
+    for number, order in enumerate(("xyba", "baxy", "ybax")):
+        spread = seed[number * third : (number + 1) * third]
+        reached = [0, 1]
+        for name in order:
+            moves = [(i, i ^ MASKS[name]) for i in reached]
+            got = lax.ppermute(spread, "dev", moves)
+            targets = [t for s, t in moves]
+            is_target = jnp.array([i in targets for i in range(count)])[me]
+            spread = jnp.where(is_target, got, spread)
+            reached = reached + targets
+        spread_parts.append(spread)
+    spread = jnp.concatenate(spread_parts)
     other = lax.ppermute(spread, "dev", pairs(count, 1))
     is_even = me % 2 == 0
-    even = jnp.where(is_even, spread, other)[0]
-    odd = jnp.where(is_even, other, spread)[0]
-    rest = EMBED_FLAT - stem_piece
-    embed_flat = [
-        jnp.concatenate([even[m * stem_piece : (m + 1) * stem_piece], odd[m * stem_piece : m * stem_piece + rest]])
+    even = jnp.where(is_even, spread, other)
+    odd = jnp.where(is_even, other, spread)
+    embed_all = [
+        jnp.concatenate(
+            [
+                even[m * embed_rows : m * embed_rows + early_rows],
+                odd[m * embed_rows : m * embed_rows + EMBED_ROWS - early_rows],
+            ]
+        )
         for m in range(2)
     ]
-    vectors_all = even[2 * stem_piece :].reshape(2, LAYERS, 6, D)
+    vectors_all = even[2 * embed_rows :].reshape(2, LAYERS, 8, D)[:, :, :6]
 
     def layer_weights(model, layer_index):
-        flat = gathered[:, model * LAYERS + layer_index].reshape(MATRIX_ROWS, D)
+        chosen = gathered[:, :, model * LAYERS + layer_index]
+        flat = jnp.concatenate([chosen[:, 0], chosen[half // 2 :, 1], chosen[: half // 2, 1]]).reshape(MATRIX_ROWS, D)
         return (
             flat[: 3 * D].reshape(D, 3 * D),
             flat[3 * D : 4 * D],
@@ -596,12 +754,18 @@
             vectors_all[model, layer_index],
         )
 
-    def head_weights(model):
-        one = gathered_head[:, model]
-        w_one = one[1:first_w2].reshape((first_w2 - 1) * slot, ROW)
-        w_two = one[first_w2:first_w3].reshape((first_w3 - first_w2) * slot, ROW)
-        w_three = jnp.concatenate([one[i, : sizes[i]] for i in range(first_w3, count)]).reshape(HID, BOT)
-        return (w_one, w_two, w_three)
+    def head_slots(first, last):
+        pieces = []
+        i = first
+        while i < last:
+            side = i >= half
+            at = i ^ across if side else i
+            stop = i + 1
+            while stop < last and (stop >= half) == side and (stop ^ across if side else stop) == at + stop - i:
+                stop += 1
+            pieces.append(gathered_head[at : at + stop - i, 1 if side else 0])
+            i = stop
+        return pieces
 
     def pad_columns(values, first, last, origin):
         pieces = []
@@ -616,30 +780,19 @@
     def cut_columns(values, first, last, origin):
         pieces = []
         for i in range(first, last):
-            low, high = bounds[i] - origin, bounds[i + 1] - origin
+            low = bounds[i] - origin
             at = (i - first) * slot
             pieces.append(values[..., at + max(-low, 0) : at + sizes[i]])
         return jnp.concatenate(pieces, axis=-1)
 
     def embed_parts(model):
-        patch_w = embed_flat[model][: PIX * D].reshape(PIX, D)
-        position = embed_flat[model][PIX * D : (PIX + SEQ) * D].reshape(SEQ, D)
-        extras = embed_flat[model][(PIX + SEQ) * D :].reshape(4, D)
-        return (patch_w, position, extras, None, None, None)
-
-    def head_up(stream, extras, weights):
-        w_one, w_two, w_three = weights
+        rows = embed_all[model]
+        return (rows[:PIX], rows[PIX : PIX + SEQ], rows[PIX + SEQ :], None, None, None)
+
+    def head_rows(stream, extras):
         chosen = jnp.take_along_axis(stream, row_index[:, :, None], axis=1).reshape(rows_here, D)
         normed = layer_norm(chosen, extras[2].astype(single), extras[3].astype(single)).astype(narrow)
-        normed_wide = pad_columns(normed, 1, first_w2, 0)
-        pre_one = contract("rd,dh->rh", normed_wide, w_one)
-        hidden_one = jax.nn.gelu(pre_one).astype(narrow)
-        hidden_wide = pad_columns(hidden_one, first_w2, first_w3, D)
-        pre_two = contract("rh,hk->rk", hidden_wide, w_two)
-        hidden_two = jax.nn.gelu(pre_two).astype(narrow)
-        bottleneck = contract("rh,hb->rb", hidden_two, w_three)
-        unit_z = unit_rows(bottleneck).astype(narrow)
-        return unit_z, (chosen, normed_wide, pre_one, hidden_wide, pre_two, hidden_two, bottleneck)
+        return chosen, normed
 
     student_parts = embed_parts(1)
     stream = embed(student_parts, patches, masked_here, True)
@@ -654,14 +807,38 @@
     teacher_stream = embed(teacher_parts, patches, masked_here, False)
     for layer_index in range(LAYERS):
         teacher_stream = block_forward(teacher_stream, layer_weights(0, layer_index))[0]
-    student_head = head_weights(1)
-    teacher_z, _ = head_up(teacher_stream, teacher_parts[2], head_weights(0))
-    student_z, head_saved = head_up(stream, student_parts[2], student_head)
+    chosen, student_normed = head_rows(stream, student_parts[2])
+    teacher_normed = head_rows(teacher_stream, teacher_parts[2])[1]
+
+    normed_got = lax.ppermute(
+        jnp.where(student_side, teacher_normed, student_normed), "dev", pairs(count, across)
+    )
+    normed = jnp.where(
+        student_side,
+        jnp.concatenate([normed_got, student_normed]),
+        jnp.concatenate([teacher_normed, normed_got]),
+    )
+    w_one = jnp.concatenate(head_slots(1, first_w2)).reshape(-1, ROW)
+    w_two = jnp.concatenate(head_slots(first_w2, first_w3)).reshape(-1, ROW)
+    w_three = jnp.concatenate(
+        [head_slots(i, i + 1)[0][0, : sizes[i]] for i in range(first_w3, count)]
+    ).reshape(HID, BOT)
+    pre_one = contract("rd,dh->rh", pad_columns(normed, 1, first_w2, 0), w_one)
+    hidden_one = jax.nn.gelu(pre_one).astype(narrow)
+    pre_two = contract("rh,hk->rk", pad_columns(hidden_one, first_w2, first_w3, D), w_two)
+    hidden_two = jax.nn.gelu(pre_two).astype(narrow)
+    bottleneck = contract("rh,hb->rb", hidden_two, w_three)
+    unit_z = unit_rows(bottleneck).astype(narrow)
+    inputs_all = lax.all_gather(
+        jnp.concatenate([normed, hidden_one, hidden_two], axis=1), "dev", axis=0, axis_index_groups=groups
+    ).reshape(half * 2 * rows_here, D + 2 * HID)
 
     all_rows = count * rows_here
     kept_row = jnp.broadcast_to(kept[:, None], (images_here, 17)).reshape(1, rows_here)
-    all_kept = cube_gather([kept_row], ("xyabc",))[0].reshape(all_rows)
-    z_all = cube_gather([jnp.stack([teacher_z, student_z])], ("xyabc",))[0]
+    all_kept = cube_gather(kept_row, "bxygc").reshape(all_rows)
+    z_pair = cube_gather(unit_z, "b")
+    z_all = cube_gather(z_pair, "xygc")
+    z_all = z_all.reshape(half, 2, 2 * rows_here, BOT)
     teacher_z_all = z_all[:, 0].reshape(all_rows, BOT)
     student_z_all = z_all[:, 1].reshape(all_rows, BOT)
     own_student = lax.optimization_barrier(protos.astype(narrow)).astype(single)
@@ -691,7 +868,7 @@
         jnp.where(is_class, all_kept, 0.0)[:, None] * teacher_logits, axis=0
     )
     own_new_centre = centre_keep * own_centre + (1.0 - centre_keep) * centre_sum / count_total
-    new_centre = cube_gather([own_new_centre.reshape(1, protos_here)], ("cxyab",))[0].reshape(-1)
+    new_centre = cube_gather(own_new_centre.reshape(1, protos_here), "cxyab").reshape(-1)
     scale = row_weight / tau_student
     grad_logits = (
         student_exp * (scale / sums[1])[:, None] - teacher_exp * (scale / sums[0])[:, None]
@@ -699,39 +876,30 @@
     z_partial = contract("rk,kb->rb", grad_logits, unit_student)
     proto_unit_grad = contract("rk,rb->kb", grad_logits, student_z_all)
     proto_grad = jax.vjp(unit_rows, own_student)[1](proto_unit_grad)[0]
-    grad_unit_z = cube_scatter(
-        [split_bits(z_partial.reshape(count, rows_here, BOT))], ("cbayx",), ("cbayx",)
+    z_own = cube_scatter(
+        [z_partial.reshape((2,) * 4 + (2 * rows_here, BOT))], ("cgyx",), ("cgyx",)
     )[0]
-
-    chosen, normed_wide, pre_one, hidden_wide, pre_two, hidden_two, bottleneck = head_saved
-    w_one, w_two, w_three = student_head
+    grad_unit_z = z_own + lax.ppermute(z_own, "dev", [(i, i ^ across) for i in range(half)])
+
     grad_bottle = jax.vjp(unit_rows, bottleneck)[1](grad_unit_z)[0].astype(narrow)
-    grad_third = contract("rh,rb->hb", hidden_two, grad_bottle)
     grad_pre_two = gelu_back(pre_two, contract("rb,hb->rh", grad_bottle, w_three)).astype(narrow)
-    grad_second = contract("rh,rk->hk", hidden_wide, grad_pre_two)
     grad_hidden = cut_columns(contract("rk,hk->rh", grad_pre_two, w_two), first_w2, first_w3, D)
     grad_pre_one = gelu_back(pre_one, grad_hidden).astype(narrow)
-    grad_first = contract("rd,rh->dh", normed_wide, grad_pre_one)
     grad_normed = cut_columns(contract("rh,dh->rd", grad_pre_one, w_one), 1, first_w2, 0)
+    grads_all = lax.all_gather(
+        jnp.concatenate([grad_pre_one, grad_pre_two, grad_bottle], axis=1),
+        "dev",
+        axis=0,
+        axis_index_groups=groups,
+    ).reshape(half * 2 * rows_here, 2 * HID + BOT)
+    normed_back = lax.ppermute(
+        grad_normed[:rows_here], "dev", [(i, i ^ across) for i in range(half, count)]
+    )
+    own_grad_normed = jnp.where(student_side, grad_normed[rows_here:], normed_back)
     extras = student_parts[2].astype(single)
     grad_chosen, grad_gain, grad_bias = jax.vjp(layer_norm, chosen, extras[2], extras[3])[1](
-        grad_normed
-    )
-    third_rows = grad_third.reshape(BOT, ROW).astype(narrow)
-    third_pieces = []
-    for i in range(first_w3, count):
-        at = bounds[i] - (D + HID)
-        third_pieces.append(third_rows[at : at + sizes[i]])
-        third_pieces.append(jnp.zeros((slot - sizes[i], ROW), narrow))
-    head_grads = jnp.concatenate(
-        [
-            jnp.zeros((slot, ROW), narrow),
-            grad_first.astype(narrow),
-            grad_second.astype(narrow),
-        ]
-        + third_pieces
-    ).reshape(count, slot, ROW)
-    head_block_grad = scatter_rows(head_grads, (768, 768), 2).astype(single)
+        own_grad_normed
+    )
     image_index = jnp.arange(images_here, dtype=jnp.int32)[:, None]
     grad_stream = (
         jnp.zeros(stream.shape, single)
@@ -748,13 +916,13 @@
         grad_qkv, grad_proj, grad_up, grad_down, vector_grads[layer_index] = grads
         flat = jnp.concatenate(
             [
-                grad_qkv.astype(narrow).reshape(3 * D, D),
-                grad_proj.astype(narrow),
-                grad_up.astype(narrow).reshape(FF, D),
-                grad_down.astype(narrow),
+                grad_qkv.reshape(3 * D, D),
+                grad_proj,
+                grad_up.reshape(FF, D),
+                grad_down,
             ]
         ).reshape(count, block_rows, D)
-        layer_block_grads[layer_index] = scatter_rows(flat, (64, 48), 1).astype(single)
+        layer_block_grads[layer_index] = scatter_rows(flat)
     grad_patch_w, grad_position, grad_cls, grad_mask_token = embed_backward(
         grad_stream, patches, masked_here
     )
@@ -773,6 +941,33 @@
     )[0]
     layer_block = jnp.stack(layer_block_grads)
 
+    padded = jnp.pad(inputs_all[:, : D + HID], ((0, 0), (-min(bounds[1], 0), slot)))
+
+    def block_product(owner, grads):
+        window = lax.dynamic_slice(
+            padded, (0, jnp.array(bounds, jnp.int32)[owner] - bounds[1]), (all_rows, slot)
+        )
+        valid = jnp.arange(slot) < jnp.array(sizes, jnp.int32)[owner]
+        return contract("rs,rh->sh", jnp.where(valid, window, 0), grads)
+
+    partner = me ^ across
+    grads_one, grads_two = grads_all[:, :HID], grads_all[:, HID : 2 * HID]
+    third_from = [max(bounds[i] - (D + HID), 0) * (ROW // BOT) for i in range(count)]
+    third_window = lax.dynamic_slice(
+        jnp.pad(inputs_all[:, D + HID :], ((0, 0), (0, slot * ROW // BOT))),
+        (0, jnp.array(third_from, jnp.int32)[me]),
+        (all_rows, slot * ROW // BOT),
+    )
+    third_valid = jnp.arange(slot * ROW // BOT) < jnp.array(sizes, jnp.int32)[me] * (ROW // BOT)
+    third_grad = contract(
+        "rs,rb->sb", jnp.where(third_valid, third_window, 0), grads_all[:, 2 * HID :]
+    ).reshape(slot, ROW)
+    own_block_grad = jnp.where(me >= first_w3, third_grad, block_product(me, grads_two))
+    partner_block_grad = block_product(partner, jnp.where(partner < first_w2, grads_one, grads_two))
+    block_got = lax.ppermute(partner_block_grad, "dev", [(i, i ^ across) for i in range(half, count)])
+    head_block_grad = jnp.where(student_side, own_block_grad, block_got)
+    head_block_grad = jnp.where(me == 0, 0.0, head_block_grad)
+
     square_local = (
         jnp.sum(head_block_grad * head_block_grad)
         + jnp.sum(layer_block * layer_block)
@@ -780,24 +975,25 @@
         + jnp.sum(proto_grad * proto_grad)
     )
     square_total = cube_sum(square_local.reshape(1, 1))[0, 0]
-    small_all = cube_gather([small_block], ("cxyab",))[0].reshape(small_rows * count, D)
+    small_all = cube_gather(small_block, "cxyab").reshape(small_rows * count, D)
     embed_grad = small_all[:EMBED_ROWS].reshape(-1)
-    vector_grad = small_all[EMBED_ROWS : EMBED_ROWS + 6 * LAYERS].reshape(LAYERS, 6 * D)
-
-    layer_block = layer_block.reshape(LAYERS, block)
-    behind = lax.ppermute(layer_block[:, :tail], "dev", step_pairs(count, -1))
+    vector_grad = small_all[EMBED_ROWS : EMBED_ROWS + 6 * LAYERS].reshape(LAYERS, 6, D)
+
+    behind = lax.ppermute(layer_block[:, :6], "dev", step_pairs(count, -1))
     behind = jnp.where(me == count - 1, vector_grad, behind)
-    layer_grad = lax.dynamic_slice(
-        jnp.concatenate([layer_block, behind], axis=1), (0, drift * me), (LAYERS, layer_piece)
-    )
     last_rows = lax.dynamic_slice(
         head_block_grad, (jnp.array(sizes, jnp.int32)[me] - GROUP, 0), (GROUP, ROW)
     )
     previous = lax.ppermute(last_rows, "dev", step_pairs(count, 1))
-    joined = jnp.concatenate(
-        [previous.reshape(-1), head_block_grad.reshape(-1), jnp.zeros((head_span,), single)]
-    )
-    stem_grad = lax.dynamic_slice(joined, (head_span - start_here,), (stem_piece,))
+    stem_at = head_span - start_here
+    layer_at = drift * me
+    place = jnp.stack([stem_at // 128, stem_at % 128, layer_at // 128, layer_at % 128]).astype(jnp.int32)
+    stem_lines, layer_lines = own_shards(
+        place, head_block_grad, previous, layer_block, behind, lane_rows(stem_piece), lane_rows(layer_piece)
+    )
+    layer_grad = layer_lines.reshape(LAYERS, -1)[:, :layer_piece]
+    stem_grad = stem_lines.reshape(-1)[:stem_piece]
+    rest = EMBED_FLAT - stem_piece
     second_part = jnp.concatenate([embed_grad[stem_piece:], stem_grad[rest:]])
     stem_grad = jnp.where(
         me == 0, embed_grad[:stem_piece], jnp.where(me == 1, second_part, stem_grad)

time: 1180 us -> 1090 us (0.924)
  local copies, waits for them, and re-layouts: 308 us -> 227 us
  other arithmetic: 168 us -> 128 us
  matrix products: 182 us -> 200 us
  starting transfers between devices: 101 us -> 115 us
    ppermute x55 -> x29, waiting for transfers between devices: 197 us -> 36.9 us  [cube_scatter(): lax.ppermute(s, 'dev', pairs(count, MASKS[order[turn]]))]
    all_gather x2 -> x4, waiting for transfers between devices: 57.2 us -> 185 us  [the longest x1 159 us: close_local(): lax.all_gather(both_layers, 'dev', axis=0, axis_index_groups=groups)]
    slice x25 -> x11, local copies, waits for them, and re-layouts: 75 us -> 9.41 us  [the longest x1 5.3 us: close_local(): inputs_all[:, :D + HID]]
    ppermute x23 -> x29, waiting for transfers between devices: 43.9 us -> 106 us  [the longest x20 42.1 us: cube_gather(): got = lax.ppermute(held, 'dev', pairs(count, MASKS[name]))]
    ppermute x4 -> x12, waiting for transfers between devices: 57.8 us -> 24.8 us  [close_local(): got = lax.ppermute(spread, 'dev', moves)]
    squeeze x3 -> x15, local copies, waits for them, and re-layouts: 12.1 us -> 31.3 us  [the longest x4 14.4 us: head_slots(): pieces.append(gathered_head[at:at + stop - i, 1 if side else 0])]
    ppermute x23 -> x29, starting transfers between devices: 28.3 us -> 46.5 us  [the longest x20 29.5 us: cube_gather(): got = lax.ppermute(held, 'dev', pairs(count, MASKS[name]))]
    dot_general x64 -> x62, matrix products: 182 us -> 200 us  [contract(): return jnp.einsum(form, left_arg, right_arg, preferred_element_type=single)]
  transfers between devices with their start and end apart: 97 -> 87, of which waited for: 58 -> 48; matrix products, arithmetic and copies ran while one was open for 37% -> 47% of each run, Pallas kernels for 0% -> 0%
where the time goes in v2:
time: 1090 us; the launch traced here: 1080 us
  waiting for transfers between devices  367 us (34%)
  local copies, waits for them, and re-layouts  227 us (21%)
  matrix products  200 us (18%)
  other arithmetic  128 us (12%)
  starting transfers between devices  115 us (11%)
  between operations  34.3 us (3%)
    dot_general x62, matrix products, contract(): return jnp.einsum(form, left_arg, right_arg, preferred_element_type=single)  200 us
    all_gather x1, waiting for transfers between devices, close_local(): lax.all_gather(both_layers, 'dev', axis=0, axis_index_groups=groups)  159 us
    unnamed x442, local copies, waits for them, and re-layouts  60.5 us
    ppermute x20, waiting for transfers between devices, cube_gather(): got = lax.ppermute(held, 'dev', pairs(count, MASKS[name]))  42.1 us
    ppermute x29, waiting for transfers between devices, cube_scatter(): lax.ppermute(s, 'dev', pairs(count, MASKS[order[turn]]))  36.9 us
    ppermute x29, starting transfers between devices, cube_scatter(): lax.ppermute(s, 'dev', pairs(count, MASKS[order[turn]]))  33 us
    ppermute x20, starting transfers between devices, cube_gather(): got = lax.ppermute(held, 'dev', pairs(count, MASKS[name]))  29.5 us
    all_gather x1, waiting for transfers between devices, close_local(): lax.all_gather(both_head, 'dev', axis=0, axis_index_groups=groups)  26.2 us
  transfers between devices with their start and end apart: 87, of which 48 were waited for; matrix products, arithmetic and copies ran while one was open for 47% of the time, Pallas kernels for 0%

profile of v2, /device:TPU:8, one launch (start us, length us, event | category | flops | bytes accessed | tf_op | source)
XLA Modules:
  0.0 1075.5 jit_solution(16824477071118303696)
XLA Ops:
  27.9 25.8 %collective-permute-done.23 = bf16[96,2048]{1,0:T(8,128)(2,1)S(1)} collective-permute-done((bf16[96,2048]{1,0:T(8,128)(2,1)S(1)}, bf16[96,2048]{1,0:T(8,128)(2,1)S(1)}, u32[]{:S(2)}, u32[]{:S(2)}) %collective-permute-start.23) | collective-permute-done | bytes 393248 | tf_op jit(solution)/shard_map/ppermute | solution.py:709
  56.4 9.6 collective-permute-done.21
  121.5 8.2 collective-permute-done.12
  147.8 6.7 collective-permute-done.19
  165.6 26.2 %all-gather.11.cloned.1.call-done = bf16[16,2,96,2048]{3,2,1,0:T(8,128)(2,1)} async-done(((bf16[1,2,96,2048]{3,2,1,0:T(8,128)(2,1)}), bf16[16,2,96,2048]{3,2,1,0:T(8,128)(2,1)}) %all-gather.11.cloned.1.call-update) | async-done | bytes 12582928 | tf_op jit(solution)/shard_map/all_gather | solution.py:713
  204.8 159.3 %all-gather.9.cloned.1.call-done = bf16[16,2,4,144,384]{4,3,2,1,0:T(8,128)(2,1)} async-done(((bf16[1,2,4,144,384]{4,3,2,1,0:T(8,128)(2,1)}), bf16[16,2,4,144,384]{4,3,2,1,0:T(8,128)(2,1)}) %all-gather.9.cloned.1.call-update) | async-done | bytes 14155792 | tf_op jit(solution)/shard_map/all_gather | solution.py:706
  364.1 6.0 slice_bitcast_fusion.1
  416.9 11.0 %copy.326 = bf16[2,257,1152]{1,2,0:T(8,128)(2,1)} copy(bf16[2,257,1152]{2,1,0:T(8,128)(2,1)} %convolution_convert_fusion.2) | data formatting | bytes 2368512 | tf_op jit(solution)/shard_map/convert_element_type | solution.py:83
  514.4 7.5 pad_maximum_fusion
  527.1 6.2 multiply_convert_fusion.8
  550.7 7.9 collective-permute-done.25
  572.1 7.8 collective-permute-done.27
  704.5 10.2 fusion.124
  714.7 10.3 fusion.127
  749.8 10.3 fusion.130
  760.1 10.3 fusion.133
  864.9 7.5 collective-permute-done.79
  882.2 6.2 collective-permute-done.42
  935.5 10.4 reshape.2197
  951.3 10.3 reshape.2199
  961.5 6.0 fusion.8
  978.0 24.2 %collective-permute-done.39 = f32[96,2048]{1,0:T(8,128)} collective-permute-done((f32[96,2048]{1,0:T(8,128)}, f32[96,2048]{1,0:T(8,128)}, u32[]{:S(2)}, u32[]{:S(2)}) %collective-permute-start.39) | collective-permute-done | bytes 786464 | tf_op jit(solution)/shard_map/ppermute | solution.py:967
  1017.6 7.0 collective-permute-start.68
  1035.5 7.2 multiply_add_fusion
  (1062 shorter events, 639.3 us)
Async XLA Ops:
  7.2 184.5 %all-gather.11.cloned.1.call-start = ((), (), s32[]{:S(2)}) async-start(), calls=%async_computation.1 | async-start | bytes 13369344 | tf_op jit(solution)/shard_map/all_gather | solution.py:713
  26.3 27.3 %collective-permute-start.23 = (bf16[96,2048]{1,0:T(8,128)(2,1)S(1)}, bf16[96,2048]{1,0:T(8,128)(2,1)S(1)}, u32[]{:S(2)}, u32[]{:S(2)}) collective-permute-start(bf16[96,2048]{1,0:T(8,128)(2,1)S(1)} %get-tuple-element.244), channel_id=1, source_target_pairs={{0,24},{1,25},{2,26},{3,27},{4,28},{5,29},{6,30},{7,31},{8,16},{9,... | collective-permute-start | bytes 1179656 | tf_op jit(solution)/shard_map/ppermute | solution.py:709
  54.7 309.4 %all-gather.9.cloned.1.call-start = ((), (), s32[]{:S(2)}) async-start(), calls=%async_computation | async-start | bytes 15040512 | tf_op jit(solution)/shard_map/all_gather | solution.py:706
  67.1 868.5 %all-gather.13.cloned.1.call-start = ((), (), s32[]{:S(2)}) async-start(), calls=%async_computation.2 | async-start | bytes 10967040 | tf_op jit(solution)/shard_map/all_gather | solution.py:832
  67.3 90.1 %collective-permute-start = (f32[1,1,34]{2,1,0:T(1,128)S(1)}, f32[1,1,34]{2,1,0:T(1,128)S(1)}, u32[]{:S(2)}, u32[]{:S(2)}) collective-permute-start(f32[1,1,34]{2,1,0:T(1,128)S(1)} %broadcast_in_dim_reshape.6), channel_id=1, source_target_pairs={{0,24},{1,25},{2,26},{3,27},{4,28},{5,29},{6,30},{7,31},{8,16},{9,... | collective-permute-start | bytes 416 | tf_op jit(solution)/shard_map/ppermute | solution.py:444
  86.1 30.1 %collective-permute-start.17 = (bf16[320,384]{1,0:T(8,128)(2,1)}, bf16[320,384]{1,0:T(8,128)(2,1)}, u32[]{:S(2)}, u32[]{:S(2)}) collective-permute-start(bf16[320,384]{1,0:T(8,128)(2,1)} %broadcast_select_fusion.12), channel_id=1, source_target_pairs={{0,24},{1,25},{4,28},{5,29}} | collective-permute-start | bytes 737288 | tf_op jit(solution)/shard_map/ppermute | solution.py:724
  89.5 29.6 %collective-permute-start.8 = (bf16[336,384]{1,0:T(8,128)(2,1)}, bf16[336,384]{1,0:T(8,128)(2,1)S(1)}, u32[]{:S(2)}, u32[]{:S(2)}) collective-permute-start(bf16[336,384]{1,0:T(8,128)(2,1)} %get-tuple-element.252), channel_id=1, source_target_pairs={{0,4},{1,5},{2,6},{3,7}} | collective-permute-start | bytes 774152 | tf_op jit(solution)/shard_map/ppermute | solution.py:724
  117.8 19.7 %collective-permute-start.18 = (bf16[320,384]{1,0:T(8,128)(2,1)S(1)}, bf16[320,384]{1,0:T(8,128)(2,1)S(1)}, u32[]{:S(2)}, u32[]{:S(2)}) collective-permute-start(bf16[320,384]{1,0:T(8,128)(2,1)S(1)} %broadcast_select_fusion.13), channel_id=1, source_target_pairs={{0,8},{1,9},{4,12},{5,13},{24,16},{25,17},{28,20},{29,21}} | collective-permute-start | bytes 737288 | tf_op jit(solution)/shard_map/ppermute | solution.py:724
  120.8 18.8 %collective-permute-start.9 = (bf16[336,384]{1,0:T(8,128)(2,1)S(1)}, bf16[336,384]{1,0:T(8,128)(2,1)S(1)}, u32[]{:S(2)}, u32[]{:S(2)}) collective-permute-start(bf16[336,384]{1,0:T(8,128)(2,1)S(1)} %broadcast_select_fusion.9), channel_id=1, source_target_pairs={{0,24},{1,25},{2,26},{3,27},{4,28},{5,29},{6,30},{7,31}} | collective-permute-start | bytes 774152 | tf_op jit(solution)/shard_map/ppermute | solution.py:724
  158.1 382.7 %collective-permute-start.1 = (f32[2,1,34]{2,1,0:T(1,128)}, f32[2,1,34]{2,1,0:T(1,128)}, u32[]{:S(2)}, u32[]{:S(2)}) collective-permute-start(f32[2,1,34]{2,1,0:T(1,128)} %broadcast_select_fusion.22), channel_id=1, source_target_pairs={{0,2},{1,3},{2,0},{3,1},{4,6},{5,7},{6,4},{7,5},{8,10},{9,11},{10,... | collective-permute-start | bytes 824 | tf_op jit(solution)/shard_map/ppermute | solution.py:444
  534.2 417.1 %all-gather.15.cloned.1.call-start = ((), (), s32[]{:S(2)}) async-start(), calls=%async_computation.3 | async-start | bytes 10653696 | tf_op jit(solution)/shard_map/all_gather | solution.py:889
  541.5 21.5 %collective-permute-start.2 = (f32[4,1,34]{2,1,0:T(1,128)S(1)}, f32[4,1,34]{2,1,0:T(1,128)S(1)}, u32[]{:S(2)}, u32[]{:S(2)}) collective-permute-start(f32[4,1,34]{2,1,0:T(1,128)S(1)} %broadcast_select_fusion.21), channel_id=1, source_target_pairs={{0,4},{1,5},{2,6},{3,7},{4,0},{5,1},{6,2},{7,3},{8,12},{9,13},{10,... | collective-permute-start | bytes 1640 | tf_op jit(solution)/shard_map/ppermute | solution.py:444
  618.6 36.2 %collective-permute-start.74 = (f32[8,1,2048]{2,1,0:T(1,128)}, f32[8,1,2048]{2,1,0:T(1,128)}, u32[]{:S(2)}, u32[]{:S(2)}) collective-permute-start(f32[8,1,2048]{2,1,0:T(1,128)} %copy.397), channel_id=1, source_target_pairs={{0,8},{1,9},{2,10},{3,11},{4,12},{5,13},{6,14},{7,15},{8,0},{9,1},... | collective-permute-start | bytes 196616 | tf_op jit(solution)/shard_map/ppermute | solution.py:444
  796.7 24.7 %collective-permute-start.61 = (f32[2,2,2,2,27,384]{5,3,4,2,1,0:T(2,128)}, f32[2,2,2,2,27,384]{5,3,4,2,1,0:T(2,128)}, u32[]{:S(2)}, u32[]{:S(2)}) collective-permute-start(f32[2,2,2,2,27,384]{5,3,4,2,1,0:T(2,128)} %copy.387), channel_id=1, source_target_pairs={{0,1},{1,0},{2,3},{3,2},{4,5},{5,4},{6,7},{7,6},{8,9},{9,8},{10,11... | collective-permute-start | bytes 1990664 | tf_op jit(solution)/shard_map/ppermute | solution.py:470
  808.6 64.6 %collective-permute-start.41 = (f32[2,2,2,2,72,384]{5,4,1,0,2,3:T(8,128)}, f32[2,2,2,2,72,384]{5,4,1,0,2,3:T(8,128)}, u32[]{:S(2)}, u32[]{:S(2)}) collective-permute-start(f32[2,2,2,2,72,384]{5,4,1,0,2,3:T(8,128)} %select_bitcast_fusion.3), channel_id=1, source_target_pairs={{0,1},{1,0},{2,3},{3,2},{4,5},{5,4},{6,7},{7,6},{8,9},{9,8},{10,11... | collective-permute-start | bytes 5308424 | tf_op jit(solution)/shard_map/ppermute | solution.py:470
  832.8 43.2 %collective-permute-start.46 = (f32[2,2,2,2,72,384]{5,4,1,0,3,2:T(8,128)}, f32[2,2,2,2,72,384]{5,4,1,0,3,2:T(8,128)}, u32[]{:S(2)}, u32[]{:S(2)}) collective-permute-start(f32[2,2,2,2,72,384]{5,4,1,0,3,2:T(8,128)} %select_bitcast_fusion.2), channel_id=1, source_target_pairs={{0,1},{1,0},{2,3},{3,2},{4,5},{5,4},{6,7},{7,6},{8,9},{9,8},{10,11... | collective-permute-start | bytes 5308424 | tf_op jit(solution)/shard_map/ppermute | solution.py:470
  852.3 27.1 %collective-permute-start.51 = (f32[2,2,2,2,72,384]{5,4,1,0,3,2:T(8,128)S(1)}, f32[2,2,2,2,72,384]{5,4,1,0,3,2:T(8,128)S(1)}, u32[]{:S(2)}, u32[]{:S(2)}) collective-permute-start(f32[2,2,2,2,72,384]{5,4,1,0,3,2:T(8,128)S(1)} %select_bitcast_fusion.1), channel_id=1, source_target_pairs={{0,1},{1,0},{2,3},{3,2},{4,5},{5,4},{6,7},{7,6},{8,9},{9,8},{10,11... | collective-permute-start | bytes 5308424 | tf_op jit(solution)/shard_map/ppermute | solution.py:470
  872.8 29.4 %collective-permute-start.80 = (f32[16,27,384]{2,0,1:T(8,128)S(1)}, f32[16,27,384]{2,0,1:T(8,128)S(1)}, u32[]{:S(2)}, u32[]{:S(2)}) collective-permute-start(f32[16,27,384]{2,0,1:T(8,128)S(1)} %copy.398), channel_id=1, source_target_pairs={{0,24},{1,25},{2,26},{3,27},{4,28},{5,29},{6,30},{7,31},{8,16},{9,... | collective-permute-start | bytes 1990664 | tf_op jit(solution)/shard_map/ppermute | solution.py:444
  881.8 18.8 %collective-permute-start.57 = (bf16[2,2,2,72,384]{4,3,1,0,2:T(8,128)(2,1)S(1)}, bf16[2,2,2,72,384]{4,3,1,0,2:T(8,128)(2,1)S(1)}, u32[]{:S(2)}, u32[]{:S(2)}) collective-permute-start(bf16[2,2,2,72,384]{4,3,1,0,2:T(8,128)(2,1)S(1)} %fusion.194), channel_id=1, source_target_pairs={{0,4},{1,5},{2,6},{3,7},{4,0},{5,1},{6,2},{7,3},{8,12},{9,13},{10,... | collective-permute-start | bytes 1327112 | tf_op jit(solution)/shard_map/ppermute | solution.py:470
  888.7 23.0 %collective-permute-start.43 = (bf16[2,2,72,384]{3,2,1,0:T(8,128)(2,1)S(1)}, bf16[2,2,72,384]{3,2,1,0:T(8,128)(2,1)}, u32[]{:S(2)}, u32[]{:S(2)}) collective-permute-start(bf16[2,2,72,384]{3,2,1,0:T(8,128)(2,1)S(1)} %fusion.230), channel_id=1, source_target_pairs={{0,4},{1,5},{2,6},{3,7},{4,0},{5,1},{6,2},{7,3},{8,12},{9,13},{10,... | collective-permute-start | bytes 663560 | tf_op jit(solution)/shard_map/ppermute | solution.py:470
  892.0 22.5 %collective-permute-start.48 = (bf16[2,2,72,384]{3,2,1,0:T(8,128)(2,1)}, bf16[2,2,72,384]{3,2,1,0:T(8,128)(2,1)}, u32[]{:S(2)}, u32[]{:S(2)}) collective-permute-start(bf16[2,2,72,384]{3,2,1,0:T(8,128)(2,1)} %fusion.231), channel_id=1, source_target_pairs={{0,2},{1,3},{2,0},{3,1},{4,6},{5,7},{6,4},{7,5},{8,10},{9,11},{10,... | collective-permute-start | bytes 663560 | tf_op jit(solution)/shard_map/ppermute | solution.py:470
  900.8 18.3 %collective-permute-start.58 = (bf16[2,2,72,384]{3,2,1,0:T(8,128)(2,1)S(1)}, bf16[2,2,72,384]{3,2,1,0:T(8,128)(2,1)}, u32[]{:S(2)}, u32[]{:S(2)}) collective-permute-start(bf16[2,2,72,384]{3,2,1,0:T(8,128)(2,1)S(1)} %fusion.233), channel_id=1, source_target_pairs={{0,2},{1,3},{2,0},{3,1},{4,6},{5,7},{6,4},{7,5},{8,10},{9,11},{10,... | collective-permute-start | bytes 663560 | tf_op jit(solution)/shard_map/ppermute | solution.py:470
  967.5 34.7 %collective-permute-start.39 = (f32[96,2048]{1,0:T(8,128)}, f32[96,2048]{1,0:T(8,128)}, u32[]{:S(2)}, u32[]{:S(2)}) collective-permute-start(f32[96,2048]{1,0:T(8,128)} %fusion.8), channel_id=1, source_target_pairs={{16,8},{17,9},{18,10},{19,11},{20,12},{21,13},{22,14},{23,15},{24,... | collective-permute-start | bytes 2359304 | tf_op jit(solution)/shard_map/ppermute | solution.py:967
  1010.4 47.1 %collective-permute-start.81 = (f32[16,2048]{1,0:T(8,128)S(1)}, f32[16,2048]{1,0:T(8,128)S(1)}, u32[]{:S(2)}, u32[]{:S(2)}) collective-permute-start(f32[16,2048]{1,0:T(8,128)S(1)} %constant_dynamic-slice_fusion), channel_id=1, source_target_pairs={{0,1},{1,2},{2,3},{3,4},{4,5},{5,6},{6,7},{7,8},{8,9},{9,10},{10,1... | collective-permute-start | bytes 393224 | tf_op jit(solution)/shard_map/ppermute | solution.py:987
  (278 other events, 7182.8 us)
Sparse Core Ops, SparseCore 0:
  54.8 136.8 all-gather.10
  193.8 170.2 all-gather.8
  534.3 118.4 all-gather.12
  680.2 108.6 all-gather.14

commit v3 on v2

--- a/solution.py
+++ b/solution.py
@@ -450,7 +450,7 @@
     return held
 
 
-def cube_scatter(parts, orders, axes):
+def cube_scatter(parts, orders, axes, lead=0):
     count = 1 << len(BITS)
     flags = bit_flags(lax.axis_index("dev"))
     held = list(parts)
@@ -458,14 +458,14 @@
     for turn in range(len(orders[0])):
         sent, kept = [], []
         for h, order, name in zip(held, orders, names):
-            place = name.index(order[turn])
+            place = name.index(order[turn]) + lead
             low = lax.index_in_dim(h, 0, place, keepdims=False)
             high = lax.index_in_dim(h, 1, place, keepdims=False)
             flag = flags[order[turn]] == 1
             out = jnp.where(flag, low, high)
             sent.append(out if order[turn] == "c" else out.astype(narrow))
             kept.append(jnp.where(flag, high, low))
-            name.pop(place)
+            name.pop(place - lead)
         got = [
             lax.ppermute(s, "dev", pairs(count, MASKS[order[turn]])) for s, order in zip(sent, orders)
         ]
@@ -479,16 +479,8 @@
     return values
 
 
-def split_bits(array):
-    return array.reshape((2,) * len(BITS) + array.shape[1:])
-
-
-def scatter_rows(array):
-    half = array.shape[1] // 2
-    done = cube_scatter(
-        [split_bits(array[:, :half]), split_bits(array[:, half:])], ("cxyba", "cyxba"), (BITS, BITS)
-    )
-    return jnp.concatenate(done, axis=0)
+def split_bits(array, lead=0):
+    return array.reshape(array.shape[:lead] + (2,) * len(BITS) + array.shape[lead + 1 :])
 
 
 def step_pairs(count, step):
@@ -598,19 +590,18 @@
         line_ref[pl.ds(extra * per_row + chunk, slot, stride=per_row), :] = head_ref[:, spot]
     stem_ref[...] = shifted(line_ref, place_ref[0], place_ref[1], 0, stem_ref.shape[0], 1)
     per_row = D // 128
-    rows = block_ref.shape[1]
+    rows = block_ref.shape[2]
     for part in range(block_ref.shape[0]):
         for chunk in range(per_row):
-            spot = pl.ds(chunk * 128, 128)
-            flat_ref[pl.ds(chunk, rows, stride=per_row), :] = block_ref[part, :, spot]
-            flat_ref[pl.ds(rows * per_row + chunk, 6, stride=per_row), :] = behind_ref[part, pl.ds(0, 6), spot]
+            flat_ref[pl.ds(chunk, rows, stride=per_row), :] = block_ref[part, chunk]
+            flat_ref[pl.ds(rows * per_row + chunk, 6, stride=per_row), :] = behind_ref[part, chunk]
         layer_ref[part] = shifted(flat_ref, place_ref[2], place_ref[3], 0, layer_ref.shape[1], 1)
 
 
 def own_shards(place, head_grad, previous, block_grad, behind, stem_lines, layer_lines):
     per_row = ROW // 128
     lines = (head_grad.shape[0] + previous.shape[0]) * per_row + 256
-    flats = max(block_grad.shape[1] * 3 + 18, layer_lines + 18) + 16
+    flats = max(block_grad.shape[2] * 3 + 18, layer_lines + 18) + 16
     return pl.pallas_call(
         shards_kernel,
         out_shape=[
@@ -622,6 +613,404 @@
         scratch_shapes=[pltpu.VMEM((lines, 128), single), pltpu.VMEM((flats, 128), single)],
         compiler_params=pltpu.CompilerParams(vmem_limit_bytes=40 << 20),
     )(place, head_grad, previous, block_grad, behind)
+
+
+PAD_SEQ = 272
+GELU_SCALE = 0.7978845608028654
+GELU_CUBE = 0.044715
+
+
+def product_plain(left, right):
+    return lax.dot_general(left, right, (((1,), (0,)), ((), ())), preferred_element_type=single)
+
+
+def product_right(left, right):
+    return lax.dot_general(left, right, (((1,), (1,)), ((), ())), preferred_element_type=single)
+
+
+def product_left(left, right):
+    return lax.dot_general(left, right, (((0,), (0,)), ((), ())), preferred_element_type=single)
+
+
+def norm_parts(values):
+    centred = values - jnp.mean(values, axis=-1, keepdims=True)
+    spread = lax.rsqrt(jnp.mean(centred * centred, axis=-1, keepdims=True) + 1e-06)
+    return centred * spread, spread
+
+
+def norm_back(grad, unit, spread, gain):
+    grad_unit = grad * gain
+    mean_one = jnp.mean(grad_unit, axis=-1, keepdims=True)
+    mean_two = jnp.mean(grad_unit * unit, axis=-1, keepdims=True)
+    return spread * (grad_unit - mean_one - unit * mean_two)
+
+
+def gelu_tanh(values):
+    return jnp.tanh(GELU_SCALE * (values + GELU_CUBE * values * values * values))
+
+
+def fetch_rows(side_ref, part, gathered_ref, flat_ref, sems):
+    quarter = flat_ref.shape[0] // 4
+    side = side_ref[0]
+    first, second = side * quarter, (1 - side) * quarter
+    copies = [
+        pltpu.make_async_copy(
+            gathered_ref.at[pl.ds(at, quarter), owner, part],
+            flat_ref.at[pl.ds(spot * quarter, quarter)],
+            sems.at[spot],
+        )
+        for spot, (at, owner) in enumerate(((first, 0), (second, 0), (second, 1), (first, 1)))
+    ]
+    for copy in copies:
+        copy.start()
+    for copy in copies:
+        copy.wait()
+
+
+def matrix_rows(flat_ref, first_row, length):
+    rows = flat_ref.shape[1]
+    low, high = first_row // rows, -(-(first_row + length) // rows)
+    lines = flat_ref[pl.ds(low, high - low)].reshape((high - low) * rows, D)
+    at = first_row - low * rows
+    return lines[at : at + length]
+
+
+def spread_columns(flat_ref, first_row, width, wide_ref, out_ref):
+    length = width * D
+    lines = matrix_rows(flat_ref, first_row, length)
+    for column in range(D // 128):
+        lane = slice(column * 128, (column + 1) * 128)
+        wide_ref[column, pl.ds(0, length), :] = lines[:, lane].astype(single)
+    for group in range(width):
+        for column in range(D // 128):
+            out_ref[group, :, pl.ds(column * 128, 128)] = wide_ref[
+                column, pl.ds(group, D, stride=width), :
+            ].astype(narrow)
+
+
+def head_lanes(values, odd):
+    lanes = lax.broadcasted_iota(jnp.int32, values.shape, 1)
+    return jnp.where((lanes >= HEAD_DIM) == odd, values, jnp.zeros_like(values))
+
+
+def join_lanes(even, odd):
+    lanes = lax.broadcasted_iota(jnp.int32, even.shape, 1)
+    return jnp.where(lanes >= HEAD_DIM, odd, even)
+
+
+def soft_rows(query, key):
+    scores = product_right(query, key) * HEAD_DIM ** (-0.5)
+    spots = lax.broadcasted_iota(jnp.int32, scores.shape, 1)
+    scores = jnp.where(spots < SEQ, scores, -1e30)
+    terms = jnp.exp(scores - jnp.max(scores, axis=-1, keepdims=True))
+    return terms / jnp.sum(terms, axis=-1, keepdims=True)
+
+
+def forward_kernel(part, keep, side_ref, stream_ref, vector_ref, gathered_ref, *refs):
+    out_ref = refs[0]
+    if keep:
+        packed_ref, mixed_ref, attn_ref, pre_ref, mlp_ref = refs[1:6]
+        flat_ref, wide_ref, qkv_ref, up_ref, hidden_ref, sems = refs[6:]
+    else:
+        flat_ref, wide_ref, qkv_ref, up_ref, hidden_ref, packed_ref, mixed_ref, sems = refs[1:]
+    fetch_rows(side_ref, part, gathered_ref, flat_ref, sems)
+    spread_columns(flat_ref, 0, 3, wide_ref, qkv_ref)
+    spread_columns(flat_ref, 4 * D, FF // D, wide_ref, up_ref)
+    w_proj = matrix_rows(flat_ref, 3 * D, D)
+    w_down = matrix_rows(flat_ref, 4 * D + FF, FF)
+    vectors = vector_ref[...].astype(single)
+    stream = stream_ref[...]
+    normed = (norm_parts(stream)[0] * vectors[0:1] + vectors[1:2]).astype(narrow)
+    for group in range(3):
+        packed_ref[:, pl.ds(group * D, D)] = product_plain(normed, qkv_ref[group]).astype(narrow)
+    for image in range(stream.shape[0] // PAD_SEQ):
+        rows = pl.ds(image * PAD_SEQ, PAD_SEQ)
+        for pair in range(HEADS // 2):
+            query, key, value = [
+                packed_ref[rows, pl.ds(group * D + pair * 128, 128)] for group in range(3)
+            ]
+            done = [
+                product_plain(soft_rows(head_lanes(query, odd), key).astype(narrow), value)
+                for odd in (False, True)
+            ]
+            mixed_ref[rows, pl.ds(pair * 128, 128)] = join_lanes(*done).astype(narrow)
+    attn = product_plain(mixed_ref[...], w_proj)
+    middle = stream + vectors[2:3] * attn
+    normed_two = (norm_parts(middle)[0] * vectors[3:4] + vectors[4:5]).astype(narrow)
+    for group in range(FF // D):
+        spot = pl.ds(group * D, D)
+        pre = product_plain(normed_two, up_ref[group])
+        if keep:
+            pre_ref[:, spot] = pre
+        hidden_ref[:, spot] = (0.5 * pre * (1.0 + gelu_tanh(pre))).astype(narrow)
+    mlp = product_plain(hidden_ref[...], w_down)
+    out_ref[...] = middle + vectors[5:6] * mlp
+    if keep:
+        attn_ref[...] = attn
+        mlp_ref[...] = mlp
+
+
+def layer_scratch(gathered):
+    rows, blocks = gathered.shape[3], 2 * gathered.shape[0]
+    return [
+        pltpu.VMEM((blocks, rows, D), narrow),
+        pltpu.VMEM((D // 128, FF, 128), single),
+        pltpu.VMEM((3, D, D), narrow),
+        pltpu.VMEM((FF // D, D, D), narrow),
+    ]
+
+
+def layer_specs_in(count):
+    return (
+        [pl.BlockSpec(memory_space=pltpu.SMEM)]
+        + [pl.BlockSpec(memory_space=pltpu.VMEM)] * (count - 2)
+        + [pl.BlockSpec(memory_space=pl.ANY)]
+    )
+
+
+def layer_forward(side, stream, vectors, gathered, part, keep):
+    tokens = stream.shape[0]
+    shapes = [jax.ShapeDtypeStruct((tokens, D), single)]
+    extra = [
+        jax.ShapeDtypeStruct((tokens, 3 * D), narrow),
+        jax.ShapeDtypeStruct((tokens, D), narrow),
+        jax.ShapeDtypeStruct((tokens, D), single),
+        jax.ShapeDtypeStruct((tokens, FF), single),
+        jax.ShapeDtypeStruct((tokens, D), single),
+    ]
+    scratch = layer_scratch(gathered) + [pltpu.VMEM((tokens, FF), narrow)]
+    if keep:
+        shapes = shapes + extra
+    else:
+        scratch = scratch + [pltpu.VMEM((tokens, 3 * D), narrow), pltpu.VMEM((tokens, D), narrow)]
+    scratch.append(pltpu.SemaphoreType.DMA((4,)))
+    return pl.pallas_call(
+        lambda *refs: forward_kernel(part, keep, *refs),
+        out_shape=shapes,
+        in_specs=layer_specs_in(4),
+        out_specs=[pl.BlockSpec(memory_space=pltpu.VMEM)] * len(shapes),
+        scratch_shapes=scratch,
+        compiler_params=pltpu.CompilerParams(vmem_limit_bytes=56 << 20),
+        cost_estimate=pl.CostEstimate(flops=2 * 10**9, bytes_accessed=2 * 10**7, transcendentals=2 * 10**6),
+    )(side, stream, vectors, gathered)
+
+
+def mlp_back_kernel(
+    part,
+    side_ref,
+    grad_ref,
+    stream_ref,
+    attn_ref,
+    pre_ref,
+    mlp_ref,
+    vector_ref,
+    gathered_ref,
+    *refs,
+):
+    grad_mid_ref, all_grad_ref, vector_grad_ref = refs[-10:-7]
+    flat_ref, wide_ref, up_ref, hidden_ref, grad_pre_ref, weight_grad_ref, sems = refs[-7:]
+    fetch_rows(side_ref, part, gathered_ref, flat_ref, sems)
+    spread_columns(flat_ref, 4 * D, FF // D, wide_ref, up_ref)
+    w_down = matrix_rows(flat_ref, 4 * D + FF, FF)
+    vectors = vector_ref[...].astype(single)
+    grad_out = grad_ref[...]
+    vector_grad_ref[...] = jnp.zeros_like(vector_grad_ref)
+    attn = attn_ref[...]
+    middle = stream_ref[...] + vectors[2:3] * attn
+    unit_two, spread_two = norm_parts(middle)
+    normed_two = (unit_two * vectors[3:4] + vectors[4:5]).astype(narrow)
+    vector_grad_ref[pl.ds(5, 1), :] = jnp.sum(grad_out * mlp_ref[...], axis=0, keepdims=True)
+    grad_mlp = (grad_out * vectors[5:6]).astype(narrow)
+    grad_normed_two = jnp.zeros_like(grad_out)
+    for group in range(FF // D):
+        spot = pl.ds(group * D, D)
+        pre = pre_ref[:, spot]
+        bent = gelu_tanh(pre)
+        hidden_ref[:, spot] = (0.5 * pre * (1.0 + bent)).astype(narrow)
+        slope = 0.5 * (1.0 + bent) + 0.5 * pre * (1.0 - bent * bent) * GELU_SCALE * (
+            1.0 + 3.0 * GELU_CUBE * pre * pre
+        )
+        grad_hidden = product_right(grad_mlp, w_down[group * D : (group + 1) * D])
+        grad_pre = (grad_hidden * slope).astype(narrow)
+        grad_pre_ref[:, spot] = grad_pre
+        grad_normed_two = grad_normed_two + product_right(grad_pre, up_ref[group])
+    for group in range(FF // D):
+        spot = pl.ds(group * D, D)
+        up_grad = product_left(normed_two, grad_pre_ref[:, spot])
+        down_grad = product_left(hidden_ref[:, spot], grad_mlp)
+        for column in range(D // 128):
+            lane = slice(column * 128, (column + 1) * 128)
+            weight_grad_ref[column, pl.ds(group, D, stride=FF // D), :] = up_grad[:, lane]
+            weight_grad_ref[column, pl.ds(FF + group * D, D), :] = down_grad[:, lane]
+    vector_grad_ref[pl.ds(3, 1), :] = jnp.sum(grad_normed_two * unit_two, axis=0, keepdims=True)
+    vector_grad_ref[pl.ds(4, 1), :] = jnp.sum(grad_normed_two, axis=0, keepdims=True)
+    grad_mid = grad_out + norm_back(grad_normed_two, unit_two, spread_two, vectors[3:4])
+    vector_grad_ref[pl.ds(2, 1), :] = jnp.sum(grad_mid * attn, axis=0, keepdims=True)
+    grad_mid_ref[...] = grad_mid
+    store_rows(weight_grad_ref, all_grad_ref, 4 * D, sems.at[0])
+
+
+def attention_back_kernel(
+    part,
+    side_ref,
+    grad_ref,
+    stream_ref,
+    packed_ref,
+    mixed_ref,
+    vector_ref,
+    gathered_ref,
+    *refs,
+):
+    grad_in_ref, all_grad_ref, vector_grad_ref = refs[-10:-7]
+    flat_ref, wide_ref, qkv_ref, grad_mixed_ref, grad_packed_ref, weight_grad_ref, sems = refs[-7:]
+    fetch_rows(side_ref, part, gathered_ref, flat_ref, sems)
+    spread_columns(flat_ref, 0, 3, wide_ref, qkv_ref)
+    w_proj = matrix_rows(flat_ref, 3 * D, D)
+    vectors = vector_ref[...].astype(single)
+    vector_grad_ref[...] = jnp.zeros_like(vector_grad_ref)
+    grad_mid = grad_ref[...]
+    stream = stream_ref[...]
+    grad_attn = (grad_mid * vectors[2:3]).astype(narrow)
+    proj_grad = product_left(mixed_ref[...], grad_attn)
+    for column in range(D // 128):
+        weight_grad_ref[column, pl.ds(3 * D, D), :] = proj_grad[:, column * 128 : (column + 1) * 128]
+    grad_mixed_ref[...] = product_right(grad_attn, w_proj).astype(narrow)
+    for image in range(stream.shape[0] // PAD_SEQ):
+        rows = pl.ds(image * PAD_SEQ, PAD_SEQ)
+        for pair in range(HEADS // 2):
+            query, key, value = [
+                packed_ref[rows, pl.ds(group * D + pair * 128, 128)] for group in range(3)
+            ]
+            grad_mixed = grad_mixed_ref[rows, pl.ds(pair * 128, 128)]
+            parts = []
+            for odd in (False, True):
+                probs = soft_rows(head_lanes(query, odd), key)
+                grad_probs = product_right(head_lanes(grad_mixed, odd), value)
+                grad_value = product_left(probs.astype(narrow), grad_mixed)
+                grad_scores = probs * (grad_probs - jnp.sum(probs * grad_probs, axis=-1, keepdims=True))
+                grad_raw = (grad_scores * HEAD_DIM ** (-0.5)).astype(narrow)
+                parts.append((product_plain(grad_raw, key), product_left(grad_raw, query), grad_value))
+            for group in range(3):
+                grad_packed_ref[rows, pl.ds(group * D + pair * 128, 128)] = join_lanes(
+                    parts[0][group], parts[1][group]
+                ).astype(narrow)
+    unit_one, spread_one = norm_parts(stream)
+    normed = (unit_one * vectors[0:1] + vectors[1:2]).astype(narrow)
+    grad_normed = jnp.zeros_like(grad_mid)
+    for group in range(3):
+        grad_part = grad_packed_ref[:, pl.ds(group * D, D)]
+        grad_normed = grad_normed + product_right(grad_part, qkv_ref[group])
+        qkv_grad = product_left(normed, grad_part)
+        for column in range(D // 128):
+            lane = slice(column * 128, (column + 1) * 128)
+            weight_grad_ref[column, pl.ds(group, D, stride=3), :] = qkv_grad[:, lane]
+    vector_grad_ref[pl.ds(0, 1), :] = jnp.sum(grad_normed * unit_one, axis=0, keepdims=True)
+    vector_grad_ref[pl.ds(1, 1), :] = jnp.sum(grad_normed, axis=0, keepdims=True)
+    grad_in_ref[...] = grad_mid + norm_back(grad_normed, unit_one, spread_one, vectors[0:1])
+    store_rows(weight_grad_ref, all_grad_ref, 0, sems.at[0])
+
+
+def store_rows(weight_grad_ref, all_grad_ref, first_row, sem):
+    copy = pltpu.make_async_copy(
+        weight_grad_ref, all_grad_ref.at[:, pl.ds(first_row, weight_grad_ref.shape[1])], sem
+    )
+    copy.start()
+    copy.wait()
+
+
+def layer_back(kernel, part, weight_rows, side, inputs, vectors, gathered, started, waits, columns, buffers):
+    tokens = inputs[0].shape[0]
+    rows, blocks = gathered.shape[3], 2 * gathered.shape[0]
+    return pl.pallas_call(
+        lambda *refs: kernel(part, *refs),
+        out_shape=[
+            jax.ShapeDtypeStruct((tokens, D), single),
+            jax.ShapeDtypeStruct((D // 128, MATRIX_ROWS, 128), single),
+            jax.ShapeDtypeStruct((8, D), single),
+        ],
+        in_specs=layer_specs_in(len(inputs) + 3)
+        + [pl.BlockSpec(memory_space=pl.ANY)] * (len(started) + len(waits)),
+        out_specs=[
+            pl.BlockSpec(memory_space=pltpu.VMEM),
+            pl.BlockSpec(memory_space=pl.ANY),
+            pl.BlockSpec(memory_space=pltpu.VMEM),
+        ],
+        input_output_aliases={len(inputs) + 3: 1} if started else {},
+        scratch_shapes=[
+            pltpu.VMEM((blocks, rows, D), narrow),
+            pltpu.VMEM((D // 128, columns * D, 128), single),
+            pltpu.VMEM((columns, D, D), narrow),
+        ]
+        + [pltpu.VMEM((tokens, width), narrow) for width in buffers]
+        + [pltpu.VMEM((D // 128, weight_rows, 128), single), pltpu.SemaphoreType.DMA((4,))],
+        compiler_params=pltpu.CompilerParams(vmem_limit_bytes=56 << 20),
+        cost_estimate=pl.CostEstimate(flops=5 * 10**9, bytes_accessed=4 * 10**7, transcendentals=2 * 10**6),
+    )(side, *inputs, vectors, gathered, *started, *waits)
+
+
+def mlp_back(side, grad_out, saved, vectors, gathered, part, waits):
+    stream, packed, mixed, attn, pre, mlp = saved
+    return layer_back(
+        mlp_back_kernel, part, 2 * FF, side, (grad_out, stream, attn, pre, mlp), vectors, gathered, (), waits,
+        FF // D, (FF, FF),
+    )
+
+
+def attention_back(side, grad_mid, saved, vectors, gathered, part, started, waits):
+    stream, packed, mixed, attn, pre, mlp = saved
+    return layer_back(
+        attention_back_kernel, part, 4 * D, side, (grad_mid, stream, packed, mixed), vectors, gathered, (started,), waits,
+        3, (D, 3 * D),
+    )
+
+
+def after_kernel(value_ref, token_ref, out_ref, sem):
+    copy = pltpu.make_async_copy(value_ref, out_ref, sem)
+    copy.start()
+    copy.wait()
+
+
+def after(value, token):
+    return pl.pallas_call(
+        after_kernel,
+        out_shape=jax.ShapeDtypeStruct(value.shape, value.dtype),
+        in_specs=[pl.BlockSpec(memory_space=pl.ANY)] * 2,
+        out_specs=pl.BlockSpec(memory_space=pl.ANY),
+        scratch_shapes=[pltpu.SemaphoreType.DMA(())],
+    )(value, token)
+
+
+def embed_back_kernel(grad_ref, patch_ref, shown_ref, gain_ref, vector_ref, out_ref):
+    grad = grad_ref[...]
+    images = grad.shape[0] // PAD_SEQ
+    shown = shown_ref[...]
+    position = jnp.zeros((PAD_SEQ, D), single)
+    token = jnp.zeros((1, D), single)
+    patch_grads = []
+    for image in range(images):
+        here = grad[image * PAD_SEQ : (image + 1) * PAD_SEQ]
+        position = position + here
+        rows = here[1:SEQ]
+        seen = shown[image * PATCHES : (image + 1) * PATCHES]
+        token = token + jnp.sum(rows * (1.0 - seen), axis=0, keepdims=True)
+        patch_grads.append((rows * seen).astype(narrow))
+    out_ref[...] = jnp.zeros_like(out_ref)
+    out_ref[pl.ds(0, PIX), :] = product_left(patch_ref[...], jnp.concatenate(patch_grads))
+    out_ref[pl.ds(PIX, SEQ), :] = position[:SEQ]
+    out_ref[pl.ds(PIX + SEQ, 1), :] = position[0:1]
+    out_ref[pl.ds(PIX + SEQ + 1, 1), :] = token
+    out_ref[pl.ds(PIX + SEQ + 2, 2), :] = gain_ref[...]
+    out_ref[pl.ds(EMBED_ROWS, vector_ref.shape[0]), :] = vector_ref[...]
+
+
+def embed_back(grad, patch_rows, shown, gains, vector_grads, rows):
+    return pl.pallas_call(
+        embed_back_kernel,
+        out_shape=jax.ShapeDtypeStruct((rows, D), single),
+        in_specs=[pl.BlockSpec(memory_space=pltpu.VMEM)] * 5,
+        out_specs=pl.BlockSpec(memory_space=pltpu.VMEM),
+        compiler_params=pltpu.CompilerParams(vmem_limit_bytes=40 << 20),
+    )(grad, patch_rows, shown, gains, vector_grads)
 
 
 def close_local(
@@ -647,7 +1036,10 @@
     me = lax.axis_index("dev")
     across = MASKS["b"]
     student_side = me >= half
-    groups = [list(range(half)), [i ^ across for i in range(half)]]
+    groups = [list(range(half)), list(range(half, count))]
+    quarter = half // 2
+    swap = jnp.where(student_side, quarter, 0)
+    side = student_side.astype(jnp.int32).reshape(1)
     images_here = patches.shape[0]
     rows_here = images_here * 17
     stem_piece = stem.shape[0]
@@ -677,7 +1069,7 @@
     before = lax.ppermute(own_tail, "dev", step_pairs(count, 1))
     head_span = GROUP * ROW
     stems = jnp.stack([as_lanes(stem_teacher), as_lanes(stem)])
-    after = lax.ppermute(stems[:, : head_span // 128], "dev", step_pairs(count, -1))
+    stems_next = lax.ppermute(stems[:, : head_span // 128], "dev", step_pairs(count, -1))
     start_here = jnp.array(starts, jnp.int32)[me]
     head_at = start_here + front * 128
     embed_at = front * 128 + jnp.where(me == 0, 0, late_start)
@@ -688,7 +1080,7 @@
     head_blocks, layer_blocks, embed_blocks, vector_blocks = own_blocks(
         place,
         stems,
-        after,
+        stems_next,
         as_lanes(own_layers),
         before,
         (front, stem_piece, layer_piece, tail),
@@ -710,7 +1102,7 @@
     both_head = jnp.where(
         student_side, jnp.stack([head_got, head_keep]), jnp.stack([head_keep, head_got])
     )
-    gathered_head = lax.all_gather(both_head, "dev", axis=0, axis_index_groups=groups)
+    gathered_head = lax.all_gather(after(both_head, gathered), "dev", axis=0, axis_index_groups=groups)
 
     vectors = lax.ppermute(vector_blocks, "dev", [(count - 1, 0)])
     seed = jnp.concatenate([embed_blocks.reshape(2 * embed_rows, D), vectors.reshape(8 * 2 * LAYERS, D)])
@@ -741,29 +1133,20 @@
         )
         for m in range(2)
     ]
-    vectors_all = even[2 * embed_rows :].reshape(2, LAYERS, 8, D)[:, :, :6]
-
-    def layer_weights(model, layer_index):
-        chosen = gathered[:, :, model * LAYERS + layer_index]
-        flat = jnp.concatenate([chosen[:, 0], chosen[half // 2 :, 1], chosen[: half // 2, 1]]).reshape(MATRIX_ROWS, D)
-        return (
-            flat[: 3 * D].reshape(D, 3 * D),
-            flat[3 * D : 4 * D],
-            flat[4 * D : 4 * D + FF].reshape(D, FF),
-            flat[4 * D + FF :],
-            vectors_all[model, layer_index],
-        )
+    vectors_all = even[2 * embed_rows :].reshape(2, LAYERS, 8, D)
 
     def head_slots(first, last):
         pieces = []
         i = first
         while i < last:
-            side = i >= half
-            at = i ^ across if side else i
-            stop = i + 1
-            while stop < last and (stop >= half) == side and (stop ^ across if side else stop) == at + stop - i:
-                stop += 1
-            pieces.append(gathered_head[at : at + stop - i, 1 if side else 0])
+            stop = min(last, (i // quarter + 1) * quarter)
+            owner = 1 if i >= half else 0
+            at = (i ^ across if owner else i) ^ swap
+            pieces.append(
+                lax.dynamic_slice(
+                    gathered_head, (at, owner, 0, 0), (stop - i, 1, slot, ROW)
+                ).reshape(stop - i, slot, ROW)
+            )
             i = stop
         return pieces
 
@@ -794,19 +1177,27 @@
         normed = layer_norm(chosen, extras[2].astype(single), extras[3].astype(single)).astype(narrow)
         return chosen, normed
 
+    def start_rows(parts, student):
+        stream = embed(parts, patches, masked_here, student)
+        return jnp.pad(stream, ((0, 0), (0, PAD_SEQ - SEQ), (0, 0))).reshape(images_here * PAD_SEQ, D)
+
     student_parts = embed_parts(1)
-    stream = embed(student_parts, patches, masked_here, True)
+    stream = start_rows(student_parts, True)
     saved_layers = []
-    student_layers = []
     for layer_index in range(LAYERS):
-        weights = layer_weights(1, layer_index)
-        student_layers.append(weights)
-        stream, saved = block_forward(stream, weights)
-        saved_layers.append(saved)
+        before_layer = stream
+        stream, *saved = layer_forward(
+            side, stream, vectors_all[1, layer_index], gathered, LAYERS + layer_index, True
+        )
+        saved_layers.append((before_layer, *saved))
     teacher_parts = embed_parts(0)
-    teacher_stream = embed(teacher_parts, patches, masked_here, False)
+    teacher_stream = start_rows(teacher_parts, False)
     for layer_index in range(LAYERS):
-        teacher_stream = block_forward(teacher_stream, layer_weights(0, layer_index))[0]
+        teacher_stream = layer_forward(
+            side, teacher_stream, vectors_all[0, layer_index], gathered, layer_index, False
+        )[0]
+    stream = stream.reshape(images_here, PAD_SEQ, D)
+    teacher_stream = teacher_stream.reshape(images_here, PAD_SEQ, D)
     chosen, student_normed = head_rows(stream, student_parts[2])
     teacher_normed = head_rows(teacher_stream, teacher_parts[2])[1]
 
@@ -829,9 +1220,14 @@
     hidden_two = jax.nn.gelu(pre_two).astype(narrow)
     bottleneck = contract("rh,hb->rb", hidden_two, w_three)
     unit_z = unit_rows(bottleneck).astype(narrow)
+    pair_rows = -(-2 * rows_here // 16) * 16
+    more_rows = ((0, pair_rows - 2 * rows_here), (0, 0))
     inputs_all = lax.all_gather(
-        jnp.concatenate([normed, hidden_one, hidden_two], axis=1), "dev", axis=0, axis_index_groups=groups
-    ).reshape(half * 2 * rows_here, D + 2 * HID)
+        jnp.pad(jnp.concatenate([normed, hidden_one, hidden_two], axis=1), more_rows),
+        "dev",
+        axis=0,
+        axis_index_groups=groups,
+    ).reshape(half * pair_rows, D + 2 * HID)
 
     all_rows = count * rows_here
     kept_row = jnp.broadcast_to(kept[:, None], (images_here, 17)).reshape(1, rows_here)
@@ -887,11 +1283,11 @@
     grad_pre_one = gelu_back(pre_one, grad_hidden).astype(narrow)
     grad_normed = cut_columns(contract("rh,dh->rd", grad_pre_one, w_one), 1, first_w2, 0)
     grads_all = lax.all_gather(
-        jnp.concatenate([grad_pre_one, grad_pre_two, grad_bottle], axis=1),
+        jnp.pad(jnp.concatenate([grad_pre_one, grad_pre_two, grad_bottle], axis=1), more_rows),
         "dev",
         axis=0,
         axis_index_groups=groups,
-    ).reshape(half * 2 * rows_here, 2 * HID + BOT)
+    ).reshape(half * pair_rows, 2 * HID + BOT)
     normed_back = lax.ppermute(
         grad_normed[:rows_here], "dev", [(i, i ^ across) for i in range(half, count)]
     )
@@ -907,45 +1303,56 @@
         .add(grad_chosen.reshape(images_here, 17, D))
     )
 
-    layer_block_grads = [None] * LAYERS
+    grad_stream = grad_stream.reshape(images_here * PAD_SEQ, D)
+    middle_row = block_rows // 2
+    moving = []
     vector_grads = [None] * LAYERS
     for layer_index in reversed(range(LAYERS)):
-        grad_stream, grads = block_backward(
-            grad_stream, student_layers[layer_index], saved_layers[layer_index]
+        saved, vectors = saved_layers[layer_index], vectors_all[1, layer_index]
+        part = LAYERS + layer_index
+        grad_stream, weight_grad, late_vectors = mlp_back(
+            side, grad_stream, saved, vectors, gathered, part, ()
         )
-        grad_qkv, grad_proj, grad_up, grad_down, vector_grads[layer_index] = grads
-        flat = jnp.concatenate(
-            [
-                grad_qkv.reshape(3 * D, D),
-                grad_proj,
-                grad_up.reshape(FF, D),
-                grad_down,
-            ]
-        ).reshape(count, block_rows, D)
-        layer_block_grads[layer_index] = scatter_rows(flat)
-    grad_patch_w, grad_position, grad_cls, grad_mask_token = embed_backward(
-        grad_stream, patches, masked_here
-    )
-    small = jnp.concatenate(
+        grad_stream, weight_grad, early_vectors = attention_back(
+            side, grad_stream, saved, vectors, gathered, part, weight_grad, moving
+        )
+        vector_grads[layer_index] = (late_vectors + early_vectors)[:6]
+        owned = split_bits(weight_grad.reshape(D // 128, count, block_rows, 128), 1)
+        first = cube_scatter([owned], ("c",), (BITS,), 1)[0]
+        moving = (first,)
+        layer_first = [first] if layer_index == LAYERS - 1 else [first] + layer_first
+    layer_block = jnp.stack(
         [
-            grad_patch_w,
-            grad_position,
-            jnp.stack([grad_cls, grad_mask_token, grad_gain, grad_bias]),
+            jnp.concatenate(
+                cube_scatter(
+                    [first[..., :middle_row, :], first[..., middle_row:, :]],
+                    ("xyba", "yxba"),
+                    (BITS[:-1], BITS[:-1]),
+                    1,
+                ),
+                axis=1,
+            )
+            for first in layer_first
         ]
-        + vector_grads
-    )
-    small_rows = -(-small.shape[0] // count)
-    small = jnp.pad(small, ((0, small_rows * count - small.shape[0]), (0, 0)))
+    )
+    small_rows = -(-(EMBED_ROWS + 6 * LAYERS) // count)
+    small = embed_back(
+        grad_stream,
+        patches.reshape(images_here * PATCHES, PIX),
+        jnp.where(masked_here, 0.0, 1.0).reshape(images_here * PATCHES, 1),
+        jnp.stack([grad_gain, grad_bias]),
+        jnp.concatenate(vector_grads),
+        small_rows * count,
+    )
     small_block = cube_scatter(
         [split_bits(small.reshape(count, small_rows, D))], ("cxyba",), (BITS,)
     )[0]
-    layer_block = jnp.stack(layer_block_grads)
 
     padded = jnp.pad(inputs_all[:, : D + HID], ((0, 0), (-min(bounds[1], 0), slot)))
 
     def block_product(owner, grads):
         window = lax.dynamic_slice(
-            padded, (0, jnp.array(bounds, jnp.int32)[owner] - bounds[1]), (all_rows, slot)
+            padded, (0, jnp.array(bounds, jnp.int32)[owner] - bounds[1]), (half * pair_rows, slot)
         )
         valid = jnp.arange(slot) < jnp.array(sizes, jnp.int32)[owner]
         return contract("rs,rh->sh", jnp.where(valid, window, 0), grads)
@@ -956,7 +1363,7 @@
     third_window = lax.dynamic_slice(
         jnp.pad(inputs_all[:, D + HID :], ((0, 0), (0, slot * ROW // BOT))),
         (0, jnp.array(third_from, jnp.int32)[me]),
-        (all_rows, slot * ROW // BOT),
+        (half * pair_rows, slot * ROW // BOT),
     )
     third_valid = jnp.arange(slot * ROW // BOT) < jnp.array(sizes, jnp.int32)[me] * (ROW // BOT)
     third_grad = contract(
@@ -979,8 +1386,9 @@
     embed_grad = small_all[:EMBED_ROWS].reshape(-1)
     vector_grad = small_all[EMBED_ROWS : EMBED_ROWS + 6 * LAYERS].reshape(LAYERS, 6, D)
 
-    behind = lax.ppermute(layer_block[:, :6], "dev", step_pairs(count, -1))
-    behind = jnp.where(me == count - 1, vector_grad, behind)
+    behind = lax.ppermute(layer_block[:, :, :6], "dev", step_pairs(count, -1))
+    vector_columns = jnp.swapaxes(vector_grad.reshape(LAYERS, 6, D // 128, 128), 1, 2)
+    behind = jnp.where(me == count - 1, vector_columns, behind)
     last_rows = lax.dynamic_slice(
         head_block_grad, (jnp.array(sizes, jnp.int32)[me] - GROUP, 0), (GROUP, ROW)
     )

time: 1090 us -> 836 us (0.77)
  matrix products: 200 us -> 44.9 us
  Pallas kernels: 4.51 us -> 142 us
  local copies, waits for them, and re-layouts: 227 us -> 109 us
  waiting for transfers between devices: 367 us -> 318 us
  other arithmetic: 128 us -> 80.1 us
  starting transfers between devices: 115 us -> 97.8 us
    dot_general x62 -> x15, matrix products: 200 us -> 44.9 us  [contract(): return jnp.einsum(form, left_arg, right_arg, preferred_element_type=single)]
    pallas_call x0 -> x10, Pallas kernels: none -> 137 us  [the longest x4 64.3 us: layer_back(): pl.pallas_call(lambda *refs: kernel(part, *refs), out_shape=[jax.ShapeDty...]
    all_gather x1, waiting for transfers between devices: 159 us -> 65.6 us  [close_local(): lax.all_gather(both_layers, 'dev', axis=0, axis_index_groups=groups)]
    squeeze x13 -> x1, local copies, waits for them, and re-layouts: 31.3 us -> 0.61 us  [close_local(): vectors_all[1, layer_index]]
    ppermute x20, waiting for transfers between devices: 42.1 us -> 71.9 us  [cube_gather(): got = lax.ppermute(held, 'dev', pairs(count, MASKS[name]))]
    ppermute x12, waiting for transfers between devices: 24.8 us -> 52.1 us  [close_local(): got = lax.ppermute(spread, 'dev', moves)]
    all_gather x3, waiting for transfers between devices: 26.2 us -> 0.04 us  [the longest x1 0.02 us: close_local(): lax.all_gather(after(both_head, gathered), 'dev', axis=0, axis_index_grou...]
    reshape x13 -> x4, local copies, waits for them, and re-layouts: 34.4 us -> 8.37 us  [head_slots(): pieces.append(lax.dynamic_slice(gathered_head, (at, owner, 0, 0), (stop -...]
  transfers between devices with their start and end apart: 87 -> 85, of which waited for: 48 -> 51; matrix products, arithmetic and copies ran while one was open for 47% -> 22% of each run, Pallas kernels for 0% -> 14%
where the time goes in v3:
time: 836 us; the launch traced here: 825 us
  waiting for transfers between devices  318 us (38%)
  Pallas kernels  142 us (17%)
  local copies, waits for them, and re-layouts  109 us (13%)
  starting transfers between devices  97.8 us (12%)
  other arithmetic  80.1 us (10%)
  matrix products  44.9 us (5%)
  between operations  33.3 us (4%)
    ppermute x20, waiting for transfers between devices, cube_gather(): got = lax.ppermute(held, 'dev', pairs(count, MASKS[name]))  71.9 us
    all_gather x1, waiting for transfers between devices, close_local(): lax.all_gather(both_layers, 'dev', axis=0, axis_index_groups=groups)  65.6 us
    pallas_call x4, Pallas kernels, layer_back(): pl.pallas_call(lambda *refs: kernel(part, *refs), out_shape=[jax.ShapeDty...  64.3 us
    ppermute x12, waiting for transfers between devices, close_local(): got = lax.ppermute(spread, 'dev', moves)  52.1 us
    pallas_call x4, Pallas kernels, layer_forward(): pl.pallas_call(lambda *refs: forward_kernel(part, keep, *refs), out_shape...  47.5 us
    dot_general x15, matrix products, contract(): return jnp.einsum(form, left_arg, right_arg, preferred_element_type=single)  44.9 us
    ppermute x27, waiting for transfers between devices, cube_scatter(): lax.ppermute(s, 'dev', pairs(count, MASKS[order[turn]]))  42 us
    unnamed x187, local copies, waits for them, and re-layouts  40.8 us
  transfers between devices with their start and end apart: 85, of which 51 were waited for; matrix products, arithmetic and copies ran while one was open for 22% of the time, Pallas kernels for 14%

profile of v3, /device:TPU:8, one launch (start us, length us, event | category | flops | bytes accessed | tf_op | source)
XLA Modules:
  0.0 825.2 jit_solution(2307879334025502845)
XLA Ops:
  28.8 27.1 %collective-permute-done.21 = bf16[4,144,384]{2,1,0:T(8,128)(2,1)S(1)} collective-permute-done((bf16[4,144,384]{2,1,0:T(8,128)(2,1)S(1)}, bf16[4,144,384]{2,1,0:T(8,128)(2,1)S(1)}, u32[]{:S(2)}, u32[]{:S(2)}) %collective-permute-start.21) | collective-permute-done | bytes 442400 | tf_op jit(solution)/shard_map/ppermute | solution.py:1092
  58.8 8.5 %collective-permute-done.23 = bf16[96,2048]{1,0:T(8,128)(2,1)S(1)} collective-permute-done((bf16[96,2048]{1,0:T(8,128)(2,1)S(1)}, bf16[96,2048]{1,0:T(8,128)(2,1)S(1)}, u32[]{:S(2)}, u32[]{:S(2)}) %collective-permute-start.23) | collective-permute-done | bytes 393248 | tf_op jit(solution)/shard_map/ppermute | solution.py:1101
  68.3 65.6 %all-gather.8.cloned.1.call-done.refs_3_.token_ref.refs_7_.refs_6_ = bf16[16,2,4,144,384]{4,3,2,1,0:T(8,128)(2,1)} async-done(((bf16[1,2,4,144,384]{4,3,2,1,0:T(8,128)(2,1)}), bf16[16,2,4,144,384]{4,3,2,1,0:T(8,128)(2,1)}) %all-gather.8.cloned.1.call-update) | async-done | bytes 14155792 | tf_op jit(solution)/shard_map/all_gather | solution.py:1098
  133.9 24.9 %shard_map.488 = bf16[2,96,2048]{2,1,0:T(8,128)(2,1)} custom-call(bf16[2,96,2048]{2,1,0:T(8,128)(2,1)} %maximum_select_fusion.3.value_ref, bf16[16,2,4,144,384]{4,3,2,1,0:T(8,128)(2,1)} %all-gather.8.cloned.1.call-done.refs_3_.token_ref.refs_7_.refs_6_), custom_call_target="tpu_custom_call" | custom-call | tf_op jit(solution)/shard_map/pallas_call | solution.py:974
  177.2 27.9 %collective-permute-done.12 = bf16[336,384]{1,0:T(8,128)(2,1)S(1)} collective-permute-done((bf16[336,384]{1,0:T(8,128)(2,1)S(1)}, bf16[336,384]{1,0:T(8,128)(2,1)S(1)}, u32[]{:S(2)}, u32[]{:S(2)}) %collective-permute-start.12) | collective-permute-done | bytes 258080 | tf_op jit(solution)/shard_map/ppermute | solution.py:1116
  207.1 8.5 %collective-permute-done.18 = bf16[320,384]{1,0:T(8,128)(2,1)S(1)} collective-permute-done((bf16[320,384]{1,0:T(8,128)(2,1)S(1)}, bf16[320,384]{1,0:T(8,128)(2,1)S(1)}, u32[]{:S(2)}, u32[]{:S(2)}) %collective-permute-start.18) | collective-permute-done | bytes 245792 | tf_op jit(solution)/shard_map/ppermute | solution.py:1116
  224.9 13.2 %collective-permute-done.10 = bf16[336,384]{1,0:T(8,128)(2,1)S(1)} collective-permute-done((bf16[336,384]{1,0:T(8,128)(2,1)S(1)}, bf16[336,384]{1,0:T(8,128)(2,1)S(1)}, u32[]{:S(2)}, u32[]{:S(2)}) %collective-permute-start.10) | collective-permute-done | bytes 258080 | tf_op jit(solution)/shard_map/ppermute | solution.py:1116
  246.5 11.6 %shard_map.484.refs_1_ = f32[544,384]{1,0:T(8,128)} custom-call(s32[1]{0:T(128)} %bitcast.12.refs_0_, f32[544,384]{1,0:T(8,128)} %bitcast.387, bf16[8,384]{1,0:T(8,128)(2,1)} %get-tuple-element.258.refs_2_, bf16[16,2,4,144,384]{4,3,2,1,0:T(8,128)(2,1)} %all-gather.8.cloned.1.call-done.refs_3_.token_ref.refs_7_.refs_6_), custom_call_target="tpu_custom_call" | custom-call | flops 2000000000 | bytes 20000000 | tf_op jit(solution)/shard_map/pallas_call | solution.py:787
  258.1 11.6 %shard_map.485 = f32[544,384]{1,0:T(8,128)} custom-call(s32[1]{0:T(128)} %bitcast.12.refs_0_, f32[544,384]{1,0:T(8,128)} %shard_map.484.refs_1_, bf16[8,384]{1,0:T(8,128)(2,1)} %get-tuple-element.257.refs_2_, bf16[16,2,4,144,384]{4,3,2,1,0:T(8,128)(2,1)} %all-gather.8.cloned.1.call-done.refs_3_.token_ref.refs_7_.refs_6_), custom_call_target="tpu_custom_call" | custom-call | flops 2000000000 | bytes 20000000 | tf_op jit(solution)/shard_map/pallas_call | solution.py:787
  272.3 12.0 %shard_map.486 = (f32[544,384]{1,0:T(8,128)}, bf16[544,1152]{1,0:T(8,128)(2,1)}, bf16[544,384]{1,0:T(8,128)(2,1)}, f32[544,384]{1,0:T(8,128)}, f32[544,1536]{1,0:T(8,128)}, /*index=5*/f32[544,384]{1,0:T(8,128)}) custom-call(s32[1]{0:T(128)} %bitcast.12.refs_0_, f32[544,384]{1,0:T(8,128)} %bitcast.377, ...), custom_call_target="tpu_custom_call" | custom-call | flops 2000000000 | bytes 20000000 | tf_op jit(solution)/shard_map/pallas_call | solution.py:787
  284.3 12.2 %shard_map.487 = (f32[544,384]{1,0:T(8,128)}, bf16[544,1152]{1,0:T(8,128)(2,1)}, bf16[544,384]{1,0:T(8,128)(2,1)}, f32[544,384]{1,0:T(8,128)}, f32[544,1536]{1,0:T(8,128)}, /*index=5*/f32[544,384]{1,0:T(8,128)}) custom-call(s32[1]{0:T(128)} %bitcast.12.refs_0_, f32[544,384]{1,0:T(8,128)} %get-tuple-element.53.refs_1_.refs_2_, ...), custom_call_target="tpu_custom_call" | custom-call | flops 2000000000 | bytes 20000000 | tf_op jit(solution)/shard_map/pallas_call | solution.py:787
  361.1 12.6 %collective-permute-done.27 = bf16[4,2,68,256]{3,2,1,0:T(8,128)(2,1)S(1)} collective-permute-done((bf16[4,2,68,256]{3,2,1,0:T(8,128)(2,1)S(1)}, bf16[4,2,68,256]{3,2,1,0:T(8,128)(2,1)S(1)}, u32[]{:S(2)}, u32[]{:S(2)}) %collective-permute-start.27) | collective-permute-done | bytes 278560 | tf_op jit(solution)/shard_map/ppermute | solution.py:444
  382.6 6.8 fusion.1
  406.7 7.9 subtract_convert_fusion
  458.0 6.5 fusion.166
  487.5 14.8 %shard_map.489 = (f32[544,384]{1,0:T(8,128)}, f32[3,4608,128]{2,1,0:T(8,128)}, f32[8,384]{1,0:T(8,128)}) custom-call(s32[1]{0:T(128)} %bitcast.12.refs_0_, f32[544,384]{1,0:T(8,128)} %bitcast.384, f32[544,384]{1,0:T(8,128)} %get-tuple-element.53.refs_1_.refs_2_, f32[544,384]{1,0:T(8,128)} %get-tuple-element.56.refs_3_, ...), custom_call_target="tpu_custom_call" | custom-call | flops 5000000000 | bytes 40000000 | tf_op jit(solution)/shard_map/pallas_call | solution.py:924
  502.3 17.5 %shard_map.490 = (f32[544,384]{1,0:T(8,128)}, f32[3,4608,128]{2,1,0:T(8,128)}, f32[8,384]{1,0:T(8,128)}) custom-call(s32[1]{0:T(128)} %bitcast.12.refs_0_, f32[544,384]{1,0:T(8,128)} %get-tuple-element.59.refs_1_, f32[544,384]{1,0:T(8,128)} %get-tuple-element.53.refs_1_.refs_2_, ...), custom_call_target="tpu_custom_call", output_to_operand_aliasing={{1}: (7, {})} | custom-call | flops 5000000000 | bytes 40000000 | tf_op jit(solution)/shard_map/pallas_call | solution.py:924
  544.1 14.7 %shard_map.491 = (f32[544,384]{1,0:T(8,128)}, f32[3,4608,128]{2,1,0:T(8,128)}, f32[8,384]{1,0:T(8,128)}) custom-call(s32[1]{0:T(128)} %bitcast.12.refs_0_, f32[544,384]{1,0:T(8,128)} %get-tuple-element.63.refs_1_, f32[544,384]{1,0:T(8,128)} %bitcast.378, f32[544,384]{1,0:T(8,128)} %get-tuple-element.64.refs_3_, f32[544,1536]{1,0:T(8,128)} %get-tuple-element.65.refs_4_, ...), custom_call_target="tpu_custom_call" | custom-call | flops 5000000000 | bytes 40000000 | tf_op jit(solution)/shard_map/pallas_call | solution.py:924
  565.2 17.3 %shard_map.492 = (f32[544,384]{1,0:T(8,128)}, f32[3,4608,128]{2,1,0:T(8,128)}, f32[8,384]{1,0:T(8,128)}) custom-call(s32[1]{0:T(128)} %bitcast.12.refs_0_, f32[544,384]{1,0:T(8,128)} %get-tuple-element.67.refs_1_, f32[544,384]{1,0:T(8,128)} %bitcast.379, bf16[544,1152]{1,0:T(8,128)(2,1)} %get-tuple-element.68.refs_3_, ...), custom_call_target="tpu_custom_call", output_to_operand_aliasing={{1}: (7, {})} | custom-call | flops 5000000000 | bytes 40000000 | tf_op jit(solution)/shard_map/pallas_call | solution.py:924
  646.0 8.1 collective-permute-done.77
  660.2 22.6 %collective-permute-done.78 = f32[16,27,384]{2,0,1:T(8,128)S(1)} collective-permute-done((f32[16,27,384]{2,0,1:T(8,128)S(1)}, f32[16,27,384]{2,0,1:T(8,128)S(1)}, u32[]{:S(2)}, u32[]{:S(2)}) %collective-permute-start.78) | collective-permute-done | bytes 663584 | tf_op jit(solution)/shard_map/ppermute | solution.py:444
  713.7 6.6 fusion.2
  730.2 23.6 %collective-permute-done.39 = f32[96,2048]{1,0:T(8,128)} collective-permute-done((f32[96,2048]{1,0:T(8,128)}, f32[96,2048]{1,0:T(8,128)}, u32[]{:S(2)}, u32[]{:S(2)}) %collective-permute-start.39) | collective-permute-done | bytes 786464 | tf_op jit(solution)/shard_map/ppermute | solution.py:1374
  786.5 7.2 multiply_add_fusion
  (654 shorter events, 402.1 us)
Async XLA Ops:
  7.2 126.7 %all-gather.8.cloned.1.call-start = ((), (), s32[]{:S(2)}) async-start(), calls=%async_computation | async-start | bytes 15040512 | tf_op jit(solution)/shard_map/all_gather | solution.py:1098
  27.2 28.7 %collective-permute-start.21 = (bf16[4,144,384]{2,1,0:T(8,128)(2,1)S(1)}, bf16[4,144,384]{2,1,0:T(8,128)(2,1)S(1)}, u32[]{:S(2)}, u32[]{:S(2)}) collective-permute-start(bf16[4,144,384]{2,1,0:T(8,128)(2,1)S(1)} %get-tuple-element.52), channel_id=1, source_target_pairs={{0,24},{1,25},{2,26},{3,27},{4,28},{5,29},{6,30},{7,31},{8,16},{9,... | collective-permute-start | bytes 1327112 | tf_op jit(solution)/shard_map/ppermute | solution.py:1092
  57.0 249.0 %all-gather.10.cloned.1.call-start = ((), (), s32[]{:S(2)}) async-start(), calls=%async_computation.1 | async-start | bytes 13369344 | tf_op jit(solution)/shard_map/all_gather | solution.py:1105
  158.9 549.0 %all-gather.12.cloned.1.call-start = ((), (), s32[]{:S(2)}) async-start(), calls=%async_computation.2 | async-start | bytes 12185600 | tf_op jit(solution)/shard_map/all_gather | solution.py:1225
  172.5 32.6 %collective-permute-start.12 = (bf16[336,384]{1,0:T(8,128)(2,1)S(1)}, bf16[336,384]{1,0:T(8,128)(2,1)S(1)}, u32[]{:S(2)}, u32[]{:S(2)}) collective-permute-start(bf16[336,384]{1,0:T(8,128)(2,1)S(1)} %get-tuple-element.228), channel_id=1, source_target_pairs={{0,8},{1,9},{24,16},{25,17}} | collective-permute-start | bytes 774152 | tf_op jit(solution)/shard_map/ppermute | solution.py:1116
  174.5 41.2 %collective-permute-start.18 = (bf16[320,384]{1,0:T(8,128)(2,1)S(1)}, bf16[320,384]{1,0:T(8,128)(2,1)S(1)}, u32[]{:S(2)}, u32[]{:S(2)}) collective-permute-start(bf16[320,384]{1,0:T(8,128)(2,1)S(1)} %broadcast_select_fusion.14), channel_id=1, source_target_pairs={{0,8},{1,9},{4,12},{5,13},{24,16},{25,17},{28,20},{29,21}} | collective-permute-start | bytes 737288 | tf_op jit(solution)/shard_map/ppermute | solution.py:1116
  176.5 41.2 %collective-permute-start.9 = (bf16[336,384]{1,0:T(8,128)(2,1)S(1)}, bf16[336,384]{1,0:T(8,128)(2,1)S(1)}, u32[]{:S(2)}, u32[]{:S(2)}) collective-permute-start(bf16[336,384]{1,0:T(8,128)(2,1)S(1)} %broadcast_select_fusion.10), channel_id=1, source_target_pairs={{0,24},{1,25},{2,26},{3,27},{4,28},{5,29},{6,30},{7,31}} | collective-permute-start | bytes 774152 | tf_op jit(solution)/shard_map/ppermute | solution.py:1116
  218.3 19.7 %collective-permute-start.10 = (bf16[336,384]{1,0:T(8,128)(2,1)S(1)}, bf16[336,384]{1,0:T(8,128)(2,1)S(1)}, u32[]{:S(2)}, u32[]{:S(2)}) collective-permute-start(bf16[336,384]{1,0:T(8,128)(2,1)S(1)} %broadcast_select_fusion.11), channel_id=1, source_target_pairs={{0,8},{1,9},{2,10},{3,11},{4,12},{5,13},{6,14},{7,15},{24,16},{25,... | collective-permute-start | bytes 774152 | tf_op jit(solution)/shard_map/ppermute | solution.py:1116
  220.3 18.4 %collective-permute-start.14 = (bf16[336,384]{1,0:T(8,128)(2,1)S(1)}, bf16[336,384]{1,0:T(8,128)(2,1)S(1)}, u32[]{:S(2)}, u32[]{:S(2)}) collective-permute-start(bf16[336,384]{1,0:T(8,128)(2,1)S(1)} %broadcast_select_fusion.7), channel_id=1, source_target_pairs={{0,4},{1,5},{24,28},{25,29},{8,12},{9,13},{16,20},{17,21},{2,6},{3... | collective-permute-start | bytes 774152 | tf_op jit(solution)/shard_map/ppermute | solution.py:1116
  327.5 386.2 %all-gather.14.cloned.1.call-start = ((), (), s32[]{:S(2)}) async-start(), calls=%async_computation.3 | async-start | bytes 11837440 | tf_op jit(solution)/shard_map/all_gather | solution.py:1285
  327.7 18.0 %collective-permute-start = (f32[1,1,34]{2,1,0:T(1,128)S(1)}, f32[1,1,34]{2,1,0:T(1,128)S(1)}, u32[]{:S(2)}, u32[]{:S(2)}) collective-permute-start(f32[1,1,34]{2,1,0:T(1,128)S(1)} %broadcast_in_dim_reshape.6), channel_id=1, source_target_pairs={{0,24},{1,25},{2,26},{3,27},{4,28},{5,29},{6,30},{7,31},{8,16},{9,... | collective-permute-start | bytes 416 | tf_op jit(solution)/shard_map/ppermute | solution.py:444
  357.0 16.8 %collective-permute-start.27 = (bf16[4,2,68,256]{3,2,1,0:T(8,128)(2,1)S(1)}, bf16[4,2,68,256]{3,2,1,0:T(8,128)(2,1)S(1)}, u32[]{:S(2)}, u32[]{:S(2)}) collective-permute-start(bf16[4,2,68,256]{3,2,1,0:T(8,128)(2,1)S(1)} %maximum_select_fusion.7), channel_id=1, source_target_pairs={{0,8},{1,9},{2,10},{3,11},{4,12},{5,13},{6,14},{7,15},{8,0},{9,1},... | collective-permute-start | bytes 835592 | tf_op jit(solution)/shard_map/ppermute | solution.py:444
  434.6 18.1 %collective-permute-start.37 = (bf16[68,256]{1,0:T(8,128)(2,1)S(1)}, bf16[68,256]{1,0:T(8,128)(2,1)S(1)}, u32[]{:S(2)}, u32[]{:S(2)}) collective-permute-start(bf16[68,256]{1,0:T(8,128)(2,1)S(1)} %fusion.108), channel_id=1, source_target_pairs={{0,2},{1,3},{2,0},{3,1},{4,6},{5,7},{6,4},{7,5},{8,10},{9,11},{10,... | collective-permute-start | bytes 104456 | tf_op jit(solution)/shard_map/ppermute | solution.py:470
  477.7 48.2 %collective-permute-start.70 = (f32[2,1,2048]{2,0,1:T(2,128)S(1)}, f32[2,1,2048]{2,0,1:T(2,128)S(1)}, u32[]{:S(2)}, u32[]{:S(2)}) collective-permute-start(f32[2,1,2048]{2,0,1:T(2,128)S(1)} %maximum_select_fusion.17), channel_id=1, source_target_pairs={{0,2},{1,3},{2,0},{3,1},{4,6},{5,7},{6,4},{7,5},{8,10},{9,11},{10,... | collective-permute-start | bytes 49160 | tf_op jit(solution)/shard_map/ppermute | solution.py:444
  525.9 33.0 %collective-permute-start.41 = (f32[3,2,2,2,2,144,128]{6,5,0,2,1,3,4:T(8,128)S(1)}, f32[3,2,2,2,2,144,128]{6,5,0,2,1,3,4:T(8,128)}, u32[]{:S(2)}, u32[]{:S(2)}) collective-permute-start(f32[3,2,2,2,2,144,128]{6,5,0,2,1,3,4:T(8,128)S(1)} %get-tuple-element.206), channel_id=1, source_target_pairs={{0,1},{1,0},{2,3},{3,2},{4,5},{5,4},{6,7},{7,6},{8,9},{9,8},{10,11... | collective-permute-start | bytes 10616840 | tf_op jit(solution)/shard_map/ppermute | solution.py:470
  588.5 19.5 %collective-permute-start.59 = (f32[2,2,2,2,27,384]{5,3,4,2,1,0:T(2,128)S(1)}, f32[2,2,2,2,27,384]{5,3,4,2,1,0:T(2,128)S(1)}, u32[]{:S(2)}, u32[]{:S(2)}) collective-permute-start(f32[2,2,2,2,27,384]{5,3,4,2,1,0:T(2,128)S(1)} %copy.230), channel_id=1, source_target_pairs={{0,1},{1,0},{2,3},{3,2},{4,5},{5,4},{6,7},{7,6},{8,9},{9,8},{10,11... | collective-permute-start | bytes 1990664 | tf_op jit(solution)/shard_map/ppermute | solution.py:470
  597.7 57.0 %collective-permute-start.42 = (f32[3,2,2,2,2,144,128]{6,5,0,2,1,3,4:T(8,128)S(1)}, f32[3,2,2,2,2,144,128]{6,5,0,2,1,3,4:T(8,128)S(1)}, u32[]{:S(2)}, u32[]{:S(2)}) collective-permute-start(f32[3,2,2,2,2,144,128]{6,5,0,2,1,3,4:T(8,128)S(1)} %select_bitcast_fusion), channel_id=1, source_target_pairs={{0,1},{1,0},{2,3},{3,2},{4,5},{5,4},{6,7},{7,6},{8,9},{9,8},{10,11... | collective-permute-start | bytes 10616840 | tf_op jit(solution)/shard_map/ppermute | solution.py:470
  606.2 15.7 %collective-permute-start.56 = (bf16[3,2,2,72,128]{4,3,0,2,1:T(8,128)(2,1)S(1)}, bf16[3,2,2,72,128]{4,3,0,2,1:T(8,128)(2,1)S(1)}, u32[]{:S(2)}, u32[]{:S(2)}) collective-permute-start(bf16[3,2,2,72,128]{4,3,0,2,1:T(8,128)(2,1)S(1)} %fusion.88), channel_id=1, source_target_pairs={{0,2},{1,3},{2,0},{3,1},{4,6},{5,7},{6,4},{7,5},{8,10},{9,11},{10,... | collective-permute-start | bytes 663560 | tf_op jit(solution)/shard_map/ppermute | solution.py:470
  645.9 14.3 %collective-permute-start.58 = (bf16[3,72,128]{2,1,0:T(8,128)(2,1)S(1)}, bf16[3,72,128]{2,1,0:T(8,128)(2,1)S(1)}, u32[]{:S(2)}, u32[]{:S(2)}) collective-permute-start(bf16[3,72,128]{2,1,0:T(8,128)(2,1)S(1)} %fusion.105), channel_id=1, source_target_pairs={{0,8},{1,9},{2,10},{3,11},{4,12},{5,13},{6,14},{7,15},{8,0},{9,1},... | collective-permute-start | bytes 165896 | tf_op jit(solution)/shard_map/ppermute | solution.py:470
  654.6 28.3 %collective-permute-start.78 = (f32[16,27,384]{2,0,1:T(8,128)S(1)}, f32[16,27,384]{2,0,1:T(8,128)S(1)}, u32[]{:S(2)}, u32[]{:S(2)}) collective-permute-start(f32[16,27,384]{2,0,1:T(8,128)S(1)} %copy.241), channel_id=1, source_target_pairs={{0,24},{1,25},{2,26},{3,27},{4,28},{5,29},{6,30},{7,31},{8,16},{9,... | collective-permute-start | bytes 1990664 | tf_op jit(solution)/shard_map/ppermute | solution.py:444
  658.1 31.0 %collective-permute-start.47 = (bf16[3,2,2,2,72,128]{5,4,0,2,1,3:T(8,128)(2,1)}, bf16[3,2,2,2,72,128]{5,4,0,2,1,3:T(8,128)(2,1)S(1)}, u32[]{:S(2)}, u32[]{:S(2)}) collective-permute-start(bf16[3,2,2,2,72,128]{5,4,0,2,1,3:T(8,128)(2,1)} %fusion.75), channel_id=1, source_target_pairs={{0,4},{1,5},{2,6},{3,7},{4,0},{5,1},{6,2},{7,3},{8,12},{9,13},{10,... | collective-permute-start | bytes 1327112 | tf_op jit(solution)/shard_map/ppermute | solution.py:470
  658.8 30.3 %collective-permute-start.43 = (bf16[3,2,2,2,72,128]{5,4,0,2,1,3:T(8,128)(2,1)}, bf16[3,2,2,2,72,128]{5,4,0,2,1,3:T(8,128)(2,1)}, u32[]{:S(2)}, u32[]{:S(2)}) collective-permute-start(bf16[3,2,2,2,72,128]{5,4,0,2,1,3:T(8,128)(2,1)} %fusion.74), channel_id=1, source_target_pairs={{0,2},{1,3},{2,0},{3,1},{4,6},{5,7},{6,4},{7,5},{8,10},{9,11},{10,... | collective-permute-start | bytes 1327112 | tf_op jit(solution)/shard_map/ppermute | solution.py:470
  720.3 33.5 %collective-permute-start.39 = (f32[96,2048]{1,0:T(8,128)}, f32[96,2048]{1,0:T(8,128)}, u32[]{:S(2)}, u32[]{:S(2)}) collective-permute-start(f32[96,2048]{1,0:T(8,128)} %fusion.2), channel_id=1, source_target_pairs={{16,8},{17,9},{18,10},{19,11},{20,12},{21,13},{22,14},{23,15},{24,... | collective-permute-start | bytes 2359304 | tf_op jit(solution)/shard_map/ppermute | solution.py:1374
  762.1 46.2 %collective-permute-start.79 = (f32[16,2048]{1,0:T(8,128)S(1)}, f32[16,2048]{1,0:T(8,128)S(1)}, u32[]{:S(2)}, u32[]{:S(2)}) collective-permute-start(f32[16,2048]{1,0:T(8,128)S(1)} %constant_dynamic-slice_fusion), channel_id=1, source_target_pairs={{0,1},{1,2},{2,3},{3,4},{4,5},{5,6},{6,7},{7,8},{8,9},{9,10},{10,1... | collective-permute-start | bytes 393224 | tf_op jit(solution)/shard_map/ppermute | solution.py:1395
  (149 other events, 1059.7 us)
Sparse Core Ops, SparseCore 0:
  57.1 76.7 all-gather.7
  159.0 100.6 all-gather.9
  327.6 69.3 all-gather.11
  472.6 65.7 all-gather.13

commit v4 on v3

--- a/solution.py
+++ b/solution.py
@@ -964,23 +964,20 @@
     )
 
 
-def after_kernel(value_ref, token_ref, out_ref, sem):
-    copy = pltpu.make_async_copy(value_ref, out_ref, sem)
-    copy.start()
-    copy.wait()
-
-
-def after(value, token):
+def after(value, *tokens):
+    def kernel(*refs):
+        refs[-1][...] = refs[0][...]
+
     return pl.pallas_call(
-        after_kernel,
+        kernel,
         out_shape=jax.ShapeDtypeStruct(value.shape, value.dtype),
-        in_specs=[pl.BlockSpec(memory_space=pl.ANY)] * 2,
-        out_specs=pl.BlockSpec(memory_space=pl.ANY),
-        scratch_shapes=[pltpu.SemaphoreType.DMA(())],
-    )(value, token)
-
-
-def embed_back_kernel(grad_ref, patch_ref, shown_ref, gain_ref, vector_ref, out_ref):
+        in_specs=[pl.BlockSpec(memory_space=pltpu.VMEM)] + [pl.BlockSpec(memory_space=pl.ANY)] * len(tokens),
+        out_specs=pl.BlockSpec(memory_space=pltpu.VMEM),
+    )(value, *tokens)
+
+
+def embed_back_kernel(grad_ref, patch_ref, shown_ref, gain_ref, vector_ref, *refs):
+    out_ref = refs[-1]
     grad = grad_ref[...]
     images = grad.shape[0] // PAD_SEQ
     shown = shown_ref[...]
@@ -994,23 +991,258 @@
         seen = shown[image * PATCHES : (image + 1) * PATCHES]
         token = token + jnp.sum(rows * (1.0 - seen), axis=0, keepdims=True)
         patch_grads.append((rows * seen).astype(narrow))
+    patch_grad = product_left(patch_ref[...], jnp.concatenate(patch_grads))
     out_ref[...] = jnp.zeros_like(out_ref)
-    out_ref[pl.ds(0, PIX), :] = product_left(patch_ref[...], jnp.concatenate(patch_grads))
-    out_ref[pl.ds(PIX, SEQ), :] = position[:SEQ]
-    out_ref[pl.ds(PIX + SEQ, 1), :] = position[0:1]
-    out_ref[pl.ds(PIX + SEQ + 1, 1), :] = token
-    out_ref[pl.ds(PIX + SEQ + 2, 2), :] = gain_ref[...]
-    out_ref[pl.ds(EMBED_ROWS, vector_ref.shape[0]), :] = vector_ref[...]
-
-
-def embed_back(grad, patch_rows, shown, gains, vector_grads, rows):
+    for column in range(D // 128):
+        lane = slice(column * 128, (column + 1) * 128)
+        out_ref[column, pl.ds(0, PIX), :] = patch_grad[:, lane]
+        out_ref[column, pl.ds(PIX, SEQ), :] = position[:SEQ, lane]
+        out_ref[column, pl.ds(PIX + SEQ, 1), :] = position[0:1, lane]
+        out_ref[column, pl.ds(PIX + SEQ + 1, 1), :] = token[:, lane]
+        out_ref[column, pl.ds(PIX + SEQ + 2, 2), :] = gain_ref[:, lane]
+        out_ref[column, pl.ds(EMBED_ROWS, vector_ref.shape[0]), :] = vector_ref[:, lane]
+
+
+def embed_back(grad, patch_rows, shown, gains, vector_grads, rows, waits):
     return pl.pallas_call(
         embed_back_kernel,
-        out_shape=jax.ShapeDtypeStruct((rows, D), single),
-        in_specs=[pl.BlockSpec(memory_space=pltpu.VMEM)] * 5,
+        out_shape=jax.ShapeDtypeStruct((D // 128, rows, 128), single),
+        in_specs=[pl.BlockSpec(memory_space=pltpu.VMEM)] * 5 + [pl.BlockSpec(memory_space=pl.ANY)] * len(waits),
         out_specs=pl.BlockSpec(memory_space=pltpu.VMEM),
         compiler_params=pltpu.CompilerParams(vmem_limit_bytes=40 << 20),
-    )(grad, patch_rows, shown, gains, vector_grads)
+        cost_estimate=pl.CostEstimate(flops=10**9, bytes_accessed=2 * 10**7, transcendentals=0),
+    )(grad, patch_rows, shown, gains, vector_grads, *waits)
+
+
+def proto_units(values):
+    rounded = values.astype(narrow).astype(single)
+    scale = lax.rsqrt(jnp.sum(rounded * rounded, axis=-1, keepdims=True) + 1e-06)
+    return rounded, scale, (rounded * scale).astype(narrow)
+
+
+def proto_terms(teacher_z, student_z, teacher_unit, student_unit, centre_column):
+    teacher_logits = product_right(teacher_unit, teacher_z)
+    logits = product_right(student_unit, student_z)
+    teacher_exp = jnp.exp((teacher_logits - centre_column) * (1.0 / tau_teacher))
+    student_exp = jnp.exp(logits * (1.0 / tau_student))
+    return teacher_logits, logits, teacher_exp, student_exp
+
+
+def logits_kernel(
+    teacher_z_ref,
+    student_z_ref,
+    teacher_ref,
+    student_ref,
+    centre_ref,
+    class_ref,
+    mixed_ref,
+    sums_ref,
+    centre_sum_ref,
+    student_mix_ref,
+    teacher_mix_ref,
+    totals_ref,
+):
+    step = pl.program_id(0)
+
+    @pl.when(step == 0)
+    def _():
+        student_mix_ref[...] = jnp.zeros_like(student_mix_ref)
+        teacher_mix_ref[...] = jnp.zeros_like(teacher_mix_ref)
+        totals_ref[...] = jnp.zeros_like(totals_ref)
+
+    teacher_unit = proto_units(teacher_ref[...])[2]
+    student_unit = proto_units(student_ref[...])[2]
+    teacher_logits, logits, teacher_exp, student_exp = proto_terms(
+        teacher_z_ref[...], student_z_ref[...], teacher_unit, student_unit, centre_ref[...]
+    )
+    totals_ref[pl.ds(0, 1), :] += jnp.sum(teacher_exp, axis=0, keepdims=True)
+    totals_ref[pl.ds(1, 1), :] += jnp.sum(student_exp, axis=0, keepdims=True)
+    totals_ref[pl.ds(2, 1), :] += jnp.sum(teacher_exp * logits, axis=0, keepdims=True)
+    centre_sum_ref[...] = jnp.sum(teacher_logits * class_ref[0:1], axis=1, keepdims=True)
+    student_mix_ref[...] += product_left(student_unit, student_exp.astype(narrow))
+    teacher_mix_ref[...] += product_left(student_unit, teacher_exp.astype(narrow))
+
+    @pl.when(step == pl.num_programs(0) - 1)
+    def _():
+        mixed_ref[:, pl.ds(0, BOT)] = student_mix_ref[...].T
+        mixed_ref[:, pl.ds(BOT, BOT)] = teacher_mix_ref[...].T
+        sums_ref[...] = totals_ref[...]
+
+
+def proto_specs(rows, block):
+    whole = pl.BlockSpec((rows, BOT), lambda i: (0, 0))
+    table = pl.BlockSpec((block, BOT), lambda i: (i, 0))
+    column = pl.BlockSpec((block, 1), lambda i: (i, 0))
+    lines = pl.BlockSpec((8, rows), lambda i: (0, 0))
+    return whole, table, column, lines
+
+
+def logits_pass(teacher_z, student_z, teacher, student, centre_column, class_lines):
+    rows, protos_here = teacher_z.shape[0], student.shape[0]
+    block = protos_here // 4
+    whole, table, column, lines = proto_specs(rows, block)
+    return pl.pallas_call(
+        logits_kernel,
+        grid=(4,),
+        out_shape=[
+            jax.ShapeDtypeStruct((rows, 2 * BOT), single),
+            jax.ShapeDtypeStruct((8, rows), single),
+            jax.ShapeDtypeStruct((protos_here, 1), single),
+        ],
+        in_specs=[whole, whole, table, table, column, lines],
+        out_specs=[pl.BlockSpec((rows, 2 * BOT), lambda i: (0, 0)), lines, column],
+        scratch_shapes=[
+            pltpu.VMEM((BOT, rows), single),
+            pltpu.VMEM((BOT, rows), single),
+            pltpu.VMEM((8, rows), single),
+        ],
+        compiler_params=pltpu.CompilerParams(vmem_limit_bytes=56 << 20),
+        cost_estimate=pl.CostEstimate(flops=5 * 10**9, bytes_accessed=10**7, transcendentals=5 * 10**6),
+    )(teacher_z, student_z, teacher, student, centre_column, class_lines)
+
+
+def proto_grad_kernel(
+    teacher_z_ref, student_z_ref, teacher_ref, student_ref, centre_ref, scale_ref, grad_ref, square_ref
+):
+    step = pl.program_id(0)
+
+    @pl.when(step == 0)
+    def _():
+        square_ref[...] = jnp.zeros_like(square_ref)
+
+    teacher_unit = proto_units(teacher_ref[...])[2]
+    rounded, scale, student_unit = proto_units(student_ref[...])
+    student_z = student_z_ref[...]
+    _, _, teacher_exp, student_exp = proto_terms(
+        teacher_z_ref[...], student_z, teacher_unit, student_unit, centre_ref[...]
+    )
+    grad_logits = (student_exp * scale_ref[0:1] - teacher_exp * scale_ref[1:2]).astype(narrow)
+    unit_grad = product_plain(grad_logits, student_z)
+    along = jnp.sum(unit_grad * rounded, axis=-1, keepdims=True)
+    grad = scale * (unit_grad - rounded * (along * scale * scale))
+    grad_ref[...] = grad
+    square_ref[...] += jnp.broadcast_to(jnp.sum(grad * grad), square_ref.shape)
+
+
+def proto_grad_pass(teacher_z, student_z, teacher, student, centre_column, scale_lines):
+    rows, protos_here = teacher_z.shape[0], student.shape[0]
+    block = protos_here // 4
+    whole, table, column, lines = proto_specs(rows, block)
+    return pl.pallas_call(
+        proto_grad_kernel,
+        grid=(4,),
+        out_shape=[
+            jax.ShapeDtypeStruct((protos_here, BOT), single),
+            jax.ShapeDtypeStruct((8, 128), single),
+        ],
+        in_specs=[whole, whole, table, table, column, lines],
+        out_specs=[table, pl.BlockSpec((8, 128), lambda i: (0, 0))],
+        compiler_params=pltpu.CompilerParams(vmem_limit_bytes=56 << 20),
+        cost_estimate=pl.CostEstimate(flops=4 * 10**9, bytes_accessed=10**7, transcendentals=5 * 10**6),
+    )(teacher_z, student_z, teacher, student, centre_column, scale_lines)
+
+
+def proto_update(factor, student, moment, second, teacher, grad):
+    def kernel(factor_ref, *refs):
+        weight, moment, second, teacher, grad = [ref[...] for ref in refs[:5]]
+        done = adam_update(weight, moment, second, grad * factor_ref[0], teacher)
+        for ref, value in zip(refs[5:], done):
+            ref[...] = value
+
+    block = student.shape[0] // 4
+    table = pl.BlockSpec((block, BOT), lambda i: (i, 0))
+    return pl.pallas_call(
+        kernel,
+        grid=(4,),
+        out_shape=[
+            jax.ShapeDtypeStruct(student.shape, narrow if number == 3 else single) for number in range(5)
+        ],
+        in_specs=[pl.BlockSpec(memory_space=pltpu.SMEM)] + [table] * 5,
+        out_specs=[table] * 5,
+        compiler_params=pltpu.CompilerParams(vmem_limit_bytes=40 << 20),
+        cost_estimate=pl.CostEstimate(flops=10**7, bytes_accessed=2 * 10**7, transcendentals=0),
+    )(factor.reshape(1), student, moment, second, teacher, grad)
+
+
+def head_grads_kernel(
+    place_ref, inputs_ref, grads_ref, own_ref, partner_ref, window_ref, rows_ref, product_ref,
+    third_ref, bottle_ref, line_ref, sems,
+):
+    slot = own_ref.shape[0]
+    lead = product_ref.shape[0] - window_ref.shape[1]
+    number = lax.broadcasted_iota(jnp.int32, (slot, 1), 0)
+    product_ref[pl.ds(0, lead), :] = jnp.zeros((lead, ROW), single)
+
+    def block(at, out_ref):
+        column = pl.multiple_of(place_ref[at], 128)
+        grad_column = pl.multiple_of(place_ref[at + 3], 128)
+        copies = [
+            pltpu.make_async_copy(
+                inputs_ref.at[:, pl.ds(column, window_ref.shape[1])], window_ref, sems.at[0]
+            ),
+            pltpu.make_async_copy(grads_ref.at[:, pl.ds(grad_column, ROW)], rows_ref, sems.at[1]),
+        ]
+        for copy in copies:
+            copy.start()
+        for copy in copies:
+            copy.wait()
+        window = window_ref[...]
+        for piece in range(4):
+            spot = pl.ds(piece * (ROW // 4), ROW // 4)
+            product_ref[pl.ds(lead, window.shape[1]), spot] = product_left(window, rows_ref[:, spot])
+        from_row = pl.multiple_of(lead + place_ref[at + 1], 8)
+        out_ref[...] = jnp.where(number < place_ref[at + 2], product_ref[pl.ds(from_row, slot), :], 0.0)
+
+    @pl.when(place_ref[8] == 0)
+    def _():
+        block(0, own_ref)
+
+    @pl.when(place_ref[8] == 1)
+    def _():
+        column = pl.multiple_of(place_ref[9], 128)
+        copies = [
+            pltpu.make_async_copy(
+                inputs_ref.at[:, pl.ds(column, third_ref.shape[1])], third_ref, sems.at[0]
+            ),
+            pltpu.make_async_copy(grads_ref.at[:, pl.ds(2 * HID, BOT)], bottle_ref, sems.at[1]),
+        ]
+        for copy in copies:
+            copy.start()
+        for copy in copies:
+            copy.wait()
+        third = product_left(third_ref[...], bottle_ref[...])
+        for lane in range(BOT // 128):
+            line_ref[lane] = third[:, lane * 128 : (lane + 1) * 128]
+        for group in range(ROW // BOT):
+            for lane in range(BOT // 128):
+                value = line_ref[lane, pl.ds(group, slot, stride=ROW // BOT), :]
+                own_ref[:, pl.ds(group * BOT + lane * 128, 128)] = jnp.where(
+                    number < place_ref[2], value, 0.0
+                )
+
+    block(4, partner_ref)
+
+
+def head_grads(place, inputs_all, grads_all, slot, lead):
+    rows = inputs_all.shape[0]
+    wide = slot * ROW // BOT
+    return pl.pallas_call(
+        head_grads_kernel,
+        out_shape=[jax.ShapeDtypeStruct((slot, ROW), single)] * 2,
+        in_specs=[pl.BlockSpec(memory_space=pltpu.SMEM)] + [pl.BlockSpec(memory_space=pl.ANY)] * 2,
+        out_specs=[pl.BlockSpec(memory_space=pltpu.VMEM)] * 2,
+        scratch_shapes=[
+            pltpu.VMEM((rows, 256), narrow),
+            pltpu.VMEM((rows, ROW), narrow),
+            pltpu.VMEM((lead + 256, ROW), single),
+            pltpu.VMEM((rows, wide), narrow),
+            pltpu.VMEM((rows, BOT), narrow),
+            pltpu.VMEM((BOT // 128, wide, 128), single),
+            pltpu.SemaphoreType.DMA((2,)),
+        ],
+        compiler_params=pltpu.CompilerParams(vmem_limit_bytes=56 << 20),
+        cost_estimate=pl.CostEstimate(flops=4 * 10**9, bytes_accessed=2 * 10**7, transcendentals=0),
+    )(place, inputs_all, grads_all)
 
 
 def close_local(
@@ -1102,7 +1334,6 @@
     both_head = jnp.where(
         student_side, jnp.stack([head_got, head_keep]), jnp.stack([head_keep, head_got])
     )
-    gathered_head = lax.all_gather(after(both_head, gathered), "dev", axis=0, axis_index_groups=groups)
 
     vectors = lax.ppermute(vector_blocks, "dev", [(count - 1, 0)])
     seed = jnp.concatenate([embed_blocks.reshape(2 * embed_rows, D), vectors.reshape(8 * 2 * LAYERS, D)])
@@ -1133,6 +1364,7 @@
         )
         for m in range(2)
     ]
+    gathered_head = lax.all_gather(after(both_head, gathered, even, odd), "dev", axis=0, axis_index_groups=groups)
     vectors_all = even[2 * embed_rows :].reshape(2, LAYERS, 8, D)
 
     def head_slots(first, last):
@@ -1222,12 +1454,14 @@
     unit_z = unit_rows(bottleneck).astype(narrow)
     pair_rows = -(-2 * rows_here // 16) * 16
     more_rows = ((0, pair_rows - 2 * rows_here), (0, 0))
+    third_end = (bounds[-2] - D - HID + slot) * (ROW // BOT)
+    more_inputs = (more_rows[0], (0, max(third_end - HID, 0)))
     inputs_all = lax.all_gather(
-        jnp.pad(jnp.concatenate([normed, hidden_one, hidden_two], axis=1), more_rows),
+        jnp.pad(jnp.concatenate([normed, hidden_one, hidden_two], axis=1), more_inputs),
         "dev",
         axis=0,
         axis_index_groups=groups,
-    ).reshape(half * pair_rows, D + 2 * HID)
+    ).reshape(half * pair_rows, -1)
 
     all_rows = count * rows_here
     kept_row = jnp.broadcast_to(kept[:, None], (images_here, 17)).reshape(1, rows_here)
@@ -1235,47 +1469,51 @@
     z_pair = cube_gather(unit_z, "b")
     z_all = cube_gather(z_pair, "xygc")
     z_all = z_all.reshape(half, 2, 2 * rows_here, BOT)
-    teacher_z_all = z_all[:, 0].reshape(all_rows, BOT)
-    student_z_all = z_all[:, 1].reshape(all_rows, BOT)
-    own_student = lax.optimization_barrier(protos.astype(narrow)).astype(single)
-    own_teacher = lax.optimization_barrier(proto_teacher.astype(narrow)).astype(single)
-    unit_student = unit_rows(own_student).astype(narrow)
-    unit_teacher = unit_rows(own_teacher).astype(narrow)
+    wide_rows = -(-all_rows // 128) * 128
+    teacher_z_all, student_z_all = [
+        jnp.pad(z_all[:, model].reshape(all_rows, BOT), ((0, wide_rows - all_rows), (0, 0))) for model in range(2)
+    ]
     protos_here = protos.shape[0]
     own_centre = lax.dynamic_slice(centre, (me * protos_here,), (protos_here,))
-    teacher_logits = contract("rb,kb->rk", teacher_z_all, unit_teacher)
-    logits = contract("rb,kb->rk", student_z_all, unit_student)
-    teacher_exp = jnp.exp((teacher_logits - own_centre) / tau_teacher)
-    student_exp = jnp.exp(logits / tau_student)
-    sums = jnp.stack(
-        [
-            jnp.sum(teacher_exp, axis=1),
-            jnp.sum(student_exp, axis=1),
-            jnp.sum(teacher_exp * logits, axis=1),
-        ]
-    )
-    sums = cube_sum(sums)
+    centre_column = own_centre.reshape(protos_here, 1)
     is_class = (jnp.arange(all_rows) % 17) == 0
-    row_weight = all_kept * jnp.where(is_class, 1.0, 1.0 / 16.0)
+    class_kept = jnp.where(is_class, all_kept, 0.0)
+    row_weight = jnp.where(is_class, all_kept, all_kept * (1.0 / 16.0))
+    count_total = jnp.sum(class_kept)
+
+    def lines(*values):
+        held = jnp.pad(jnp.stack(values), ((0, 8 - len(values)), (0, wide_rows - all_rows)))
+        return held
+
+    mixed_rows, sums, centre_sum = logits_pass(
+        teacher_z_all, student_z_all, proto_teacher, protos, centre_column, lines(class_kept)
+    )
+    mixed_own = cube_scatter(
+        [mixed_rows[:all_rows].reshape((2,) * 4 + (2 * rows_here, 2 * BOT))], ("cgyx",), ("cgyx",)
+    )[0]
+    mixed_own = mixed_own + lax.ppermute(
+        mixed_own.astype(narrow), "dev", [(i, i ^ across) for i in range(half)]
+    ).astype(single)
+    sums = cube_sum(sums[:3, :all_rows])
     cross = jnp.log(sums[1]) - sums[2] / (sums[0] * tau_student)
     loss_total = jnp.sum(row_weight * cross)
-    count_total = jnp.sum(jnp.where(is_class, all_kept, 0.0))
-    centre_sum = jnp.sum(
-        jnp.where(is_class, all_kept, 0.0)[:, None] * teacher_logits, axis=0
-    )
-    own_new_centre = centre_keep * own_centre + (1.0 - centre_keep) * centre_sum / count_total
+    scale = row_weight / tau_student
+    student_scale, teacher_scale = scale / sums[1], scale / sums[0]
+    flags = bit_flags(me)
+    pair_at = flags["c"] * 8 + flags["g"] * 4 + flags["y"] * 2 + flags["x"]
+    own_scales = lax.dynamic_slice(
+        jnp.stack([student_scale, teacher_scale]), (0, pair_at * 2 * rows_here), (2, 2 * rows_here)
+    )
+    grad_unit_z = (
+        mixed_own[:, :BOT] * own_scales[0][:, None] - mixed_own[:, BOT:] * own_scales[1][:, None]
+    )
+    own_new_centre = (
+        centre_keep * own_centre + (1.0 - centre_keep) * centre_sum.reshape(protos_here) / count_total
+    )
     new_centre = cube_gather(own_new_centre.reshape(1, protos_here), "cxyab").reshape(-1)
-    scale = row_weight / tau_student
-    grad_logits = (
-        student_exp * (scale / sums[1])[:, None] - teacher_exp * (scale / sums[0])[:, None]
-    ).astype(narrow)
-    z_partial = contract("rk,kb->rb", grad_logits, unit_student)
-    proto_unit_grad = contract("rk,rb->kb", grad_logits, student_z_all)
-    proto_grad = jax.vjp(unit_rows, own_student)[1](proto_unit_grad)[0]
-    z_own = cube_scatter(
-        [z_partial.reshape((2,) * 4 + (2 * rows_here, BOT))], ("cgyx",), ("cgyx",)
-    )[0]
-    grad_unit_z = z_own + lax.ppermute(z_own, "dev", [(i, i ^ across) for i in range(half)])
+    proto_grad, proto_square = proto_grad_pass(
+        teacher_z_all, student_z_all, proto_teacher, protos, centre_column, lines(student_scale, teacher_scale)
+    )
 
     grad_bottle = jax.vjp(unit_rows, bottleneck)[1](grad_unit_z)[0].astype(narrow)
     grad_pre_two = gelu_back(pre_two, contract("rb,hb->rh", grad_bottle, w_three)).astype(narrow)
@@ -1305,8 +1543,11 @@
 
     grad_stream = grad_stream.reshape(images_here * PAD_SEQ, D)
     middle_row = block_rows // 2
-    moving = []
+    small_rows = -(-(EMBED_ROWS + 6 * LAYERS) // (16 * count)) * 16
     vector_grads = [None] * LAYERS
+    firsts = [None] * LAYERS
+    seconds = [None] * LAYERS
+    waits = ()
     for layer_index in reversed(range(LAYERS)):
         saved, vectors = saved_layers[layer_index], vectors_all[1, layer_index]
         part = LAYERS + layer_index
@@ -1314,28 +1555,48 @@
             side, grad_stream, saved, vectors, gathered, part, ()
         )
         grad_stream, weight_grad, early_vectors = attention_back(
-            side, grad_stream, saved, vectors, gathered, part, weight_grad, moving
+            side, grad_stream, saved, vectors, gathered, part, weight_grad, waits
         )
         vector_grads[layer_index] = (late_vectors + early_vectors)[:6]
         owned = split_bits(weight_grad.reshape(D // 128, count, block_rows, 128), 1)
-        first = cube_scatter([owned], ("c",), (BITS,), 1)[0]
-        moving = (first,)
-        layer_first = [first] if layer_index == LAYERS - 1 else [first] + layer_first
-    layer_block = jnp.stack(
+        firsts[layer_index] = cube_scatter([owned], ("c",), (BITS,), 1)[0]
+        waits = (firsts[layer_index],)
+
+    def second_round(parts):
+        return cube_scatter(parts, ("x", "y"), ("bayx", "bayx"), 1)
+
+    def halves(array):
+        return [array[..., : array.shape[-2] // 2, :], array[..., array.shape[-2] // 2 :, :]]
+
+    def table(values):
+        return jnp.array(values, jnp.int32)
+
+    columns = [max(bound, 0) // 128 * 128 for bound in bounds[:-1]]
+    offsets = [bound - column for bound, column in zip(bounds, columns)]
+    offsets[0] = 0
+    valid = [0] + sizes[1:]
+    thirds = [D + HID + max(bound - D - HID, 0) * (ROW // BOT) for bound in bounds[:-1]]
+    partner = me ^ across
+    is_third = (me >= first_w3).astype(jnp.int32)
+    place = jnp.stack(
         [
-            jnp.concatenate(
-                cube_scatter(
-                    [first[..., :middle_row, :], first[..., middle_row:, :]],
-                    ("xyba", "yxba"),
-                    (BITS[:-1], BITS[:-1]),
-                    1,
-                ),
-                axis=1,
-            )
-            for first in layer_first
+            jnp.where(is_third == 1, 0, table(columns)[me]),
+            jnp.where(is_third == 1, 0, table(offsets)[me]),
+            table(valid)[me],
+            jnp.int32(HID),
+            table(columns)[partner],
+            table(offsets)[partner],
+            table(valid)[partner],
+            jnp.where(partner < first_w2, 0, HID),
+            is_third,
+            table(thirds)[me],
         ]
-    )
-    small_rows = -(-(EMBED_ROWS + 6 * LAYERS) // count)
+    ).astype(jnp.int32)
+    own_block_grad, partner_block_grad = head_grads(place, inputs_all, grads_all, slot, -min(bounds[1], 0))
+    block_got = lax.ppermute(partner_block_grad, "dev", [(i, i ^ across) for i in range(half, count)])
+    head_block_grad = jnp.where(student_side, own_block_grad, block_got)
+
+    later = [second_round(halves(firsts[i])) for i in range(1, LAYERS)]
     small = embed_back(
         grad_stream,
         patches.reshape(images_here * PATCHES, PIX),
@@ -1343,46 +1604,33 @@
         jnp.stack([grad_gain, grad_bias]),
         jnp.concatenate(vector_grads),
         small_rows * count,
-    )
-    small_block = cube_scatter(
-        [split_bits(small.reshape(count, small_rows, D))], ("cxyba",), (BITS,)
+        [array for pair in later for array in pair] + [own_block_grad],
+    )
+    small_first = cube_scatter(
+        [split_bits(small.reshape(D // 128, count, small_rows, 128), 1)], ("c",), (BITS,), 1
     )[0]
-
-    padded = jnp.pad(inputs_all[:, : D + HID], ((0, 0), (-min(bounds[1], 0), slot)))
-
-    def block_product(owner, grads):
-        window = lax.dynamic_slice(
-            padded, (0, jnp.array(bounds, jnp.int32)[owner] - bounds[1]), (half * pair_rows, slot)
-        )
-        valid = jnp.arange(slot) < jnp.array(sizes, jnp.int32)[owner]
-        return contract("rs,rh->sh", jnp.where(valid, window, 0), grads)
-
-    partner = me ^ across
-    grads_one, grads_two = grads_all[:, :HID], grads_all[:, HID : 2 * HID]
-    third_from = [max(bounds[i] - (D + HID), 0) * (ROW // BOT) for i in range(count)]
-    third_window = lax.dynamic_slice(
-        jnp.pad(inputs_all[:, D + HID :], ((0, 0), (0, slot * ROW // BOT))),
-        (0, jnp.array(third_from, jnp.int32)[me]),
-        (half * pair_rows, slot * ROW // BOT),
-    )
-    third_valid = jnp.arange(slot * ROW // BOT) < jnp.array(sizes, jnp.int32)[me] * (ROW // BOT)
-    third_grad = contract(
-        "rs,rb->sb", jnp.where(third_valid, third_window, 0), grads_all[:, 2 * HID :]
-    ).reshape(slot, ROW)
-    own_block_grad = jnp.where(me >= first_w3, third_grad, block_product(me, grads_two))
-    partner_block_grad = block_product(partner, jnp.where(partner < first_w2, grads_one, grads_two))
-    block_got = lax.ppermute(partner_block_grad, "dev", [(i, i ^ across) for i in range(half, count)])
-    head_block_grad = jnp.where(student_side, own_block_grad, block_got)
-    head_block_grad = jnp.where(me == 0, 0.0, head_block_grad)
+    last = second_round(
+        [jnp.concatenate(pair, axis=-2) for pair in zip(halves(firsts[0]), halves(small_first))]
+    )
+    joined = [jnp.concatenate(parts, axis=-2) for parts in zip(last, *later)]
+    done = cube_scatter(joined, ("yba", "xba"), ("bay", "bax"), 1)
+    middle_row, small_middle = block_rows // 2, small_rows // 2
+    small_block = jnp.concatenate([part[:, middle_row : middle_row + small_middle] for part in done], axis=1)
+    blocks = [jnp.concatenate([part[:, :middle_row] for part in done], axis=1)]
+    for number in range(LAYERS - 1):
+        at = middle_row + small_middle + number * middle_row
+        blocks.append(jnp.concatenate([part[:, at : at + middle_row] for part in done], axis=1))
+    layer_block = jnp.stack(blocks)
 
     square_local = (
         jnp.sum(head_block_grad * head_block_grad)
         + jnp.sum(layer_block * layer_block)
         + jnp.sum(small_block * small_block)
-        + jnp.sum(proto_grad * proto_grad)
+        + proto_square[0, 0]
     )
     square_total = cube_sum(square_local.reshape(1, 1))[0, 0]
-    small_all = cube_gather(small_block, "cxyab").reshape(small_rows * count, D)
+    small_all = cube_gather(small_block, "cxyab").reshape((count,) + small_block.shape)
+    small_all = jnp.transpose(small_all, (0, 2, 1, 3)).reshape(small_rows * count, D)
     embed_grad = small_all[:EMBED_ROWS].reshape(-1)
     vector_grad = small_all[EMBED_ROWS : EMBED_ROWS + 6 * LAYERS].reshape(LAYERS, 6, D)
 
@@ -1411,8 +1659,8 @@
     factor = jnp.minimum(1.0, clip_limit / (grad_norm + 1e-06)) / count_total
     stem_set = adam_update(stem, stem_moment, stem_second, stem_grad * factor, stem_teacher)
     layer_set = adam_update(layers, layer_moment, layer_second, layer_grad * factor, layer_teacher)
-    proto_set = adam_update(protos, proto_moment, proto_second, proto_grad * factor, proto_teacher)
-    return (loss_total, count_total, grad_norm, new_centre) + stem_set + layer_set + proto_set
+    proto_set = proto_update(factor, protos, proto_moment, proto_second, proto_teacher, proto_grad)
+    return (loss_total, count_total, grad_norm, new_centre) + stem_set + layer_set + tuple(proto_set)
 
 
 def solution(mesh):

time: 836 us -> 731 us (0.87)
  waiting for transfers between devices: 318 us -> 255 us
  matrix products: 44.9 us -> 18 us
  starting transfers between devices: 97.8 us -> 82.7 us
  Pallas kernels: 142 us -> 156 us
  other arithmetic: 80.1 us -> 71.5 us
    all_gather x1, waiting for transfers between devices: 65.6 us -> 16 us  [close_local(): lax.all_gather(both_layers, 'dev', axis=0, axis_index_groups=groups)]
    ppermute x20, waiting for transfers between devices: 71.9 us -> 34.1 us  [cube_gather(): got = lax.ppermute(held, 'dev', pairs(count, MASKS[name]))]
    dot_general x15 -> x8, matrix products: 44.9 us -> 18 us  [contract(): return jnp.einsum(form, left_arg, right_arg, preferred_element_type=single)]
    ppermute x27 -> x17, waiting for transfers between devices: 42 us -> 61.2 us  [cube_scatter(): lax.ppermute(s, 'dev', pairs(count, MASKS[order[turn]]))]
    ppermute x27 -> x17, starting transfers between devices: 25.6 us -> 9.01 us  [cube_scatter(): lax.ppermute(s, 'dev', pairs(count, MASKS[order[turn]]))]
    pallas_call x2 -> x6, Pallas kernels: 25.5 us -> 40.4 us  [the longest x1 12.8 us: logits_pass(): pl.pallas_call(logits_kernel, grid=(4,), out_shape=[jax.ShapeDtypeStruct(...]
    unnamed x187 -> x189, local copies, waits for them, and re-layouts: 40.8 us -> 27.3 us
    convert_element_type x3 -> x1, other arithmetic: 10.2 us -> 0.02 us  [close_local(): mixed_own.astype(narrow)]
  transfers between devices with their start and end apart: 85 -> 75, of which waited for: 51 -> 40; matrix products, arithmetic and copies ran while one was open for 22% -> 19% of each run, Pallas kernels for 14% -> 21%
where the time goes in v4:
time: 731 us; the launch traced here: 720 us
  waiting for transfers between devices  255 us (35%)
  Pallas kernels  156 us (21%)
  local copies, waits for them, and re-layouts  107 us (15%)
  starting transfers between devices  82.7 us (11%)
  other arithmetic  71.5 us (10%)
  between operations  28.8 us (4%)
  matrix products  18 us (2%)
    pallas_call x4, Pallas kernels, layer_back(): pl.pallas_call(lambda *refs: kernel(part, *refs), out_shape=[jax.ShapeDty...  63.6 us
    ppermute x17, waiting for transfers between devices, cube_scatter(): lax.ppermute(s, 'dev', pairs(count, MASKS[order[turn]]))  61.2 us
    pallas_call x4, Pallas kernels, layer_forward(): pl.pallas_call(lambda *refs: forward_kernel(part, keep, *refs), out_shape...  47.9 us
    ppermute x12, waiting for transfers between devices, close_local(): got = lax.ppermute(spread, 'dev', moves)  42.2 us
    ppermute x20, waiting for transfers between devices, cube_gather(): got = lax.ppermute(held, 'dev', pairs(count, MASKS[name]))  34.1 us
    ppermute x1, waiting for transfers between devices, close_local(): lax.ppermute(partner_block_grad, 'dev', [(i, i ^ across) for i in range(h...  32.3 us
    unnamed x189, local copies, waits for them, and re-layouts  27.3 us
    ppermute x20, starting transfers between devices, cube_gather(): got = lax.ppermute(held, 'dev', pairs(count, MASKS[name]))  26 us
  transfers between devices with their start and end apart: 75, of which 40 were waited for; matrix products, arithmetic and copies ran while one was open for 19% of the time, Pallas kernels for 21%

profile of v4, /device:TPU:8, one launch (start us, length us, event | category | flops | bytes accessed | tf_op | source)
XLA Modules:
  0.0 720.1 jit_solution(8615511633142256298)
XLA Ops:
  28.8 18.7 %collective-permute-done.21 = bf16[4,144,384]{2,1,0:T(8,128)(2,1)S(1)} collective-permute-done((bf16[4,144,384]{2,1,0:T(8,128)(2,1)S(1)}, bf16[4,144,384]{2,1,0:T(8,128)(2,1)S(1)}, u32[]{:S(2)}, u32[]{:S(2)}) %collective-permute-start.21) | collective-permute-done | bytes 442400 | tf_op jit(solution)/shard_map/ppermute | solution.py:1324
  67.0 18.8 %collective-permute-done.12 = bf16[336,384]{1,0:T(8,128)(2,1)S(1)} collective-permute-done((bf16[336,384]{1,0:T(8,128)(2,1)S(1)}, bf16[336,384]{1,0:T(8,128)(2,1)S(1)}, u32[]{:S(2)}, u32[]{:S(2)}) %collective-permute-start.12) | collective-permute-done | bytes 258080 | tf_op jit(solution)/shard_map/ppermute | solution.py:1347
  87.8 8.5 %collective-permute-done.18 = bf16[320,384]{1,0:T(8,128)(2,1)S(1)} collective-permute-done((bf16[320,384]{1,0:T(8,128)(2,1)S(1)}, bf16[320,384]{1,0:T(8,128)(2,1)S(1)}, u32[]{:S(2)}, u32[]{:S(2)}) %collective-permute-start.18) | collective-permute-done | bytes 245792 | tf_op jit(solution)/shard_map/ppermute | solution.py:1347
  105.6 12.3 %collective-permute-done.10 = bf16[336,384]{1,0:T(8,128)(2,1)S(1)} collective-permute-done((bf16[336,384]{1,0:T(8,128)(2,1)S(1)}, bf16[336,384]{1,0:T(8,128)(2,1)S(1)}, u32[]{:S(2)}, u32[]{:S(2)}) %collective-permute-start.10) | collective-permute-done | bytes 258080 | tf_op jit(solution)/shard_map/ppermute | solution.py:1347
  123.0 17.7 %collective-permute-done.23 = bf16[96,2048]{1,0:T(8,128)(2,1)S(1)} collective-permute-done((bf16[96,2048]{1,0:T(8,128)(2,1)S(1)}, bf16[96,2048]{1,0:T(8,128)(2,1)S(1)}, u32[]{:S(2)}, u32[]{:S(2)}) %collective-permute-start.23) | collective-permute-done | bytes 393248 | tf_op jit(solution)/shard_map/ppermute | solution.py:1333
  143.1 16.0 %all-gather.8.cloned.1.call-done.refs_3_.refs_1_.refs_7_.refs_6_ = bf16[16,2,4,144,384]{4,3,2,1,0:T(8,128)(2,1)} async-done(((bf16[1,2,4,144,384]{4,3,2,1,0:T(8,128)(2,1)}), bf16[16,2,4,144,384]{4,3,2,1,0:T(8,128)(2,1)}) %all-gather.8.cloned.1.call-update) | async-done | bytes 14155792 | tf_op jit(solution)/shard_map/all_gather | solution.py:1330
  167.6 11.5 %shard_map.493.refs_1_ = f32[544,384]{1,0:T(8,128)} custom-call(s32[1]{0:T(128)} %bitcast.12.refs_0_, f32[544,384]{1,0:T(8,128)} %bitcast.323, bf16[8,384]{1,0:T(8,128)(2,1)} %get-tuple-element.203.refs_2_, bf16[16,2,4,144,384]{4,3,2,1,0:T(8,128)(2,1)} %all-gather.8.cloned.1.call-done.refs_3_.refs_1_.refs_7_.refs_6_), custom_call_target="tpu_custom_call" | custom-call | flops 2000000000 | bytes 20000000 | tf_op jit(solution)/shard_map/pallas_call | solution.py:787
  179.1 11.8 %shard_map.494 = f32[544,384]{1,0:T(8,128)} custom-call(s32[1]{0:T(128)} %bitcast.12.refs_0_, f32[544,384]{1,0:T(8,128)} %shard_map.493.refs_1_, bf16[8,384]{1,0:T(8,128)(2,1)} %get-tuple-element.202.refs_2_, bf16[16,2,4,144,384]{4,3,2,1,0:T(8,128)(2,1)} %all-gather.8.cloned.1.call-done.refs_3_.refs_1_.refs_7_.refs_6_), custom_call_target="tpu_custom_call" | custom-call | flops 2000000000 | bytes 20000000 | tf_op jit(solution)/shard_map/pallas_call | solution.py:787
  193.5 12.1 %shard_map.495 = (f32[544,384]{1,0:T(8,128)}, bf16[544,1152]{1,0:T(8,128)(2,1)}, bf16[544,384]{1,0:T(8,128)(2,1)}, f32[544,384]{1,0:T(8,128)}, f32[544,1536]{1,0:T(8,128)}, /*index=5*/f32[544,384]{1,0:T(8,128)}) custom-call(s32[1]{0:T(128)} %bitcast.12.refs_0_, f32[544,384]{1,0:T(8,128)} %bitcast.312, ...), custom_call_target="tpu_custom_call" | custom-call | flops 2000000000 | bytes 20000000 | tf_op jit(solution)/shard_map/pallas_call | solution.py:787
  205.6 12.5 %shard_map.496 = (f32[544,384]{1,0:T(8,128)}, bf16[544,1152]{1,0:T(8,128)(2,1)}, bf16[544,384]{1,0:T(8,128)(2,1)}, f32[544,384]{1,0:T(8,128)}, f32[544,1536]{1,0:T(8,128)}, /*index=5*/f32[544,384]{1,0:T(8,128)}) custom-call(s32[1]{0:T(128)} %bitcast.12.refs_0_, f32[544,384]{1,0:T(8,128)} %get-tuple-element.65.refs_1_.refs_2_, ...), custom_call_target="tpu_custom_call" | custom-call | flops 2000000000 | bytes 20000000 | tf_op jit(solution)/shard_map/pallas_call | solution.py:787
  282.6 12.8 %collective-permute-done.27 = bf16[4,2,68,256]{3,2,1,0:T(8,128)(2,1)S(1)} collective-permute-done((bf16[4,2,68,256]{3,2,1,0:T(8,128)(2,1)S(1)}, bf16[4,2,68,256]{3,2,1,0:T(8,128)(2,1)S(1)}, u32[]{:S(2)}, u32[]{:S(2)}) %collective-permute-start.27) | collective-permute-done | bytes 278560 | tf_op jit(solution)/shard_map/ppermute | solution.py:444
  308.0 12.8 %shard_map.498 = (f32[1152,512]{1,0:T(8,128)}, f32[8,1152]{1,0:T(8,128)}, f32[2048,1]{1,0:T(8,128)}) custom-call(bf16[1152,256]{1,0:T(8,128)(2,1)} %pad.47.teacher_z_ref, bf16[1152,256]{1,0:T(8,128)(2,1)} %pad.48.student_z_ref, f32[2048,256]{1,0:T(8,128)} %refs_3_.1, f32[2048,256]{1,0:T(8,128)} %refs_0_.1, f32[2048,1]{1,0:T(8,128)} %copy.151.centre_ref, ...), custom_call_target="tpu_custom_call" | custom-call | flops 5000000000 | bytes 10000000 | tf_op jit(solution)/shard_map/pallas_call | solution.py:1084
  371.3 6.5 fusion.116
  397.9 14.8 %shard_map.500 = (f32[544,384]{1,0:T(8,128)}, f32[3,4608,128]{2,1,0:T(8,128)}, f32[8,384]{1,0:T(8,128)}) custom-call(s32[1]{0:T(128)} %bitcast.12.refs_0_, f32[544,384]{1,0:T(8,128)} %bitcast.320, f32[544,384]{1,0:T(8,128)} %get-tuple-element.65.refs_1_.refs_2_, f32[544,384]{1,0:T(8,128)} %get-tuple-element.72.refs_3_, ...), custom_call_target="tpu_custom_call" | custom-call | flops 5000000000 | bytes 40000000 | tf_op jit(solution)/shard_map/pallas_call | solution.py:924
  412.7 17.3 %shard_map.501 = (f32[544,384]{1,0:T(8,128)}, f32[3,4608,128]{2,1,0:T(8,128)}, f32[8,384]{1,0:T(8,128)}) custom-call(s32[1]{0:T(128)} %bitcast.12.refs_0_, f32[544,384]{1,0:T(8,128)} %get-tuple-element.75.refs_1_, f32[544,384]{1,0:T(8,128)} %get-tuple-element.65.refs_1_.refs_2_, ...), custom_call_target="tpu_custom_call", output_to_operand_aliasing={{1}: (7, {})} | custom-call | flops 5000000000 | bytes 40000000 | tf_op jit(solution)/shard_map/pallas_call | solution.py:924
  450.0 14.5 %shard_map.502 = (f32[544,384]{1,0:T(8,128)}, f32[3,4608,128]{2,1,0:T(8,128)}, f32[8,384]{1,0:T(8,128)}) custom-call(s32[1]{0:T(128)} %bitcast.12.refs_0_, f32[544,384]{1,0:T(8,128)} %get-tuple-element.79.refs_1_, f32[544,384]{1,0:T(8,128)} %bitcast.313, f32[544,384]{1,0:T(8,128)} %get-tuple-element.80.refs_3_, f32[544,1536]{1,0:T(8,128)} %get-tuple-element.81.refs_4_, ...), custom_call_target="tpu_custom_call" | custom-call | flops 5000000000 | bytes 40000000 | tf_op jit(solution)/shard_map/pallas_call | solution.py:924
  471.6 17.0 %shard_map.503 = (f32[544,384]{1,0:T(8,128)}, f32[3,4608,128]{2,1,0:T(8,128)}, f32[8,384]{1,0:T(8,128)}) custom-call(s32[1]{0:T(128)} %bitcast.12.refs_0_, f32[544,384]{1,0:T(8,128)} %get-tuple-element.83.refs_1_, f32[544,384]{1,0:T(8,128)} %bitcast.314, bf16[544,1152]{1,0:T(8,128)(2,1)} %get-tuple-element.84.refs_3_, ...), custom_call_target="tpu_custom_call", output_to_operand_aliasing={{1}: (7, {})} | custom-call | flops 5000000000 | bytes 40000000 | tf_op jit(solution)/shard_map/pallas_call | solution.py:924
  503.7 10.1 %collective-permute-done.44 = bf16[3,2,2,2,72,128]{5,4,0,2,1,3:T(8,128)(2,1)S(1)} collective-permute-done((bf16[3,2,2,2,72,128]{5,4,0,2,1,3:T(8,128)(2,1)S(1)}, bf16[3,2,2,2,72,128]{5,4,0,2,1,3:T(8,128)(2,1)S(1)}, u32[]{:S(2)}, u32[]{:S(2)}) %collective-permute-start.44) | collective-permute-done | bytes 442400 | tf_op jit(solution)/shard_map/ppermute | solution.py:470
  516.0 10.4 %shard_map.499 = (f32[96,2048]{1,0:T(8,128)}, f32[96,2048]{1,0:T(8,128)}) custom-call(s32[10]{0:T(128)} %stack.122.place_ref, bf16[1280,4608]{1,0:T(8,128)(2,1)} %all-gather.12.cloned.1.call-done.inputs_ref, bf16[1280,4352]{1,0:T(8,128)(2,1)} %all-gather.14.cloned.1.call-done.grads_ref), custom_call_target="tpu_custom_call" | custom-call | flops 4000000000 | bytes 20000000 | tf_op jit(solution)/shard_map/pallas_call | solution.py:1229
  548.6 8.0 %collective-permute-done.50 = bf16[3,2,2,2,88,128]{5,4,0,2,1,3:T(8,128)(2,1)S(1)} collective-permute-done((bf16[3,2,2,2,88,128]{5,4,0,2,1,3:T(8,128)(2,1)S(1)}, bf16[3,2,2,2,88,128]{5,4,0,2,1,3:T(8,128)(2,1)S(1)}, u32[]{:S(2)}, u32[]{:S(2)}) %collective-permute-start.50) | collective-permute-done | bytes 540704 | tf_op jit(solution)/shard_map/ppermute | solution.py:470
  566.7 14.7 %collective-permute-done.48 = bf16[3,2,160,128]{3,2,0,1:T(8,128)(2,1)S(1)} collective-permute-done((bf16[3,2,160,128]{3,2,0,1:T(8,128)(2,1)S(1)}, bf16[3,2,160,128]{3,2,0,1:T(8,128)(2,1)S(1)}, u32[]{:S(2)}, u32[]{:S(2)}) %collective-permute-start.48) | collective-permute-done | bytes 245792 | tf_op jit(solution)/shard_map/ppermute | solution.py:470
  593.7 10.2 %shard_map.505 = (f32[2048,256]{1,0:T(8,128)}, f32[8,128]{1,0:T(8,128)}) custom-call(bf16[1152,256]{1,0:T(8,128)(2,1)} %pad.47.teacher_z_ref, bf16[1152,256]{1,0:T(8,128)(2,1)} %pad.48.student_z_ref, f32[2048,256]{1,0:T(8,128)} %refs_3_.1, f32[2048,256]{1,0:T(8,128)} %refs_0_.1, f32[2048,1]{1,0:T(8,128)} %copy.151.centre_ref, f32[8,1152]{1,0:T(8,128)} %pad.52.scale_ref), custom_call_target="tpu_custom_call" | custom-call | flops 4000000000 | bytes 10000000 | tf_op jit(solution)/shard_map/pallas_call | solution.py:1131
  606.3 10.7 %collective-permute-done.63 = f32[16,1,2048]{2,1,0:T(1,128)S(1)} collective-permute-done((f32[16,1,2048]{2,1,0:T(1,128)S(1)}, f32[16,1,2048]{2,1,0:T(1,128)S(1)}, u32[]{:S(2)}, u32[]{:S(2)}) %collective-permute-start.63) | collective-permute-done | bytes 131104 | tf_op jit(solution)/shard_map/ppermute | solution.py:444
  618.1 32.3 %collective-permute-done.39 = f32[96,2048]{1,0:T(8,128)S(1)} collective-permute-done((f32[96,2048]{1,0:T(8,128)S(1)}, f32[96,2048]{1,0:T(8,128)S(1)}, u32[]{:S(2)}, u32[]{:S(2)}) %collective-permute-start.39) | collective-permute-done | bytes 786464 | tf_op jit(solution)/shard_map/ppermute | solution.py:1596
  (609 shorter events, 359.2 us)
Async XLA Ops:
  7.2 151.9 %all-gather.8.cloned.1.call-start = ((), (), s32[]{:S(2)}) async-start(), calls=%async_computation | async-start | bytes 15040512 | tf_op jit(solution)/shard_map/all_gather | solution.py:1330
  27.2 20.3 %collective-permute-start.21 = (bf16[4,144,384]{2,1,0:T(8,128)(2,1)S(1)}, bf16[4,144,384]{2,1,0:T(8,128)(2,1)S(1)}, u32[]{:S(2)}, u32[]{:S(2)}) collective-permute-start(bf16[4,144,384]{2,1,0:T(8,128)(2,1)S(1)} %get-tuple-element.64), channel_id=1, source_target_pairs={{0,24},{1,25},{2,26},{3,27},{4,28},{5,29},{6,30},{7,31},{8,16},{9,... | collective-permute-start | bytes 1327112 | tf_op jit(solution)/shard_map/ppermute | solution.py:1324
  48.6 179.4 %all-gather.10.cloned.1.call-start = ((), (), s32[]{:S(2)}) async-start(), calls=%async_computation.1 | async-start | bytes 13369344 | tf_op jit(solution)/shard_map/all_gather | solution.py:1367
  62.3 23.5 %collective-permute-start.12 = (bf16[336,384]{1,0:T(8,128)(2,1)S(1)}, bf16[336,384]{1,0:T(8,128)(2,1)S(1)}, u32[]{:S(2)}, u32[]{:S(2)}) collective-permute-start(bf16[336,384]{1,0:T(8,128)(2,1)S(1)} %get-tuple-element.169), channel_id=1, source_target_pairs={{0,8},{1,9},{24,16},{25,17}} | collective-permute-start | bytes 774152 | tf_op jit(solution)/shard_map/ppermute | solution.py:1347
  64.3 32.1 %collective-permute-start.18 = (bf16[320,384]{1,0:T(8,128)(2,1)S(1)}, bf16[320,384]{1,0:T(8,128)(2,1)S(1)}, u32[]{:S(2)}, u32[]{:S(2)}) collective-permute-start(bf16[320,384]{1,0:T(8,128)(2,1)S(1)} %broadcast_select_fusion.15), channel_id=1, source_target_pairs={{0,8},{1,9},{4,12},{5,13},{24,16},{25,17},{28,20},{29,21}} | collective-permute-start | bytes 737288 | tf_op jit(solution)/shard_map/ppermute | solution.py:1347
  66.3 32.1 %collective-permute-start.9 = (bf16[336,384]{1,0:T(8,128)(2,1)S(1)}, bf16[336,384]{1,0:T(8,128)(2,1)S(1)}, u32[]{:S(2)}, u32[]{:S(2)}) collective-permute-start(bf16[336,384]{1,0:T(8,128)(2,1)S(1)} %broadcast_select_fusion.11), channel_id=1, source_target_pairs={{0,24},{1,25},{2,26},{3,27},{4,28},{5,29},{6,30},{7,31}} | collective-permute-start | bytes 774152 | tf_op jit(solution)/shard_map/ppermute | solution.py:1347
  99.0 18.9 %collective-permute-start.10 = (bf16[336,384]{1,0:T(8,128)(2,1)S(1)}, bf16[336,384]{1,0:T(8,128)(2,1)S(1)}, u32[]{:S(2)}, u32[]{:S(2)}) collective-permute-start(bf16[336,384]{1,0:T(8,128)(2,1)S(1)} %broadcast_select_fusion.12), channel_id=1, source_target_pairs={{0,8},{1,9},{2,10},{3,11},{4,12},{5,13},{6,14},{7,15},{24,16},{25,... | collective-permute-start | bytes 774152 | tf_op jit(solution)/shard_map/ppermute | solution.py:1347
  101.0 17.6 %collective-permute-start.14 = (bf16[336,384]{1,0:T(8,128)(2,1)S(1)}, bf16[336,384]{1,0:T(8,128)(2,1)S(1)}, u32[]{:S(2)}, u32[]{:S(2)}) collective-permute-start(bf16[336,384]{1,0:T(8,128)(2,1)S(1)} %broadcast_select_fusion.8), channel_id=1, source_target_pairs={{0,4},{1,5},{24,28},{25,29},{8,12},{9,13},{16,20},{17,21},{2,6},{3... | collective-permute-start | bytes 774152 | tf_op jit(solution)/shard_map/ppermute | solution.py:1347
  119.4 22.3 %collective-permute-start.20 = (bf16[992,384]{1,0:T(8,128)(2,1)S(1)}, bf16[992,384]{1,0:T(8,128)(2,1)S(1)}, u32[]{:S(2)}, u32[]{:S(2)}) collective-permute-start(bf16[992,384]{1,0:T(8,128)(2,1)S(1)} %pad_maximum_fusion.8), channel_id=1, source_target_pairs={{0,1},{1,0},{2,3},{3,2},{4,5},{5,4},{6,7},{7,6},{8,9},{9,8},{10,11... | collective-permute-start | bytes 2285576 | tf_op jit(solution)/shard_map/ppermute | solution.py:1354
  119.6 21.1 %collective-permute-start.23 = (bf16[96,2048]{1,0:T(8,128)(2,1)S(1)}, bf16[96,2048]{1,0:T(8,128)(2,1)S(1)}, u32[]{:S(2)}, u32[]{:S(2)}) collective-permute-start(bf16[96,2048]{1,0:T(8,128)(2,1)S(1)} %get-tuple-element.160), channel_id=1, source_target_pairs={{0,24},{1,25},{2,26},{3,27},{4,28},{5,29},{6,30},{7,31},{8,16},{9,... | collective-permute-start | bytes 1179656 | tf_op jit(solution)/shard_map/ppermute | solution.py:1333
  161.3 354.8 %all-gather.12.cloned.1.call-start = ((), (), s32[]{:S(2)}) async-start(), calls=%async_computation.2 | async-start | bytes 12533760 | tf_op jit(solution)/shard_map/all_gather | solution.py:1459
  250.2 265.9 %all-gather.14.cloned.1.call-start = ((), (), s32[]{:S(2)}) async-start(), calls=%async_computation.3 | async-start | bytes 11837440 | tf_op jit(solution)/shard_map/all_gather | solution.py:1523
  437.8 26.7 %collective-permute-start.41 = (f32[3,2,2,2,2,144,128]{6,5,0,2,1,3,4:T(8,128)}, f32[3,2,2,2,2,144,128]{6,5,0,2,1,3,4:T(8,128)}, u32[]{:S(2)}, u32[]{:S(2)}) collective-permute-start(f32[3,2,2,2,2,144,128]{6,5,0,2,1,3,4:T(8,128)} %select_bitcast_fusion.1), channel_id=1, source_target_pairs={{0,1},{1,0},{2,3},{3,2},{4,5},{5,4},{6,7},{7,6},{8,9},{9,8},{10,11... | collective-permute-start | bytes 10616840 | tf_op jit(solution)/shard_map/ppermute | solution.py:470
  449.5 46.7 %collective-permute-start.59 = (f32[1,1,2048]{2,0,1:T(1,128)S(1)}, f32[1,1,2048]{2,0,1:T(1,128)S(1)}, u32[]{:S(2)}, u32[]{:S(2)}) collective-permute-start(f32[1,1,2048]{2,0,1:T(1,128)S(1)} %bitcast.331), channel_id=1, source_target_pairs={{0,1},{1,0},{2,3},{3,2},{4,5},{5,4},{6,7},{7,6},{8,9},{9,8},{10,11... | collective-permute-start | bytes 24584 | tf_op jit(solution)/shard_map/ppermute | solution.py:444
  496.1 32.4 %collective-permute-start.42 = (f32[3,2,2,2,2,144,128]{6,5,0,2,1,3,4:T(8,128)}, f32[3,2,2,2,2,144,128]{6,5,0,2,1,3,4:T(8,128)}, u32[]{:S(2)}, u32[]{:S(2)}) collective-permute-start(f32[3,2,2,2,2,144,128]{6,5,0,2,1,3,4:T(8,128)} %select_bitcast_fusion), channel_id=1, source_target_pairs={{0,1},{1,0},{2,3},{3,2},{4,5},{5,4},{6,7},{7,6},{8,9},{9,8},{10,11... | collective-permute-start | bytes 10616840 | tf_op jit(solution)/shard_map/ppermute | solution.py:470
  500.6 34.0 %collective-permute-start.61 = (f32[4,1,2048]{2,0,1:T(4,128)}, f32[4,1,2048]{2,0,1:T(4,128)}, u32[]{:S(2)}, u32[]{:S(2)}) collective-permute-start(f32[4,1,2048]{2,0,1:T(4,128)} %maximum_select_fusion.15), channel_id=1, source_target_pairs={{0,4},{1,5},{2,6},{3,7},{4,0},{5,1},{6,2},{7,3},{8,12},{9,13},{10,... | collective-permute-start | bytes 98312 | tf_op jit(solution)/shard_map/ppermute | solution.py:444
  535.8 55.1 %collective-permute-start.62 = (f32[8,1,2048]{2,1,0:T(1,128)S(1)}, f32[8,1,2048]{2,1,0:T(1,128)S(1)}, u32[]{:S(2)}, u32[]{:S(2)}) collective-permute-start(f32[8,1,2048]{2,1,0:T(1,128)S(1)} %copy.174), channel_id=1, source_target_pairs={{0,8},{1,9},{2,10},{3,11},{4,12},{5,13},{6,14},{7,15},{8,0},{9,1},... | collective-permute-start | bytes 196616 | tf_op jit(solution)/shard_map/ppermute | solution.py:444
  566.0 19.1 %collective-permute-start.52 = (bf16[3,2,160,128]{3,2,0,1:T(8,128)(2,1)S(1)}, bf16[3,2,160,128]{3,2,0,1:T(8,128)(2,1)S(1)}, u32[]{:S(2)}, u32[]{:S(2)}) collective-permute-start(bf16[3,2,160,128]{3,2,0,1:T(8,128)(2,1)S(1)} %fusion.58), channel_id=1, source_target_pairs={{0,24},{1,25},{2,26},{3,27},{4,28},{5,29},{6,30},{7,31},{8,16},{9,... | collective-permute-start | bytes 737288 | tf_op jit(solution)/shard_map/ppermute | solution.py:470
  591.0 26.0 %collective-permute-start.63 = (f32[16,1,2048]{2,1,0:T(1,128)S(1)}, f32[16,1,2048]{2,1,0:T(1,128)S(1)}, u32[]{:S(2)}, u32[]{:S(2)}) collective-permute-start(f32[16,1,2048]{2,1,0:T(1,128)S(1)} %broadcast_select_fusion.5), channel_id=1, source_target_pairs={{0,24},{1,25},{2,26},{3,27},{4,28},{5,29},{6,30},{7,31},{8,16},{9,... | collective-permute-start | bytes 393224 | tf_op jit(solution)/shard_map/ppermute | solution.py:444
  591.4 59.0 %collective-permute-start.39 = (f32[96,2048]{1,0:T(8,128)S(1)}, f32[96,2048]{1,0:T(8,128)S(1)}, u32[]{:S(2)}, u32[]{:S(2)}) collective-permute-start(f32[96,2048]{1,0:T(8,128)S(1)} %copy-done.72), channel_id=1, source_target_pairs={{16,8},{17,9},{18,10},{19,11},{20,12},{21,13},{22,14},{23,15},{24,... | collective-permute-start | bytes 2359304 | tf_op jit(solution)/shard_map/ppermute | solution.py:1596
  618.0 35.7 %collective-permute-start.67 = (f32[8,3,32,128]{3,2,1,0:T(8,128)S(1)}, f32[8,3,32,128]{3,2,1,0:T(8,128)S(1)}, u32[]{:S(2)}, u32[]{:S(2)}) collective-permute-start(f32[8,3,32,128]{3,2,1,0:T(8,128)S(1)} %maximum_select_fusion.6), channel_id=1, source_target_pairs={{0,8},{1,9},{2,10},{3,11},{4,12},{5,13},{6,14},{7,15},{8,0},{9,1},... | collective-permute-start | bytes 1179656 | tf_op jit(solution)/shard_map/ppermute | solution.py:444
  651.8 47.7 %collective-permute-start.69 = (f32[16,2048]{1,0:T(8,128)}, f32[16,2048]{1,0:T(8,128)S(1)}, u32[]{:S(2)}, u32[]{:S(2)}) collective-permute-start(f32[16,2048]{1,0:T(8,128)} %constant_dynamic-slice_fusion), channel_id=1, source_target_pairs={{0,1},{1,2},{2,3},{3,4},{4,5},{5,6},{6,7},{7,8},{8,9},{9,10},{10,1... | collective-permute-start | bytes 393224 | tf_op jit(solution)/shard_map/ppermute | solution.py:1643
  654.7 40.9 %collective-permute-start.68 = (f32[16,3,32,128]{3,2,1,0:T(8,128)}, f32[16,3,32,128]{3,2,1,0:T(8,128)}, u32[]{:S(2)}, u32[]{:S(2)}) collective-permute-start(f32[16,3,32,128]{3,2,1,0:T(8,128)} %maximum_select_fusion.4), channel_id=1, source_target_pairs={{0,24},{1,25},{2,26},{3,27},{4,28},{5,29},{6,30},{7,31},{8,16},{9,... | collective-permute-start | bytes 2359304 | tf_op jit(solution)/shard_map/ppermute | solution.py:444
  661.5 38.0 %collective-permute-start.70 = (f32[2,3,6,128]{3,2,1,0:T(8,128)S(1)}, f32[2,3,6,128]{3,2,1,0:T(8,128)S(1)}, u32[]{:S(2)}, u32[]{:S(2)}) collective-permute-start(f32[2,3,6,128]{3,2,1,0:T(8,128)S(1)} %fusion.68), channel_id=1, source_target_pairs={{1,0},{2,1},{3,2},{4,3},{5,4},{6,5},{7,6},{8,7},{9,8},{10,9},{11,1... | collective-permute-start | bytes 55304 | tf_op jit(solution)/shard_map/ppermute | solution.py:1637
  (142 other events, 925.4 us)
Sparse Core Ops, SparseCore 0:
  48.7 110.3 all-gather.7
  161.4 66.5 all-gather.9
  250.3 71.5 all-gather.11
  385.8 64.9 all-gather.13

commit v5 on v4

--- a/solution.py
+++ b/solution.py
@@ -450,27 +450,24 @@
     return held
 
 
-def cube_scatter(parts, orders, axes, lead=0):
-    count = 1 << len(BITS)
-    flags = bit_flags(lax.axis_index("dev"))
-    held = list(parts)
-    names = [list(a) for a in axes]
-    for turn in range(len(orders[0])):
-        sent, kept = [], []
-        for h, order, name in zip(held, orders, names):
-            place = name.index(order[turn]) + lead
-            low = lax.index_in_dim(h, 0, place, keepdims=False)
-            high = lax.index_in_dim(h, 1, place, keepdims=False)
-            flag = flags[order[turn]] == 1
-            out = jnp.where(flag, low, high)
-            sent.append(out if order[turn] == "c" else out.astype(narrow))
-            kept.append(jnp.where(flag, high, low))
-            name.pop(place - lead)
-        got = [
-            lax.ppermute(s, "dev", pairs(count, MASKS[order[turn]])) for s, order in zip(sent, orders)
-        ]
-        held = [k + g.astype(single) for k, g in zip(kept, got)]
-    return held
+def cut(array, names, name, lead):
+    flag = bit_flags(lax.axis_index("dev"))[name] == 1
+    place = names.index(name) + lead
+    low = lax.index_in_dim(array, 0, place, keepdims=False)
+    high = lax.index_in_dim(array, 1, place, keepdims=False)
+    sent = jnp.where(flag, low, high)
+    return (sent if name == "c" else sent.astype(narrow)), jnp.where(flag, high, low), names.replace(name, "")
+
+
+def move(sent, kept, name):
+    return kept + lax.ppermute(sent, "dev", pairs(1 << len(BITS), MASKS[name])).astype(single)
+
+
+def cube_scatter(array, names, order, lead=0):
+    for name in order:
+        sent, kept, names = cut(array, names, name, lead)
+        array = move(sent, kept, name)
+    return array
 
 
 def cube_sum(values):
@@ -1102,8 +1099,9 @@
 
 
 def proto_grad_kernel(
-    teacher_z_ref, student_z_ref, teacher_ref, student_ref, centre_ref, scale_ref, grad_ref, square_ref
+    teacher_z_ref, student_z_ref, teacher_ref, student_ref, centre_ref, scale_ref, *refs
 ):
+    grad_ref, square_ref = refs[-2:]
     step = pl.program_id(0)
 
     @pl.when(step == 0)
@@ -1124,7 +1122,7 @@
     square_ref[...] += jnp.broadcast_to(jnp.sum(grad * grad), square_ref.shape)
 
 
-def proto_grad_pass(teacher_z, student_z, teacher, student, centre_column, scale_lines):
+def proto_grad_pass(teacher_z, student_z, teacher, student, centre_column, scale_lines, waits):
     rows, protos_here = teacher_z.shape[0], student.shape[0]
     block = protos_here // 4
     whole, table, column, lines = proto_specs(rows, block)
@@ -1135,11 +1133,12 @@
             jax.ShapeDtypeStruct((protos_here, BOT), single),
             jax.ShapeDtypeStruct((8, 128), single),
         ],
-        in_specs=[whole, whole, table, table, column, lines],
+        in_specs=[whole, whole, table, table, column, lines]
+        + [pl.BlockSpec(memory_space=pl.ANY)] * len(waits),
         out_specs=[table, pl.BlockSpec((8, 128), lambda i: (0, 0))],
         compiler_params=pltpu.CompilerParams(vmem_limit_bytes=56 << 20),
         cost_estimate=pl.CostEstimate(flops=4 * 10**9, bytes_accessed=10**7, transcendentals=5 * 10**6),
-    )(teacher_z, student_z, teacher, student, centre_column, scale_lines)
+    )(teacher_z, student_z, teacher, student, centre_column, scale_lines, *waits)
 
 
 def proto_update(factor, student, moment, second, teacher, grad):
@@ -1165,9 +1164,9 @@
 
 
 def head_grads_kernel(
-    place_ref, inputs_ref, grads_ref, own_ref, partner_ref, window_ref, rows_ref, product_ref,
-    third_ref, bottle_ref, line_ref, sems,
+    place_ref, inputs_ref, grads_ref, *refs,
 ):
+    own_ref, partner_ref, window_ref, rows_ref, product_ref, third_ref, bottle_ref, line_ref, sems = refs[-9:]
     slot = own_ref.shape[0]
     lead = product_ref.shape[0] - window_ref.shape[1]
     number = lax.broadcasted_iota(jnp.int32, (slot, 1), 0)
@@ -1191,7 +1190,8 @@
             spot = pl.ds(piece * (ROW // 4), ROW // 4)
             product_ref[pl.ds(lead, window.shape[1]), spot] = product_left(window, rows_ref[:, spot])
         from_row = pl.multiple_of(lead + place_ref[at + 1], 8)
-        out_ref[...] = jnp.where(number < place_ref[at + 2], product_ref[pl.ds(from_row, slot), :], 0.0)
+        kept = jnp.where(number < place_ref[at + 2], product_ref[pl.ds(from_row, slot), :], 0.0)
+        out_ref[...] = kept.astype(out_ref.dtype)
 
     @pl.when(place_ref[8] == 0)
     def _():
@@ -1223,13 +1223,14 @@
     block(4, partner_ref)
 
 
-def head_grads(place, inputs_all, grads_all, slot, lead):
+def head_grads(place, inputs_all, grads_all, slot, lead, waits):
     rows = inputs_all.shape[0]
     wide = slot * ROW // BOT
     return pl.pallas_call(
         head_grads_kernel,
-        out_shape=[jax.ShapeDtypeStruct((slot, ROW), single)] * 2,
-        in_specs=[pl.BlockSpec(memory_space=pltpu.SMEM)] + [pl.BlockSpec(memory_space=pl.ANY)] * 2,
+        out_shape=[jax.ShapeDtypeStruct((slot, ROW), kind) for kind in (single, narrow)],
+        in_specs=[pl.BlockSpec(memory_space=pltpu.SMEM)]
+        + [pl.BlockSpec(memory_space=pl.ANY)] * (2 + len(waits)),
         out_specs=[pl.BlockSpec(memory_space=pltpu.VMEM)] * 2,
         scratch_shapes=[
             pltpu.VMEM((rows, 256), narrow),
@@ -1242,7 +1243,7 @@
         ],
         compiler_params=pltpu.CompilerParams(vmem_limit_bytes=56 << 20),
         cost_estimate=pl.CostEstimate(flops=4 * 10**9, bytes_accessed=2 * 10**7, transcendentals=0),
-    )(place, inputs_all, grads_all)
+    )(place, inputs_all, grads_all, *waits)
 
 
 def close_local(
@@ -1274,6 +1275,8 @@
     side = student_side.astype(jnp.int32).reshape(1)
     images_here = patches.shape[0]
     rows_here = images_here * 17
+    pair_rows = -(-2 * rows_here // 16) * 16
+    more_rows = pair_rows - 2 * rows_here
     stem_piece = stem.shape[0]
     layer_piece = layers.shape[1]
     block_rows = MATRIX_ROWS // count
@@ -1441,6 +1444,7 @@
         jnp.concatenate([normed_got, student_normed]),
         jnp.concatenate([teacher_normed, normed_got]),
     )
+    normed = jnp.pad(normed, ((0, more_rows), (0, 0)))
     w_one = jnp.concatenate(head_slots(1, first_w2)).reshape(-1, ROW)
     w_two = jnp.concatenate(head_slots(first_w2, first_w3)).reshape(-1, ROW)
     w_three = jnp.concatenate(
@@ -1452,10 +1456,8 @@
     hidden_two = jax.nn.gelu(pre_two).astype(narrow)
     bottleneck = contract("rh,hb->rb", hidden_two, w_three)
     unit_z = unit_rows(bottleneck).astype(narrow)
-    pair_rows = -(-2 * rows_here // 16) * 16
-    more_rows = ((0, pair_rows - 2 * rows_here), (0, 0))
     third_end = (bounds[-2] - D - HID + slot) * (ROW // BOT)
-    more_inputs = (more_rows[0], (0, max(third_end - HID, 0)))
+    more_inputs = ((0, 0), (0, max(third_end - HID, 0)))
     inputs_all = lax.all_gather(
         jnp.pad(jnp.concatenate([normed, hidden_one, hidden_two], axis=1), more_inputs),
         "dev",
@@ -1463,38 +1465,35 @@
         axis_index_groups=groups,
     ).reshape(half * pair_rows, -1)
 
-    all_rows = count * rows_here
+    all_rows = half * pair_rows
     kept_row = jnp.broadcast_to(kept[:, None], (images_here, 17)).reshape(1, rows_here)
-    all_kept = cube_gather(kept_row, "bxygc").reshape(all_rows)
+    kept_pair = cube_gather(kept_row, "b").reshape(1, 2 * rows_here)
+    kept_pair = jnp.pad(kept_pair, ((0, 0), (0, more_rows)))
+    all_kept = cube_gather(kept_pair, "xygc").reshape(all_rows)
     z_pair = cube_gather(unit_z, "b")
-    z_all = cube_gather(z_pair, "xygc")
-    z_all = z_all.reshape(half, 2, 2 * rows_here, BOT)
-    wide_rows = -(-all_rows // 128) * 128
-    teacher_z_all, student_z_all = [
-        jnp.pad(z_all[:, model].reshape(all_rows, BOT), ((0, wide_rows - all_rows), (0, 0))) for model in range(2)
-    ]
+    teacher_z_all = cube_gather(z_pair[0], "xygc").reshape(all_rows, BOT)
+    student_z_all = cube_gather(z_pair[1], "gxyc").reshape((2,) * 4 + (pair_rows, BOT))
+    student_z_all = jnp.transpose(student_z_all, (0, 3, 1, 2, 4, 5)).reshape(all_rows, BOT)
     protos_here = protos.shape[0]
     own_centre = lax.dynamic_slice(centre, (me * protos_here,), (protos_here,))
     centre_column = own_centre.reshape(protos_here, 1)
-    is_class = (jnp.arange(all_rows) % 17) == 0
+    spot_in_pair = jnp.arange(all_rows) % pair_rows
+    is_class = (spot_in_pair % 17) == 0
     class_kept = jnp.where(is_class, all_kept, 0.0)
     row_weight = jnp.where(is_class, all_kept, all_kept * (1.0 / 16.0))
     count_total = jnp.sum(class_kept)
 
     def lines(*values):
-        held = jnp.pad(jnp.stack(values), ((0, 8 - len(values)), (0, wide_rows - all_rows)))
-        return held
+        return jnp.pad(jnp.stack(values), ((0, 8 - len(values)), (0, 0)))
 
     mixed_rows, sums, centre_sum = logits_pass(
         teacher_z_all, student_z_all, proto_teacher, protos, centre_column, lines(class_kept)
     )
-    mixed_own = cube_scatter(
-        [mixed_rows[:all_rows].reshape((2,) * 4 + (2 * rows_here, 2 * BOT))], ("cgyx",), ("cgyx",)
-    )[0]
+    mixed_own = cube_scatter(mixed_rows.reshape((2,) * 4 + (pair_rows, 2 * BOT)), "cgyx", "cgyx")
     mixed_own = mixed_own + lax.ppermute(
         mixed_own.astype(narrow), "dev", [(i, i ^ across) for i in range(half)]
     ).astype(single)
-    sums = cube_sum(sums[:3, :all_rows])
+    sums = cube_sum(sums[:3])
     cross = jnp.log(sums[1]) - sums[2] / (sums[0] * tau_student)
     loss_total = jnp.sum(row_weight * cross)
     scale = row_weight / tau_student
@@ -1502,7 +1501,7 @@
     flags = bit_flags(me)
     pair_at = flags["c"] * 8 + flags["g"] * 4 + flags["y"] * 2 + flags["x"]
     own_scales = lax.dynamic_slice(
-        jnp.stack([student_scale, teacher_scale]), (0, pair_at * 2 * rows_here), (2, 2 * rows_here)
+        jnp.stack([student_scale, teacher_scale]), (0, pair_at * pair_rows), (2, pair_rows)
     )
     grad_unit_z = (
         mixed_own[:, :BOT] * own_scales[0][:, None] - mixed_own[:, BOT:] * own_scales[1][:, None]
@@ -1511,9 +1510,6 @@
         centre_keep * own_centre + (1.0 - centre_keep) * centre_sum.reshape(protos_here) / count_total
     )
     new_centre = cube_gather(own_new_centre.reshape(1, protos_here), "cxyab").reshape(-1)
-    proto_grad, proto_square = proto_grad_pass(
-        teacher_z_all, student_z_all, proto_teacher, protos, centre_column, lines(student_scale, teacher_scale)
-    )
 
     grad_bottle = jax.vjp(unit_rows, bottleneck)[1](grad_unit_z)[0].astype(narrow)
     grad_pre_two = gelu_back(pre_two, contract("rb,hb->rh", grad_bottle, w_three)).astype(narrow)
@@ -1521,7 +1517,7 @@
     grad_pre_one = gelu_back(pre_one, grad_hidden).astype(narrow)
     grad_normed = cut_columns(contract("rh,dh->rd", grad_pre_one, w_one), 1, first_w2, 0)
     grads_all = lax.all_gather(
-        jnp.pad(jnp.concatenate([grad_pre_one, grad_pre_two, grad_bottle], axis=1), more_rows),
+        jnp.concatenate([grad_pre_one, grad_pre_two, grad_bottle], axis=1),
         "dev",
         axis=0,
         axis_index_groups=groups,
@@ -1529,7 +1525,7 @@
     normed_back = lax.ppermute(
         grad_normed[:rows_here], "dev", [(i, i ^ across) for i in range(half, count)]
     )
-    own_grad_normed = jnp.where(student_side, grad_normed[rows_here:], normed_back)
+    own_grad_normed = jnp.where(student_side, grad_normed[rows_here : 2 * rows_here], normed_back)
     extras = student_parts[2].astype(single)
     grad_chosen, grad_gain, grad_bias = jax.vjp(layer_norm, chosen, extras[2], extras[3])[1](
         own_grad_normed
@@ -1545,28 +1541,83 @@
     middle_row = block_rows // 2
     small_rows = -(-(EMBED_ROWS + 6 * LAYERS) // (16 * count)) * 16
     vector_grads = [None] * LAYERS
-    firsts = [None] * LAYERS
-    seconds = [None] * LAYERS
+
+    def halves(array):
+        middle = array.shape[-2] // 2
+        return [array[..., :middle, :], array[..., middle:, :]]
+
+    def cuts(parts, names, order):
+        return [cut(part, name, axis, 1) for part, name, axis in zip(parts, names, order)]
+
+    def moves(pieces, order):
+        return [move(sent, kept, axis) for (sent, kept, left), axis in zip(pieces, order)]
+
+    def blocks_of(weight_grad, rows):
+        return split_bits(weight_grad.reshape(D // 128, count, rows, 128), 1)
+
+    rounds = (("c",), ("x", "y"), ("y", "x"), ("b", "b"), ("a", "a"))
+
+    def advance(state):
+        pieces, stage = state
+        parts = moves(pieces, rounds[stage])
+        names = [left for sent, kept, left in pieces]
+        if stage == 0:
+            parts, names = halves(parts[0]), names * 2
+        return cuts(parts, names, rounds[stage + 1]), stage + 1
+
+    def finish(state):
+        while state[1] < len(rounds) - 1:
+            state = advance(state)
+        return moves(state[0], rounds[-1])
+
+    def sends(states):
+        return tuple(sent for pieces, stage in states for sent, kept, left in pieces)
+
+    started = []
     waits = ()
     for layer_index in reversed(range(LAYERS)):
         saved, vectors = saved_layers[layer_index], vectors_all[1, layer_index]
         part = LAYERS + layer_index
+        started = [advance(state) for state in started]
         grad_stream, weight_grad, late_vectors = mlp_back(
-            side, grad_stream, saved, vectors, gathered, part, ()
+            side, grad_stream, saved, vectors, gathered, part, waits + sends(started)
         )
+        started = [advance(state) for state in started]
         grad_stream, weight_grad, early_vectors = attention_back(
-            side, grad_stream, saved, vectors, gathered, part, weight_grad, waits
+            side, grad_stream, saved, vectors, gathered, part, weight_grad, sends(started)
         )
         vector_grads[layer_index] = (late_vectors + early_vectors)[:6]
-        owned = split_bits(weight_grad.reshape(D // 128, count, block_rows, 128), 1)
-        firsts[layer_index] = cube_scatter([owned], ("c",), (BITS,), 1)[0]
-        waits = (firsts[layer_index],)
-
-    def second_round(parts):
-        return cube_scatter(parts, ("x", "y"), ("bayx", "bayx"), 1)
-
-    def halves(array):
-        return [array[..., : array.shape[-2] // 2, :], array[..., array.shape[-2] // 2 :, :]]
+        first = (cuts([blocks_of(weight_grad, block_rows)], ["bayxc"], rounds[0]), 0)
+        if layer_index == LAYERS - 1:
+            proto_grad, proto_square = proto_grad_pass(
+                teacher_z_all,
+                student_z_all,
+                proto_teacher,
+                protos,
+                centre_column,
+                lines(student_scale, teacher_scale),
+                sends([first]),
+            )
+            waits = (proto_square,)
+        if layer_index > 0:
+            started.append(first)
+    started = [advance(state) for state in started]
+    small = embed_back(
+        grad_stream,
+        patches.reshape(images_here * PATCHES, PIX),
+        jnp.where(masked_here, 0.0, 1.0).reshape(images_here * PATCHES, 1),
+        jnp.stack([grad_gain, grad_bias]),
+        jnp.concatenate(vector_grads),
+        small_rows * count,
+        sends([first] + started),
+    )
+    small_first = cuts([blocks_of(small, small_rows)], ["bayxc"], rounds[0])
+    joined = [
+        jnp.concatenate(pair, axis=-2)
+        for pair in zip(halves(moves(first[0], "c")[0]), halves(moves(small_first, "c")[0]))
+    ]
+    last = (cuts(joined, ["bayx"] * 2, rounds[1]), 1)
+    later_blocks = [jnp.concatenate(finish(state), axis=1) for state in started]
 
     def table(values):
         return jnp.array(values, jnp.int32)
@@ -1592,35 +1643,18 @@
             table(thirds)[me],
         ]
     ).astype(jnp.int32)
-    own_block_grad, partner_block_grad = head_grads(place, inputs_all, grads_all, slot, -min(bounds[1], 0))
+    own_block_grad, partner_block_grad = head_grads(
+        place, inputs_all, grads_all, slot, -min(bounds[1], 0), sends([last])
+    )
     block_got = lax.ppermute(partner_block_grad, "dev", [(i, i ^ across) for i in range(half, count)])
-    head_block_grad = jnp.where(student_side, own_block_grad, block_got)
-
-    later = [second_round(halves(firsts[i])) for i in range(1, LAYERS)]
-    small = embed_back(
-        grad_stream,
-        patches.reshape(images_here * PATCHES, PIX),
-        jnp.where(masked_here, 0.0, 1.0).reshape(images_here * PATCHES, 1),
-        jnp.stack([grad_gain, grad_bias]),
-        jnp.concatenate(vector_grads),
-        small_rows * count,
-        [array for pair in later for array in pair] + [own_block_grad],
-    )
-    small_first = cube_scatter(
-        [split_bits(small.reshape(D // 128, count, small_rows, 128), 1)], ("c",), (BITS,), 1
-    )[0]
-    last = second_round(
-        [jnp.concatenate(pair, axis=-2) for pair in zip(halves(firsts[0]), halves(small_first))]
-    )
-    joined = [jnp.concatenate(parts, axis=-2) for parts in zip(last, *later)]
-    done = cube_scatter(joined, ("yba", "xba"), ("bay", "bax"), 1)
-    middle_row, small_middle = block_rows // 2, small_rows // 2
-    small_block = jnp.concatenate([part[:, middle_row : middle_row + small_middle] for part in done], axis=1)
-    blocks = [jnp.concatenate([part[:, :middle_row] for part in done], axis=1)]
-    for number in range(LAYERS - 1):
-        at = middle_row + small_middle + number * middle_row
-        blocks.append(jnp.concatenate([part[:, at : at + middle_row] for part in done], axis=1))
-    layer_block = jnp.stack(blocks)
+    head_block_grad = jnp.where(student_side, own_block_grad, block_got.astype(single))
+    pieces, stage = advance(last)
+    parts = finish(([(after(sent, own_block_grad), stay, left) for sent, stay, left in pieces], stage))
+    middle_row = block_rows // 2
+    small_block = jnp.concatenate([part[:, middle_row:] for part in parts], axis=1)
+    layer_block = jnp.stack(
+        [jnp.concatenate([part[:, :middle_row] for part in parts], axis=1)] + later_blocks[::-1]
+    )
 
     square_local = (
         jnp.sum(head_block_grad * head_block_grad)
@@ -1628,9 +1662,15 @@
         + jnp.sum(small_block * small_block)
         + proto_square[0, 0]
     )
-    square_total = cube_sum(square_local.reshape(1, 1))[0, 0]
-    small_all = cube_gather(small_block, "cxyab").reshape((count,) + small_block.shape)
-    small_all = jnp.transpose(small_all, (0, 2, 1, 3)).reshape(small_rows * count, D)
+    high = square_local.astype(narrow)
+    middle = (square_local - high.astype(single)).astype(narrow)
+    low = (square_local - high.astype(single) - middle.astype(single)).astype(narrow)
+    tile = jnp.pad(jnp.stack([high, middle, low]).reshape(3, 1, 1), ((0, 0), (0, 15), (0, 127)))
+    shared = cube_gather(jnp.concatenate([small_block.astype(narrow), tile], axis=1), "xyabc")
+    shared = jnp.moveaxis(shared.reshape((2,) + (half,) + shared.shape[1:]), 0, 1)
+    shared = shared.reshape((count,) + shared.shape[2:]).astype(single)
+    square_total = jnp.sum(shared[:, :, small_rows, 0])
+    small_all = jnp.transpose(shared[:, :, :small_rows], (0, 2, 1, 3)).reshape(small_rows * count, D)
     embed_grad = small_all[:EMBED_ROWS].reshape(-1)
     vector_grad = small_all[EMBED_ROWS : EMBED_ROWS + 6 * LAYERS].reshape(LAYERS, 6, D)
 

time: 731 us -> 677 us (0.926)
  waiting for transfers between devices: 255 us -> 210 us
  local copies, waits for them, and re-layouts: 107 us -> 93.6 us
  starting transfers between devices: 82.7 us -> 91.7 us
    ppermute x17 -> x23, waiting for transfers between devices: 61.2 us -> 28.1 us  [move(): lax.ppermute(sent, 'dev', pairs(1 << len(BITS), MASKS[name])).astype(single)]
    ppermute x17 -> x23, starting transfers between devices: 9.01 us -> 26.7 us  [move(): lax.ppermute(sent, 'dev', pairs(1 << len(BITS), MASKS[name])).astype(single)]
    unnamed x189 -> x155, local copies, waits for them, and re-layouts: 27.3 us -> 14.9 us
    ppermute x1, waiting for transfers between devices: 32.3 us -> 20.3 us  [close_local(): lax.ppermute(partner_block_grad, 'dev', [(i, i ^ across) for i in range(h...]
    ppermute x10 -> x5, waiting for transfers between devices: 20.3 us -> 11.9 us  [cube_sum(): lax.ppermute(values, 'dev', pairs(1 << len(BITS), MASKS[name]))]
    ppermute x20 -> x24, waiting for transfers between devices: 34.1 us -> 41.9 us  [cube_gather(): got = lax.ppermute(held, 'dev', pairs(count, MASKS[name]))]
    ppermute x10 -> x5, starting transfers between devices: 11.3 us -> 3.46 us  [cube_sum(): lax.ppermute(values, 'dev', pairs(1 << len(BITS), MASKS[name]))]
    convert_element_type x0 -> x11, local copies, waits for them, and re-layouts: none -> 7.81 us  [the longest x10 7.54 us: cut(): sent.astype(narrow)]
  transfers between devices with their start and end apart: 75 -> 80, of which waited for: 40 -> 40; matrix products, arithmetic and copies ran while one was open for 19% -> 20% of each run, Pallas kernels for 21% -> 22%
where the time goes in v5:
time: 677 us; the launch traced here: 669 us
  waiting for transfers between devices  210 us (31%)
  Pallas kernels  161 us (24%)
  local copies, waits for them, and re-layouts  93.6 us (14%)
  starting transfers between devices  91.7 us (14%)
  other arithmetic  68.4 us (10%)
  between operations  26.2 us (4%)
  matrix products  18.2 us (3%)
    pallas_call x4, Pallas kernels, layer_back(): pl.pallas_call(lambda *refs: kernel(part, *refs), out_shape=[jax.ShapeDty...  63.8 us
    pallas_call x4, Pallas kernels, layer_forward(): pl.pallas_call(lambda *refs: forward_kernel(part, keep, *refs), out_shape...  47.7 us
    ppermute x12, waiting for transfers between devices, close_local(): got = lax.ppermute(spread, 'dev', moves)  42.3 us
    ppermute x24, waiting for transfers between devices, cube_gather(): got = lax.ppermute(held, 'dev', pairs(count, MASKS[name]))  41.9 us
    ppermute x23, waiting for transfers between devices, move(): lax.ppermute(sent, 'dev', pairs(1 << len(BITS), MASKS[name])).astype(single)  28.1 us
    ppermute x23, starting transfers between devices, move(): lax.ppermute(sent, 'dev', pairs(1 << len(BITS), MASKS[name])).astype(single)  26.7 us
    ppermute x24, starting transfers between devices, cube_gather(): got = lax.ppermute(held, 'dev', pairs(count, MASKS[name]))  23.9 us
    ppermute x1, waiting for transfers between devices, close_local(): lax.ppermute(partner_block_grad, 'dev', [(i, i ^ across) for i in range(h...  20.3 us
  transfers between devices with their start and end apart: 80, of which 40 were waited for; matrix products, arithmetic and copies ran while one was open for 20% of the time, Pallas kernels for 22%

profile of v5, /device:TPU:8, one launch (start us, length us, event | category | flops | bytes accessed | tf_op | source)
XLA Modules:
  0.0 669.3 jit_solution(10831358478819987990)
XLA Ops:
  28.8 18.7 %collective-permute-done.21 = bf16[4,144,384]{2,1,0:T(8,128)(2,1)S(1)} collective-permute-done((bf16[4,144,384]{2,1,0:T(8,128)(2,1)S(1)}, bf16[4,144,384]{2,1,0:T(8,128)(2,1)S(1)}, u32[]{:S(2)}, u32[]{:S(2)}) %collective-permute-start.21) | collective-permute-done | bytes 442400 | tf_op jit(solution)/shard_map/ppermute | solution.py:1327
  66.8 19.0 %collective-permute-done.12 = bf16[336,384]{1,0:T(8,128)(2,1)S(1)} collective-permute-done((bf16[336,384]{1,0:T(8,128)(2,1)S(1)}, bf16[336,384]{1,0:T(8,128)(2,1)S(1)}, u32[]{:S(2)}, u32[]{:S(2)}) %collective-permute-start.12) | collective-permute-done | bytes 258080 | tf_op jit(solution)/shard_map/ppermute | solution.py:1350
  87.8 8.5 %collective-permute-done.18 = bf16[320,384]{1,0:T(8,128)(2,1)S(1)} collective-permute-done((bf16[320,384]{1,0:T(8,128)(2,1)S(1)}, bf16[320,384]{1,0:T(8,128)(2,1)S(1)}, u32[]{:S(2)}, u32[]{:S(2)}) %collective-permute-start.18) | collective-permute-done | bytes 245792 | tf_op jit(solution)/shard_map/ppermute | solution.py:1350
  105.8 12.1 %collective-permute-done.10 = bf16[336,384]{1,0:T(8,128)(2,1)S(1)} collective-permute-done((bf16[336,384]{1,0:T(8,128)(2,1)S(1)}, bf16[336,384]{1,0:T(8,128)(2,1)S(1)}, u32[]{:S(2)}, u32[]{:S(2)}) %collective-permute-start.10) | collective-permute-done | bytes 258080 | tf_op jit(solution)/shard_map/ppermute | solution.py:1350
  123.0 17.7 %collective-permute-done.23 = bf16[96,2048]{1,0:T(8,128)(2,1)S(1)} collective-permute-done((bf16[96,2048]{1,0:T(8,128)(2,1)S(1)}, bf16[96,2048]{1,0:T(8,128)(2,1)S(1)}, u32[]{:S(2)}, u32[]{:S(2)}) %collective-permute-start.23) | collective-permute-done | bytes 393248 | tf_op jit(solution)/shard_map/ppermute | solution.py:1336
  143.1 15.9 %all-gather.8.cloned.1.call-done.refs_3_.refs_1_.refs_7_.refs_6_ = bf16[16,2,4,144,384]{4,3,2,1,0:T(8,128)(2,1)} async-done(((bf16[1,2,4,144,384]{4,3,2,1,0:T(8,128)(2,1)}), bf16[16,2,4,144,384]{4,3,2,1,0:T(8,128)(2,1)}) %all-gather.8.cloned.1.call-update) | async-done | bytes 14155792 | tf_op jit(solution)/shard_map/all_gather | solution.py:1333
  167.8 11.5 %shard_map.493.refs_1_ = f32[544,384]{1,0:T(8,128)} custom-call(s32[1]{0:T(128)} %bitcast.10.refs_0_, f32[544,384]{1,0:T(8,128)} %bitcast.345, bf16[8,384]{1,0:T(8,128)(2,1)} %get-tuple-element.198.refs_2_, bf16[16,2,4,144,384]{4,3,2,1,0:T(8,128)(2,1)} %all-gather.8.cloned.1.call-done.refs_3_.refs_1_.refs_7_.refs_6_), custom_call_target="tpu_custom_call" | custom-call | flops 2000000000 | bytes 20000000 | tf_op jit(solution)/shard_map/pallas_call | solution.py:784
  179.3 11.7 %shard_map.494 = f32[544,384]{1,0:T(8,128)} custom-call(s32[1]{0:T(128)} %bitcast.10.refs_0_, f32[544,384]{1,0:T(8,128)} %shard_map.493.refs_1_, bf16[8,384]{1,0:T(8,128)(2,1)} %get-tuple-element.197.refs_2_, bf16[16,2,4,144,384]{4,3,2,1,0:T(8,128)(2,1)} %all-gather.8.cloned.1.call-done.refs_3_.refs_1_.refs_7_.refs_6_), custom_call_target="tpu_custom_call" | custom-call | flops 2000000000 | bytes 20000000 | tf_op jit(solution)/shard_map/pallas_call | solution.py:784
  193.6 12.1 %shard_map.495 = (f32[544,384]{1,0:T(8,128)}, bf16[544,1152]{1,0:T(8,128)(2,1)}, bf16[544,384]{1,0:T(8,128)(2,1)}, f32[544,384]{1,0:T(8,128)}, f32[544,1536]{1,0:T(8,128)}, /*index=5*/f32[544,384]{1,0:T(8,128)}) custom-call(s32[1]{0:T(128)} %bitcast.10.refs_0_, f32[544,384]{1,0:T(8,128)} %bitcast.330, ...), custom_call_target="tpu_custom_call" | custom-call | flops 2000000000 | bytes 20000000 | tf_op jit(solution)/shard_map/pallas_call | solution.py:784
  205.8 12.4 %shard_map.496 = (f32[544,384]{1,0:T(8,128)}, bf16[544,1152]{1,0:T(8,128)(2,1)}, bf16[544,384]{1,0:T(8,128)(2,1)}, f32[544,384]{1,0:T(8,128)}, f32[544,1536]{1,0:T(8,128)}, /*index=5*/f32[544,384]{1,0:T(8,128)}) custom-call(s32[1]{0:T(128)} %bitcast.10.refs_0_, f32[544,384]{1,0:T(8,128)} %get-tuple-element.65.refs_1_.refs_2_, ...), custom_call_target="tpu_custom_call" | custom-call | flops 2000000000 | bytes 20000000 | tf_op jit(solution)/shard_map/pallas_call | solution.py:784
  243.1 6.3 multiply_convert_fusion
  300.8 13.5 %shard_map.498 = (f32[1280,512]{1,0:T(8,128)}, f32[8,1280]{1,0:T(8,128)}, f32[2048,1]{1,0:T(8,128)}) custom-call(bf16[1280,256]{1,0:T(8,128)(2,1)} %bitcast.352, bf16[1280,256]{1,0:T(8,128)(2,1)} %bitcast.350, f32[2048,256]{1,0:T(8,128)} %refs_3_.1, f32[2048,256]{1,0:T(8,128)} %refs_0_.1, f32[2048,1]{1,0:T(8,128)} %copy.175.centre_ref, f32[8,1280]{1,0:T(8,128)} %pad.50.class_ref), custom_call_target="tpu_custom_call" | custom-call | flops 5000000000 | bytes 10000000 | tf_op jit(solution)/shard_map/pallas_call | solution.py:1081
  358.8 6.4 fusion.111
  384.9 14.7 %shard_map.499 = (f32[544,384]{1,0:T(8,128)}, f32[3,4608,128]{2,1,0:T(8,128)}, f32[8,384]{1,0:T(8,128)}) custom-call(s32[1]{0:T(128)} %bitcast.10.refs_0_, f32[544,384]{1,0:T(8,128)} %bitcast.340, f32[544,384]{1,0:T(8,128)} %get-tuple-element.65.refs_1_.refs_2_, f32[544,384]{1,0:T(8,128)} %get-tuple-element.70.refs_3_, ...), custom_call_target="tpu_custom_call" | custom-call | flops 5000000000 | bytes 40000000 | tf_op jit(solution)/shard_map/pallas_call | solution.py:921
  399.6 17.3 %shard_map.500 = (f32[544,384]{1,0:T(8,128)}, f32[3,4608,128]{2,1,0:T(8,128)}, f32[8,384]{1,0:T(8,128)}) custom-call(s32[1]{0:T(128)} %bitcast.10.refs_0_, f32[544,384]{1,0:T(8,128)} %get-tuple-element.73.refs_1_, f32[544,384]{1,0:T(8,128)} %get-tuple-element.65.refs_1_.refs_2_, ...), custom_call_target="tpu_custom_call", output_to_operand_aliasing={{1}: (7, {})} | custom-call | flops 5000000000 | bytes 40000000 | tf_op jit(solution)/shard_map/pallas_call | solution.py:921
  439.9 11.0 %shard_map.501 = (f32[2048,256]{1,0:T(8,128)}, f32[8,128]{1,0:T(8,128)}) custom-call(bf16[1280,256]{1,0:T(8,128)(2,1)} %bitcast.353, bf16[1280,256]{1,0:T(8,128)(2,1)} %bitcast.351, f32[2048,256]{1,0:T(8,128)} %refs_3_.1, f32[2048,256]{1,0:T(8,128)} %refs_0_.1, f32[2048,1]{1,0:T(8,128)} %copy.175.centre_ref, f32[8,1280]{1,0:T(8,128)} %pad.51.scale_ref, ...), custom_call_target="tpu_custom_call" | custom-call | flops 4000000000 | bytes 10000000 | tf_op jit(solution)/shard_map/pallas_call | solution.py:1129
  460.9 14.6 %shard_map.502 = (f32[544,384]{1,0:T(8,128)}, f32[3,4608,128]{2,1,0:T(8,128)}, f32[8,384]{1,0:T(8,128)}) custom-call(s32[1]{0:T(128)} %bitcast.10.refs_0_, f32[544,384]{1,0:T(8,128)} %get-tuple-element.77.refs_1_, f32[544,384]{1,0:T(8,128)} %bitcast.331, f32[544,384]{1,0:T(8,128)} %get-tuple-element.78.refs_3_, f32[544,1536]{1,0:T(8,128)} %get-tuple-element.79.refs_4_, ...), custom_call_target="tpu_custom_call" | custom-call | flops 5000000000 | bytes 40000000 | tf_op jit(solution)/shard_map/pallas_call | solution.py:921
  478.5 17.2 %shard_map.503 = (f32[544,384]{1,0:T(8,128)}, f32[3,4608,128]{2,1,0:T(8,128)}, f32[8,384]{1,0:T(8,128)}) custom-call(s32[1]{0:T(128)} %bitcast.10.refs_0_, f32[544,384]{1,0:T(8,128)} %get-tuple-element.83.refs_1_, f32[544,384]{1,0:T(8,128)} %bitcast.332, bf16[544,1152]{1,0:T(8,128)(2,1)} %get-tuple-element.84.refs_3_, ...), custom_call_target="tpu_custom_call", output_to_operand_aliasing={{1}: (7, {})} | custom-call | flops 5000000000 | bytes 40000000 | tf_op jit(solution)/shard_map/pallas_call | solution.py:921
  506.5 6.3 collective-permute-start.61
  525.3 6.4 collective-permute-done.51
  532.7 10.1 %shard_map.505 = (f32[96,2048]{1,0:T(8,128)}, bf16[96,2048]{1,0:T(8,128)(2,1)}) custom-call(s32[10]{0:T(128)} %stack.136.place_ref, bf16[1280,4608]{1,0:T(8,128)(2,1)} %all-gather.12.cloned.1.call-done.inputs_ref, bf16[1280,4352]{1,0:T(8,128)(2,1)} %all-gather.14.cloned.1.call-done.grads_ref, bf16[3,2,2,2,88,128]{5,4,3,2,1,0:T(8,128)(2,1)} %copy.199.refs_0_, ...), custom_call_target="tpu_custom_call" | custom-call | flops 4000000000 | bytes 20000000 | tf_op jit(solution)/shard_map/pallas_call | solution.py:1229
  560.1 20.3 %collective-permute-done.59 = bf16[96,2048]{1,0:T(8,128)(2,1)S(1)} collective-permute-done((bf16[96,2048]{1,0:T(8,128)(2,1)}, bf16[96,2048]{1,0:T(8,128)(2,1)S(1)}, u32[]{:S(2)}, u32[]{:S(2)}) %collective-permute-start.59) | collective-permute-done | bytes 393248 | tf_op jit(solution)/shard_map/ppermute | solution.py:1649
  611.6 11.0 %collective-permute-done.67 = bf16[8,3,48,128]{3,2,1,0:T(8,128)(2,1)S(1)} collective-permute-done((bf16[8,3,48,128]{3,2,1,0:T(8,128)(2,1)S(1)}, bf16[8,3,48,128]{3,2,1,0:T(8,128)(2,1)S(1)}, u32[]{:S(2)}, u32[]{:S(2)}) %collective-permute-start.67) | collective-permute-done | bytes 294944 | tf_op jit(solution)/shard_map/ppermute | solution.py:444
  628.8 5.2 collective-permute-start.75
  (615 shorter events, 343.1 us)
Async XLA Ops:
  7.2 151.8 %all-gather.8.cloned.1.call-start = ((), (), s32[]{:S(2)}) async-start(), calls=%async_computation | async-start | bytes 15040512 | tf_op jit(solution)/shard_map/all_gather | solution.py:1333
  27.2 20.3 %collective-permute-start.21 = (bf16[4,144,384]{2,1,0:T(8,128)(2,1)S(1)}, bf16[4,144,384]{2,1,0:T(8,128)(2,1)S(1)}, u32[]{:S(2)}, u32[]{:S(2)}) collective-permute-start(bf16[4,144,384]{2,1,0:T(8,128)(2,1)S(1)} %get-tuple-element.64), channel_id=1, source_target_pairs={{0,24},{1,25},{2,26},{3,27},{4,28},{5,29},{6,30},{7,31},{8,16},{9,... | collective-permute-start | bytes 1327112 | tf_op jit(solution)/shard_map/ppermute | solution.py:1327
  48.6 179.3 %all-gather.10.cloned.1.call-start = ((), (), s32[]{:S(2)}) async-start(), calls=%async_computation.1 | async-start | bytes 13369344 | tf_op jit(solution)/shard_map/all_gather | solution.py:1370
  62.1 23.7 %collective-permute-start.12 = (bf16[336,384]{1,0:T(8,128)(2,1)S(1)}, bf16[336,384]{1,0:T(8,128)(2,1)S(1)}, u32[]{:S(2)}, u32[]{:S(2)}) collective-permute-start(bf16[336,384]{1,0:T(8,128)(2,1)S(1)} %get-tuple-element.176), channel_id=1, source_target_pairs={{0,8},{1,9},{24,16},{25,17}} | collective-permute-start | bytes 774152 | tf_op jit(solution)/shard_map/ppermute | solution.py:1350
  64.1 32.2 %collective-permute-start.18 = (bf16[320,384]{1,0:T(8,128)(2,1)S(1)}, bf16[320,384]{1,0:T(8,128)(2,1)S(1)}, u32[]{:S(2)}, u32[]{:S(2)}) collective-permute-start(bf16[320,384]{1,0:T(8,128)(2,1)S(1)} %broadcast_select_fusion.14), channel_id=1, source_target_pairs={{0,8},{1,9},{4,12},{5,13},{24,16},{25,17},{28,20},{29,21}} | collective-permute-start | bytes 737288 | tf_op jit(solution)/shard_map/ppermute | solution.py:1350
  66.1 32.2 %collective-permute-start.9 = (bf16[336,384]{1,0:T(8,128)(2,1)S(1)}, bf16[336,384]{1,0:T(8,128)(2,1)S(1)}, u32[]{:S(2)}, u32[]{:S(2)}) collective-permute-start(bf16[336,384]{1,0:T(8,128)(2,1)S(1)} %broadcast_select_fusion.10), channel_id=1, source_target_pairs={{0,24},{1,25},{2,26},{3,27},{4,28},{5,29},{6,30},{7,31}} | collective-permute-start | bytes 774152 | tf_op jit(solution)/shard_map/ppermute | solution.py:1350
  99.0 18.9 %collective-permute-start.10 = (bf16[336,384]{1,0:T(8,128)(2,1)S(1)}, bf16[336,384]{1,0:T(8,128)(2,1)S(1)}, u32[]{:S(2)}, u32[]{:S(2)}) collective-permute-start(bf16[336,384]{1,0:T(8,128)(2,1)S(1)} %broadcast_select_fusion.11), channel_id=1, source_target_pairs={{0,8},{1,9},{2,10},{3,11},{4,12},{5,13},{6,14},{7,15},{24,16},{25,... | collective-permute-start | bytes 774152 | tf_op jit(solution)/shard_map/ppermute | solution.py:1350
  101.0 17.5 %collective-permute-start.14 = (bf16[336,384]{1,0:T(8,128)(2,1)S(1)}, bf16[336,384]{1,0:T(8,128)(2,1)S(1)}, u32[]{:S(2)}, u32[]{:S(2)}) collective-permute-start(bf16[336,384]{1,0:T(8,128)(2,1)S(1)} %broadcast_select_fusion.7), channel_id=1, source_target_pairs={{0,4},{1,5},{24,28},{25,29},{8,12},{9,13},{16,20},{17,21},{2,6},{3... | collective-permute-start | bytes 774152 | tf_op jit(solution)/shard_map/ppermute | solution.py:1350
  119.4 22.3 %collective-permute-start.20 = (bf16[992,384]{1,0:T(8,128)(2,1)S(1)}, bf16[992,384]{1,0:T(8,128)(2,1)S(1)}, u32[]{:S(2)}, u32[]{:S(2)}) collective-permute-start(bf16[992,384]{1,0:T(8,128)(2,1)S(1)} %pad_maximum_fusion.6), channel_id=1, source_target_pairs={{0,1},{1,0},{2,3},{3,2},{4,5},{5,4},{6,7},{7,6},{8,9},{9,8},{10,11... | collective-permute-start | bytes 2285576 | tf_op jit(solution)/shard_map/ppermute | solution.py:1357
  119.5 21.1 %collective-permute-start.23 = (bf16[96,2048]{1,0:T(8,128)(2,1)S(1)}, bf16[96,2048]{1,0:T(8,128)(2,1)S(1)}, u32[]{:S(2)}, u32[]{:S(2)}) collective-permute-start(bf16[96,2048]{1,0:T(8,128)(2,1)S(1)} %get-tuple-element.158), channel_id=1, source_target_pairs={{0,24},{1,25},{2,26},{3,27},{4,28},{5,29},{6,30},{7,31},{8,16},{9,... | collective-permute-start | bytes 1179656 | tf_op jit(solution)/shard_map/ppermute | solution.py:1336
  161.1 371.6 %all-gather.12.cloned.1.call-start = ((), (), s32[]{:S(2)}) async-start(), calls=%async_computation.2 | async-start | bytes 12533760 | tf_op jit(solution)/shard_map/all_gather | solution.py:1461
  250.4 282.3 %all-gather.14.cloned.1.call-start = ((), (), s32[]{:S(2)}) async-start(), calls=%async_computation.3 | async-start | bytes 11837440 | tf_op jit(solution)/shard_map/all_gather | solution.py:1519
  273.4 17.7 %collective-permute-start.4 = (f32[8,1,80]{2,0,1:T(8,128)S(1)}, f32[8,1,80]{2,0,1:T(8,128)S(1)}, u32[]{:S(2)}, u32[]{:S(2)}) collective-permute-start(f32[8,1,80]{2,0,1:T(8,128)S(1)} %maximum_select_fusion.23), channel_id=1, source_target_pairs={{0,1},{1,0},{2,3},{3,2},{4,5},{5,4},{6,7},{7,6},{8,9},{9,8},{10,11... | collective-permute-start | bytes 7688 | tf_op jit(solution)/shard_map/ppermute | solution.py:444
  323.3 16.9 %collective-permute-start.39 = (bf16[2,2,80,512]{3,2,1,0:T(8,128)(2,1)}, bf16[2,2,80,512]{3,2,1,0:T(8,128)(2,1)S(1)}, u32[]{:S(2)}, u32[]{:S(2)}) collective-permute-start(bf16[2,2,80,512]{3,2,1,0:T(8,128)(2,1)} %fusion.38), channel_id=1, source_target_pairs={{0,8},{1,9},{2,10},{3,11},{4,12},{5,13},{6,14},{7,15},{8,0},{9,1},... | collective-permute-start | bytes 983048 | tf_op jit(solution)/shard_map/ppermute | solution.py:463
  423.6 28.6 %collective-permute-start.44 = (f32[3,2,2,2,2,144,128]{6,5,0,2,1,4,3:T(8,128)}, f32[3,2,2,2,2,144,128]{6,5,0,2,1,4,3:T(8,128)}, u32[]{:S(2)}, u32[]{:S(2)}) collective-permute-start(f32[3,2,2,2,2,144,128]{6,5,0,2,1,4,3:T(8,128)} %select_bitcast_fusion.1), channel_id=1, source_target_pairs={{0,1},{1,0},{2,3},{3,2},{4,5},{5,4},{6,7},{7,6},{8,9},{9,8},{10,11... | collective-permute-start | bytes 10616840 | tf_op jit(solution)/shard_map/ppermute | solution.py:463
  434.9 159.4 %collective-permute-start.70 = (f32[2,1,2048]{2,0,1:T(2,128)}, f32[2,1,2048]{2,0,1:T(2,128)S(1)}, u32[]{:S(2)}, u32[]{:S(2)}) collective-permute-start(f32[2,1,2048]{2,0,1:T(2,128)} %maximum_select_fusion.21), channel_id=1, source_target_pairs={{0,2},{1,3},{2,0},{3,1},{4,6},{5,7},{6,4},{7,5},{8,10},{9,11},{10,... | collective-permute-start | bytes 49160 | tf_op jit(solution)/shard_map/ppermute | solution.py:444
  456.1 19.4 %collective-permute-start.46 = (bf16[3,2,2,2,72,128]{5,4,0,2,1,3:T(8,128)(2,1)S(1)}, bf16[3,2,2,2,72,128]{5,4,0,2,1,3:T(8,128)(2,1)S(1)}, u32[]{:S(2)}, u32[]{:S(2)}) collective-permute-start(bf16[3,2,2,2,72,128]{5,4,0,2,1,3:T(8,128)(2,1)S(1)} %fusion.36), channel_id=1, source_target_pairs={{0,4},{1,5},{2,6},{3,7},{4,0},{5,1},{6,2},{7,3},{8,12},{9,13},{10,... | collective-permute-start | bytes 1327112 | tf_op jit(solution)/shard_map/ppermute | solution.py:463
  458.0 17.5 %collective-permute-start.45 = (bf16[3,2,2,2,72,128]{5,4,0,2,1,3:T(8,128)(2,1)S(1)}, bf16[3,2,2,2,72,128]{5,4,0,2,1,3:T(8,128)(2,1)S(1)}, u32[]{:S(2)}, u32[]{:S(2)}) collective-permute-start(bf16[3,2,2,2,72,128]{5,4,0,2,1,3:T(8,128)(2,1)S(1)} %fusion.37), channel_id=1, source_target_pairs={{0,2},{1,3},{2,0},{3,1},{4,6},{5,7},{6,4},{7,5},{8,10},{9,11},{10,... | collective-permute-start | bytes 1327112 | tf_op jit(solution)/shard_map/ppermute | solution.py:463
  476.6 23.9 %collective-permute-start.49 = (bf16[3,2,2,72,128]{4,3,0,2,1:T(8,128)(2,1)S(1)}, bf16[3,2,2,72,128]{4,3,0,2,1:T(8,128)(2,1)S(1)}, u32[]{:S(2)}, u32[]{:S(2)}) collective-permute-start(bf16[3,2,2,72,128]{4,3,0,2,1:T(8,128)(2,1)S(1)} %fusion.43), channel_id=1, source_target_pairs={{0,2},{1,3},{2,0},{3,1},{4,6},{5,7},{6,4},{7,5},{8,10},{9,11},{10,... | collective-permute-start | bytes 663560 | tf_op jit(solution)/shard_map/ppermute | solution.py:463
  477.4 23.0 %collective-permute-start.48 = (bf16[3,2,2,72,128]{4,3,0,2,1:T(8,128)(2,1)S(1)}, bf16[3,2,2,72,128]{4,3,0,2,1:T(8,128)(2,1)S(1)}, u32[]{:S(2)}, u32[]{:S(2)}) collective-permute-start(bf16[3,2,2,72,128]{4,3,0,2,1:T(8,128)(2,1)S(1)} %fusion.42), channel_id=1, source_target_pairs={{0,4},{1,5},{2,6},{3,7},{4,0},{5,1},{6,2},{7,3},{8,12},{9,13},{10,... | collective-permute-start | bytes 663560 | tf_op jit(solution)/shard_map/ppermute | solution.py:463
  524.4 22.8 %collective-permute-start.55 = (bf16[3,2,2,2,88,128]{5,4,0,2,1,3:T(8,128)(2,1)}, bf16[3,2,2,2,88,128]{5,4,0,2,1,3:T(8,128)(2,1)}, u32[]{:S(2)}, u32[]{:S(2)}) collective-permute-start(bf16[3,2,2,2,88,128]{5,4,0,2,1,3:T(8,128)(2,1)} %fusion.28), channel_id=1, source_target_pairs={{0,4},{1,5},{2,6},{3,7},{4,0},{5,1},{6,2},{7,3},{8,12},{9,13},{10,... | collective-permute-start | bytes 1622024 | tf_op jit(solution)/shard_map/ppermute | solution.py:463
  554.7 25.8 %collective-permute-start.59 = (bf16[96,2048]{1,0:T(8,128)(2,1)}, bf16[96,2048]{1,0:T(8,128)(2,1)S(1)}, u32[]{:S(2)}, u32[]{:S(2)}) collective-permute-start(bf16[96,2048]{1,0:T(8,128)(2,1)} %get-tuple-element.94), channel_id=1, source_target_pairs={{16,8},{17,9},{18,10},{19,11},{20,12},{21,13},{22,14},{23,15},{24,... | collective-permute-start | bytes 1179656 | tf_op jit(solution)/shard_map/ppermute | solution.py:1649
  557.2 26.2 %collective-permute-start.53 = (bf16[3,2,88,128]{3,2,0,1:T(8,128)(2,1)S(1)}, bf16[3,2,88,128]{3,2,0,1:T(8,128)(2,1)S(1)}, u32[]{:S(2)}, u32[]{:S(2)}) collective-permute-start(bf16[3,2,88,128]{3,2,0,1:T(8,128)(2,1)S(1)} %fusion.45), channel_id=1, source_target_pairs={{0,24},{1,25},{2,26},{3,27},{4,28},{5,29},{6,30},{7,31},{8,16},{9,... | collective-permute-start | bytes 405512 | tf_op jit(solution)/shard_map/ppermute | solution.py:463
  560.0 25.2 %collective-permute-start.57 = (bf16[3,2,88,128]{3,2,0,1:T(8,128)(2,1)S(1)}, bf16[3,2,88,128]{3,2,0,1:T(8,128)(2,1)S(1)}, u32[]{:S(2)}, u32[]{:S(2)}) collective-permute-start(bf16[3,2,88,128]{3,2,0,1:T(8,128)(2,1)S(1)} %fusion.46), channel_id=1, source_target_pairs={{0,24},{1,25},{2,26},{3,27},{4,28},{5,29},{6,30},{7,31},{8,16},{9,... | collective-permute-start | bytes 405512 | tf_op jit(solution)/shard_map/ppermute | solution.py:463
  (130 other events, 899.4 us)
Sparse Core Ops, SparseCore 0:
  48.7 110.2 all-gather.7
  161.2 66.5 all-gather.9
  250.5 69.8 all-gather.11
  373.2 64.6 all-gather.13

commit v6 on v5

--- a/solution.py
+++ b/solution.py
@@ -644,6 +644,132 @@
 
 def gelu_tanh(values):
     return jnp.tanh(GELU_SCALE * (values + GELU_CUBE * values * values * values))
+
+
+def gelu_value(values):
+    return 0.5 * values * (1.0 + gelu_tanh(values))
+
+
+def gelu_slope(values):
+    bent = gelu_tanh(values)
+    return 0.5 * (1.0 + bent) + 0.5 * values * (1.0 - bent * bent) * GELU_SCALE * (
+        1.0 + 3.0 * GELU_CUBE * values * values
+    )
+
+
+def head_copies(plan, side_ref, gathered_ref, one_ref, two_ref, lines_ref, sems):
+    quarter = gathered_ref.shape[0] // 2
+    shift = side_ref[0] * quarter
+    targets = (one_ref, two_ref, lines_ref)
+    copies = []
+    for number, (at, owner, first, rows, target, row) in enumerate(plan):
+        spot = at + shift if at < quarter else at - shift
+        copies.append(
+            pltpu.make_async_copy(
+                gathered_ref.at[spot, owner, pl.ds(first, rows)],
+                targets[target].at[pl.ds(row, rows)],
+                sems.at[number],
+            )
+        )
+    for copy in copies:
+        copy.start()
+    return [[copy for copy, item in zip(copies, plan) if item[4] == target] for target in range(3)]
+
+
+def wait_all(copies):
+    for copy in copies:
+        copy.wait()
+
+
+def spread_third(lines_ref, wide_ref, third_ref):
+    groups = ROW // BOT
+    for lane in range(BOT // 128):
+        for group in range(groups):
+            at = group * BOT + lane * 128
+            wide_ref[lane, pl.ds(group, lines_ref.shape[0], stride=groups), :] = lines_ref[
+                :, at : at + 128
+            ].astype(single)
+        third_ref[:, pl.ds(lane * 128, 128)] = wide_ref[lane].astype(narrow)
+
+
+def head_up_kernel(
+    plan, side_ref, normed_ref, gathered_ref, unit_ref, acts_ref, bottle_ref, pre_one_ref, pre_two_ref,
+    one_ref, two_ref, lines_ref, wide_ref, third_ref, sems,
+):
+    copies = head_copies(plan, side_ref, gathered_ref, one_ref, two_ref, lines_ref, sems)
+    acts_ref[...] = jnp.zeros_like(acts_ref)
+    normed = normed_ref[...]
+    acts_ref[:, pl.ds(0, D)] = normed
+    piece = HID // 4
+    wait_all(copies[0])
+    for number in range(4):
+        spot = pl.ds(number * piece, piece)
+        pre = product_plain(normed, one_ref[:, spot])
+        pre_one_ref[:, spot] = pre
+        acts_ref[:, pl.ds(D + number * piece, piece)] = gelu_value(pre).astype(narrow)
+    wait_all(copies[2])
+    spread_third(lines_ref, wide_ref, third_ref)
+    wait_all(copies[1])
+    hidden = acts_ref[:, pl.ds(D, HID)]
+    for number in range(4):
+        spot = pl.ds(number * piece, piece)
+        pre = product_plain(hidden, two_ref[:, spot])
+        pre_two_ref[:, spot] = pre
+        acts_ref[:, pl.ds(D + HID + number * piece, piece)] = gelu_value(pre).astype(narrow)
+    bottle = product_plain(acts_ref[:, pl.ds(D + HID, HID)], third_ref[...])
+    bottle_ref[...] = bottle
+    unit_ref[...] = (
+        bottle * lax.rsqrt(jnp.sum(bottle * bottle, axis=-1, keepdims=True) + 1e-06)
+    ).astype(narrow)
+
+
+def head_down_kernel(
+    plan, side_ref, grad_ref, bottle_ref, pre_one_ref, pre_two_ref, gathered_ref, grads_ref, normed_grad_ref,
+    one_ref, two_ref, lines_ref, wide_ref, third_ref, sems,
+):
+    copies = head_copies(plan, side_ref, gathered_ref, one_ref, two_ref, lines_ref, sems)
+    grad, bottle = grad_ref[...], bottle_ref[...]
+    scale = lax.rsqrt(jnp.sum(bottle * bottle, axis=-1, keepdims=True) + 1e-06)
+    along = jnp.sum(grad * bottle, axis=-1, keepdims=True)
+    grad_bottle = (scale * (grad - bottle * (along * scale * scale))).astype(narrow)
+    grads_ref[:, pl.ds(2 * HID, BOT)] = grad_bottle
+    wait_all(copies[2])
+    spread_third(lines_ref, wide_ref, third_ref)
+    piece = HID // 4
+    for number in range(4):
+        spot = pl.ds(number * piece, piece)
+        back = product_right(grad_bottle, third_ref[spot, :])
+        grads_ref[:, pl.ds(HID + number * piece, piece)] = (back * gelu_slope(pre_two_ref[:, spot])).astype(narrow)
+    wait_all(copies[1])
+    grad_two = grads_ref[:, pl.ds(HID, HID)]
+    for number in range(4):
+        spot = pl.ds(number * piece, piece)
+        back = product_right(grad_two, two_ref[spot, :])
+        grads_ref[:, spot] = (back * gelu_slope(pre_one_ref[:, spot])).astype(narrow)
+    wait_all(copies[0])
+    normed_grad_ref[...] = product_right(grads_ref[:, pl.ds(0, HID)], one_ref[...])
+
+
+def head_pass(kernel, plan, side, inputs, gathered, shapes, waits=()):
+    read = len(inputs) + 2
+    return pl.pallas_call(
+        lambda *refs: kernel(plan, *refs[:read], *refs[read + len(waits) :]),
+        out_shape=shapes,
+        in_specs=[pl.BlockSpec(memory_space=pltpu.SMEM)]
+        + [pl.BlockSpec(memory_space=pltpu.VMEM)] * len(inputs)
+        + [pl.BlockSpec(memory_space=pl.ANY)] * (1 + len(waits)),
+        out_specs=[pl.BlockSpec(memory_space=pltpu.VMEM)] * len(shapes),
+        scratch_shapes=[
+            pltpu.VMEM((D, HID), narrow),
+            pltpu.VMEM((HID, HID), narrow),
+            pltpu.VMEM((BOT, ROW), narrow),
+            pltpu.VMEM((BOT // 128, HID, 128), single),
+            pltpu.VMEM((HID, BOT), narrow),
+            pltpu.SemaphoreType.DMA((len(plan),)),
+        ],
+        compiler_params=pltpu.CompilerParams(vmem_limit_bytes=56 << 20),
+        cost_estimate=pl.CostEstimate(flops=10**9, bytes_accessed=2 * 10**7, transcendentals=10**6),
+    )(side, *inputs, gathered, *waits)
 
 
 def fetch_rows(side_ref, part, gathered_ref, flat_ref, sems):
@@ -1063,6 +1189,8 @@
     def _():
         mixed_ref[:, pl.ds(0, BOT)] = student_mix_ref[...].T
         mixed_ref[:, pl.ds(BOT, BOT)] = teacher_mix_ref[...].T
+        lower = jnp.zeros((128 - totals_ref.shape[0], totals_ref.shape[1]), single)
+        mixed_ref[:, pl.ds(2 * BOT, 128)] = jnp.concatenate([totals_ref[...], lower]).T
         sums_ref[...] = totals_ref[...]
 
 
@@ -1082,12 +1210,12 @@
         logits_kernel,
         grid=(4,),
         out_shape=[
-            jax.ShapeDtypeStruct((rows, 2 * BOT), single),
+            jax.ShapeDtypeStruct((rows, 2 * BOT + 128), single),
             jax.ShapeDtypeStruct((8, rows), single),
             jax.ShapeDtypeStruct((protos_here, 1), single),
         ],
         in_specs=[whole, whole, table, table, column, lines],
-        out_specs=[pl.BlockSpec((rows, 2 * BOT), lambda i: (0, 0)), lines, column],
+        out_specs=[pl.BlockSpec((rows, 2 * BOT + 128), lambda i: (0, 0)), lines, column],
         scratch_shapes=[
             pltpu.VMEM((BOT, rows), single),
             pltpu.VMEM((BOT, rows), single),
@@ -1305,13 +1433,18 @@
     head_span = GROUP * ROW
     stems = jnp.stack([as_lanes(stem_teacher), as_lanes(stem)])
     stems_next = lax.ppermute(stems[:, : head_span // 128], "dev", step_pairs(count, -1))
-    start_here = jnp.array(starts, jnp.int32)[me]
-    head_at = start_here + front * 128
-    embed_at = front * 128 + jnp.where(me == 0, 0, late_start)
-    block_at = tail - drift * me
-    place = jnp.stack(
-        [head_at // 128, head_at % 128, embed_at // 128, embed_at % 128, block_at // 128, block_at % 128]
-    ).astype(jnp.int32)
+    def per_device(rows):
+        return lax.dynamic_slice(jnp.array(rows, jnp.int32), (me, 0), (1, len(rows[0]))).reshape(-1)
+
+    def spots(*values):
+        return [part for value in values for part in (value // 128, value % 128)]
+
+    place = per_device(
+        [
+            spots(starts[i] + front * 128, front * 128 + (0 if i == 0 else late_start), tail - drift * i)
+            for i in range(count)
+        ]
+    )
     head_blocks, layer_blocks, embed_blocks, vector_blocks = own_blocks(
         place,
         stems,
@@ -1370,38 +1503,13 @@
     gathered_head = lax.all_gather(after(both_head, gathered, even, odd), "dev", axis=0, axis_index_groups=groups)
     vectors_all = even[2 * embed_rows :].reshape(2, LAYERS, 8, D)
 
-    def head_slots(first, last):
-        pieces = []
-        i = first
-        while i < last:
-            stop = min(last, (i // quarter + 1) * quarter)
-            owner = 1 if i >= half else 0
-            at = (i ^ across if owner else i) ^ swap
-            pieces.append(
-                lax.dynamic_slice(
-                    gathered_head, (at, owner, 0, 0), (stop - i, 1, slot, ROW)
-                ).reshape(stop - i, slot, ROW)
-            )
-            i = stop
-        return pieces
-
-    def pad_columns(values, first, last, origin):
-        pieces = []
-        for i in range(first, last):
-            low, high = bounds[i] - origin, bounds[i + 1] - origin
-            if low < 0:
-                pieces.append(jnp.zeros(values.shape[:-1] + (-low,), values.dtype))
-            pieces.append(values[..., max(low, 0) : high])
-            pieces.append(jnp.zeros(values.shape[:-1] + (slot - sizes[i],), values.dtype))
-        return jnp.concatenate([p for p in pieces if p.shape[-1]], axis=-1)
-
-    def cut_columns(values, first, last, origin):
-        pieces = []
-        for i in range(first, last):
-            low = bounds[i] - origin
-            at = (i - first) * slot
-            pieces.append(values[..., at + max(-low, 0) : at + sizes[i]])
-        return jnp.concatenate(pieces, axis=-1)
+    plan = []
+    for i in range(1, count):
+        target = 0 if i < first_w2 else 1 if i < first_w3 else 2
+        row = bounds[i] - (0, D, D + HID)[target]
+        skip = max(-row, 0)
+        owner = 1 if i >= half else 0
+        plan.append((i ^ across if owner else i, owner, skip, sizes[i] - skip, target, row + skip))
 
     def embed_parts(model):
         rows = embed_all[model]
@@ -1445,25 +1553,23 @@
         jnp.concatenate([teacher_normed, normed_got]),
     )
     normed = jnp.pad(normed, ((0, more_rows), (0, 0)))
-    w_one = jnp.concatenate(head_slots(1, first_w2)).reshape(-1, ROW)
-    w_two = jnp.concatenate(head_slots(first_w2, first_w3)).reshape(-1, ROW)
-    w_three = jnp.concatenate(
-        [head_slots(i, i + 1)[0][0, : sizes[i]] for i in range(first_w3, count)]
-    ).reshape(HID, BOT)
-    pre_one = contract("rd,dh->rh", pad_columns(normed, 1, first_w2, 0), w_one)
-    hidden_one = jax.nn.gelu(pre_one).astype(narrow)
-    pre_two = contract("rh,hk->rk", pad_columns(hidden_one, first_w2, first_w3, D), w_two)
-    hidden_two = jax.nn.gelu(pre_two).astype(narrow)
-    bottleneck = contract("rh,hb->rb", hidden_two, w_three)
-    unit_z = unit_rows(bottleneck).astype(narrow)
     third_end = (bounds[-2] - D - HID + slot) * (ROW // BOT)
-    more_inputs = ((0, 0), (0, max(third_end - HID, 0)))
-    inputs_all = lax.all_gather(
-        jnp.pad(jnp.concatenate([normed, hidden_one, hidden_two], axis=1), more_inputs),
-        "dev",
-        axis=0,
-        axis_index_groups=groups,
-    ).reshape(half * pair_rows, -1)
+    acts_width = D + HID + max(third_end, HID)
+    unit_z, acts, bottleneck, pre_one, pre_two = head_pass(
+        head_up_kernel,
+        plan,
+        side,
+        (normed,),
+        gathered_head,
+        [
+            jax.ShapeDtypeStruct((pair_rows, BOT), narrow),
+            jax.ShapeDtypeStruct((pair_rows, acts_width), narrow),
+            jax.ShapeDtypeStruct((pair_rows, BOT), single),
+            jax.ShapeDtypeStruct((pair_rows, HID), single),
+            jax.ShapeDtypeStruct((pair_rows, HID), single),
+        ],
+    )
+    inputs_all = lax.all_gather(acts, "dev", axis=0, axis_index_groups=groups).reshape(half * pair_rows, -1)
 
     all_rows = half * pair_rows
     kept_row = jnp.broadcast_to(kept[:, None], (images_here, 17)).reshape(1, rows_here)
@@ -1489,39 +1595,43 @@
     mixed_rows, sums, centre_sum = logits_pass(
         teacher_z_all, student_z_all, proto_teacher, protos, centre_column, lines(class_kept)
     )
-    mixed_own = cube_scatter(mixed_rows.reshape((2,) * 4 + (pair_rows, 2 * BOT)), "cgyx", "cgyx")
+    mixed_own = cube_scatter(mixed_rows.reshape((2,) * 4 + (pair_rows, 2 * BOT + 128)), "cgyx", "cgyx")
     mixed_own = mixed_own + lax.ppermute(
         mixed_own.astype(narrow), "dev", [(i, i ^ across) for i in range(half)]
     ).astype(single)
-    sums = cube_sum(sums[:3])
+    stages = [sums[:3]]
+    for name in "cxyab":
+        stages.append(stages[-1] + lax.ppermute(stages[-1], "dev", pairs(count, MASKS[name])))
+    sums = stages[-1]
     cross = jnp.log(sums[1]) - sums[2] / (sums[0] * tau_student)
     loss_total = jnp.sum(row_weight * cross)
     scale = row_weight / tau_student
     student_scale, teacher_scale = scale / sums[1], scale / sums[0]
     flags = bit_flags(me)
     pair_at = flags["c"] * 8 + flags["g"] * 4 + flags["y"] * 2 + flags["x"]
-    own_scales = lax.dynamic_slice(
-        jnp.stack([student_scale, teacher_scale]), (0, pair_at * pair_rows), (2, pair_rows)
-    )
-    grad_unit_z = (
-        mixed_own[:, :BOT] * own_scales[0][:, None] - mixed_own[:, BOT:] * own_scales[1][:, None]
+    own_scale = lax.dynamic_slice(scale, (pair_at * pair_rows,), (pair_rows,))[:, None]
+    grad_unit_z = own_scale * (
+        mixed_own[:, :BOT] / mixed_own[:, 2 * BOT + 1 : 2 * BOT + 2]
+        - mixed_own[:, BOT : 2 * BOT] / mixed_own[:, 2 * BOT : 2 * BOT + 1]
     )
     own_new_centre = (
         centre_keep * own_centre + (1.0 - centre_keep) * centre_sum.reshape(protos_here) / count_total
     )
     new_centre = cube_gather(own_new_centre.reshape(1, protos_here), "cxyab").reshape(-1)
 
-    grad_bottle = jax.vjp(unit_rows, bottleneck)[1](grad_unit_z)[0].astype(narrow)
-    grad_pre_two = gelu_back(pre_two, contract("rb,hb->rh", grad_bottle, w_three)).astype(narrow)
-    grad_hidden = cut_columns(contract("rk,hk->rh", grad_pre_two, w_two), first_w2, first_w3, D)
-    grad_pre_one = gelu_back(pre_one, grad_hidden).astype(narrow)
-    grad_normed = cut_columns(contract("rh,dh->rd", grad_pre_one, w_one), 1, first_w2, 0)
-    grads_all = lax.all_gather(
-        jnp.concatenate([grad_pre_one, grad_pre_two, grad_bottle], axis=1),
-        "dev",
-        axis=0,
-        axis_index_groups=groups,
-    ).reshape(half * pair_rows, 2 * HID + BOT)
+    grads, grad_normed = head_pass(
+        head_down_kernel,
+        plan,
+        side,
+        (grad_unit_z, bottleneck, pre_one, pre_two),
+        gathered_head,
+        [
+            jax.ShapeDtypeStruct((pair_rows, 2 * HID + BOT), narrow),
+            jax.ShapeDtypeStruct((pair_rows, D), single),
+        ],
+        (stages[2],),
+    )
+    grads_all = lax.all_gather(grads, "dev", axis=0, axis_index_groups=groups).reshape(half * pair_rows, -1)
     normed_back = lax.ppermute(
         grad_normed[:rows_here], "dev", [(i, i ^ across) for i in range(half, count)]
     )
@@ -1555,7 +1665,7 @@
     def blocks_of(weight_grad, rows):
         return split_bits(weight_grad.reshape(D // 128, count, rows, 128), 1)
 
-    rounds = (("c",), ("x", "y"), ("y", "x"), ("b", "b"), ("a", "a"))
+    rounds = (("c",), ("x", "b"), ("y", "a"), ("b", "x"), ("a", "y"))
 
     def advance(state):
         pieces, stage = state
@@ -1574,7 +1684,7 @@
         return tuple(sent for pieces, stage in states for sent, kept, left in pieces)
 
     started = []
-    waits = ()
+    waits, later_waits = (stages[3],), (stages[4],)
     for layer_index in reversed(range(LAYERS)):
         saved, vectors = saved_layers[layer_index], vectors_all[1, layer_index]
         part = LAYERS + layer_index
@@ -1584,8 +1694,9 @@
         )
         started = [advance(state) for state in started]
         grad_stream, weight_grad, early_vectors = attention_back(
-            side, grad_stream, saved, vectors, gathered, part, weight_grad, sends(started)
+            side, grad_stream, saved, vectors, gathered, part, weight_grad, later_waits + sends(started)
         )
+        waits, later_waits = (), ()
         vector_grads[layer_index] = (late_vectors + early_vectors)[:6]
         first = (cuts([blocks_of(weight_grad, block_rows)], ["bayxc"], rounds[0]), 0)
         if layer_index == LAYERS - 1:
@@ -1619,30 +1730,22 @@
     last = (cuts(joined, ["bayx"] * 2, rounds[1]), 1)
     later_blocks = [jnp.concatenate(finish(state), axis=1) for state in started]
 
-    def table(values):
-        return jnp.array(values, jnp.int32)
-
-    columns = [max(bound, 0) // 128 * 128 for bound in bounds[:-1]]
-    offsets = [bound - column for bound, column in zip(bounds, columns)]
-    offsets[0] = 0
-    valid = [0] + sizes[1:]
-    thirds = [D + HID + max(bound - D - HID, 0) * (ROW // BOT) for bound in bounds[:-1]]
-    partner = me ^ across
-    is_third = (me >= first_w3).astype(jnp.int32)
-    place = jnp.stack(
+    def block_place(i):
+        column = max(bounds[i], 0) // 128 * 128
+        grad_column = 0 if i < first_w2 else HID
+        return [column, bounds[i] - column if i else 0, sizes[i] if i else 0, grad_column]
+
+    def third_place(i):
+        return [0, 0, sizes[i], 0]
+
+    place = per_device(
         [
-            jnp.where(is_third == 1, 0, table(columns)[me]),
-            jnp.where(is_third == 1, 0, table(offsets)[me]),
-            table(valid)[me],
-            jnp.int32(HID),
-            table(columns)[partner],
-            table(offsets)[partner],
-            table(valid)[partner],
-            jnp.where(partner < first_w2, 0, HID),
-            is_third,
-            table(thirds)[me],
+            (third_place(i) if i >= first_w3 else block_place(i))
+            + block_place(i ^ across)
+            + [int(i >= first_w3), D + HID + max(bounds[i] - D - HID, 0) * (ROW // BOT)]
+            for i in range(count)
         ]
-    ).astype(jnp.int32)
+    )
     own_block_grad, partner_block_grad = head_grads(
         place, inputs_all, grads_all, slot, -min(bounds[1], 0), sends([last])
     )
@@ -1666,28 +1769,31 @@
     middle = (square_local - high.astype(single)).astype(narrow)
     low = (square_local - high.astype(single) - middle.astype(single)).astype(narrow)
     tile = jnp.pad(jnp.stack([high, middle, low]).reshape(3, 1, 1), ((0, 0), (0, 15), (0, 127)))
-    shared = cube_gather(jnp.concatenate([small_block.astype(narrow), tile], axis=1), "xyabc")
-    shared = jnp.moveaxis(shared.reshape((2,) + (half,) + shared.shape[1:]), 0, 1)
-    shared = shared.reshape((count,) + shared.shape[2:]).astype(single)
+    behind = lax.ppermute(layer_block[:, :, :6], "dev", step_pairs(count, -1))
+    last_rows = lax.dynamic_slice(
+        head_block_grad, (jnp.array(sizes, jnp.int32)[me] - GROUP, 0), (GROUP, ROW)
+    )
+    previous = lax.ppermute(last_rows, "dev", step_pairs(count, 1))
+    place = per_device([spots(head_span - starts[i], drift * i) for i in range(count)])
+    stem_lines, layer_lines = own_shards(
+        place, head_block_grad, previous, layer_block, behind, lane_rows(stem_piece), lane_rows(layer_piece)
+    )
+    shared = cube_gather(jnp.concatenate([small_block.astype(narrow), tile], axis=1), "xya")
+    shared = cube_gather(after(shared, stem_lines), "bc")
+    shared = jnp.moveaxis(shared.reshape((2, 2) + shared.shape[1:]), 0, 2)
+    shared = shared.reshape((count,) + shared.shape[3:]).astype(single)
     square_total = jnp.sum(shared[:, :, small_rows, 0])
     small_all = jnp.transpose(shared[:, :, :small_rows], (0, 2, 1, 3)).reshape(small_rows * count, D)
     embed_grad = small_all[:EMBED_ROWS].reshape(-1)
-    vector_grad = small_all[EMBED_ROWS : EMBED_ROWS + 6 * LAYERS].reshape(LAYERS, 6, D)
-
-    behind = lax.ppermute(layer_block[:, :, :6], "dev", step_pairs(count, -1))
-    vector_columns = jnp.swapaxes(vector_grad.reshape(LAYERS, 6, D // 128, 128), 1, 2)
-    behind = jnp.where(me == count - 1, vector_columns, behind)
-    last_rows = lax.dynamic_slice(
-        head_block_grad, (jnp.array(sizes, jnp.int32)[me] - GROUP, 0), (GROUP, ROW)
-    )
-    previous = lax.ppermute(last_rows, "dev", step_pairs(count, 1))
-    stem_at = head_span - start_here
-    layer_at = drift * me
-    place = jnp.stack([stem_at // 128, stem_at % 128, layer_at // 128, layer_at % 128]).astype(jnp.int32)
-    stem_lines, layer_lines = own_shards(
-        place, head_block_grad, previous, layer_block, behind, lane_rows(stem_piece), lane_rows(layer_piece)
-    )
+    vector_grad = small_all[EMBED_ROWS : EMBED_ROWS + 6 * LAYERS].reshape(LAYERS, 6 * D)
     layer_grad = layer_lines.reshape(LAYERS, -1)[:, :layer_piece]
+    layer_grad = jnp.concatenate(
+        [
+            layer_grad[:, : layer_piece - tail],
+            jnp.where(me == count - 1, vector_grad, layer_grad[:, layer_piece - tail :]),
+        ],
+        axis=1,
+    )
     stem_grad = stem_lines.reshape(-1)[:stem_piece]
     rest = EMBED_FLAT - stem_piece
     second_part = jnp.concatenate([embed_grad[stem_piece:], stem_grad[rest:]])

time: 677 us -> 651 us (0.962)
  local copies, waits for them, and re-layouts: 93.6 us -> 67.9 us
  Pallas kernels: 161 us -> 183 us
  matrix products: 18.2 us -> 1.1 us
  waiting for transfers between devices: 210 us -> 217 us
    pallas_call x0 -> x2, Pallas kernels: none -> 19.5 us  [head_pass(): pl.pallas_call(lambda *refs: kernel(plan, *refs[:read], *refs[read + len(...]
    ppermute x23, waiting for transfers between devices: 28.1 us -> 47.6 us  [move(): lax.ppermute(sent, 'dev', pairs(1 << len(BITS), MASKS[name])).astype(single)]
    dot_general x8 -> x2, matrix products: 18.2 us -> 1.1 us  [contract(): return jnp.einsum(form, left_arg, right_arg, preferred_element_type=single)]
    reshape x5 -> x4, local copies, waits for them, and re-layouts: 11.1 us -> 2.67 us  [the longest x3 2.66 us: per_device(): lax.dynamic_slice(jnp.array(rows, jnp.int32), (me, 0), (1, len(rows[0])))]
    concatenate x5 -> x0, other arithmetic: 7.91 us -> none  [the longest x1 4.16 us: close_local(): w_two = jnp.concatenate(head_slots(first_w2, first_w3)).reshape(-1, ROW)]
    unnamed x155 -> x125, local copies, waits for them, and re-layouts: 14.9 us -> 11.8 us
  transfers between devices with their start and end apart: 80 -> 80, of which waited for: 40 -> 42; matrix products, arithmetic and copies ran while one was open for 20% -> 16% of each run, Pallas kernels for 22% -> 26%
where the time goes in v6:
time: 651 us; the launch traced here: 643 us
  waiting for transfers between devices  217 us (33%)
  Pallas kernels  183 us (28%)
  starting transfers between devices  87.2 us (13%)
  local copies, waits for them, and re-layouts  67.9 us (10%)
  other arithmetic  62.7 us (10%)
  between operations  23.1 us (4%)
    pallas_call x4, Pallas kernels, layer_back(): pl.pallas_call(lambda *refs: kernel(part, *refs), out_shape=[jax.ShapeDty...  64.4 us
    pallas_call x4, Pallas kernels, layer_forward(): pl.pallas_call(lambda *refs: forward_kernel(part, keep, *refs), out_shape...  47.8 us
    ppermute x23, waiting for transfers between devices, move(): lax.ppermute(sent, 'dev', pairs(1 << len(BITS), MASKS[name])).astype(single)  47.6 us
    ppermute x24, waiting for transfers between devices, cube_gather(): got = lax.ppermute(held, 'dev', pairs(count, MASKS[name]))  39.5 us
    ppermute x12, waiting for transfers between devices, close_local(): got = lax.ppermute(spread, 'dev', moves)  39 us
    ppermute x24, starting transfers between devices, cube_gather(): got = lax.ppermute(held, 'dev', pairs(count, MASKS[name]))  24.4 us
    ppermute x23, starting transfers between devices, move(): lax.ppermute(sent, 'dev', pairs(1 << len(BITS), MASKS[name])).astype(single)  20.1 us
    ppermute x1, waiting for transfers between devices, close_local(): other_layers = lax.ppermute(layer_blocks, 'dev', pairs(count, across))  19.9 us
  transfers between devices with their start and end apart: 80, of which 42 were waited for; matrix products, arithmetic and copies ran while one was open for 16% of the time, Pallas kernels for 26%

profile of v6, /device:TPU:8, one launch (start us, length us, event | category | flops | bytes accessed | tf_op | source)
XLA Modules:
  0.0 642.8 jit_solution(11804800983609694862)
XLA Ops:
  27.0 19.9 %collective-permute-done.21 = bf16[4,144,384]{2,1,0:T(8,128)(2,1)S(1)} collective-permute-done((bf16[4,144,384]{2,1,0:T(8,128)(2,1)S(1)}, bf16[4,144,384]{2,1,0:T(8,128)(2,1)S(1)}, u32[]{:S(2)}, u32[]{:S(2)}) %collective-permute-start.21) | collective-permute-done | bytes 442400 | tf_op jit(solution)/shard_map/ppermute | solution.py:1460
  66.3 15.1 %collective-permute-done.12 = bf16[336,384]{1,0:T(8,128)(2,1)S(1)} collective-permute-done((bf16[336,384]{1,0:T(8,128)(2,1)S(1)}, bf16[336,384]{1,0:T(8,128)(2,1)S(1)}, u32[]{:S(2)}, u32[]{:S(2)}) %collective-permute-start.12) | collective-permute-done | bytes 258080 | tf_op jit(solution)/shard_map/ppermute | solution.py:1483
  83.4 8.5 %collective-permute-done.18 = bf16[320,384]{1,0:T(8,128)(2,1)S(1)} collective-permute-done((bf16[320,384]{1,0:T(8,128)(2,1)S(1)}, bf16[320,384]{1,0:T(8,128)(2,1)S(1)}, u32[]{:S(2)}, u32[]{:S(2)}) %collective-permute-start.18) | collective-permute-done | bytes 245792 | tf_op jit(solution)/shard_map/ppermute | solution.py:1483
  101.6 12.3 %collective-permute-done.10 = bf16[336,384]{1,0:T(8,128)(2,1)S(1)} collective-permute-done((bf16[336,384]{1,0:T(8,128)(2,1)S(1)}, bf16[336,384]{1,0:T(8,128)(2,1)S(1)}, u32[]{:S(2)}, u32[]{:S(2)}) %collective-permute-start.10) | collective-permute-done | bytes 258080 | tf_op jit(solution)/shard_map/ppermute | solution.py:1483
  119.2 17.9 %collective-permute-done.23 = bf16[96,2048]{1,0:T(8,128)(2,1)S(1)} collective-permute-done((bf16[96,2048]{1,0:T(8,128)(2,1)}, bf16[96,2048]{1,0:T(8,128)(2,1)S(1)}, u32[]{:S(2)}, u32[]{:S(2)}) %collective-permute-start.23) | collective-permute-done | bytes 393248 | tf_op jit(solution)/shard_map/ppermute | solution.py:1469
  139.6 16.5 %all-gather.8.cloned.1.call-done.refs_3_.refs_1_.refs_7_.refs_6_ = bf16[16,2,4,144,384]{4,3,2,1,0:T(8,128)(2,1)} async-done(((bf16[1,2,4,144,384]{4,3,2,1,0:T(8,128)(2,1)}), bf16[16,2,4,144,384]{4,3,2,1,0:T(8,128)(2,1)}) %all-gather.8.cloned.1.call-update) | async-done | bytes 14155792 | tf_op jit(solution)/shard_map/all_gather | solution.py:1466
  164.0 11.5 %shard_map.448.refs_1_ = f32[544,384]{1,0:T(8,128)} custom-call(s32[1]{0:T(128)} %bitcast.8.refs_0_, f32[544,384]{1,0:T(8,128)} %bitcast.321, bf16[8,384]{1,0:T(8,128)(2,1)} %get-tuple-element.187.refs_2_, bf16[16,2,4,144,384]{4,3,2,1,0:T(8,128)(2,1)} %all-gather.8.cloned.1.call-done.refs_3_.refs_1_.refs_7_.refs_6_), custom_call_target="tpu_custom_call" | custom-call | flops 2000000000 | bytes 20000000 | tf_op jit(solution)/shard_map/pallas_call | solution.py:910
  175.4 11.8 %shard_map.449 = f32[544,384]{1,0:T(8,128)} custom-call(s32[1]{0:T(128)} %bitcast.8.refs_0_, f32[544,384]{1,0:T(8,128)} %shard_map.448.refs_1_, bf16[8,384]{1,0:T(8,128)(2,1)} %get-tuple-element.186.refs_2_, bf16[16,2,4,144,384]{4,3,2,1,0:T(8,128)(2,1)} %all-gather.8.cloned.1.call-done.refs_3_.refs_1_.refs_7_.refs_6_), custom_call_target="tpu_custom_call" | custom-call | flops 2000000000 | bytes 20000000 | tf_op jit(solution)/shard_map/pallas_call | solution.py:910
  189.2 12.0 %shard_map.450 = (f32[544,384]{1,0:T(8,128)}, bf16[544,1152]{1,0:T(8,128)(2,1)}, bf16[544,384]{1,0:T(8,128)(2,1)}, f32[544,384]{1,0:T(8,128)}, f32[544,1536]{1,0:T(8,128)}, /*index=5*/f32[544,384]{1,0:T(8,128)}) custom-call(s32[1]{0:T(128)} %bitcast.8.refs_0_, f32[544,384]{1,0:T(8,128)} %bitcast.310, ...), custom_call_target="tpu_custom_call" | custom-call | flops 2000000000 | bytes 20000000 | tf_op jit(solution)/shard_map/pallas_call | solution.py:910
  201.2 12.6 %shard_map.451 = (f32[544,384]{1,0:T(8,128)}, bf16[544,1152]{1,0:T(8,128)(2,1)}, bf16[544,384]{1,0:T(8,128)(2,1)}, f32[544,384]{1,0:T(8,128)}, f32[544,1536]{1,0:T(8,128)}, /*index=5*/f32[544,384]{1,0:T(8,128)}) custom-call(s32[1]{0:T(128)} %bitcast.8.refs_0_, f32[544,384]{1,0:T(8,128)} %get-tuple-element.72.refs_1_.refs_2_, ...), custom_call_target="tpu_custom_call" | custom-call | flops 2000000000 | bytes 20000000 | tf_op jit(solution)/shard_map/pallas_call | solution.py:910
  225.0 8.7 %shard_map.453 = (bf16[80,256]{1,0:T(8,128)(2,1)}, bf16[80,4608]{1,0:T(8,128)(2,1)}, f32[80,256]{1,0:T(8,128)}, f32[80,2048]{1,0:T(8,128)}, f32[80,2048]{1,0:T(8,128)}) custom-call(s32[1]{0:T(128)} %bitcast.8.refs_0_, bf16[80,384]{1,0:T(8,128)(2,1)} %pad.45.refs_1_, bf16[16,2,96,2048]{3,2,1,0:T(8,128)(2,1)} %bitcast.306), custom_call_target="tpu_custom_call" | custom-call | flops 1000000000 | bytes 20000000 | tf_op jit(solution)/shard_map/pallas_call | solution.py:755
  277.2 14.0 %shard_map.454 = (f32[1280,640]{1,0:T(8,128)}, f32[8,1280]{1,0:T(8,128)}, f32[2048,1]{1,0:T(8,128)}) custom-call(bf16[1280,256]{1,0:T(8,128)(2,1)} %bitcast.331, bf16[1280,256]{1,0:T(8,128)(2,1)} %bitcast.329, f32[2048,256]{1,0:T(8,128)} %refs_3_.1, f32[2048,256]{1,0:T(8,128)} %refs_0_.1, f32[2048,1]{1,0:T(8,128)} %copy.186.centre_ref, f32[8,1280]{1,0:T(8,128)} %pad.46.class_ref), custom_call_target="tpu_custom_call" | custom-call | flops 5000000000 | bytes 10000000 | tf_op jit(solution)/shard_map/pallas_call | solution.py:1209
  299.4 11.2 %collective-permute-done.39 = bf16[2,2,80,640]{3,2,1,0:T(8,128)(2,1)S(1)} collective-permute-done((bf16[2,2,80,640]{3,2,1,0:T(8,128)(2,1)S(1)}, bf16[2,2,80,640]{3,2,1,0:T(8,128)(2,1)S(1)}, u32[]{:S(2)}, u32[]{:S(2)}) %collective-permute-start.39) | collective-permute-done | bytes 409632 | tf_op jit(solution)/shard_map/ppermute | solution.py:463
  331.5 10.8 %shard_map.455 = (bf16[80,4352]{1,0:T(8,128)(2,1)}, f32[80,384]{1,0:T(8,128)}) custom-call(s32[1]{0:T(128)} %bitcast.8.refs_0_, f32[80,256]{1,0:T(8,128)} %fusion.35.refs_1_, f32[80,256]{1,0:T(8,128)} %get-tuple-element.78.refs_2_, f32[80,2048]{1,0:T(8,128)} %get-tuple-element.79.refs_3_, f32[80,2048]{1,0:T(8,128)} %get-tuple-element.80.refs_4_, ...), custom_call_target="tpu_custom_call" | custom-call | flops 1000000000 | bytes 20000000 | tf_op jit(solution)/shard_map/pallas_call | solution.py:755
  358.8 14.7 %shard_map.456 = (f32[544,384]{1,0:T(8,128)}, f32[3,4608,128]{2,1,0:T(8,128)}, f32[8,384]{1,0:T(8,128)}) custom-call(s32[1]{0:T(128)} %bitcast.8.refs_0_, f32[544,384]{1,0:T(8,128)} %bitcast.317, f32[544,384]{1,0:T(8,128)} %get-tuple-element.72.refs_1_.refs_2_, f32[544,384]{1,0:T(8,128)} %get-tuple-element.82.refs_3_, ...), custom_call_target="tpu_custom_call" | custom-call | flops 5000000000 | bytes 40000000 | tf_op jit(solution)/shard_map/pallas_call | solution.py:1047
  373.6 17.6 %shard_map.457 = (f32[544,384]{1,0:T(8,128)}, f32[3,4608,128]{2,1,0:T(8,128)}, f32[8,384]{1,0:T(8,128)}) custom-call(s32[1]{0:T(128)} %bitcast.8.refs_0_, f32[544,384]{1,0:T(8,128)} %get-tuple-element.85.refs_1_, f32[544,384]{1,0:T(8,128)} %get-tuple-element.72.refs_1_.refs_2_, ...), custom_call_target="tpu_custom_call", output_to_operand_aliasing={{1}: (7, {})} | custom-call | flops 5000000000 | bytes 40000000 | tf_op jit(solution)/shard_map/pallas_call | solution.py:1047
  416.1 10.7 %shard_map.458 = (f32[2048,256]{1,0:T(8,128)}, f32[8,128]{1,0:T(8,128)}) custom-call(bf16[1280,256]{1,0:T(8,128)(2,1)} %bitcast.332, bf16[1280,256]{1,0:T(8,128)(2,1)} %bitcast.330, f32[2048,256]{1,0:T(8,128)} %refs_3_.1, f32[2048,256]{1,0:T(8,128)} %refs_0_.1, f32[2048,1]{1,0:T(8,128)} %copy.186.centre_ref, f32[8,1280]{1,0:T(8,128)} %select_maximum_fusion.scale_ref, ...), custom_call_target="tpu_custom_call" | custom-call | flops 4000000000 | bytes 10000000 | tf_op jit(solution)/shard_map/pallas_call | solution.py:1257
  435.6 14.7 %shard_map.459 = (f32[544,384]{1,0:T(8,128)}, f32[3,4608,128]{2,1,0:T(8,128)}, f32[8,384]{1,0:T(8,128)}) custom-call(s32[1]{0:T(128)} %bitcast.8.refs_0_, f32[544,384]{1,0:T(8,128)} %get-tuple-element.89.refs_1_, f32[544,384]{1,0:T(8,128)} %bitcast.311, f32[544,384]{1,0:T(8,128)} %get-tuple-element.90.refs_3_, f32[544,1536]{1,0:T(8,128)} %get-tuple-element.91.refs_4_, ...), custom_call_target="tpu_custom_call" | custom-call | flops 5000000000 | bytes 40000000 | tf_op jit(solution)/shard_map/pallas_call | solution.py:1047
  454.5 17.4 %shard_map.460 = (f32[544,384]{1,0:T(8,128)}, f32[3,4608,128]{2,1,0:T(8,128)}, f32[8,384]{1,0:T(8,128)}) custom-call(s32[1]{0:T(128)} %bitcast.8.refs_0_, f32[544,384]{1,0:T(8,128)} %get-tuple-element.95.refs_1_, f32[544,384]{1,0:T(8,128)} %bitcast.312, bf16[544,1152]{1,0:T(8,128)(2,1)} %get-tuple-element.96.refs_3_, ...), custom_call_target="tpu_custom_call", output_to_operand_aliasing={{1}: (7, {})} | custom-call | flops 5000000000 | bytes 40000000 | tf_op jit(solution)/shard_map/pallas_call | solution.py:1047
  479.4 5.8 collective-permute-done.48
  503.8 6.1 collective-permute-done.51
  510.9 10.1 %shard_map.462 = (f32[96,2048]{1,0:T(8,128)}, bf16[96,2048]{1,0:T(8,128)(2,1)}) custom-call(s32[10]{0:T(128)} %fusion.75.place_ref, bf16[1280,4608]{1,0:T(8,128)(2,1)} %all-gather.12.cloned.1.call-done.inputs_ref, bf16[1280,4352]{1,0:T(8,128)(2,1)} %all-gather.14.cloned.1.call-done.grads_ref, bf16[3,2,2,2,88,128]{5,4,3,2,1,0:T(8,128)(2,1)} %copy.216.refs_0_, ...), custom_call_target="tpu_custom_call" | custom-call | flops 4000000000 | bytes 20000000 | tf_op jit(solution)/shard_map/pallas_call | solution.py:1357
  540.5 16.6 %collective-permute-done.59 = bf16[96,2048]{1,0:T(8,128)(2,1)S(1)} collective-permute-done((bf16[96,2048]{1,0:T(8,128)(2,1)S(1)}, bf16[96,2048]{1,0:T(8,128)(2,1)S(1)}, u32[]{:S(2)}, u32[]{:S(2)}) %collective-permute-start.59) | collective-permute-done | bytes 393248 | tf_op jit(solution)/shard_map/ppermute | solution.py:1752
  588.6 11.5 %collective-permute-done.69 = bf16[1,8,3,48,128]{4,3,2,1,0:T(8,128)(2,1)S(1)} collective-permute-done((bf16[1,8,3,48,128]{4,3,2,1,0:T(8,128)(2,1)}, bf16[1,8,3,48,128]{4,3,2,1,0:T(8,128)(2,1)S(1)}, u32[]{:S(2)}, u32[]{:S(2)}) %collective-permute-start.69) | collective-permute-done | bytes 294944 | tf_op jit(solution)/shard_map/ppermute | solution.py:444
  (545 shorter events, 311.8 us)
Async XLA Ops:
  7.2 148.8 %all-gather.8.cloned.1.call-start = ((), (), s32[]{:S(2)}) async-start(), calls=%async_computation | async-start | bytes 15040512 | tf_op jit(solution)/shard_map/all_gather | solution.py:1466
  25.3 21.5 %collective-permute-start.21 = (bf16[4,144,384]{2,1,0:T(8,128)(2,1)S(1)}, bf16[4,144,384]{2,1,0:T(8,128)(2,1)S(1)}, u32[]{:S(2)}, u32[]{:S(2)}) collective-permute-start(bf16[4,144,384]{2,1,0:T(8,128)(2,1)S(1)} %get-tuple-element.71), channel_id=1, source_target_pairs={{0,24},{1,25},{2,26},{3,27},{4,28},{5,29},{6,30},{7,31},{8,16},{9,... | collective-permute-start | bytes 1327112 | tf_op jit(solution)/shard_map/ppermute | solution.py:1460
  47.9 177.0 %all-gather.10.cloned.1.call-start = ((), (), s32[]{:S(2)}) async-start(), calls=%async_computation.1 | async-start | bytes 13369344 | tf_op jit(solution)/shard_map/all_gather | solution.py:1503
  61.6 19.8 %collective-permute-start.12 = (bf16[336,384]{1,0:T(8,128)(2,1)S(1)}, bf16[336,384]{1,0:T(8,128)(2,1)S(1)}, u32[]{:S(2)}, u32[]{:S(2)}) collective-permute-start(bf16[336,384]{1,0:T(8,128)(2,1)S(1)} %get-tuple-element.174), channel_id=1, source_target_pairs={{0,8},{1,9},{24,16},{25,17}} | collective-permute-start | bytes 774152 | tf_op jit(solution)/shard_map/ppermute | solution.py:1483
  63.6 28.3 %collective-permute-start.18 = (bf16[320,384]{1,0:T(8,128)(2,1)S(1)}, bf16[320,384]{1,0:T(8,128)(2,1)S(1)}, u32[]{:S(2)}, u32[]{:S(2)}) collective-permute-start(bf16[320,384]{1,0:T(8,128)(2,1)S(1)} %broadcast_select_fusion.14), channel_id=1, source_target_pairs={{0,8},{1,9},{4,12},{5,13},{24,16},{25,17},{28,20},{29,21}} | collective-permute-start | bytes 737288 | tf_op jit(solution)/shard_map/ppermute | solution.py:1483
  65.6 28.3 %collective-permute-start.9 = (bf16[336,384]{1,0:T(8,128)(2,1)S(1)}, bf16[336,384]{1,0:T(8,128)(2,1)S(1)}, u32[]{:S(2)}, u32[]{:S(2)}) collective-permute-start(bf16[336,384]{1,0:T(8,128)(2,1)S(1)} %broadcast_select_fusion.10), channel_id=1, source_target_pairs={{0,24},{1,25},{2,26},{3,27},{4,28},{5,29},{6,30},{7,31}} | collective-permute-start | bytes 774152 | tf_op jit(solution)/shard_map/ppermute | solution.py:1483
  94.6 19.3 %collective-permute-start.10 = (bf16[336,384]{1,0:T(8,128)(2,1)S(1)}, bf16[336,384]{1,0:T(8,128)(2,1)S(1)}, u32[]{:S(2)}, u32[]{:S(2)}) collective-permute-start(bf16[336,384]{1,0:T(8,128)(2,1)S(1)} %broadcast_select_fusion.11), channel_id=1, source_target_pairs={{0,8},{1,9},{2,10},{3,11},{4,12},{5,13},{6,14},{7,15},{24,16},{25,... | collective-permute-start | bytes 774152 | tf_op jit(solution)/shard_map/ppermute | solution.py:1483
  96.6 18.0 %collective-permute-start.14 = (bf16[336,384]{1,0:T(8,128)(2,1)S(1)}, bf16[336,384]{1,0:T(8,128)(2,1)S(1)}, u32[]{:S(2)}, u32[]{:S(2)}) collective-permute-start(bf16[336,384]{1,0:T(8,128)(2,1)S(1)} %broadcast_select_fusion.7), channel_id=1, source_target_pairs={{0,4},{1,5},{24,28},{25,29},{8,12},{9,13},{16,20},{17,21},{2,6},{3... | collective-permute-start | bytes 774152 | tf_op jit(solution)/shard_map/ppermute | solution.py:1483
  115.4 22.8 %collective-permute-start.20 = (bf16[992,384]{1,0:T(8,128)(2,1)S(1)}, bf16[992,384]{1,0:T(8,128)(2,1)S(1)}, u32[]{:S(2)}, u32[]{:S(2)}) collective-permute-start(bf16[992,384]{1,0:T(8,128)(2,1)S(1)} %pad_maximum_fusion.4), channel_id=1, source_target_pairs={{0,1},{1,0},{2,3},{3,2},{4,5},{5,4},{6,7},{7,6},{8,9},{9,8},{10,11... | collective-permute-start | bytes 2285576 | tf_op jit(solution)/shard_map/ppermute | solution.py:1490
  116.3 20.9 %collective-permute-start.23 = (bf16[96,2048]{1,0:T(8,128)(2,1)}, bf16[96,2048]{1,0:T(8,128)(2,1)S(1)}, u32[]{:S(2)}, u32[]{:S(2)}) collective-permute-start(bf16[96,2048]{1,0:T(8,128)(2,1)} %get-tuple-element.165), channel_id=1, source_target_pairs={{0,24},{1,25},{2,26},{3,27},{4,28},{5,29},{6,30},{7,31},{8,16},{9,... | collective-permute-start | bytes 1179656 | tf_op jit(solution)/shard_map/ppermute | solution.py:1469
  158.2 352.7 %all-gather.12.cloned.1.call-start = ((), (), s32[]{:S(2)}) async-start(), calls=%async_computation.2 | async-start | bytes 12533760 | tf_op jit(solution)/shard_map/all_gather | solution.py:1572
  233.7 277.2 %all-gather.14.cloned.1.call-start = ((), (), s32[]{:S(2)}) async-start(), calls=%async_computation.3 | async-start | bytes 11837440 | tf_op jit(solution)/shard_map/all_gather | solution.py:1634
  249.7 17.6 %collective-permute-start.4 = (f32[8,1,80]{2,0,1:T(8,128)S(1)}, f32[8,1,80]{2,0,1:T(8,128)S(1)}, u32[]{:S(2)}, u32[]{:S(2)}) collective-permute-start(f32[8,1,80]{2,0,1:T(8,128)S(1)} %maximum_select_fusion.23), channel_id=1, source_target_pairs={{0,1},{1,0},{2,3},{3,2},{4,5},{5,4},{6,7},{7,6},{8,9},{9,8},{10,11... | collective-permute-start | bytes 7688 | tf_op jit(solution)/shard_map/ppermute | solution.py:444
  398.8 29.3 %collective-permute-start.44 = (f32[3,2,2,2,2,144,128]{6,5,0,3,4,2,1:T(8,128)}, f32[3,2,2,2,2,144,128]{6,5,0,3,4,2,1:T(8,128)}, u32[]{:S(2)}, u32[]{:S(2)}) collective-permute-start(f32[3,2,2,2,2,144,128]{6,5,0,3,4,2,1:T(8,128)} %select_bitcast_fusion.1), channel_id=1, source_target_pairs={{0,1},{1,0},{2,3},{3,2},{4,5},{5,4},{6,7},{7,6},{8,9},{9,8},{10,11... | collective-permute-start | bytes 10616840 | tf_op jit(solution)/shard_map/ppermute | solution.py:463
  409.2 168.6 %collective-permute-start.72 = (f32[2,1,2048]{2,0,1:T(2,128)}, f32[2,1,2048]{2,0,1:T(2,128)}, u32[]{:S(2)}, u32[]{:S(2)}) collective-permute-start(f32[2,1,2048]{2,0,1:T(2,128)} %maximum_select_fusion.21), channel_id=1, source_target_pairs={{0,2},{1,3},{2,0},{3,1},{4,6},{5,7},{6,4},{7,5},{8,10},{9,11},{10,... | collective-permute-start | bytes 49160 | tf_op jit(solution)/shard_map/ppermute | solution.py:444
  431.9 20.7 %collective-permute-start.46 = (bf16[3,2,2,2,72,128]{5,4,0,2,3,1:T(8,128)(2,1)S(1)}, bf16[3,2,2,2,72,128]{5,4,0,2,3,1:T(8,128)(2,1)S(1)}, u32[]{:S(2)}, u32[]{:S(2)}) collective-permute-start(bf16[3,2,2,2,72,128]{5,4,0,2,3,1:T(8,128)(2,1)S(1)} %fusion.19), channel_id=1, source_target_pairs={{0,24},{1,25},{2,26},{3,27},{4,28},{5,29},{6,30},{7,31},{8,16},{9,... | collective-permute-start | bytes 1327112 | tf_op jit(solution)/shard_map/ppermute | solution.py:463
  434.7 18.8 %collective-permute-start.45 = (bf16[3,2,2,2,72,128]{5,4,0,3,2,1:T(8,128)(2,1)S(1)}, bf16[3,2,2,2,72,128]{5,4,0,3,2,1:T(8,128)(2,1)S(1)}, u32[]{:S(2)}, u32[]{:S(2)}) collective-permute-start(bf16[3,2,2,2,72,128]{5,4,0,3,2,1:T(8,128)(2,1)S(1)} %fusion.20), channel_id=1, source_target_pairs={{0,2},{1,3},{2,0},{3,1},{4,6},{5,7},{6,4},{7,5},{8,10},{9,11},{10,... | collective-permute-start | bytes 1327112 | tf_op jit(solution)/shard_map/ppermute | solution.py:463
  476.1 18.2 %collective-permute-start.47 = (f32[3,2,2,2,2,144,128]{6,5,0,3,4,2,1:T(8,128)S(1)}, f32[3,2,2,2,2,144,128]{6,5,0,3,4,2,1:T(8,128)}, u32[]{:S(2)}, u32[]{:S(2)}) collective-permute-start(f32[3,2,2,2,2,144,128]{6,5,0,3,4,2,1:T(8,128)S(1)} %select_bitcast_fusion), channel_id=1, source_target_pairs={{0,1},{1,0},{2,3},{3,2},{4,5},{5,4},{6,7},{7,6},{8,9},{9,8},{10,11... | collective-permute-start | bytes 10616840 | tf_op jit(solution)/shard_map/ppermute | solution.py:463
  503.8 23.9 %collective-permute-start.55 = (bf16[3,2,2,2,88,128]{5,4,0,2,3,1:T(8,128)(2,1)}, bf16[3,2,2,2,88,128]{5,4,0,2,3,1:T(8,128)(2,1)}, u32[]{:S(2)}, u32[]{:S(2)}) collective-permute-start(bf16[3,2,2,2,88,128]{5,4,0,2,3,1:T(8,128)(2,1)} %fusion.11), channel_id=1, source_target_pairs={{0,24},{1,25},{2,26},{3,27},{4,28},{5,29},{6,30},{7,31},{8,16},{9,... | collective-permute-start | bytes 1622024 | tf_op jit(solution)/shard_map/ppermute | solution.py:463
  533.5 23.6 %collective-permute-start.59 = (bf16[96,2048]{1,0:T(8,128)(2,1)S(1)}, bf16[96,2048]{1,0:T(8,128)(2,1)S(1)}, u32[]{:S(2)}, u32[]{:S(2)}) collective-permute-start(bf16[96,2048]{1,0:T(8,128)(2,1)S(1)} %copy-done.44), channel_id=1, source_target_pairs={{16,8},{17,9},{18,10},{19,11},{20,12},{21,13},{22,14},{23,15},{24,... | collective-permute-start | bytes 1179656 | tf_op jit(solution)/shard_map/ppermute | solution.py:1752
  535.9 22.6 %collective-permute-start.53 = (bf16[3,2,88,128]{3,2,0,1:T(8,128)(2,1)S(1)}, bf16[3,2,88,128]{3,2,0,1:T(8,128)(2,1)S(1)}, u32[]{:S(2)}, u32[]{:S(2)}) collective-permute-start(bf16[3,2,88,128]{3,2,0,1:T(8,128)(2,1)S(1)} %fusion.29), channel_id=1, source_target_pairs={{0,24},{1,25},{2,26},{3,27},{4,28},{5,29},{6,30},{7,31},{8,16},{9,... | collective-permute-start | bytes 405512 | tf_op jit(solution)/shard_map/ppermute | solution.py:463
  540.1 18.6 %collective-permute-start.57 = (bf16[3,2,88,128]{3,2,0,1:T(8,128)(2,1)S(1)}, bf16[3,2,88,128]{3,2,0,1:T(8,128)(2,1)S(1)}, u32[]{:S(2)}, u32[]{:S(2)}) collective-permute-start(bf16[3,2,88,128]{3,2,0,1:T(8,128)(2,1)S(1)} %fusion.30), channel_id=1, source_target_pairs={{0,2},{1,3},{2,0},{3,1},{4,6},{5,7},{6,4},{7,5},{8,10},{9,11},{10,... | collective-permute-start | bytes 405512 | tf_op jit(solution)/shard_map/ppermute | solution.py:463
  585.2 14.9 %collective-permute-start.69 = (bf16[1,8,3,48,128]{4,3,2,1,0:T(8,128)(2,1)}, bf16[1,8,3,48,128]{4,3,2,1,0:T(8,128)(2,1)S(1)}, u32[]{:S(2)}, u32[]{:S(2)}) collective-permute-start(bf16[1,8,3,48,128]{4,3,2,1,0:T(8,128)(2,1)} %bitcast.327), channel_id=1, source_target_pairs={{0,24},{1,25},{2,26},{3,27},{4,28},{5,29},{6,30},{7,31},{8,16},{9,... | collective-permute-start | bytes 884744 | tf_op jit(solution)/shard_map/ppermute | solution.py:444
  586.1 15.2 %collective-permute-start.74 = (f32[8,1,2048]{2,1,0:T(1,128)S(1)}, f32[8,1,2048]{2,1,0:T(1,128)S(1)}, u32[]{:S(2)}, u32[]{:S(2)}) collective-permute-start(f32[8,1,2048]{2,1,0:T(1,128)S(1)} %copy.224), channel_id=1, source_target_pairs={{0,8},{1,9},{2,10},{3,11},{4,12},{5,13},{6,14},{7,15},{8,0},{9,1},... | collective-permute-start | bytes 196616 | tf_op jit(solution)/shard_map/ppermute | solution.py:444
  (115 other events, 765.4 us)
Sparse Core Ops, SparseCore 0:
  48.0 107.9 all-gather.7
  158.3 66.5 all-gather.9
  233.8 70.8 all-gather.11
  342.5 63.4 all-gather.13

commit v7 on v6

--- a/solution.py
+++ b/solution.py
@@ -768,7 +768,7 @@
             pltpu.SemaphoreType.DMA((len(plan),)),
         ],
         compiler_params=pltpu.CompilerParams(vmem_limit_bytes=56 << 20),
-        cost_estimate=pl.CostEstimate(flops=10**9, bytes_accessed=2 * 10**7, transcendentals=10**6),
+        cost_estimate=pl.CostEstimate(flops=100 * 10**6, bytes_accessed=370 * 10**5, transcendentals=0),
     )(side, *inputs, gathered, *waits)
 
 
@@ -914,7 +914,7 @@
         out_specs=[pl.BlockSpec(memory_space=pltpu.VMEM)] * len(shapes),
         scratch_shapes=scratch,
         compiler_params=pltpu.CompilerParams(vmem_limit_bytes=56 << 20),
-        cost_estimate=pl.CostEstimate(flops=2 * 10**9, bytes_accessed=2 * 10**7, transcendentals=2 * 10**6),
+        cost_estimate=pl.CostEstimate(flops=100 * 10**6, bytes_accessed=430 * 10**5, transcendentals=0),
     )(side, stream, vectors, gathered)
 
 
@@ -930,8 +930,10 @@
     gathered_ref,
     *refs,
 ):
-    grad_mid_ref, all_grad_ref, vector_grad_ref = refs[-10:-7]
-    flat_ref, wide_ref, up_ref, hidden_ref, grad_pre_ref, weight_grad_ref, sems = refs[-7:]
+    grad_mid_ref, weight_grad_ref, vector_grad_ref = refs[-9:-6]
+    flat_ref, wide_ref, up_ref, hidden_ref, grad_pre_ref, sems = refs[-6:]
+    lead = weight_grad_ref.shape[1] - 2 * FF
+    weight_grad_ref[:, pl.ds(0, lead), :] = jnp.zeros((D // 128, lead, 128), single)
     fetch_rows(side_ref, part, gathered_ref, flat_ref, sems)
     spread_columns(flat_ref, 4 * D, FF // D, wide_ref, up_ref)
     w_down = matrix_rows(flat_ref, 4 * D + FF, FF)
@@ -963,14 +965,13 @@
         down_grad = product_left(hidden_ref[:, spot], grad_mlp)
         for column in range(D // 128):
             lane = slice(column * 128, (column + 1) * 128)
-            weight_grad_ref[column, pl.ds(group, D, stride=FF // D), :] = up_grad[:, lane]
-            weight_grad_ref[column, pl.ds(FF + group * D, D), :] = down_grad[:, lane]
+            weight_grad_ref[column, pl.ds(lead + group, D, stride=FF // D), :] = up_grad[:, lane]
+            weight_grad_ref[column, pl.ds(lead + FF + group * D, D), :] = down_grad[:, lane]
     vector_grad_ref[pl.ds(3, 1), :] = jnp.sum(grad_normed_two * unit_two, axis=0, keepdims=True)
     vector_grad_ref[pl.ds(4, 1), :] = jnp.sum(grad_normed_two, axis=0, keepdims=True)
     grad_mid = grad_out + norm_back(grad_normed_two, unit_two, spread_two, vectors[3:4])
     vector_grad_ref[pl.ds(2, 1), :] = jnp.sum(grad_mid * attn, axis=0, keepdims=True)
     grad_mid_ref[...] = grad_mid
-    store_rows(weight_grad_ref, all_grad_ref, 4 * D, sems.at[0])
 
 
 def attention_back_kernel(
@@ -984,8 +985,10 @@
     gathered_ref,
     *refs,
 ):
-    grad_in_ref, all_grad_ref, vector_grad_ref = refs[-10:-7]
-    flat_ref, wide_ref, qkv_ref, grad_mixed_ref, grad_packed_ref, weight_grad_ref, sems = refs[-7:]
+    grad_in_ref, weight_grad_ref, vector_grad_ref = refs[-9:-6]
+    flat_ref, wide_ref, qkv_ref, grad_mixed_ref, grad_packed_ref, sems = refs[-6:]
+    rest = weight_grad_ref.shape[1] - 4 * D
+    weight_grad_ref[:, pl.ds(4 * D, rest), :] = jnp.zeros((D // 128, rest, 128), single)
     fetch_rows(side_ref, part, gathered_ref, flat_ref, sems)
     spread_columns(flat_ref, 0, 3, wide_ref, qkv_ref)
     w_proj = matrix_rows(flat_ref, 3 * D, D)
@@ -1030,59 +1033,51 @@
     vector_grad_ref[pl.ds(0, 1), :] = jnp.sum(grad_normed * unit_one, axis=0, keepdims=True)
     vector_grad_ref[pl.ds(1, 1), :] = jnp.sum(grad_normed, axis=0, keepdims=True)
     grad_in_ref[...] = grad_mid + norm_back(grad_normed, unit_one, spread_one, vectors[0:1])
-    store_rows(weight_grad_ref, all_grad_ref, 0, sems.at[0])
-
-
-def store_rows(weight_grad_ref, all_grad_ref, first_row, sem):
-    copy = pltpu.make_async_copy(
-        weight_grad_ref, all_grad_ref.at[:, pl.ds(first_row, weight_grad_ref.shape[1])], sem
-    )
-    copy.start()
-    copy.wait()
-
-
-def layer_back(kernel, part, weight_rows, side, inputs, vectors, gathered, started, waits, columns, buffers):
+
+
+def layer_back(kernel, part, weight_rows, side, inputs, vectors, gathered, waits, columns, buffers):
     tokens = inputs[0].shape[0]
     rows, blocks = gathered.shape[3], 2 * gathered.shape[0]
     return pl.pallas_call(
         lambda *refs: kernel(part, *refs),
         out_shape=[
             jax.ShapeDtypeStruct((tokens, D), single),
-            jax.ShapeDtypeStruct((D // 128, MATRIX_ROWS, 128), single),
+            jax.ShapeDtypeStruct((D // 128, weight_rows, 128), single),
             jax.ShapeDtypeStruct((8, D), single),
         ],
-        in_specs=layer_specs_in(len(inputs) + 3)
-        + [pl.BlockSpec(memory_space=pl.ANY)] * (len(started) + len(waits)),
-        out_specs=[
-            pl.BlockSpec(memory_space=pltpu.VMEM),
-            pl.BlockSpec(memory_space=pl.ANY),
-            pl.BlockSpec(memory_space=pltpu.VMEM),
-        ],
-        input_output_aliases={len(inputs) + 3: 1} if started else {},
+        in_specs=layer_specs_in(len(inputs) + 3) + [pl.BlockSpec(memory_space=pl.ANY)] * len(waits),
+        out_specs=[pl.BlockSpec(memory_space=pltpu.VMEM)] * 3,
         scratch_shapes=[
             pltpu.VMEM((blocks, rows, D), narrow),
             pltpu.VMEM((D // 128, columns * D, 128), single),
             pltpu.VMEM((columns, D, D), narrow),
         ]
         + [pltpu.VMEM((tokens, width), narrow) for width in buffers]
-        + [pltpu.VMEM((D // 128, weight_rows, 128), single), pltpu.SemaphoreType.DMA((4,))],
+        + [pltpu.SemaphoreType.DMA((4,))],
         compiler_params=pltpu.CompilerParams(vmem_limit_bytes=56 << 20),
-        cost_estimate=pl.CostEstimate(flops=5 * 10**9, bytes_accessed=4 * 10**7, transcendentals=2 * 10**6),
-    )(side, *inputs, vectors, gathered, *started, *waits)
+        cost_estimate=pl.CostEstimate(flops=100 * 10**6, bytes_accessed=600 * 10**5, transcendentals=0),
+    )(side, *inputs, vectors, gathered, *waits)
+
+
+def pair_rows_of(block_rows):
+    pair = 2 * block_rows
+    return 4 * D // pair * pair, -(-4 * D // pair) * pair
 
 
 def mlp_back(side, grad_out, saved, vectors, gathered, part, waits):
     stream, packed, mixed, attn, pre, mlp = saved
     return layer_back(
-        mlp_back_kernel, part, 2 * FF, side, (grad_out, stream, attn, pre, mlp), vectors, gathered, (), waits,
+        mlp_back_kernel, part, MATRIX_ROWS - pair_rows_of(gathered.shape[3])[0], side,
+        (grad_out, stream, attn, pre, mlp), vectors, gathered, waits,
         FF // D, (FF, FF),
     )
 
 
-def attention_back(side, grad_mid, saved, vectors, gathered, part, started, waits):
+def attention_back(side, grad_mid, saved, vectors, gathered, part, waits):
     stream, packed, mixed, attn, pre, mlp = saved
     return layer_back(
-        attention_back_kernel, part, 4 * D, side, (grad_mid, stream, packed, mixed), vectors, gathered, (started,), waits,
+        attention_back_kernel, part, pair_rows_of(gathered.shape[3])[1], side,
+        (grad_mid, stream, packed, mixed), vectors, gathered, waits,
         3, (D, 3 * D),
     )
 
@@ -1133,7 +1128,7 @@
         in_specs=[pl.BlockSpec(memory_space=pltpu.VMEM)] * 5 + [pl.BlockSpec(memory_space=pl.ANY)] * len(waits),
         out_specs=pl.BlockSpec(memory_space=pltpu.VMEM),
         compiler_params=pltpu.CompilerParams(vmem_limit_bytes=40 << 20),
-        cost_estimate=pl.CostEstimate(flops=10**9, bytes_accessed=2 * 10**7, transcendentals=0),
+        cost_estimate=pl.CostEstimate(flops=100 * 10**6, bytes_accessed=37 * 10**5, transcendentals=0),
     )(grad, patch_rows, shown, gains, vector_grads, *waits)
 
 
@@ -1222,7 +1217,7 @@
             pltpu.VMEM((8, rows), single),
         ],
         compiler_params=pltpu.CompilerParams(vmem_limit_bytes=56 << 20),
-        cost_estimate=pl.CostEstimate(flops=5 * 10**9, bytes_accessed=10**7, transcendentals=5 * 10**6),
+        cost_estimate=pl.CostEstimate(flops=100 * 10**6, bytes_accessed=520 * 10**5, transcendentals=0),
     )(teacher_z, student_z, teacher, student, centre_column, class_lines)
 
 
@@ -1265,7 +1260,7 @@
         + [pl.BlockSpec(memory_space=pl.ANY)] * len(waits),
         out_specs=[table, pl.BlockSpec((8, 128), lambda i: (0, 0))],
         compiler_params=pltpu.CompilerParams(vmem_limit_bytes=56 << 20),
-        cost_estimate=pl.CostEstimate(flops=4 * 10**9, bytes_accessed=10**7, transcendentals=5 * 10**6),
+        cost_estimate=pl.CostEstimate(flops=100 * 10**6, bytes_accessed=400 * 10**5, transcendentals=0),
     )(teacher_z, student_z, teacher, student, centre_column, scale_lines, *waits)
 
 
@@ -1292,9 +1287,10 @@
 
 
 def head_grads_kernel(
-    place_ref, inputs_ref, grads_ref, *refs,
+    held, place_ref, inputs_ref, grads_ref, *refs,
 ):
-    own_ref, partner_ref, window_ref, rows_ref, product_ref, third_ref, bottle_ref, line_ref, sems = refs[-9:]
+    own_ref, partner_ref = refs[len(refs) - 9 - held :][:2] if held else refs[-9:-7]
+    window_ref, rows_ref, product_ref, third_ref, bottle_ref, line_ref, sems = refs[-7:]
     slot = own_ref.shape[0]
     lead = product_ref.shape[0] - window_ref.shape[1]
     number = lax.broadcasted_iota(jnp.int32, (slot, 1), 0)
@@ -1351,15 +1347,18 @@
     block(4, partner_ref)
 
 
-def head_grads(place, inputs_all, grads_all, slot, lead, waits):
+def head_grads(place, inputs_all, grads_all, slot, lead, waits, held):
     rows = inputs_all.shape[0]
     wide = slot * ROW // BOT
     return pl.pallas_call(
-        head_grads_kernel,
-        out_shape=[jax.ShapeDtypeStruct((slot, ROW), kind) for kind in (single, narrow)],
+        lambda *refs: head_grads_kernel(len(held), *refs),
+        out_shape=[jax.ShapeDtypeStruct((slot, ROW), kind) for kind in (single, narrow)]
+        + [jax.ShapeDtypeStruct(array.shape, array.dtype) for array in held],
         in_specs=[pl.BlockSpec(memory_space=pltpu.SMEM)]
-        + [pl.BlockSpec(memory_space=pl.ANY)] * (2 + len(waits)),
-        out_specs=[pl.BlockSpec(memory_space=pltpu.VMEM)] * 2,
+        + [pl.BlockSpec(memory_space=pl.ANY)] * (2 + len(waits) + len(held)),
+        out_specs=[pl.BlockSpec(memory_space=pltpu.VMEM)] * 2
+        + [pl.BlockSpec(memory_space=pl.ANY)] * len(held),
+        input_output_aliases={3 + len(waits) + number: 2 + number for number in range(len(held))},
         scratch_shapes=[
             pltpu.VMEM((rows, 256), narrow),
             pltpu.VMEM((rows, ROW), narrow),
@@ -1370,8 +1369,8 @@
             pltpu.SemaphoreType.DMA((2,)),
         ],
         compiler_params=pltpu.CompilerParams(vmem_limit_bytes=56 << 20),
-        cost_estimate=pl.CostEstimate(flops=4 * 10**9, bytes_accessed=2 * 10**7, transcendentals=0),
-    )(place, inputs_all, grads_all, *waits)
+        cost_estimate=pl.CostEstimate(flops=100 * 10**6, bytes_accessed=370 * 10**5, transcendentals=0),
+    )(place, inputs_all, grads_all, *waits, *held)
 
 
 def close_local(
@@ -1553,6 +1552,11 @@
         jnp.concatenate([teacher_normed, normed_got]),
     )
     normed = jnp.pad(normed, ((0, more_rows), (0, 0)))
+    all_rows = half * pair_rows
+    kept_row = jnp.broadcast_to(kept[:, None], (images_here, 17)).reshape(1, rows_here)
+    kept_pair = cube_gather(kept_row, "b").reshape(1, 2 * rows_here)
+    kept_pair = jnp.pad(kept_pair, ((0, 0), (0, more_rows)))
+    all_kept = cube_gather(kept_pair, "xygc").reshape(all_rows)
     third_end = (bounds[-2] - D - HID + slot) * (ROW // BOT)
     acts_width = D + HID + max(third_end, HID)
     unit_z, acts, bottleneck, pre_one, pre_two = head_pass(
@@ -1568,14 +1572,10 @@
             jax.ShapeDtypeStruct((pair_rows, HID), single),
             jax.ShapeDtypeStruct((pair_rows, HID), single),
         ],
+        (all_kept,),
     )
     inputs_all = lax.all_gather(acts, "dev", axis=0, axis_index_groups=groups).reshape(half * pair_rows, -1)
 
-    all_rows = half * pair_rows
-    kept_row = jnp.broadcast_to(kept[:, None], (images_here, 17)).reshape(1, rows_here)
-    kept_pair = cube_gather(kept_row, "b").reshape(1, 2 * rows_here)
-    kept_pair = jnp.pad(kept_pair, ((0, 0), (0, more_rows)))
-    all_kept = cube_gather(kept_pair, "xygc").reshape(all_rows)
     z_pair = cube_gather(unit_z, "b")
     teacher_z_all = cube_gather(z_pair[0], "xygc").reshape(all_rows, BOT)
     student_z_all = cube_gather(z_pair[1], "gxyc").reshape((2,) * 4 + (pair_rows, BOT))
@@ -1595,7 +1595,14 @@
     mixed_rows, sums, centre_sum = logits_pass(
         teacher_z_all, student_z_all, proto_teacher, protos, centre_column, lines(class_kept)
     )
-    mixed_own = cube_scatter(mixed_rows.reshape((2,) * 4 + (pair_rows, 2 * BOT + 128)), "cgyx", "cgyx")
+    by_pair = (2,) * 4 + (pair_rows, -1)
+    mixed_own = jnp.concatenate(
+        [
+            cube_scatter(mixed_rows[:, :BOT].reshape(by_pair), "cgyx", "cgyx"),
+            cube_scatter(mixed_rows[:, BOT:].reshape(by_pair), "cgyx", "cxyg"),
+        ],
+        axis=1,
+    )
     mixed_own = mixed_own + lax.ppermute(
         mixed_own.astype(narrow), "dev", [(i, i ^ across) for i in range(half)]
     ).astype(single)
@@ -1629,7 +1636,7 @@
             jax.ShapeDtypeStruct((pair_rows, 2 * HID + BOT), narrow),
             jax.ShapeDtypeStruct((pair_rows, D), single),
         ],
-        (stages[2],),
+        (stages[3],),
     )
     grads_all = lax.all_gather(grads, "dev", axis=0, axis_index_groups=groups).reshape(half * pair_rows, -1)
     normed_back = lax.ppermute(
@@ -1649,7 +1656,6 @@
 
     grad_stream = grad_stream.reshape(images_here * PAD_SEQ, D)
     middle_row = block_rows // 2
-    small_rows = -(-(EMBED_ROWS + 6 * LAYERS) // (16 * count)) * 16
     vector_grads = [None] * LAYERS
 
     def halves(array):
@@ -1662,17 +1668,29 @@
     def moves(pieces, order):
         return [move(sent, kept, axis) for (sent, kept, left), axis in zip(pieces, order)]
 
-    def blocks_of(weight_grad, rows):
-        return split_bits(weight_grad.reshape(D // 128, count, rows, 128), 1)
-
-    rounds = (("c",), ("x", "b"), ("y", "a"), ("b", "x"), ("a", "y"))
+    def over_core(weight_grad, rows):
+        pairs_of = weight_grad.reshape(D // 128, -1, 2, rows, 128)
+        return move(*cut(pairs_of, "pc", "c", 1)[:2], "c")
+
+    def start(late, early):
+        shared_pair = 4 * D // (2 * block_rows)
+        whole = jnp.concatenate(
+            [
+                early[:, :shared_pair],
+                early[:, shared_pair:] + late[:, : early.shape[1] - shared_pair],
+                late[:, early.shape[1] - shared_pair :],
+            ],
+            axis=1,
+        )
+        by_bits = whole.reshape((D // 128, 2, 2, 2, 2, block_rows, 128))
+        return (cuts(halves(by_bits), ["bayx"] * 2, rounds[0]), 0)
+
+    rounds = (("x", "b"), ("y", "a"), ("b", "x"), ("a", "y"))
 
     def advance(state):
         pieces, stage = state
         parts = moves(pieces, rounds[stage])
         names = [left for sent, kept, left in pieces]
-        if stage == 0:
-            parts, names = halves(parts[0]), names * 2
         return cuts(parts, names, rounds[stage + 1]), stage + 1
 
     def finish(state):
@@ -1684,21 +1702,20 @@
         return tuple(sent for pieces, stage in states for sent, kept, left in pieces)
 
     started = []
-    waits, later_waits = (stages[3],), (stages[4],)
+    waits, later_waits = (stages[4],), (stages[5],)
     for layer_index in reversed(range(LAYERS)):
         saved, vectors = saved_layers[layer_index], vectors_all[1, layer_index]
         part = LAYERS + layer_index
-        started = [advance(state) for state in started]
-        grad_stream, weight_grad, late_vectors = mlp_back(
+        grad_stream, late_grad, late_vectors = mlp_back(
             side, grad_stream, saved, vectors, gathered, part, waits + sends(started)
         )
+        late = over_core(late_grad, block_rows)
         started = [advance(state) for state in started]
-        grad_stream, weight_grad, early_vectors = attention_back(
-            side, grad_stream, saved, vectors, gathered, part, weight_grad, later_waits + sends(started)
+        grad_stream, early_grad, early_vectors = attention_back(
+            side, grad_stream, saved, vectors, gathered, part, later_waits + sends(started)
         )
         waits, later_waits = (), ()
         vector_grads[layer_index] = (late_vectors + early_vectors)[:6]
-        first = (cuts([blocks_of(weight_grad, block_rows)], ["bayxc"], rounds[0]), 0)
         if layer_index == LAYERS - 1:
             proto_grad, proto_square = proto_grad_pass(
                 teacher_z_all,
@@ -1707,29 +1724,24 @@
                 protos,
                 centre_column,
                 lines(student_scale, teacher_scale),
-                sends([first]),
+                (early_vectors,),
             )
             waits = (proto_square,)
-        if layer_index > 0:
-            started.append(first)
-    started = [advance(state) for state in started]
+        started = [advance(state) for state in started]
+        started.append(start(late, over_core(early_grad, block_rows)))
+    *later_states, last = started
+    small_rows = -(-(EMBED_ROWS + 6 * LAYERS) // 64) * 64
     small = embed_back(
         grad_stream,
         patches.reshape(images_here * PATCHES, PIX),
         jnp.where(masked_here, 0.0, 1.0).reshape(images_here * PATCHES, 1),
         jnp.stack([grad_gain, grad_bias]),
         jnp.concatenate(vector_grads),
-        small_rows * count,
-        sends([first] + started),
-    )
-    small_first = cuts([blocks_of(small, small_rows)], ["bayxc"], rounds[0])
-    joined = [
-        jnp.concatenate(pair, axis=-2)
-        for pair in zip(halves(moves(first[0], "c")[0]), halves(moves(small_first, "c")[0]))
-    ]
-    last = (cuts(joined, ["bayx"] * 2, rounds[1]), 1)
-    later_blocks = [jnp.concatenate(finish(state), axis=1) for state in started]
-
+        small_rows,
+        sends([last]),
+    )
+    small_parts = halves(over_core(small, small_rows // 2)[:, 0])
+    small_sends = [part.astype(narrow) for part in small_parts]
     def block_place(i):
         column = max(bounds[i], 0) // 128 * 128
         grad_column = 0 if i < first_w2 else HID
@@ -1746,29 +1758,41 @@
             for i in range(count)
         ]
     )
-    own_block_grad, partner_block_grad = head_grads(
-        place, inputs_all, grads_all, slot, -min(bounds[1], 0), sends([last])
-    )
+    flying = [last] + later_states
+    own_block_grad, partner_block_grad, *held = head_grads(
+        place,
+        inputs_all,
+        grads_all,
+        slot,
+        -min(bounds[1], 0),
+        (),
+        [stay for pieces, stage in flying for sent, stay, left in pieces] + small_parts,
+    )
+    held = iter(held)
+    flying = [([(sent, next(held), left) for sent, _, left in pieces], stage) for pieces, stage in flying]
+    small_parts = list(held)
     block_got = lax.ppermute(partner_block_grad, "dev", [(i, i ^ across) for i in range(half, count)])
     head_block_grad = jnp.where(student_side, own_block_grad, block_got.astype(single))
-    pieces, stage = advance(last)
-    parts = finish(([(after(sent, own_block_grad), stay, left) for sent, stay, left in pieces], stage))
-    middle_row = block_rows // 2
-    small_block = jnp.concatenate([part[:, middle_row:] for part in parts], axis=1)
-    layer_block = jnp.stack(
-        [jnp.concatenate([part[:, :middle_row] for part in parts], axis=1)] + later_blocks[::-1]
-    )
+    small_parts = moves([(sent, part, "") for sent, part in zip(small_sends, small_parts)], rounds[0])
+    for order in rounds[1:]:
+        small_parts = [move(part.astype(narrow), part, axis) for part, axis in zip(small_parts, order)]
+    small_mine = jnp.concatenate(small_parts, axis=1)
+    small_other = lax.ppermute(small_mine, "dev", pairs(count, 1))
+    small_sum = jnp.where(
+        me % 2 == 0,
+        jnp.concatenate([small_mine, small_other], axis=1),
+        jnp.concatenate([small_other, small_mine], axis=1),
+    )
+    blocks = [jnp.concatenate(finish(state), axis=1) for state in flying]
+    layer_block = jnp.stack(blocks[:1] + blocks[:0:-1])
 
     square_local = (
         jnp.sum(head_block_grad * head_block_grad)
         + jnp.sum(layer_block * layer_block)
-        + jnp.sum(small_block * small_block)
+        + jnp.where(me == 0, jnp.sum(small_sum * small_sum), 0.0)
         + proto_square[0, 0]
     )
-    high = square_local.astype(narrow)
-    middle = (square_local - high.astype(single)).astype(narrow)
-    low = (square_local - high.astype(single) - middle.astype(single)).astype(narrow)
-    tile = jnp.pad(jnp.stack([high, middle, low]).reshape(3, 1, 1), ((0, 0), (0, 15), (0, 127)))
+    square_total = cube_sum(square_local.reshape(1, 1))[0, 0]
     behind = lax.ppermute(layer_block[:, :, :6], "dev", step_pairs(count, -1))
     last_rows = lax.dynamic_slice(
         head_block_grad, (jnp.array(sizes, jnp.int32)[me] - GROUP, 0), (GROUP, ROW)
@@ -1778,12 +1802,7 @@
     stem_lines, layer_lines = own_shards(
         place, head_block_grad, previous, layer_block, behind, lane_rows(stem_piece), lane_rows(layer_piece)
     )
-    shared = cube_gather(jnp.concatenate([small_block.astype(narrow), tile], axis=1), "xya")
-    shared = cube_gather(after(shared, stem_lines), "bc")
-    shared = jnp.moveaxis(shared.reshape((2, 2) + shared.shape[1:]), 0, 2)
-    shared = shared.reshape((count,) + shared.shape[3:]).astype(single)
-    square_total = jnp.sum(shared[:, :, small_rows, 0])
-    small_all = jnp.transpose(shared[:, :, :small_rows], (0, 2, 1, 3)).reshape(small_rows * count, D)
+    small_all = jnp.swapaxes(small_sum, 0, 1).reshape(small_rows, D)
     embed_grad = small_all[:EMBED_ROWS].reshape(-1)
     vector_grad = small_all[EMBED_ROWS : EMBED_ROWS + 6 * LAYERS].reshape(LAYERS, 6 * D)
     layer_grad = layer_lines.reshape(LAYERS, -1)[:, :layer_piece]

time: 651 us -> 660 us (1.014)
  local copies, waits for them, and re-layouts: 67.9 us -> 48.8 us
  other arithmetic: 62.7 us -> 76.5 us
  starting transfers between devices: 87.2 us -> 96.7 us
  Pallas kernels: 183 us -> 176 us
  waiting for transfers between devices: 217 us -> 224 us
    ppermute x23 -> x37, waiting for transfers between devices: 47.6 us -> 74 us  [move(): lax.ppermute(sent, 'dev', pairs(1 << len(BITS), MASKS[name])).astype(single)]
    ppermute x1, waiting for transfers between devices: 16.6 us -> 0.01 us  [close_local(): lax.ppermute(partner_block_grad, 'dev', [(i, i ^ across) for i in range(h...]
    ppermute x23 -> x37, starting transfers between devices: 20.1 us -> 36 us  [move(): lax.ppermute(sent, 'dev', pairs(1 << len(BITS), MASKS[name])).astype(single)]
    ppermute x24 -> x19, starting transfers between devices: 24.4 us -> 11.4 us  [cube_gather(): got = lax.ppermute(held, 'dev', pairs(count, MASKS[name]))]
    ppermute x0 -> x6, starting transfers between devices: none -> 9.71 us  [the longest x5 9.7 us: cube_sum(): lax.ppermute(values, 'dev', pairs(1 << len(BITS), MASKS[name]))]
    select_n x4 -> x6, other arithmetic: 4.93 us -> 13.8 us  [cut(): sent = jnp.where(flag, low, high)]
    ppermute x24 -> x19, waiting for transfers between devices: 39.5 us -> 36.6 us  [cube_gather(): got = lax.ppermute(held, 'dev', pairs(count, MASKS[name]))]
  transfers between devices with their start and end apart: 80 -> 95, of which waited for: 42 -> 43; matrix products, arithmetic and copies ran while one was open for 16% -> 17% of each run, Pallas kernels for 26% -> 24%
where the time goes in v7:
time: 660 us; the launch traced here: 648 us
  waiting for transfers between devices  224 us (34%)
  Pallas kernels  176 us (27%)
  starting transfers between devices  96.7 us (15%)
  other arithmetic  76.5 us (12%)
  local copies, waits for them, and re-layouts  48.8 us (7%)
  between operations  25.9 us (4%)
    ppermute x37, waiting for transfers between devices, move(): lax.ppermute(sent, 'dev', pairs(1 << len(BITS), MASKS[name])).astype(single)  74 us
    pallas_call x4, Pallas kernels, layer_back(): pl.pallas_call(lambda *refs: kernel(part, *refs), out_shape=[jax.ShapeDty...  61.2 us
    pallas_call x4, Pallas kernels, layer_forward(): pl.pallas_call(lambda *refs: forward_kernel(part, keep, *refs), out_shape...  48 us
    ppermute x12, waiting for transfers between devices, close_local(): got = lax.ppermute(spread, 'dev', moves)  38.9 us
    ppermute x19, waiting for transfers between devices, cube_gather(): got = lax.ppermute(held, 'dev', pairs(count, MASKS[name]))  36.6 us
    ppermute x37, starting transfers between devices, move(): lax.ppermute(sent, 'dev', pairs(1 << len(BITS), MASKS[name])).astype(single)  36 us
    ppermute x1, waiting for transfers between devices, close_local(): other_layers = lax.ppermute(layer_blocks, 'dev', pairs(count, across))  20.2 us
    pallas_call x2, Pallas kernels, head_pass(): pl.pallas_call(lambda *refs: kernel(plan, *refs[:read], *refs[read + len(...  19.6 us
  transfers between devices with their start and end apart: 95, of which 43 were waited for; matrix products, arithmetic and copies ran while one was open for 17% of the time, Pallas kernels for 24%

profile of v7, /device:TPU:8, one launch (start us, length us, event | category | flops | bytes accessed | tf_op | source)
XLA Modules:
  0.0 648.4 jit_solution(12783169404909437466)
XLA Ops:
  26.6 20.2 %collective-permute-done.21 = bf16[4,144,384]{2,1,0:T(8,128)(2,1)S(1)} collective-permute-done((bf16[4,144,384]{2,1,0:T(8,128)(2,1)S(1)}, bf16[4,144,384]{2,1,0:T(8,128)(2,1)S(1)}, u32[]{:S(2)}, u32[]{:S(2)}) %collective-permute-start.21) | collective-permute-done | bytes 442400 | tf_op jit(solution)/shard_map/ppermute | solution.py:1459
  66.2 15.0 %collective-permute-done.12 = bf16[336,384]{1,0:T(8,128)(2,1)S(1)} collective-permute-done((bf16[336,384]{1,0:T(8,128)(2,1)S(1)}, bf16[336,384]{1,0:T(8,128)(2,1)S(1)}, u32[]{:S(2)}, u32[]{:S(2)}) %collective-permute-start.12) | collective-permute-done | bytes 258080 | tf_op jit(solution)/shard_map/ppermute | solution.py:1482
  83.2 8.5 %collective-permute-done.18 = bf16[320,384]{1,0:T(8,128)(2,1)S(1)} collective-permute-done((bf16[320,384]{1,0:T(8,128)(2,1)S(1)}, bf16[320,384]{1,0:T(8,128)(2,1)S(1)}, u32[]{:S(2)}, u32[]{:S(2)}) %collective-permute-start.18) | collective-permute-done | bytes 245792 | tf_op jit(solution)/shard_map/ppermute | solution.py:1482
  101.6 12.1 %collective-permute-done.10 = bf16[336,384]{1,0:T(8,128)(2,1)S(1)} collective-permute-done((bf16[336,384]{1,0:T(8,128)(2,1)S(1)}, bf16[336,384]{1,0:T(8,128)(2,1)S(1)}, u32[]{:S(2)}, u32[]{:S(2)}) %collective-permute-start.10) | collective-permute-done | bytes 258080 | tf_op jit(solution)/shard_map/ppermute | solution.py:1482
  119.2 17.7 %collective-permute-done.23 = bf16[96,2048]{1,0:T(8,128)(2,1)S(1)} collective-permute-done((bf16[96,2048]{1,0:T(8,128)(2,1)S(1)}, bf16[96,2048]{1,0:T(8,128)(2,1)S(1)}, u32[]{:S(2)}, u32[]{:S(2)}) %collective-permute-start.23) | collective-permute-done | bytes 393248 | tf_op jit(solution)/shard_map/ppermute | solution.py:1468
  139.3 16.7 %all-gather.8.cloned.1.call-done.refs_3_.refs_1_.refs_7_.refs_6_ = bf16[16,2,4,144,384]{4,3,2,1,0:T(8,128)(2,1)} async-done(((bf16[1,2,4,144,384]{4,3,2,1,0:T(8,128)(2,1)}), bf16[16,2,4,144,384]{4,3,2,1,0:T(8,128)(2,1)}) %all-gather.8.cloned.1.call-update) | async-done | bytes 14155792 | tf_op jit(solution)/shard_map/all_gather | solution.py:1465
  177.2 11.5 %shard_map.448.refs_1_ = f32[544,384]{1,0:T(8,128)} custom-call(s32[1]{0:T(128)} %bitcast.8.refs_0_, f32[544,384]{1,0:T(8,128)} %bitcast.359, bf16[8,384]{1,0:T(8,128)(2,1)} %get-tuple-element.205.refs_2_, bf16[16,2,4,144,384]{4,3,2,1,0:T(8,128)(2,1)} %all-gather.8.cloned.1.call-done.refs_3_.refs_1_.refs_7_.refs_6_), custom_call_target="tpu_custom_call" | custom-call | flops 100000000 | bytes 43000000 | tf_op jit(solution)/shard_map/pallas_call | solution.py:910
  188.8 11.8 %shard_map.449 = f32[544,384]{1,0:T(8,128)} custom-call(s32[1]{0:T(128)} %bitcast.8.refs_0_, f32[544,384]{1,0:T(8,128)} %shard_map.448.refs_1_, bf16[8,384]{1,0:T(8,128)(2,1)} %get-tuple-element.204.refs_2_, bf16[16,2,4,144,384]{4,3,2,1,0:T(8,128)(2,1)} %all-gather.8.cloned.1.call-done.refs_3_.refs_1_.refs_7_.refs_6_), custom_call_target="tpu_custom_call" | custom-call | flops 100000000 | bytes 43000000 | tf_op jit(solution)/shard_map/pallas_call | solution.py:910
  202.6 12.2 %shard_map.450 = (f32[544,384]{1,0:T(8,128)}, bf16[544,1152]{1,0:T(8,128)(2,1)}, bf16[544,384]{1,0:T(8,128)(2,1)}, f32[544,384]{1,0:T(8,128)}, f32[544,1536]{1,0:T(8,128)}, /*index=5*/f32[544,384]{1,0:T(8,128)}) custom-call(s32[1]{0:T(128)} %bitcast.8.refs_0_, f32[544,384]{1,0:T(8,128)} %bitcast.345, ...), custom_call_target="tpu_custom_call" | custom-call | flops 100000000 | bytes 43000000 | tf_op jit(solution)/shard_map/pallas_call | solution.py:910
  214.8 12.5 %shard_map.451 = (f32[544,384]{1,0:T(8,128)}, bf16[544,1152]{1,0:T(8,128)(2,1)}, bf16[544,384]{1,0:T(8,128)(2,1)}, f32[544,384]{1,0:T(8,128)}, f32[544,1536]{1,0:T(8,128)}, /*index=5*/f32[544,384]{1,0:T(8,128)}) custom-call(s32[1]{0:T(128)} %bitcast.8.refs_0_, f32[544,384]{1,0:T(8,128)} %get-tuple-element.78.refs_1_.refs_2_, ...), custom_call_target="tpu_custom_call" | custom-call | flops 100000000 | bytes 43000000 | tf_op jit(solution)/shard_map/pallas_call | solution.py:910
  235.5 8.7 %shard_map.453 = (bf16[80,256]{1,0:T(8,128)(2,1)}, bf16[80,4608]{1,0:T(8,128)(2,1)}, f32[80,256]{1,0:T(8,128)}, f32[80,2048]{1,0:T(8,128)}, f32[80,2048]{1,0:T(8,128)}) custom-call(s32[1]{0:T(128)} %bitcast.8.refs_0_, bf16[80,384]{1,0:T(8,128)(2,1)} %pad.41.refs_1_, bf16[16,2,96,2048]{3,2,1,0:T(8,128)(2,1)} %bitcast.333, f32[1280]{0:T(1024)} %select_n.1240.refs_3_), custom_call_target="tpu_custom_call" | custom-call | flops 100000000 | bytes 37000000 | tf_op jit(solution)/shard_map/pallas_call | solution.py:755
  274.9 14.1 %shard_map.454 = (f32[1280,640]{1,0:T(8,128)}, f32[8,1280]{1,0:T(8,128)}, f32[2048,1]{1,0:T(8,128)}) custom-call(bf16[1280,256]{1,0:T(8,128)(2,1)} %bitcast.355, bf16[1280,256]{1,0:T(8,128)(2,1)} %bitcast.353, f32[2048,256]{1,0:T(8,128)} %refs_3_.1, f32[2048,256]{1,0:T(8,128)} %refs_0_.1, f32[2048,1]{1,0:T(8,128)} %copy.197.centre_ref, f32[8,1280]{1,0:T(8,128)} %pad.42.class_ref), custom_call_target="tpu_custom_call" | custom-call | flops 100000000 | bytes 52000000 | tf_op jit(solution)/shard_map/pallas_call | solution.py:1204
  295.7 8.0 %collective-permute-done.39 = bf16[2,2,80,256]{3,2,1,0:T(8,128)(2,1)S(1)} collective-permute-done((bf16[2,2,80,256]{3,2,1,0:T(8,128)(2,1)S(1)}, bf16[2,2,80,256]{3,2,1,0:T(8,128)(2,1)S(1)}, u32[]{:S(2)}, u32[]{:S(2)}) %collective-permute-start.39) | collective-permute-done | bytes 163872 | tf_op jit(solution)/shard_map/ppermute | solution.py:463
  308.4 5.8 collective-permute-done.43
  330.0 10.9 %shard_map.455 = (bf16[80,4352]{1,0:T(8,128)(2,1)}, f32[80,384]{1,0:T(8,128)}) custom-call(s32[1]{0:T(128)} %bitcast.8.refs_0_, f32[80,256]{1,0:T(8,128)} %fusion.37.refs_1_, f32[80,256]{1,0:T(8,128)} %get-tuple-element.85.refs_2_, f32[80,2048]{1,0:T(8,128)} %get-tuple-element.86.refs_3_, f32[80,2048]{1,0:T(8,128)} %get-tuple-element.87.refs_4_, ...), custom_call_target="tpu_custom_call" | custom-call | flops 100000000 | bytes 37000000 | tf_op jit(solution)/shard_map/pallas_call | solution.py:755
  363.3 13.8 %shard_map.456 = (f32[544,384]{1,0:T(8,128)}, f32[3,3168,128]{2,1,0:T(8,128)}, f32[8,384]{1,0:T(8,128)}) custom-call(s32[1]{0:T(128)} %bitcast.8.refs_0_, f32[544,384]{1,0:T(8,128)} %bitcast.352, f32[544,384]{1,0:T(8,128)} %get-tuple-element.78.refs_1_.refs_2_, f32[544,384]{1,0:T(8,128)} %get-tuple-element.90.refs_3_, ...), custom_call_target="tpu_custom_call" | custom-call | flops 100000000 | bytes 60000000 | tf_op jit(solution)/shard_map/pallas_call | solution.py:1041
  385.8 16.9 %shard_map.457 = (f32[544,384]{1,0:T(8,128)}, f32[3,1728,128]{2,1,0:T(8,128)}, f32[8,384]{1,0:T(8,128)}) custom-call(s32[1]{0:T(128)} %bitcast.8.refs_0_, f32[544,384]{1,0:T(8,128)} %get-tuple-element.93.refs_1_, f32[544,384]{1,0:T(8,128)} %get-tuple-element.78.refs_1_.refs_2_, bf16[544,1152]{1,0:T(8,128)(2,1)} %get-tuple-element.94.refs_3_, ...), custom_call_target="tpu_custom_call" | custom-call | flops 100000000 | bytes 60000000 | tf_op jit(solution)/shard_map/pallas_call | solution.py:1041
  412.6 10.7 %shard_map.458 = (f32[2048,256]{1,0:T(8,128)}, f32[8,128]{1,0:T(8,128)}) custom-call(bf16[1280,256]{1,0:T(8,128)(2,1)} %bitcast.356, bf16[1280,256]{1,0:T(8,128)(2,1)} %bitcast.354, f32[2048,256]{1,0:T(8,128)} %refs_3_.1, f32[2048,256]{1,0:T(8,128)} %refs_0_.1, f32[2048,1]{1,0:T(8,128)} %copy.197.centre_ref, f32[8,1280]{1,0:T(8,128)} %select_maximum_fusion.scale_ref, ...), custom_call_target="tpu_custom_call" | custom-call | flops 100000000 | bytes 40000000 | tf_op jit(solution)/shard_map/pallas_call | solution.py:1252
  436.1 13.6 %shard_map.459 = (f32[544,384]{1,0:T(8,128)}, f32[3,3168,128]{2,1,0:T(8,128)}, f32[8,384]{1,0:T(8,128)}) custom-call(s32[1]{0:T(128)} %bitcast.8.refs_0_, f32[544,384]{1,0:T(8,128)} %get-tuple-element.96.refs_1_, f32[544,384]{1,0:T(8,128)} %bitcast.346, f32[544,384]{1,0:T(8,128)} %get-tuple-element.97.refs_3_, f32[544,1536]{1,0:T(8,128)} %get-tuple-element.98.refs_4_, ...), custom_call_target="tpu_custom_call" | custom-call | flops 100000000 | bytes 60000000 | tf_op jit(solution)/shard_map/pallas_call | solution.py:1041
  460.0 16.9 %shard_map.460 = (f32[544,384]{1,0:T(8,128)}, f32[3,1728,128]{2,1,0:T(8,128)}, f32[8,384]{1,0:T(8,128)}) custom-call(s32[1]{0:T(128)} %bitcast.8.refs_0_, f32[544,384]{1,0:T(8,128)} %get-tuple-element.104.refs_1_, f32[544,384]{1,0:T(8,128)} %bitcast.347, bf16[544,1152]{1,0:T(8,128)(2,1)} %get-tuple-element.105.refs_3_, ...), custom_call_target="tpu_custom_call" | custom-call | flops 100000000 | bytes 60000000 | tf_op jit(solution)/shard_map/pallas_call | solution.py:1041
  499.7 10.3 %shard_map.462 = (f32[96,2048]{1,0:T(8,128)}, bf16[96,2048]{1,0:T(8,128)(2,1)}, f32[3,2,2,2,72,128]{5,4,3,2,1,0:T(8,128)}, f32[3,2,2,2,72,128]{5,4,3,2,1,0:T(8,1...) custom-call(s32[10]{0:T(128)} %fusion.74.refs_0_, ...), custom_call_target="tpu_custom_call", output_to_operand_aliasing={{2}: (3, {}), {3}: (4, {}), {4}: (5, {}), {5}: (6, {}), {6}... | custom-call | flops 100000000 | bytes 37000000 | tf_op jit(solution)/shard_map/pallas_call | solution.py:1353
  513.2 10.8 %collective-permute-done.74 = bf16[3,224,128]{2,1,0:T(8,128)(2,1)S(1)} collective-permute-done((bf16[3,224,128]{2,1,0:T(8,128)(2,1)S(1)}, bf16[3,224,128]{2,1,0:T(8,128)(2,1)S(1)}, u32[]{:S(2)}, u32[]{:S(2)}) %collective-permute-start.74) | collective-permute-done | bytes 172064 | tf_op jit(solution)/shard_map/ppermute | solution.py:463
  533.0 5.2 collective-permute-done.67
  549.2 24.0 %collective-permute-done.60 = bf16[3,2,72,128]{3,2,0,1:T(8,128)(2,1)S(1)} collective-permute-done((bf16[3,2,72,128]{3,2,0,1:T(8,128)(2,1)S(1)}, bf16[3,2,72,128]{3,2,0,1:T(8,128)(2,1)S(1)}, u32[]{:S(2)}, u32[]{:S(2)}) %collective-permute-start.60) | collective-permute-done | bytes 110624 | tf_op jit(solution)/shard_map/ppermute | solution.py:463
  (591 shorter events, 314.4 us)
Async XLA Ops:
  7.2 148.8 %all-gather.8.cloned.1.call-start = ((), (), s32[]{:S(2)}) async-start(), calls=%async_computation | async-start | bytes 15040512 | tf_op jit(solution)/shard_map/all_gather | solution.py:1465
  48.0 187.6 %all-gather.10.cloned.1.call-start = ((), (), s32[]{:S(2)}) async-start(), calls=%async_computation.1 | async-start | bytes 13369344 | tf_op jit(solution)/shard_map/all_gather | solution.py:1502
  63.5 28.2 %collective-permute-start.18 = (bf16[320,384]{1,0:T(8,128)(2,1)S(1)}, bf16[320,384]{1,0:T(8,128)(2,1)S(1)}, u32[]{:S(2)}, u32[]{:S(2)}) collective-permute-start(bf16[320,384]{1,0:T(8,128)(2,1)S(1)} %broadcast_select_fusion.14), channel_id=1, source_target_pairs={{0,8},{1,9},{4,12},{5,13},{24,16},{25,17},{28,20},{29,21}} | collective-permute-start | bytes 737288 | tf_op jit(solution)/shard_map/ppermute | solution.py:1482
  65.5 28.2 %collective-permute-start.9 = (bf16[336,384]{1,0:T(8,128)(2,1)S(1)}, bf16[336,384]{1,0:T(8,128)(2,1)S(1)}, u32[]{:S(2)}, u32[]{:S(2)}) collective-permute-start(bf16[336,384]{1,0:T(8,128)(2,1)S(1)} %broadcast_select_fusion.10), channel_id=1, source_target_pairs={{0,24},{1,25},{2,26},{3,27},{4,28},{5,29},{6,30},{7,31}} | collective-permute-start | bytes 774152 | tf_op jit(solution)/shard_map/ppermute | solution.py:1482
  158.2 341.5 %all-gather.12.cloned.1.call-start = ((), (), s32[]{:S(2)}) async-start(), calls=%async_computation.2 | async-start | bytes 12533760 | tf_op jit(solution)/shard_map/all_gather | solution.py:1577
  172.9 57.5 %collective-permute-start.4 = (f32[8,1,80]{2,0,1:T(8,128)S(1)}, f32[8,1,80]{2,0,1:T(8,128)S(1)}, u32[]{:S(2)}, u32[]{:S(2)}) collective-permute-start(f32[8,1,80]{2,0,1:T(8,128)S(1)} %maximum_select_fusion.19), channel_id=1, source_target_pairs={{0,1},{1,0},{2,3},{3,2},{4,5},{5,4},{6,7},{7,6},{8,9},{9,8},{10,11... | collective-permute-start | bytes 7688 | tf_op jit(solution)/shard_map/ppermute | solution.py:444
  244.3 255.4 %all-gather.14.cloned.1.call-start = ((), (), s32[]{:S(2)}) async-start(), calls=%async_computation.3 | async-start | bytes 11837440 | tf_op jit(solution)/shard_map/all_gather | solution.py:1641
  305.3 22.3 %collective-permute-start.35 = (f32[3,1280]{1,0:T(4,128)S(1)}, f32[3,1280]{1,0:T(4,128)S(1)}, u32[]{:S(2)}, u32[]{:S(2)}) collective-permute-start(f32[3,1280]{1,0:T(4,128)S(1)} %add.481), channel_id=1, source_target_pairs={{0,4},{1,5},{2,6},{3,7},{4,0},{5,1},{6,2},{7,3},{8,12},{9,13},{10,... | collective-permute-start | bytes 46088 | tf_op jit(solution)/shard_map/ppermute | solution.py:1611
  352.0 29.4 %collective-permute-start.86 = (f32[4,1,2048]{2,0,1:T(4,128)S(1)}, f32[4,1,2048]{2,0,1:T(4,128)S(1)}, u32[]{:S(2)}, u32[]{:S(2)}) collective-permute-start(f32[4,1,2048]{2,0,1:T(4,128)S(1)} %maximum_select_fusion.15), channel_id=1, source_target_pairs={{0,4},{1,5},{2,6},{3,7},{4,0},{5,1},{6,2},{7,3},{8,12},{9,13},{10,... | collective-permute-start | bytes 98312 | tf_op jit(solution)/shard_map/ppermute | solution.py:444
  381.3 43.6 %collective-permute-start.49 = (f32[3,11,144,128]{3,2,1,0:T(8,128)}, f32[3,11,144,128]{3,2,1,0:T(8,128)}, u32[]{:S(2)}, u32[]{:S(2)}) collective-permute-start(f32[3,11,144,128]{3,2,1,0:T(8,128)} %select_bitcast_fusion.1), channel_id=1, source_target_pairs={{0,1},{1,0},{2,3},{3,2},{4,5},{5,4},{6,7},{7,6},{8,9},{9,8},{10,11... | collective-permute-start | bytes 7299080 | tf_op jit(solution)/shard_map/ppermute | solution.py:463
  381.5 24.0 %collective-permute-start.87 = (f32[8,1,2048]{2,1,0:T(1,128)S(1)}, f32[8,1,2048]{2,1,0:T(1,128)S(1)}, u32[]{:S(2)}, u32[]{:S(2)}) collective-permute-start(f32[8,1,2048]{2,1,0:T(1,128)S(1)} %copy.235), channel_id=1, source_target_pairs={{0,8},{1,9},{2,10},{3,11},{4,12},{5,13},{6,14},{7,15},{8,0},{9,1},... | collective-permute-start | bytes 196616 | tf_op jit(solution)/shard_map/ppermute | solution.py:444
  430.0 23.9 %collective-permute-start.51 = (bf16[3,2,2,2,72,128]{5,4,0,2,3,1:T(8,128)(2,1)S(1)}, bf16[3,2,2,2,72,128]{5,4,0,2,3,1:T(8,128)(2,1)}, u32[]{:S(2)}, u32[]{:S(2)}) collective-permute-start(bf16[3,2,2,2,72,128]{5,4,0,2,3,1:T(8,128)(2,1)S(1)} %fusion.15), channel_id=1, source_target_pairs={{0,24},{1,25},{2,26},{3,27},{4,28},{5,29},{6,30},{7,31},{8,16},{9,... | collective-permute-start | bytes 1327112 | tf_op jit(solution)/shard_map/ppermute | solution.py:463
  432.6 25.7 %collective-permute-start.50 = (bf16[3,2,2,2,72,128]{5,4,0,2,1,3:T(8,128)(2,1)S(1)}, bf16[3,2,2,2,72,128]{5,4,0,2,1,3:T(8,128)(2,1)S(1)}, u32[]{:S(2)}, u32[]{:S(2)}) collective-permute-start(bf16[3,2,2,2,72,128]{5,4,0,2,1,3:T(8,128)(2,1)S(1)} %fusion.14), channel_id=1, source_target_pairs={{0,2},{1,3},{2,0},{3,1},{4,6},{5,7},{6,4},{7,5},{8,10},{9,11},{10,... | collective-permute-start | bytes 1327112 | tf_op jit(solution)/shard_map/ppermute | solution.py:463
  453.9 28.5 %collective-permute-start.53 = (f32[3,11,144,128]{3,2,1,0:T(8,128)}, f32[3,11,144,128]{3,2,1,0:T(8,128)}, u32[]{:S(2)}, u32[]{:S(2)}) collective-permute-start(f32[3,11,144,128]{3,2,1,0:T(8,128)} %select_bitcast_fusion), channel_id=1, source_target_pairs={{0,1},{1,0},{2,3},{3,2},{4,5},{5,4},{6,7},{7,6},{8,9},{9,8},{10,11... | collective-permute-start | bytes 7299080 | tf_op jit(solution)/shard_map/ppermute | solution.py:463
  455.8 23.4 %collective-permute-start.55 = (bf16[3,2,2,72,128]{4,3,0,1,2:T(8,128)(2,1)S(1)}, bf16[3,2,2,72,128]{4,3,0,1,2:T(8,128)(2,1)S(1)}, u32[]{:S(2)}, u32[]{:S(2)}) collective-permute-start(bf16[3,2,2,72,128]{4,3,0,1,2:T(8,128)(2,1)S(1)} %fusion.25), channel_id=1, source_target_pairs={{0,8},{1,9},{2,10},{3,11},{4,12},{5,13},{6,14},{7,15},{8,0},{9,1},... | collective-permute-start | bytes 663560 | tf_op jit(solution)/shard_map/ppermute | solution.py:463
  489.7 39.2 %collective-permute-start.66 = (bf16[3,2,72,128]{3,2,0,1:T(8,128)(2,1)S(1)}, bf16[3,2,72,128]{3,2,0,1:T(8,128)(2,1)}, u32[]{:S(2)}, u32[]{:S(2)}) collective-permute-start(bf16[3,2,72,128]{3,2,0,1:T(8,128)(2,1)S(1)} %fusion.33), channel_id=1, source_target_pairs={{0,24},{1,25},{2,26},{3,27},{4,28},{5,29},{6,30},{7,31},{8,16},{9,... | collective-permute-start | bytes 331784 | tf_op jit(solution)/shard_map/ppermute | solution.py:463
  492.3 39.6 %collective-permute-start.68 = (bf16[3,2,72,128]{3,2,0,1:T(8,128)(2,1)}, bf16[3,2,72,128]{3,2,0,1:T(8,128)(2,1)}, u32[]{:S(2)}, u32[]{:S(2)}) collective-permute-start(bf16[3,2,72,128]{3,2,0,1:T(8,128)(2,1)} %fusion.34), channel_id=1, source_target_pairs={{0,2},{1,3},{2,0},{3,1},{4,6},{5,7},{6,4},{7,5},{8,10},{9,11},{10,... | collective-permute-start | bytes 331784 | tf_op jit(solution)/shard_map/ppermute | solution.py:463
  494.3 32.0 %collective-permute-start.58 = (bf16[3,2,2,2,72,128]{5,4,0,2,1,3:T(8,128)(2,1)S(1)}, bf16[3,2,2,2,72,128]{5,4,0,2,1,3:T(8,128)(2,1)}, u32[]{:S(2)}, u32[]{:S(2)}) collective-permute-start(bf16[3,2,2,2,72,128]{5,4,0,2,1,3:T(8,128)(2,1)S(1)} %fusion.16), channel_id=1, source_target_pairs={{0,2},{1,3},{2,0},{3,1},{4,6},{5,7},{6,4},{7,5},{8,10},{9,11},{10,... | collective-permute-start | bytes 1327112 | tf_op jit(solution)/shard_map/ppermute | solution.py:463
  494.4 33.5 %collective-permute-start.62 = (bf16[3,2,2,2,72,128]{5,4,0,2,3,1:T(8,128)(2,1)S(1)}, bf16[3,2,2,2,72,128]{5,4,0,2,3,1:T(8,128)(2,1)S(1)}, u32[]{:S(2)}, u32[]{:S(2)}) collective-permute-start(bf16[3,2,2,2,72,128]{5,4,0,2,3,1:T(8,128)(2,1)S(1)} %fusion.17), channel_id=1, source_target_pairs={{0,24},{1,25},{2,26},{3,27},{4,28},{5,29},{6,30},{7,31},{8,16},{9,... | collective-permute-start | bytes 1327112 | tf_op jit(solution)/shard_map/ppermute | solution.py:463
  542.3 41.4 %collective-permute-start.57 = (bf16[96,2048]{1,0:T(8,128)(2,1)S(1)}, bf16[96,2048]{1,0:T(8,128)(2,1)S(1)}, u32[]{:S(2)}, u32[]{:S(2)}) collective-permute-start(bf16[96,2048]{1,0:T(8,128)(2,1)S(1)} %copy-done.43), channel_id=1, source_target_pairs={{16,8},{17,9},{18,10},{19,11},{20,12},{21,13},{22,14},{23,15},{24,... | collective-permute-start | bytes 1179656 | tf_op jit(solution)/shard_map/ppermute | solution.py:1774
  543.8 31.1 %collective-permute-start.72 = (bf16[3,224,128]{2,1,0:T(8,128)(2,1)S(1)}, bf16[3,224,128]{2,1,0:T(8,128)(2,1)S(1)}, u32[]{:S(2)}, u32[]{:S(2)}) collective-permute-start(bf16[3,224,128]{2,1,0:T(8,128)(2,1)S(1)} %fusion.79), channel_id=1, source_target_pairs={{0,24},{1,25},{2,26},{3,27},{4,28},{5,29},{6,30},{7,31},{8,16},{9,... | collective-permute-start | bytes 516104 | tf_op jit(solution)/shard_map/ppermute | solution.py:463
  546.6 30.5 %collective-permute-start.76 = (bf16[3,224,128]{2,1,0:T(8,128)(2,1)S(1)}, bf16[3,224,128]{2,1,0:T(8,128)(2,1)S(1)}, u32[]{:S(2)}, u32[]{:S(2)}) collective-permute-start(bf16[3,224,128]{2,1,0:T(8,128)(2,1)S(1)} %fusion.80), channel_id=1, source_target_pairs={{0,2},{1,3},{2,0},{3,1},{4,6},{5,7},{6,4},{7,5},{8,10},{9,11},{10,... | collective-permute-start | bytes 516104 | tf_op jit(solution)/shard_map/ppermute | solution.py:463
  548.9 24.3 %collective-permute-start.60 = (bf16[3,2,72,128]{3,2,0,1:T(8,128)(2,1)S(1)}, bf16[3,2,72,128]{3,2,0,1:T(8,128)(2,1)S(1)}, u32[]{:S(2)}, u32[]{:S(2)}) collective-permute-start(bf16[3,2,72,128]{3,2,0,1:T(8,128)(2,1)S(1)} %fusion.31), channel_id=1, source_target_pairs={{0,24},{1,25},{2,26},{3,27},{4,28},{5,29},{6,30},{7,31},{8,16},{9,... | collective-permute-start | bytes 331784 | tf_op jit(solution)/shard_map/ppermute | solution.py:463
  549.1 24.3 %collective-permute-start.64 = (bf16[3,2,72,128]{3,2,0,1:T(8,128)(2,1)S(1)}, bf16[3,2,72,128]{3,2,0,1:T(8,128)(2,1)S(1)}, u32[]{:S(2)}, u32[]{:S(2)}) collective-permute-start(bf16[3,2,72,128]{3,2,0,1:T(8,128)(2,1)S(1)} %fusion.32), channel_id=1, source_target_pairs={{0,2},{1,3},{2,0},{3,1},{4,6},{5,7},{6,4},{7,5},{8,10},{9,11},{10,... | collective-permute-start | bytes 331784 | tf_op jit(solution)/shard_map/ppermute | solution.py:463
  (131 other events, 1039.0 us)
Sparse Core Ops, SparseCore 0:
  48.1 107.8 all-gather.7
  158.3 66.5 all-gather.9
  244.4 69.6 all-gather.11
  341.1 66.9 all-gather.13

commit v8 on v7

--- a/solution.py
+++ b/solution.py
@@ -577,7 +577,9 @@
     )(place, stems, after, layer_rows, before)
 
 
-def shards_kernel(place_ref, head_ref, previous_ref, block_ref, behind_ref, stem_ref, layer_ref, line_ref, flat_ref):
+def shards_kernel(held, place_ref, head_ref, previous_ref, block_ref, behind_ref, *refs):
+    stem_ref, layer_ref = refs[held : held + 2]
+    line_ref, flat_ref = refs[-2:]
     per_row = ROW // 128
     extra = previous_ref.shape[0]
     slot = head_ref.shape[0]
@@ -595,21 +597,25 @@
         layer_ref[part] = shifted(flat_ref, place_ref[2], place_ref[3], 0, layer_ref.shape[1], 1)
 
 
-def own_shards(place, head_grad, previous, block_grad, behind, stem_lines, layer_lines):
+def own_shards(place, head_grad, previous, block_grad, behind, stem_lines, layer_lines, held):
     per_row = ROW // 128
     lines = (head_grad.shape[0] + previous.shape[0]) * per_row + 256
     flats = max(block_grad.shape[2] * 3 + 18, layer_lines + 18) + 16
     return pl.pallas_call(
-        shards_kernel,
+        lambda *refs: shards_kernel(len(held), *refs),
         out_shape=[
             jax.ShapeDtypeStruct((stem_lines, 128), single),
             jax.ShapeDtypeStruct((block_grad.shape[0], layer_lines, 128), single),
-        ],
-        in_specs=[pl.BlockSpec(memory_space=pltpu.SMEM)] + [pl.BlockSpec(memory_space=pltpu.VMEM)] * 4,
-        out_specs=[pl.BlockSpec(memory_space=pltpu.VMEM)] * 2,
+        ]
+        + [jax.ShapeDtypeStruct(array.shape, array.dtype) for array in held],
+        in_specs=[pl.BlockSpec(memory_space=pltpu.SMEM)]
+        + [pl.BlockSpec(memory_space=pltpu.VMEM)] * 4
+        + [pl.BlockSpec(memory_space=pl.ANY)] * len(held),
+        out_specs=[pl.BlockSpec(memory_space=pltpu.VMEM)] * 2 + [pl.BlockSpec(memory_space=pl.ANY)] * len(held),
+        input_output_aliases={5 + number: 2 + number for number in range(len(held))},
         scratch_shapes=[pltpu.VMEM((lines, 128), single), pltpu.VMEM((flats, 128), single)],
         compiler_params=pltpu.CompilerParams(vmem_limit_bytes=40 << 20),
-    )(place, head_grad, previous, block_grad, behind)
+    )(place, head_grad, previous, block_grad, behind, *held)
 
 
 PAD_SEQ = 272
@@ -1222,9 +1228,9 @@
 
 
 def proto_grad_kernel(
-    teacher_z_ref, student_z_ref, teacher_ref, student_ref, centre_ref, scale_ref, *refs
+    held, teacher_z_ref, student_z_ref, teacher_ref, student_ref, centre_ref, scale_ref, *refs
 ):
-    grad_ref, square_ref = refs[-2:]
+    grad_ref, square_ref = refs[held : held + 2]
     step = pl.program_id(0)
 
     @pl.when(step == 0)
@@ -1245,23 +1251,26 @@
     square_ref[...] += jnp.broadcast_to(jnp.sum(grad * grad), square_ref.shape)
 
 
-def proto_grad_pass(teacher_z, student_z, teacher, student, centre_column, scale_lines, waits):
+def proto_grad_pass(teacher_z, student_z, teacher, student, centre_column, scale_lines, held):
     rows, protos_here = teacher_z.shape[0], student.shape[0]
     block = protos_here // 4
     whole, table, column, lines = proto_specs(rows, block)
     return pl.pallas_call(
-        proto_grad_kernel,
+        lambda *refs: proto_grad_kernel(len(held), *refs),
         grid=(4,),
         out_shape=[
             jax.ShapeDtypeStruct((protos_here, BOT), single),
             jax.ShapeDtypeStruct((8, 128), single),
-        ],
+        ]
+        + [jax.ShapeDtypeStruct(array.shape, array.dtype) for array in held],
         in_specs=[whole, whole, table, table, column, lines]
-        + [pl.BlockSpec(memory_space=pl.ANY)] * len(waits),
-        out_specs=[table, pl.BlockSpec((8, 128), lambda i: (0, 0))],
+        + [pl.BlockSpec(memory_space=pl.ANY)] * len(held),
+        out_specs=[table, pl.BlockSpec((8, 128), lambda i: (0, 0))]
+        + [pl.BlockSpec(memory_space=pl.ANY)] * len(held),
+        input_output_aliases={6 + number: 2 + number for number in range(len(held))},
         compiler_params=pltpu.CompilerParams(vmem_limit_bytes=56 << 20),
         cost_estimate=pl.CostEstimate(flops=100 * 10**6, bytes_accessed=400 * 10**5, transcendentals=0),
-    )(teacher_z, student_z, teacher, student, centre_column, scale_lines, *waits)
+    )(teacher_z, student_z, teacher, student, centre_column, scale_lines, *held)
 
 
 def proto_update(factor, student, moment, second, teacher, grad):
@@ -1672,7 +1681,10 @@
         pairs_of = weight_grad.reshape(D // 128, -1, 2, rows, 128)
         return move(*cut(pairs_of, "pc", "c", 1)[:2], "c")
 
-    def start(late, early):
+    def core_cut(weight_grad, rows):
+        return cut(weight_grad.reshape(D // 128, -1, 2, rows, 128), "pc", "c", 1)[:2]
+
+    def start(late, early, *others):
         shared_pair = 4 * D // (2 * block_rows)
         whole = jnp.concatenate(
             [
@@ -1682,8 +1694,9 @@
             ],
             axis=1,
         )
-        by_bits = whole.reshape((D // 128, 2, 2, 2, 2, block_rows, 128))
-        return (cuts(halves(by_bits), ["bayx"] * 2, rounds[0]), 0)
+        parts = [jnp.concatenate(pieces, axis=2) for pieces in zip(*[halves(array) for array in (whole, *others)])]
+        by_bits = [part.reshape((D // 128, 2, 2, 2, 2) + part.shape[2:]) for part in parts]
+        return (cuts(by_bits, ["bayx"] * 2, rounds[0]), 0)
 
     rounds = (("x", "b"), ("y", "a"), ("b", "x"), ("a", "y"))
 
@@ -1701,8 +1714,24 @@
     def sends(states):
         return tuple(sent for pieces, stage in states for sent, kept, left in pieces)
 
+    def block_place(i):
+        column = max(bounds[i], 0) // 128 * 128
+        grad_column = 0 if i < first_w2 else HID
+        return [column, bounds[i] - column if i else 0, sizes[i] if i else 0, grad_column]
+
+    def third_place(i):
+        return [0, 0, sizes[i], 0]
+
+    place = per_device(
+        [
+            (third_place(i) if i >= first_w3 else block_place(i))
+            + block_place(i ^ across)
+            + [int(i >= first_w3), D + HID + max(bounds[i] - D - HID, 0) * (ROW // BOT)]
+            for i in range(count)
+        ]
+    )
     started = []
-    waits, later_waits = (stages[4],), (stages[5],)
+    waits, later_waits = (), ()
     for layer_index in reversed(range(LAYERS)):
         saved, vectors = saved_layers[layer_index], vectors_all[1, layer_index]
         part = LAYERS + layer_index
@@ -1714,95 +1743,80 @@
         grad_stream, early_grad, early_vectors = attention_back(
             side, grad_stream, saved, vectors, gathered, part, later_waits + sends(started)
         )
-        waits, later_waits = (), ()
         vector_grads[layer_index] = (late_vectors + early_vectors)[:6]
         if layer_index == LAYERS - 1:
-            proto_grad, proto_square = proto_grad_pass(
-                teacher_z_all,
-                student_z_all,
-                proto_teacher,
-                protos,
-                centre_column,
-                lines(student_scale, teacher_scale),
-                (early_vectors,),
+            sent, stay = core_cut(early_grad, block_rows)
+            own_block_grad, partner_block_grad, stay = head_grads(
+                place, inputs_all, grads_all, slot, -min(bounds[1], 0), (early_vectors,), [stay]
             )
-            waits = (proto_square,)
+            block_got = lax.ppermute(partner_block_grad, "dev", [(i, i ^ across) for i in range(half, count)])
+            waits, later_waits = (own_block_grad, stages[4]), (stages[5], block_got, new_centre)
         started = [advance(state) for state in started]
-        started.append(start(late, over_core(early_grad, block_rows)))
-    *later_states, last = started
-    small_rows = -(-(EMBED_ROWS + 6 * LAYERS) // 64) * 64
+        if layer_index > 0:
+            started.append(start(late, move(sent, stay, "c")))
+    head_block_grad = jnp.where(student_side, own_block_grad, block_got.astype(single))
+    early = over_core(early_grad, block_rows)
+    small_rows = -(-(EMBED_ROWS + 6 * LAYERS) // (16 * count)) * 16
     small = embed_back(
         grad_stream,
         patches.reshape(images_here * PATCHES, PIX),
         jnp.where(masked_here, 0.0, 1.0).reshape(images_here * PATCHES, 1),
         jnp.stack([grad_gain, grad_bias]),
         jnp.concatenate(vector_grads),
-        small_rows,
-        sends([last]),
-    )
-    small_parts = halves(over_core(small, small_rows // 2)[:, 0])
-    small_sends = [part.astype(narrow) for part in small_parts]
-    def block_place(i):
-        column = max(bounds[i], 0) // 128 * 128
-        grad_column = 0 if i < first_w2 else HID
-        return [column, bounds[i] - column if i else 0, sizes[i] if i else 0, grad_column]
-
-    def third_place(i):
-        return [0, 0, sizes[i], 0]
-
-    place = per_device(
-        [
-            (third_place(i) if i >= first_w3 else block_place(i))
-            + block_place(i ^ across)
-            + [int(i >= first_w3), D + HID + max(bounds[i] - D - HID, 0) * (ROW // BOT)]
-            for i in range(count)
-        ]
-    )
-    flying = [last] + later_states
-    own_block_grad, partner_block_grad, *held = head_grads(
-        place,
-        inputs_all,
-        grads_all,
-        slot,
-        -min(bounds[1], 0),
+        small_rows * count,
         (),
-        [stay for pieces, stage in flying for sent, stay, left in pieces] + small_parts,
-    )
+    )
+    started.append(start(late, early, over_core(small, small_rows)))
+    last_rows = lax.dynamic_slice(
+        head_block_grad, (jnp.array(sizes, jnp.int32)[me] - GROUP, 0), (GROUP, ROW)
+    )
+    previous = lax.ppermute(last_rows, "dev", step_pairs(count, 1))
+    proto_grad, proto_square, *held = proto_grad_pass(
+        teacher_z_all,
+        student_z_all,
+        proto_teacher,
+        protos,
+        centre_column,
+        lines(student_scale, teacher_scale),
+        [previous] + [stay for pieces, stage in started for sent, stay, left in pieces],
+    )
+    previous, *held = held
     held = iter(held)
-    flying = [([(sent, next(held), left) for sent, _, left in pieces], stage) for pieces, stage in flying]
-    small_parts = list(held)
-    block_got = lax.ppermute(partner_block_grad, "dev", [(i, i ^ across) for i in range(half, count)])
-    head_block_grad = jnp.where(student_side, own_block_grad, block_got.astype(single))
-    small_parts = moves([(sent, part, "") for sent, part in zip(small_sends, small_parts)], rounds[0])
-    for order in rounds[1:]:
-        small_parts = [move(part.astype(narrow), part, axis) for part, axis in zip(small_parts, order)]
-    small_mine = jnp.concatenate(small_parts, axis=1)
-    small_other = lax.ppermute(small_mine, "dev", pairs(count, 1))
-    small_sum = jnp.where(
-        me % 2 == 0,
-        jnp.concatenate([small_mine, small_other], axis=1),
-        jnp.concatenate([small_other, small_mine], axis=1),
-    )
-    blocks = [jnp.concatenate(finish(state), axis=1) for state in flying]
-    layer_block = jnp.stack(blocks[:1] + blocks[:0:-1])
+    started = [([(sent, next(held), left) for sent, _, left in pieces], stage) for pieces, stage in started]
+    blocks = [finish(state) for state in started][::-1]
+    middle_row = block_rows // 2
+    layer_block = jnp.stack([jnp.concatenate([part[:, :middle_row] for part in parts], axis=1) for parts in blocks])
+    small_block = jnp.concatenate([part[:, middle_row:] for part in blocks[0]], axis=1)
 
     square_local = (
         jnp.sum(head_block_grad * head_block_grad)
         + jnp.sum(layer_block * layer_block)
-        + jnp.where(me == 0, jnp.sum(small_sum * small_sum), 0.0)
+        + jnp.sum(small_block * small_block)
         + proto_square[0, 0]
     )
-    square_total = cube_sum(square_local.reshape(1, 1))[0, 0]
+    high = square_local.astype(narrow)
+    middle = (square_local - high.astype(single)).astype(narrow)
+    low = (square_local - high.astype(single) - middle.astype(single)).astype(narrow)
+    tile = jnp.pad(jnp.stack([high, middle, low]).reshape(1, 1, 3), ((0, 0), (0, 15), (0, 125)))
+    first_rows = small_block[:2].astype(narrow)
+    other_rows = jnp.concatenate([small_block[2:].astype(narrow), tile], axis=1)
+    first_rows = cube_gather(first_rows, "xya")
+    other_rows = cube_gather(other_rows, "abx")
     behind = lax.ppermute(layer_block[:, :, :6], "dev", step_pairs(count, -1))
-    last_rows = lax.dynamic_slice(
-        head_block_grad, (jnp.array(sizes, jnp.int32)[me] - GROUP, 0), (GROUP, ROW)
-    )
-    previous = lax.ppermute(last_rows, "dev", step_pairs(count, 1))
     place = per_device([spots(head_span - starts[i], drift * i) for i in range(count)])
-    stem_lines, layer_lines = own_shards(
-        place, head_block_grad, previous, layer_block, behind, lane_rows(stem_piece), lane_rows(layer_piece)
-    )
-    small_all = jnp.swapaxes(small_sum, 0, 1).reshape(small_rows, D)
+    stem_lines, layer_lines, first_rows, other_rows = own_shards(
+        place, head_block_grad, previous, layer_block, behind, lane_rows(stem_piece), lane_rows(layer_piece),
+        [first_rows, other_rows],
+    )
+    first_rows = jnp.moveaxis(cube_gather(first_rows, "bc").reshape((2, 2, 8) + first_rows.shape[1:]), 0, 2)
+    other_rows = cube_gather(other_rows, "yc")
+    other_rows = other_rows.reshape((2,) * 5 + other_rows.shape[2:])
+    other_rows = jnp.transpose(other_rows, (3, 4, 1, 2, 0, 5, 6, 7))
+    first_rows = first_rows.reshape((count,) + first_rows.shape[3:])
+    other_rows = other_rows.reshape((count,) + other_rows.shape[5:])
+    square_total = jnp.sum(other_rows[:, 0, small_rows, :3].astype(single))
+    small_all = jnp.concatenate([first_rows, other_rows[:, :, :small_rows]], axis=1).astype(single)
+    small_all = jnp.transpose(small_all, (0, 2, 1, 3)).reshape(small_rows * count, D)
     embed_grad = small_all[:EMBED_ROWS].reshape(-1)
     vector_grad = small_all[EMBED_ROWS : EMBED_ROWS + 6 * LAYERS].reshape(LAYERS, 6 * D)
     layer_grad = layer_lines.reshape(LAYERS, -1)[:, :layer_piece]

time: 660 us -> 643 us (0.974)
  waiting for transfers between devices: 224 us -> 204 us
  local copies, waits for them, and re-layouts: 48.8 us -> 60.5 us
    ppermute x37 -> x29, waiting for transfers between devices: 74 us -> 39.6 us  [move(): lax.ppermute(sent, 'dev', pairs(1 << len(BITS), MASKS[name])).astype(single)]
    ppermute x1, waiting for transfers between devices: 0.01 us -> 13.6 us  [close_local(): lax.ppermute(partner_block_grad, 'dev', [(i, i ^ across) for i in range(h...]
    ppermute x19 -> x29, starting transfers between devices: 11.4 us -> 22.2 us  [cube_gather(): got = lax.ppermute(held, 'dev', pairs(count, MASKS[name]))]
    unnamed x126 -> x129, local copies, waits for them, and re-layouts: 8.24 us -> 18.9 us
    ppermute x6 -> x0, starting transfers between devices: 9.71 us -> none  [the longest x5 9.7 us: cube_sum(): lax.ppermute(values, 'dev', pairs(1 << len(BITS), MASKS[name]))]
    ppermute x37 -> x29, starting transfers between devices: 36 us -> 28.7 us  [move(): lax.ppermute(sent, 'dev', pairs(1 << len(BITS), MASKS[name])).astype(single)]
    ppermute x19 -> x29, waiting for transfers between devices: 36.6 us -> 43.5 us  [cube_gather(): got = lax.ppermute(held, 'dev', pairs(count, MASKS[name]))]
  transfers between devices with their start and end apart: 95 -> 91, of which waited for: 43 -> 42; matrix products, arithmetic and copies ran while one was open for 17% -> 15% of each run, Pallas kernels for 24% -> 25%
where the time goes in v8:
time: 643 us; the launch traced here: 632 us
  waiting for transfers between devices  204 us (32%)
  Pallas kernels  174 us (27%)
  starting transfers between devices  91.6 us (14%)
  other arithmetic  77 us (12%)
  local copies, waits for them, and re-layouts  60.5 us (9%)
  between operations  23.5 us (4%)
    pallas_call x4, Pallas kernels, layer_back(): pl.pallas_call(lambda *refs: kernel(part, *refs), out_shape=[jax.ShapeDty...  60.6 us
    pallas_call x4, Pallas kernels, layer_forward(): pl.pallas_call(lambda *refs: forward_kernel(part, keep, *refs), out_shape...  47.9 us
    ppermute x29, waiting for transfers between devices, cube_gather(): got = lax.ppermute(held, 'dev', pairs(count, MASKS[name]))  43.5 us
    ppermute x29, waiting for transfers between devices, move(): lax.ppermute(sent, 'dev', pairs(1 << len(BITS), MASKS[name])).astype(single)  39.6 us
    ppermute x12, waiting for transfers between devices, close_local(): got = lax.ppermute(spread, 'dev', moves)  38.9 us
    ppermute x29, starting transfers between devices, move(): lax.ppermute(sent, 'dev', pairs(1 << len(BITS), MASKS[name])).astype(single)  28.7 us
    ppermute x29, starting transfers between devices, cube_gather(): got = lax.ppermute(held, 'dev', pairs(count, MASKS[name]))  22.2 us
    ppermute x1, waiting for transfers between devices, close_local(): other_layers = lax.ppermute(layer_blocks, 'dev', pairs(count, across))  20.2 us
  transfers between devices with their start and end apart: 91, of which 42 were waited for; matrix products, arithmetic and copies ran while one was open for 15% of the time, Pallas kernels for 25%

profile of v8, /device:TPU:8, one launch (start us, length us, event | category | flops | bytes accessed | tf_op | source)
XLA Modules:
  0.0 631.7 jit_solution(14677412634742456195)
XLA Ops:
  26.6 20.2 %collective-permute-done.21 = bf16[4,144,384]{2,1,0:T(8,128)(2,1)S(1)} collective-permute-done((bf16[4,144,384]{2,1,0:T(8,128)(2,1)S(1)}, bf16[4,144,384]{2,1,0:T(8,128)(2,1)S(1)}, u32[]{:S(2)}, u32[]{:S(2)}) %collective-permute-start.21) | collective-permute-done | bytes 442400 | tf_op jit(solution)/shard_map/ppermute | solution.py:1468
  66.2 15.0 %collective-permute-done.12 = bf16[336,384]{1,0:T(8,128)(2,1)S(1)} collective-permute-done((bf16[336,384]{1,0:T(8,128)(2,1)S(1)}, bf16[336,384]{1,0:T(8,128)(2,1)S(1)}, u32[]{:S(2)}, u32[]{:S(2)}) %collective-permute-start.12) | collective-permute-done | bytes 258080 | tf_op jit(solution)/shard_map/ppermute | solution.py:1491
  83.2 8.5 %collective-permute-done.18 = bf16[320,384]{1,0:T(8,128)(2,1)S(1)} collective-permute-done((bf16[320,384]{1,0:T(8,128)(2,1)S(1)}, bf16[320,384]{1,0:T(8,128)(2,1)S(1)}, u32[]{:S(2)}, u32[]{:S(2)}) %collective-permute-start.18) | collective-permute-done | bytes 245792 | tf_op jit(solution)/shard_map/ppermute | solution.py:1491
  101.5 12.2 %collective-permute-done.10 = bf16[336,384]{1,0:T(8,128)(2,1)S(1)} collective-permute-done((bf16[336,384]{1,0:T(8,128)(2,1)S(1)}, bf16[336,384]{1,0:T(8,128)(2,1)S(1)}, u32[]{:S(2)}, u32[]{:S(2)}) %collective-permute-start.10) | collective-permute-done | bytes 258080 | tf_op jit(solution)/shard_map/ppermute | solution.py:1491
  119.2 17.7 %collective-permute-done.23 = bf16[96,2048]{1,0:T(8,128)(2,1)S(1)} collective-permute-done((bf16[96,2048]{1,0:T(8,128)(2,1)S(1)}, bf16[96,2048]{1,0:T(8,128)(2,1)S(1)}, u32[]{:S(2)}, u32[]{:S(2)}) %collective-permute-start.23) | collective-permute-done | bytes 393248 | tf_op jit(solution)/shard_map/ppermute | solution.py:1477
  139.4 16.6 %all-gather.8.cloned.1.call-done.refs_3_.refs_1_.refs_7_.refs_6_ = bf16[16,2,4,144,384]{4,3,2,1,0:T(8,128)(2,1)} async-done(((bf16[1,2,4,144,384]{4,3,2,1,0:T(8,128)(2,1)}), bf16[16,2,4,144,384]{4,3,2,1,0:T(8,128)(2,1)}) %all-gather.8.cloned.1.call-update) | async-done | bytes 14155792 | tf_op jit(solution)/shard_map/all_gather | solution.py:1474
  177.2 11.5 %shard_map.448.refs_1_ = f32[544,384]{1,0:T(8,128)} custom-call(s32[1]{0:T(128)} %bitcast.8.refs_0_, f32[544,384]{1,0:T(8,128)} %bitcast.403, bf16[8,384]{1,0:T(8,128)(2,1)} %get-tuple-element.211.refs_2_, bf16[16,2,4,144,384]{4,3,2,1,0:T(8,128)(2,1)} %all-gather.8.cloned.1.call-done.refs_3_.refs_1_.refs_7_.refs_6_), custom_call_target="tpu_custom_call" | custom-call | flops 100000000 | bytes 43000000 | tf_op jit(solution)/shard_map/pallas_call | solution.py:916
  188.7 11.8 %shard_map.449 = f32[544,384]{1,0:T(8,128)} custom-call(s32[1]{0:T(128)} %bitcast.8.refs_0_, f32[544,384]{1,0:T(8,128)} %shard_map.448.refs_1_, bf16[8,384]{1,0:T(8,128)(2,1)} %get-tuple-element.210.refs_2_, bf16[16,2,4,144,384]{4,3,2,1,0:T(8,128)(2,1)} %all-gather.8.cloned.1.call-done.refs_3_.refs_1_.refs_7_.refs_6_), custom_call_target="tpu_custom_call" | custom-call | flops 100000000 | bytes 43000000 | tf_op jit(solution)/shard_map/pallas_call | solution.py:916
  202.5 12.1 %shard_map.450 = (f32[544,384]{1,0:T(8,128)}, bf16[544,1152]{1,0:T(8,128)(2,1)}, bf16[544,384]{1,0:T(8,128)(2,1)}, f32[544,384]{1,0:T(8,128)}, f32[544,1536]{1,0:T(8,128)}, /*index=5*/f32[544,384]{1,0:T(8,128)}) custom-call(s32[1]{0:T(128)} %bitcast.8.refs_0_, f32[544,384]{1,0:T(8,128)} %bitcast.384, ...), custom_call_target="tpu_custom_call" | custom-call | flops 100000000 | bytes 43000000 | tf_op jit(solution)/shard_map/pallas_call | solution.py:916
  214.6 12.5 %shard_map.451 = (f32[544,384]{1,0:T(8,128)}, bf16[544,1152]{1,0:T(8,128)(2,1)}, bf16[544,384]{1,0:T(8,128)(2,1)}, f32[544,384]{1,0:T(8,128)}, f32[544,1536]{1,0:T(8,128)}, /*index=5*/f32[544,384]{1,0:T(8,128)}) custom-call(s32[1]{0:T(128)} %bitcast.8.refs_0_, f32[544,384]{1,0:T(8,128)} %get-tuple-element.80.refs_1_.refs_2_, ...), custom_call_target="tpu_custom_call" | custom-call | flops 100000000 | bytes 43000000 | tf_op jit(solution)/shard_map/pallas_call | solution.py:916
  235.3 8.7 %shard_map.453 = (bf16[80,256]{1,0:T(8,128)(2,1)}, bf16[80,4608]{1,0:T(8,128)(2,1)}, f32[80,256]{1,0:T(8,128)}, f32[80,2048]{1,0:T(8,128)}, f32[80,2048]{1,0:T(8,128)}) custom-call(s32[1]{0:T(128)} %bitcast.8.refs_0_, bf16[80,384]{1,0:T(8,128)(2,1)} %pad.45.refs_1_, bf16[16,2,96,2048]{3,2,1,0:T(8,128)(2,1)} %bitcast.376, f32[1280]{0:T(1024)} %select_n.1386.refs_3_), custom_call_target="tpu_custom_call" | custom-call | flops 100000000 | bytes 37000000 | tf_op jit(solution)/shard_map/pallas_call | solution.py:761
  274.6 14.0 %shard_map.454 = (f32[1280,640]{1,0:T(8,128)}, f32[8,1280]{1,0:T(8,128)}, f32[2048,1]{1,0:T(8,128)}) custom-call(bf16[1280,256]{1,0:T(8,128)(2,1)} %bitcast.397, bf16[1280,256]{1,0:T(8,128)(2,1)} %bitcast.395, f32[2048,256]{1,0:T(8,128)} %refs_3_.3, f32[2048,256]{1,0:T(8,128)} %refs_0_.1, f32[2048,1]{1,0:T(8,128)} %copy.200.centre_ref.refs_4_, ...), custom_call_target="tpu_custom_call" | custom-call | flops 100000000 | bytes 52000000 | tf_op jit(solution)/shard_map/pallas_call | solution.py:1210
  295.5 8.2 %collective-permute-done.39 = bf16[2,2,80,256]{3,2,1,0:T(8,128)(2,1)S(1)} collective-permute-done((bf16[2,2,80,256]{3,2,1,0:T(8,128)(2,1)S(1)}, bf16[2,2,80,256]{3,2,1,0:T(8,128)(2,1)S(1)}, u32[]{:S(2)}, u32[]{:S(2)}) %collective-permute-start.39) | collective-permute-done | bytes 163872 | tf_op jit(solution)/shard_map/ppermute | solution.py:463
  308.5 6.0 collective-permute-done.43
  330.5 10.9 %shard_map.455 = (bf16[80,4352]{1,0:T(8,128)(2,1)}, f32[80,384]{1,0:T(8,128)}) custom-call(s32[1]{0:T(128)} %bitcast.8.refs_0_, f32[80,256]{1,0:T(8,128)} %fusion.31.refs_1_, f32[80,256]{1,0:T(8,128)} %get-tuple-element.87.refs_2_, f32[80,2048]{1,0:T(8,128)} %get-tuple-element.88.refs_3_, f32[80,2048]{1,0:T(8,128)} %get-tuple-element.89.refs_4_, ...), custom_call_target="tpu_custom_call" | custom-call | flops 100000000 | bytes 37000000 | tf_op jit(solution)/shard_map/pallas_call | solution.py:761
  358.8 13.8 %shard_map.456 = (f32[544,384]{1,0:T(8,128)}, f32[3,3168,128]{2,1,0:T(8,128)}, f32[8,384]{1,0:T(8,128)}) custom-call(s32[1]{0:T(128)} %bitcast.8.refs_0_, f32[544,384]{1,0:T(8,128)} %bitcast.394, f32[544,384]{1,0:T(8,128)} %get-tuple-element.80.refs_1_.refs_2_, f32[544,384]{1,0:T(8,128)} %get-tuple-element.92.refs_3_, ...), custom_call_target="tpu_custom_call" | custom-call | flops 100000000 | bytes 60000000 | tf_op jit(solution)/shard_map/pallas_call | solution.py:1047
  377.9 5.5 collective-permute-start.36
  391.3 16.7 %shard_map.457 = (f32[544,384]{1,0:T(8,128)}, f32[3,1728,128]{2,1,0:T(8,128)}, f32[8,384]{1,0:T(8,128)}) custom-call(s32[1]{0:T(128)} %bitcast.8.refs_0_, f32[544,384]{1,0:T(8,128)} %get-tuple-element.95.refs_1_, f32[544,384]{1,0:T(8,128)} %get-tuple-element.80.refs_1_.refs_2_, bf16[544,1152]{1,0:T(8,128)(2,1)} %get-tuple-element.96.refs_3_, ...), custom_call_target="tpu_custom_call" | custom-call | flops 100000000 | bytes 60000000 | tf_op jit(solution)/shard_map/pallas_call | solution.py:1047
  411.9 5.3 collective-permute-done.60
  422.4 10.1 %shard_map.458 = (f32[96,2048]{1,0:T(8,128)}, bf16[96,2048]{1,0:T(8,128)(2,1)}, f32[3,6,144,128]{3,2,1,0:T(8,128)}) custom-call(s32[10]{0:T(128)} %fusion.76.refs_0_, bf16[1280,4608]{1,0:T(8,128)(2,1)} %all-gather.12.cloned.1.call-done.refs_1_, bf16[1280,4352]{1,0:T(8,128)(2,1)} %all-gather.14.cloned.1.call-done.refs_2_, ...), custom_call_target="tpu_custom_call", output_to_operand_aliasing={{2}: (4, {})} | custom-call | flops 100000000 | bytes 37000000 | tf_op jit(solution)/shard_map/pallas_call | solution.py:1362
  444.5 13.6 %shard_map.459 = (f32[544,384]{1,0:T(8,128)}, f32[3,3168,128]{2,1,0:T(8,128)}, f32[8,384]{1,0:T(8,128)}) custom-call(s32[1]{0:T(128)} %bitcast.8.refs_0_, f32[544,384]{1,0:T(8,128)} %get-tuple-element.104.refs_1_, f32[544,384]{1,0:T(8,128)} %bitcast.385, f32[544,384]{1,0:T(8,128)} %get-tuple-element.105.refs_3_, f32[544,1536]{1,0:T(8,128)} %get-tuple-element.106.refs_4_, ...), custom_call_target="tpu_custom_call" | custom-call | flops 100000000 | bytes 60000000 | tf_op jit(solution)/shard_map/pallas_call | solution.py:1047
  462.4 13.6 %collective-permute-done.48.refs_8_ = bf16[96,2048]{1,0:T(8,128)(2,1)S(1)} collective-permute-done((bf16[96,2048]{1,0:T(8,128)(2,1)S(1)}, bf16[96,2048]{1,0:T(8,128)(2,1)S(1)}, u32[]{:S(2)}, u32[]{:S(2)}) %collective-permute-start.48) | collective-permute-done | bytes 393248 | tf_op jit(solution)/shard_map/ppermute | solution.py:1752
  482.5 16.4 %shard_map.460 = (f32[544,384]{1,0:T(8,128)}, f32[3,1728,128]{2,1,0:T(8,128)}, f32[8,384]{1,0:T(8,128)}) custom-call(s32[1]{0:T(128)} %bitcast.8.refs_0_, f32[544,384]{1,0:T(8,128)} %get-tuple-element.108.refs_1_, f32[544,384]{1,0:T(8,128)} %bitcast.386, bf16[544,1152]{1,0:T(8,128)(2,1)} %get-tuple-element.109.refs_3_, ...), custom_call_target="tpu_custom_call" | custom-call | flops 100000000 | bytes 60000000 | tf_op jit(solution)/shard_map/pallas_call | solution.py:1047
  520.8 10.4 %shard_map.462 = (f32[2048,256]{1,0:T(8,128)}, f32[8,128]{1,0:T(8,128)}, f32[16,2048]{1,0:T(8,128)}, f32[3,2,72,128]{3,2,1,0:T(8,128)}, f32[3,2,72,128]{3,2,1,0:...) custom-call(bf16[1280,256]{1,0:T(8,128)(2,1)} %bitcast.398, ...), custom_call_target="tpu_custom_call", output_to_operand_aliasing={{2}: (6, {}), {3}: (7, {}), {4}: (8, {}), {5}: (9, {}), {6}... | custom-call | flops 100000000 | bytes 40000000 | tf_op jit(solution)/shard_map/pallas_call | solution.py:1258
  (607 shorter events, 316.8 us)
Async XLA Ops:
  7.2 148.8 %all-gather.8.cloned.1.call-start = ((), (), s32[]{:S(2)}) async-start(), calls=%async_computation | async-start | bytes 15040512 | tf_op jit(solution)/shard_map/all_gather | solution.py:1474
  24.9 21.9 %collective-permute-start.21 = (bf16[4,144,384]{2,1,0:T(8,128)(2,1)S(1)}, bf16[4,144,384]{2,1,0:T(8,128)(2,1)S(1)}, u32[]{:S(2)}, u32[]{:S(2)}) collective-permute-start(bf16[4,144,384]{2,1,0:T(8,128)(2,1)S(1)} %get-tuple-element.79), channel_id=1, source_target_pairs={{0,24},{1,25},{2,26},{3,27},{4,28},{5,29},{6,30},{7,31},{8,16},{9,... | collective-permute-start | bytes 1327112 | tf_op jit(solution)/shard_map/ppermute | solution.py:1468
  47.9 187.4 %all-gather.10.cloned.1.call-start = ((), (), s32[]{:S(2)}) async-start(), calls=%async_computation.1 | async-start | bytes 13369344 | tf_op jit(solution)/shard_map/all_gather | solution.py:1511
  63.5 28.2 %collective-permute-start.18 = (bf16[320,384]{1,0:T(8,128)(2,1)S(1)}, bf16[320,384]{1,0:T(8,128)(2,1)S(1)}, u32[]{:S(2)}, u32[]{:S(2)}) collective-permute-start(bf16[320,384]{1,0:T(8,128)(2,1)S(1)} %broadcast_select_fusion.14), channel_id=1, source_target_pairs={{0,8},{1,9},{4,12},{5,13},{24,16},{25,17},{28,20},{29,21}} | collective-permute-start | bytes 737288 | tf_op jit(solution)/shard_map/ppermute | solution.py:1491
  65.5 28.2 %collective-permute-start.9 = (bf16[336,384]{1,0:T(8,128)(2,1)S(1)}, bf16[336,384]{1,0:T(8,128)(2,1)S(1)}, u32[]{:S(2)}, u32[]{:S(2)}) collective-permute-start(bf16[336,384]{1,0:T(8,128)(2,1)S(1)} %broadcast_select_fusion.10), channel_id=1, source_target_pairs={{0,24},{1,25},{2,26},{3,27},{4,28},{5,29},{6,30},{7,31}} | collective-permute-start | bytes 774152 | tf_op jit(solution)/shard_map/ppermute | solution.py:1491
  116.1 21.8 %collective-permute-start.20 = (bf16[992,384]{1,0:T(8,128)(2,1)}, bf16[992,384]{1,0:T(8,128)(2,1)S(1)}, u32[]{:S(2)}, u32[]{:S(2)}) collective-permute-start(bf16[992,384]{1,0:T(8,128)(2,1)} %pad_maximum_fusion.6), channel_id=1, source_target_pairs={{0,1},{1,0},{2,3},{3,2},{4,5},{5,4},{6,7},{7,6},{8,9},{9,8},{10,11... | collective-permute-start | bytes 2285576 | tf_op jit(solution)/shard_map/ppermute | solution.py:1498
  158.1 264.2 %all-gather.12.cloned.1.call-start = ((), (), s32[]{:S(2)}) async-start(), calls=%async_computation.2 | async-start | bytes 12533760 | tf_op jit(solution)/shard_map/all_gather | solution.py:1586
  172.9 57.6 %collective-permute-start.4 = (f32[8,1,80]{2,0,1:T(8,128)S(1)}, f32[8,1,80]{2,0,1:T(8,128)S(1)}, u32[]{:S(2)}, u32[]{:S(2)}) collective-permute-start(f32[8,1,80]{2,0,1:T(8,128)S(1)} %maximum_select_fusion.29), channel_id=1, source_target_pairs={{0,1},{1,0},{2,3},{3,2},{4,5},{5,4},{6,7},{7,6},{8,9},{9,8},{10,11... | collective-permute-start | bytes 7688 | tf_op jit(solution)/shard_map/ppermute | solution.py:444
  244.1 178.3 %all-gather.14.cloned.1.call-start = ((), (), s32[]{:S(2)}) async-start(), calls=%async_computation.3 | async-start | bytes 11837440 | tf_op jit(solution)/shard_map/all_gather | solution.py:1650
  305.4 22.8 %collective-permute-start.35 = (f32[3,1280]{1,0:T(4,128)S(1)}, f32[3,1280]{1,0:T(4,128)S(1)}, u32[]{:S(2)}, u32[]{:S(2)}) collective-permute-start(f32[3,1280]{1,0:T(4,128)S(1)} %add.443), channel_id=1, source_target_pairs={{0,4},{1,5},{2,6},{3,7},{4,0},{5,1},{6,2},{7,3},{8,12},{9,13},{10,... | collective-permute-start | bytes 46088 | tf_op jit(solution)/shard_map/ppermute | solution.py:1620
  348.8 28.1 %collective-permute-start.57 = (f32[2,1,2048]{2,0,1:T(2,128)S(1)}, f32[2,1,2048]{2,0,1:T(2,128)S(1)}, u32[]{:S(2)}, u32[]{:S(2)}) collective-permute-start(f32[2,1,2048]{2,0,1:T(2,128)S(1)} %maximum_select_fusion.27), channel_id=1, source_target_pairs={{0,2},{1,3},{2,0},{3,1},{4,6},{5,7},{6,4},{7,5},{8,10},{9,11},{10,... | collective-permute-start | bytes 49160 | tf_op jit(solution)/shard_map/ppermute | solution.py:444
  376.9 41.3 %collective-permute-start.51 = (f32[3,11,144,128]{3,2,1,0:T(8,128)}, f32[3,11,144,128]{3,2,1,0:T(8,128)S(1)}, u32[]{:S(2)}, u32[]{:S(2)}) collective-permute-start(f32[3,11,144,128]{3,2,1,0:T(8,128)} %select_bitcast_fusion.1), channel_id=1, source_target_pairs={{0,1},{1,0},{2,3},{3,2},{4,5},{5,4},{6,7},{7,6},{8,9},{9,8},{10,11... | collective-permute-start | bytes 7299080 | tf_op jit(solution)/shard_map/ppermute | solution.py:463
  383.5 27.5 %collective-permute-start.59 = (f32[8,1,2048]{2,1,0:T(1,128)S(1)}, f32[8,1,2048]{2,1,0:T(1,128)S(1)}, u32[]{:S(2)}, u32[]{:S(2)}) collective-permute-start(f32[8,1,2048]{2,1,0:T(1,128)S(1)} %copy.215), channel_id=1, source_target_pairs={{0,8},{1,9},{2,10},{3,11},{4,12},{5,13},{6,14},{7,15},{8,0},{9,1},... | collective-permute-start | bytes 196616 | tf_op jit(solution)/shard_map/ppermute | solution.py:444
  437.8 41.3 %collective-permute-start.54 = (bf16[3,2,2,2,72,128]{5,4,0,2,3,1:T(8,128)(2,1)S(1)}, bf16[3,2,2,2,72,128]{5,4,0,2,3,1:T(8,128)(2,1)S(1)}, u32[]{:S(2)}, u32[]{:S(2)}) collective-permute-start(bf16[3,2,2,2,72,128]{5,4,0,2,3,1:T(8,128)(2,1)S(1)} %fusion.15), channel_id=1, source_target_pairs={{0,24},{1,25},{2,26},{3,27},{4,28},{5,29},{6,30},{7,31},{8,16},{9,... | collective-permute-start | bytes 1327112 | tf_op jit(solution)/shard_map/ppermute | solution.py:463
  439.1 36.9 %collective-permute-start.48 = (bf16[96,2048]{1,0:T(8,128)(2,1)S(1)}, bf16[96,2048]{1,0:T(8,128)(2,1)S(1)}, u32[]{:S(2)}, u32[]{:S(2)}) collective-permute-start(bf16[96,2048]{1,0:T(8,128)(2,1)S(1)} %copy-done.44), channel_id=1, source_target_pairs={{16,8},{17,9},{18,10},{19,11},{20,12},{21,13},{22,14},{23,15},{24,... | collective-permute-start | bytes 1179656 | tf_op jit(solution)/shard_map/ppermute | solution.py:1752
  441.3 38.8 %collective-permute-start.52 = (bf16[3,2,2,2,72,128]{5,4,0,2,1,3:T(8,128)(2,1)S(1)}, bf16[3,2,2,2,72,128]{5,4,0,2,1,3:T(8,128)(2,1)}, u32[]{:S(2)}, u32[]{:S(2)}) collective-permute-start(bf16[3,2,2,2,72,128]{5,4,0,2,1,3:T(8,128)(2,1)S(1)} %fusion.14), channel_id=1, source_target_pairs={{0,2},{1,3},{2,0},{3,1},{4,6},{5,7},{6,4},{7,5},{8,10},{9,11},{10,... | collective-permute-start | bytes 1327112 | tf_op jit(solution)/shard_map/ppermute | solution.py:463
  462.4 48.3 %collective-permute-start.62 = (f32[3,11,144,128]{3,2,1,0:T(8,128)}, f32[3,11,144,128]{3,2,1,0:T(8,128)}, u32[]{:S(2)}, u32[]{:S(2)}) collective-permute-start(f32[3,11,144,128]{3,2,1,0:T(8,128)} %select_bitcast_fusion), channel_id=1, source_target_pairs={{0,1},{1,0},{2,3},{3,2},{4,5},{5,4},{6,7},{7,6},{8,9},{9,8},{10,11... | collective-permute-start | bytes 7299080 | tf_op jit(solution)/shard_map/ppermute | solution.py:463
  476.8 43.4 %collective-permute-start.49 = (f32[16,2048]{1,0:T(8,128)S(1)}, f32[16,2048]{1,0:T(8,128)S(1)}, u32[]{:S(2)}, u32[]{:S(2)}) collective-permute-start(f32[16,2048]{1,0:T(8,128)S(1)} %constant_dynamic-slice_fusion), channel_id=1, source_target_pairs={{0,1},{1,2},{2,3},{3,4},{4,5},{5,6},{6,7},{7,8},{8,9},{9,10},{10,1... | collective-permute-start | bytes 393224 | tf_op jit(solution)/shard_map/ppermute | solution.py:1773
  480.0 24.4 %collective-permute-start.55 = (bf16[3,2,2,72,128]{4,3,0,1,2:T(8,128)(2,1)S(1)}, bf16[3,2,2,72,128]{4,3,0,1,2:T(8,128)(2,1)S(1)}, u32[]{:S(2)}, u32[]{:S(2)}) collective-permute-start(bf16[3,2,2,72,128]{4,3,0,1,2:T(8,128)(2,1)S(1)} %fusion.21), channel_id=1, source_target_pairs={{0,8},{1,9},{2,10},{3,11},{4,12},{5,13},{6,14},{7,15},{8,0},{9,1},... | collective-permute-start | bytes 663560 | tf_op jit(solution)/shard_map/ppermute | solution.py:463
  481.9 22.7 %collective-permute-start.53 = (bf16[3,2,2,72,128]{4,3,0,2,1:T(8,128)(2,1)S(1)}, bf16[3,2,2,72,128]{4,3,0,2,1:T(8,128)(2,1)S(1)}, u32[]{:S(2)}, u32[]{:S(2)}) collective-permute-start(bf16[3,2,2,72,128]{4,3,0,2,1:T(8,128)(2,1)S(1)} %fusion.20), channel_id=1, source_target_pairs={{0,4},{1,5},{2,6},{3,7},{4,0},{5,1},{6,2},{7,3},{8,12},{9,13},{10,... | collective-permute-start | bytes 663560 | tf_op jit(solution)/shard_map/ppermute | solution.py:463
  506.2 25.1 %collective-permute-start.72 = (bf16[3,2,72,128]{3,2,0,1:T(8,128)(2,1)S(1)}, bf16[3,2,72,128]{3,2,0,1:T(8,128)(2,1)S(1)}, u32[]{:S(2)}, u32[]{:S(2)}) collective-permute-start(bf16[3,2,72,128]{3,2,0,1:T(8,128)(2,1)S(1)} %fusion.27), channel_id=1, source_target_pairs={{0,24},{1,25},{2,26},{3,27},{4,28},{5,29},{6,30},{7,31},{8,16},{9,... | collective-permute-start | bytes 331784 | tf_op jit(solution)/shard_map/ppermute | solution.py:463
  507.4 28.5 %collective-permute-start.74 = (bf16[3,2,72,128]{3,2,0,1:T(8,128)(2,1)S(1)}, bf16[3,2,72,128]{3,2,0,1:T(8,128)(2,1)S(1)}, u32[]{:S(2)}, u32[]{:S(2)}) collective-permute-start(bf16[3,2,72,128]{3,2,0,1:T(8,128)(2,1)S(1)} %fusion.28), channel_id=1, source_target_pairs={{0,2},{1,3},{2,0},{3,1},{4,6},{5,7},{6,4},{7,5},{8,10},{9,11},{10,... | collective-permute-start | bytes 331784 | tf_op jit(solution)/shard_map/ppermute | solution.py:463
  516.3 24.9 %collective-permute-start.64 = (bf16[3,2,2,2,88,128]{5,4,0,2,1,3:T(8,128)(2,1)S(1)}, bf16[3,2,2,2,88,128]{5,4,0,2,1,3:T(8,128)(2,1)S(1)}, u32[]{:S(2)}, u32[]{:S(2)}) collective-permute-start(bf16[3,2,2,2,88,128]{5,4,0,2,1,3:T(8,128)(2,1)S(1)} %fusion.5), channel_id=1, source_target_pairs={{0,2},{1,3},{2,0},{3,1},{4,6},{5,7},{6,4},{7,5},{8,10},{9,11},{10,... | collective-permute-start | bytes 1622024 | tf_op jit(solution)/shard_map/ppermute | solution.py:463
  519.2 25.6 %collective-permute-start.68 = (bf16[3,2,2,2,88,128]{5,4,0,2,3,1:T(8,128)(2,1)S(1)}, bf16[3,2,2,2,88,128]{5,4,0,2,3,1:T(8,128)(2,1)S(1)}, u32[]{:S(2)}, u32[]{:S(2)}) collective-permute-start(bf16[3,2,2,2,88,128]{5,4,0,2,3,1:T(8,128)(2,1)S(1)} %fusion.6), channel_id=1, source_target_pairs={{0,24},{1,25},{2,26},{3,27},{4,28},{5,29},{6,30},{7,31},{8,16},{9,... | collective-permute-start | bytes 1622024 | tf_op jit(solution)/shard_map/ppermute | solution.py:463
  (130 other events, 828.0 us)
Sparse Core Ops, SparseCore 0:
  48.0 107.9 all-gather.7
  158.3 66.5 all-gather.9
  244.2 70.1 all-gather.11
  341.6 66.1 all-gather.13

commit v9 on v8

--- a/solution.py
+++ b/solution.py
@@ -451,12 +451,11 @@
 
 
 def cut(array, names, name, lead):
-    flag = bit_flags(lax.axis_index("dev"))[name] == 1
+    mine = bit_flags(lax.axis_index("dev"))[name]
     place = names.index(name) + lead
-    low = lax.index_in_dim(array, 0, place, keepdims=False)
-    high = lax.index_in_dim(array, 1, place, keepdims=False)
-    sent = jnp.where(flag, low, high)
-    return (sent if name == "c" else sent.astype(narrow)), jnp.where(flag, high, low), names.replace(name, "")
+    sent = lax.dynamic_index_in_dim(array, 1 - mine, place, keepdims=False)
+    kept = lax.dynamic_index_in_dim(array, mine, place, keepdims=False)
+    return (sent if name == "c" else sent.astype(narrow)), kept, names.replace(name, "")
 
 
 def move(sent, kept, name):
@@ -1041,18 +1040,20 @@
     grad_in_ref[...] = grad_mid + norm_back(grad_normed, unit_one, spread_one, vectors[0:1])
 
 
-def layer_back(kernel, part, weight_rows, side, inputs, vectors, gathered, waits, columns, buffers):
+def layer_back(kernel, part, weight_rows, side, inputs, vectors, gathered, waits, held, columns, buffers):
     tokens = inputs[0].shape[0]
     rows, blocks = gathered.shape[3], 2 * gathered.shape[0]
     return pl.pallas_call(
-        lambda *refs: kernel(part, *refs),
+        lambda *refs: kernel(part, *refs[: len(refs) - 6 - len(held)], *refs[len(refs) - 6 :]),
         out_shape=[
             jax.ShapeDtypeStruct((tokens, D), single),
             jax.ShapeDtypeStruct((D // 128, weight_rows, 128), single),
             jax.ShapeDtypeStruct((8, D), single),
-        ],
-        in_specs=layer_specs_in(len(inputs) + 3) + [pl.BlockSpec(memory_space=pl.ANY)] * len(waits),
-        out_specs=[pl.BlockSpec(memory_space=pltpu.VMEM)] * 3,
+        ]
+        + [jax.ShapeDtypeStruct(array.shape, array.dtype) for array in held],
+        in_specs=layer_specs_in(len(inputs) + 3) + [pl.BlockSpec(memory_space=pl.ANY)] * (len(waits) + len(held)),
+        out_specs=[pl.BlockSpec(memory_space=pltpu.VMEM)] * 3 + [pl.BlockSpec(memory_space=pl.ANY)] * len(held),
+        input_output_aliases={len(inputs) + 3 + len(waits) + number: 3 + number for number in range(len(held))},
         scratch_shapes=[
             pltpu.VMEM((blocks, rows, D), narrow),
             pltpu.VMEM((D // 128, columns * D, 128), single),
@@ -1062,7 +1063,7 @@
         + [pltpu.SemaphoreType.DMA((4,))],
         compiler_params=pltpu.CompilerParams(vmem_limit_bytes=56 << 20),
         cost_estimate=pl.CostEstimate(flops=100 * 10**6, bytes_accessed=600 * 10**5, transcendentals=0),
-    )(side, *inputs, vectors, gathered, *waits)
+    )(side, *inputs, vectors, gathered, *waits, *held)
 
 
 def pair_rows_of(block_rows):
@@ -1070,20 +1071,20 @@
     return 4 * D // pair * pair, -(-4 * D // pair) * pair
 
 
-def mlp_back(side, grad_out, saved, vectors, gathered, part, waits):
+def mlp_back(side, grad_out, saved, vectors, gathered, part, waits, held):
     stream, packed, mixed, attn, pre, mlp = saved
     return layer_back(
         mlp_back_kernel, part, MATRIX_ROWS - pair_rows_of(gathered.shape[3])[0], side,
-        (grad_out, stream, attn, pre, mlp), vectors, gathered, waits,
+        (grad_out, stream, attn, pre, mlp), vectors, gathered, waits, held,
         FF // D, (FF, FF),
     )
 
 
-def attention_back(side, grad_mid, saved, vectors, gathered, part, waits):
+def attention_back(side, grad_mid, saved, vectors, gathered, part, waits, held):
     stream, packed, mixed, attn, pre, mlp = saved
     return layer_back(
         attention_back_kernel, part, pair_rows_of(gathered.shape[3])[1], side,
-        (grad_mid, stream, packed, mixed), vectors, gathered, waits,
+        (grad_mid, stream, packed, mixed), vectors, gathered, waits, held,
         3, (D, 3 * D),
     )
 
@@ -1290,7 +1291,7 @@
         ],
         in_specs=[pl.BlockSpec(memory_space=pltpu.SMEM)] + [table] * 5,
         out_specs=[table] * 5,
-        compiler_params=pltpu.CompilerParams(vmem_limit_bytes=40 << 20),
+        compiler_params=pltpu.CompilerParams(vmem_limit_bytes=60 << 20),
         cost_estimate=pl.CostEstimate(flops=10**7, bytes_accessed=2 * 10**7, transcendentals=0),
     )(factor.reshape(1), student, moment, second, teacher, grad)
 
@@ -1508,7 +1509,12 @@
         )
         for m in range(2)
     ]
-    gathered_head = lax.all_gather(after(both_head, gathered, even, odd), "dev", axis=0, axis_index_groups=groups)
+    all_rows = half * pair_rows
+    kept_row = jnp.broadcast_to(kept[:, None], (images_here, 17)).reshape(1, rows_here)
+    kept_pair = cube_gather(kept_row, "b").reshape(1, 2 * rows_here)
+    kept_pair = jnp.pad(kept_pair, ((0, 0), (0, more_rows)))
+    all_kept = cube_gather(kept_pair, "xygc").reshape(all_rows)
+    gathered_head = lax.all_gather(after(both_head, gathered, even, odd, all_kept), "dev", axis=0, axis_index_groups=groups)
     vectors_all = even[2 * embed_rows :].reshape(2, LAYERS, 8, D)
 
     plan = []
@@ -1561,11 +1567,6 @@
         jnp.concatenate([teacher_normed, normed_got]),
     )
     normed = jnp.pad(normed, ((0, more_rows), (0, 0)))
-    all_rows = half * pair_rows
-    kept_row = jnp.broadcast_to(kept[:, None], (images_here, 17)).reshape(1, rows_here)
-    kept_pair = cube_gather(kept_row, "b").reshape(1, 2 * rows_here)
-    kept_pair = jnp.pad(kept_pair, ((0, 0), (0, more_rows)))
-    all_kept = cube_gather(kept_pair, "xygc").reshape(all_rows)
     third_end = (bounds[-2] - D - HID + slot) * (ROW // BOT)
     acts_width = D + HID + max(third_end, HID)
     unit_z, acts, bottleneck, pre_one, pre_two = head_pass(
@@ -1581,7 +1582,6 @@
             jax.ShapeDtypeStruct((pair_rows, HID), single),
             jax.ShapeDtypeStruct((pair_rows, HID), single),
         ],
-        (all_kept,),
     )
     inputs_all = lax.all_gather(acts, "dev", axis=0, axis_index_groups=groups).reshape(half * pair_rows, -1)
 
@@ -1615,14 +1615,7 @@
     mixed_own = mixed_own + lax.ppermute(
         mixed_own.astype(narrow), "dev", [(i, i ^ across) for i in range(half)]
     ).astype(single)
-    stages = [sums[:3]]
-    for name in "cxyab":
-        stages.append(stages[-1] + lax.ppermute(stages[-1], "dev", pairs(count, MASKS[name])))
-    sums = stages[-1]
-    cross = jnp.log(sums[1]) - sums[2] / (sums[0] * tau_student)
-    loss_total = jnp.sum(row_weight * cross)
     scale = row_weight / tau_student
-    student_scale, teacher_scale = scale / sums[1], scale / sums[0]
     flags = bit_flags(me)
     pair_at = flags["c"] * 8 + flags["g"] * 4 + flags["y"] * 2 + flags["x"]
     own_scale = lax.dynamic_slice(scale, (pair_at * pair_rows,), (pair_rows,))[:, None]
@@ -1633,7 +1626,6 @@
     own_new_centre = (
         centre_keep * own_centre + (1.0 - centre_keep) * centre_sum.reshape(protos_here) / count_total
     )
-    new_centre = cube_gather(own_new_centre.reshape(1, protos_here), "cxyab").reshape(-1)
 
     grads, grad_normed = head_pass(
         head_down_kernel,
@@ -1645,7 +1637,6 @@
             jax.ShapeDtypeStruct((pair_rows, 2 * HID + BOT), narrow),
             jax.ShapeDtypeStruct((pair_rows, D), single),
         ],
-        (stages[3],),
     )
     grads_all = lax.all_gather(grads, "dev", axis=0, axis_index_groups=groups).reshape(half * pair_rows, -1)
     normed_back = lax.ppermute(
@@ -1730,30 +1721,68 @@
             for i in range(count)
         ]
     )
+    slow = [own_new_centre.reshape(1, protos_here), sums[:3]]
+    slow_order = ["c", "x", "y", "a", "b"]
+
+    def slow_round(sent, stay):
+        name = slow_order.pop(0)
+        got = [lax.ppermute(array, "dev", pairs(count, MASKS[name])) for array in sent]
+        joined = jnp.where(
+            flags[name] == 1,
+            jnp.concatenate([got[0], stay[0]], axis=0),
+            jnp.concatenate([stay[0], got[0]], axis=0),
+        )
+        return [joined, stay[1] + got[1]]
+
     started = []
-    waits, later_waits = (), ()
+    held_block = None
+    waits = ()
     for layer_index in reversed(range(LAYERS)):
         saved, vectors = saved_layers[layer_index], vectors_all[1, layer_index]
         part = LAYERS + layer_index
-        grad_stream, late_grad, late_vectors = mlp_back(
-            side, grad_stream, saved, vectors, gathered, part, waits + sends(started)
+        grad_stream, late_grad, late_vectors, stay_one, stay_two, *held_block = mlp_back(
+            side,
+            grad_stream,
+            saved,
+            vectors,
+            gathered,
+            part,
+            waits + sends(started),
+            slow + ([partner_block_grad] if started else []),
         )
+        slow = slow_round(slow, [stay_one, stay_two])
         late = over_core(late_grad, block_rows)
         started = [advance(state) for state in started]
-        grad_stream, early_grad, early_vectors = attention_back(
-            side, grad_stream, saved, vectors, gathered, part, later_waits + sends(started)
+        if started:
+            block_got = lax.ppermute(held_block[0], "dev", [(i, i ^ across) for i in range(half, count)])
+        grad_stream, early_grad, early_vectors, stay_one, stay_two, *held_block = attention_back(
+            side,
+            grad_stream,
+            saved,
+            vectors,
+            gathered,
+            part,
+            sends(started),
+            slow + ([own_block_grad] if started else []),
         )
+        slow = slow_round(slow, [stay_one, stay_two])
         vector_grads[layer_index] = (late_vectors + early_vectors)[:6]
         if layer_index == LAYERS - 1:
             sent, stay = core_cut(early_grad, block_rows)
-            own_block_grad, partner_block_grad, stay = head_grads(
-                place, inputs_all, grads_all, slot, -min(bounds[1], 0), (early_vectors,), [stay]
+            own_block_grad, partner_block_grad, stay, stay_one, stay_two = head_grads(
+                place, inputs_all, grads_all, slot, -min(bounds[1], 0), (early_vectors,), [stay] + slow
             )
-            block_got = lax.ppermute(partner_block_grad, "dev", [(i, i ^ across) for i in range(half, count)])
-            waits, later_waits = (own_block_grad, stages[4]), (stages[5], block_got, new_centre)
+            slow = slow_round(slow, [stay_one, stay_two])
+            waits = (own_block_grad,)
         started = [advance(state) for state in started]
         if layer_index > 0:
             started.append(start(late, move(sent, stay, "c")))
+    own_block_grad = held_block[0]
+    new_centre = slow[0].reshape(-1)
+    sums = slow[1]
+    cross = jnp.log(sums[1]) - sums[2] / (sums[0] * tau_student)
+    loss_total = jnp.sum(row_weight * cross)
+    student_scale, teacher_scale = scale / sums[1], scale / sums[0]
     head_block_grad = jnp.where(student_side, own_block_grad, block_got.astype(single))
     early = over_core(early_grad, block_rows)
     small_rows = -(-(EMBED_ROWS + 6 * LAYERS) // (16 * count)) * 16
@@ -1778,9 +1807,8 @@
         protos,
         centre_column,
         lines(student_scale, teacher_scale),
-        [previous] + [stay for pieces, stage in started for sent, stay, left in pieces],
-    )
-    previous, *held = held
+        [stay for pieces, stage in started for sent, stay, left in pieces],
+    )
     held = iter(held)
     started = [([(sent, next(held), left) for sent, _, left in pieces], stage) for pieces, stage in started]
     blocks = [finish(state) for state in started][::-1]

time: 643 us -> 618 us (0.961)
  waiting for transfers between devices: 204 us -> 168 us
  starting transfers between devices: 91.6 us -> 113 us
  other arithmetic: 77 us -> 55.9 us
  local copies, waits for them, and re-layouts: 60.5 us -> 67.5 us
    ppermute x29 -> x24, waiting for transfers between devices: 43.5 us -> 24.2 us  [cube_gather(): got = lax.ppermute(held, 'dev', pairs(count, MASKS[name]))]
    ppermute x29 -> x24, starting transfers between devices: 22.2 us -> 39.5 us  [cube_gather(): got = lax.ppermute(held, 'dev', pairs(count, MASKS[name]))]
    select_n x11 -> x4, other arithmetic: 16.7 us -> 1.02 us  [slow_round(): jnp.where(flags[name] == 1, jnp.concatenate([got[0], stay[0]], axis=0), j...]
    squeeze x1 -> x11, local copies, waits for them, and re-layouts: 0.61 us -> 16.3 us  [the longest x6 12.1 us: cut(): sent = lax.dynamic_index_in_dim(array, 1 - mine, place, keepdims=False)]
    all_gather x1, waiting for transfers between devices: 16.6 us -> 5.48 us  [close_local(): lax.all_gather(both_layers, 'dev', axis=0, axis_index_groups=groups)]
    ppermute x6 -> x11, waiting for transfers between devices: 17.9 us -> 11.4 us  [the longest x10 11.4 us: slow_round(): lax.ppermute(array, 'dev', pairs(count, MASKS[name]))]
    unnamed x129 -> x141, local copies, waits for them, and re-layouts: 18.9 us -> 12.6 us
  transfers between devices with their start and end apart: 91 -> 91, of which waited for: 42 -> 37; matrix products, arithmetic and copies ran while one was open for 15% -> 16% of each run, Pallas kernels for 25% -> 27%
where the time goes in v9:
time: 618 us; the launch traced here: 607 us
  Pallas kernels  178 us (29%)
  waiting for transfers between devices  168 us (27%)
  starting transfers between devices  113 us (18%)
  local copies, waits for them, and re-layouts  67.5 us (11%)
  other arithmetic  55.9 us (9%)
  between operations  23.8 us (4%)
    pallas_call x4, Pallas kernels, layer_back(): pl.pallas_call(lambda *refs: kernel(part, *refs[:len(refs) - 6 - len(held...  60.7 us
    pallas_call x4, Pallas kernels, layer_forward(): pl.pallas_call(lambda *refs: forward_kernel(part, keep, *refs), out_shape...  47.8 us
    ppermute x29, waiting for transfers between devices, move(): lax.ppermute(sent, 'dev', pairs(1 << len(BITS), MASKS[name])).astype(single)  41 us
    ppermute x24, starting transfers between devices, cube_gather(): got = lax.ppermute(held, 'dev', pairs(count, MASKS[name]))  39.5 us
    ppermute x12, waiting for transfers between devices, close_local(): got = lax.ppermute(spread, 'dev', moves)  38.1 us
    ppermute x29, starting transfers between devices, move(): lax.ppermute(sent, 'dev', pairs(1 << len(BITS), MASKS[name])).astype(single)  28.3 us
    ppermute x24, waiting for transfers between devices, cube_gather(): got = lax.ppermute(held, 'dev', pairs(count, MASKS[name]))  24.2 us
    pallas_call x2, Pallas kernels, head_pass(): pl.pallas_call(lambda *refs: kernel(plan, *refs[:read], *refs[read + len(...  19.6 us
  transfers between devices with their start and end apart: 91, of which 37 were waited for; matrix products, arithmetic and copies ran while one was open for 16% of the time, Pallas kernels for 27%

profile of v9, /device:TPU:8, one launch (start us, length us, event | category | flops | bytes accessed | tf_op | source)
XLA Modules:
  0.0 607.0 jit_solution(5731748066111998760)
XLA Ops:
  26.8 18.3 %collective-permute-done.21 = bf16[4,144,384]{2,1,0:T(8,128)(2,1)S(1)} collective-permute-done((bf16[4,144,384]{2,1,0:T(8,128)(2,1)S(1)}, bf16[4,144,384]{2,1,0:T(8,128)(2,1)S(1)}, u32[]{:S(2)}, u32[]{:S(2)}) %collective-permute-start.21) | collective-permute-done | bytes 442400 | tf_op jit(solution)/shard_map/ppermute | solution.py:1469
  66.3 13.4 %collective-permute-start.3 = (f32[4,1,80]{2,0,1:T(4,128)S(1)}, f32[4,1,80]{2,0,1:T(4,128)S(1)}, u32[]{:S(2)}, u32[]{:S(2)}) collective-permute-start(f32[4,1,80]{2,0,1:T(4,128)S(1)} %maximum_select_fusion.30), channel_id=1, source_target_pairs={{0,8},{1,9},{2,10},{3,11},{4,12},{5,13},{6,14},{7,15},{8,0},{9,1},... | collective-permute-start | bytes 3848 | tf_op jit(solution)/shard_map/ppermute | solution.py:444
  84.4 14.7 %collective-permute-done.12 = bf16[336,384]{1,0:T(8,128)(2,1)S(1)} collective-permute-done((bf16[336,384]{1,0:T(8,128)(2,1)S(1)}, bf16[336,384]{1,0:T(8,128)(2,1)S(1)}, u32[]{:S(2)}, u32[]{:S(2)}) %collective-permute-start.12) | collective-permute-done | bytes 258080 | tf_op jit(solution)/shard_map/ppermute | solution.py:1492
  101.0 8.1 %collective-permute-done.18 = bf16[320,384]{1,0:T(8,128)(2,1)S(1)} collective-permute-done((bf16[320,384]{1,0:T(8,128)(2,1)S(1)}, bf16[320,384]{1,0:T(8,128)(2,1)S(1)}, u32[]{:S(2)}, u32[]{:S(2)}) %collective-permute-start.18) | collective-permute-done | bytes 245792 | tf_op jit(solution)/shard_map/ppermute | solution.py:1492
  117.9 13.2 %collective-permute-done.10 = bf16[336,384]{1,0:T(8,128)(2,1)S(1)} collective-permute-done((bf16[336,384]{1,0:T(8,128)(2,1)S(1)}, bf16[336,384]{1,0:T(8,128)(2,1)S(1)}, u32[]{:S(2)}, u32[]{:S(2)}) %collective-permute-start.10) | collective-permute-done | bytes 258080 | tf_op jit(solution)/shard_map/ppermute | solution.py:1492
  139.5 15.2 %collective-permute-done.23 = bf16[96,2048]{1,0:T(8,128)(2,1)S(1)} collective-permute-done((bf16[96,2048]{1,0:T(8,128)(2,1)S(1)}, bf16[96,2048]{1,0:T(8,128)(2,1)S(1)}, u32[]{:S(2)}, u32[]{:S(2)}) %collective-permute-start.23) | collective-permute-done | bytes 393248 | tf_op jit(solution)/shard_map/ppermute | solution.py:1478
  170.5 12.0 %shard_map.450 = (f32[544,384]{1,0:T(8,128)}, bf16[544,1152]{1,0:T(8,128)(2,1)}, bf16[544,384]{1,0:T(8,128)(2,1)}, f32[544,384]{1,0:T(8,128)}, f32[544,1536]{1,0:T(8,128)}, /*index=5*/f32[544,384]{1,0:T(8,128)}) custom-call(s32[1]{0:T(128)} %bitcast.8.refs_0_, f32[544,384]{1,0:T(8,128)} %bitcast.330, ...), custom_call_target="tpu_custom_call" | custom-call | flops 100000000 | bytes 43000000 | tf_op jit(solution)/shard_map/pallas_call | solution.py:915
  182.5 12.4 %shard_map.451 = (f32[544,384]{1,0:T(8,128)}, bf16[544,1152]{1,0:T(8,128)(2,1)}, bf16[544,384]{1,0:T(8,128)(2,1)}, f32[544,384]{1,0:T(8,128)}, f32[544,1536]{1,0:T(8,128)}, /*index=5*/f32[544,384]{1,0:T(8,128)}) custom-call(s32[1]{0:T(128)} %bitcast.8.refs_0_, f32[544,384]{1,0:T(8,128)} %get-tuple-element.91.refs_1_.refs_2_, ...), custom_call_target="tpu_custom_call" | custom-call | flops 100000000 | bytes 43000000 | tf_op jit(solution)/shard_map/pallas_call | solution.py:915
  196.9 11.6 %shard_map.448.refs_1_ = f32[544,384]{1,0:T(8,128)} custom-call(s32[1]{0:T(128)} %bitcast.8.refs_0_, f32[544,384]{1,0:T(8,128)} %bitcast.358, bf16[8,384]{1,0:T(8,128)(2,1)} %get-tuple-element.223.refs_2_, bf16[16,2,4,144,384]{4,3,2,1,0:T(8,128)(2,1)} %all-gather.8.cloned.1.call-done.refs_3_.refs_1_.refs_7_.refs_6_), custom_call_target="tpu_custom_call" | custom-call | flops 100000000 | bytes 43000000 | tf_op jit(solution)/shard_map/pallas_call | solution.py:915
  208.4 11.9 %shard_map.449 = f32[544,384]{1,0:T(8,128)} custom-call(s32[1]{0:T(128)} %bitcast.8.refs_0_, f32[544,384]{1,0:T(8,128)} %shard_map.448.refs_1_, bf16[8,384]{1,0:T(8,128)(2,1)} %get-tuple-element.220.refs_2_, bf16[16,2,4,144,384]{4,3,2,1,0:T(8,128)(2,1)} %all-gather.8.cloned.1.call-done.refs_3_.refs_1_.refs_7_.refs_6_), custom_call_target="tpu_custom_call" | custom-call | flops 100000000 | bytes 43000000 | tf_op jit(solution)/shard_map/pallas_call | solution.py:915
  231.5 8.7 %shard_map.453 = (bf16[80,256]{1,0:T(8,128)(2,1)}, bf16[80,4608]{1,0:T(8,128)(2,1)}, f32[80,256]{1,0:T(8,128)}, f32[80,2048]{1,0:T(8,128)}, f32[80,2048]{1,0:T(8,128)}) custom-call(s32[1]{0:T(128)} %bitcast.8.refs_0_, bf16[80,384]{1,0:T(8,128)(2,1)} %pad.45.refs_1_, bf16[16,2,96,2048]{3,2,1,0:T(8,128)(2,1)} %bitcast.328), custom_call_target="tpu_custom_call" | custom-call | flops 100000000 | bytes 37000000 | tf_op jit(solution)/shard_map/pallas_call | solution.py:760
  271.5 14.1 %shard_map.454 = (f32[1280,640]{1,0:T(8,128)}, f32[8,1280]{1,0:T(8,128)}, f32[2048,1]{1,0:T(8,128)}) custom-call(bf16[1280,256]{1,0:T(8,128)(2,1)} %bitcast.342, bf16[1280,256]{1,0:T(8,128)(2,1)} %bitcast.340, f32[2048,256]{1,0:T(8,128)} %refs_3_.3, f32[2048,256]{1,0:T(8,128)} %refs_0_.1, f32[2048,1]{1,0:T(8,128)} %copy.184.centre_ref.refs_4_, ...), custom_call_target="tpu_custom_call" | custom-call | flops 100000000 | bytes 52000000 | tf_op jit(solution)/shard_map/pallas_call | solution.py:1211
  296.7 7.2 %collective-permute-done.34 = bf16[2,2,80,256]{3,2,1,0:T(8,128)(2,1)S(1)} collective-permute-done((bf16[2,2,80,256]{3,2,1,0:T(8,128)(2,1)S(1)}, bf16[2,2,80,256]{3,2,1,0:T(8,128)(2,1)S(1)}, u32[]{:S(2)}, u32[]{:S(2)}) %collective-permute-start.34) | collective-permute-done | bytes 163872 | tf_op jit(solution)/shard_map/ppermute | solution.py:462
  304.6 5.9 collective-permute-done.38
  326.5 10.9 %shard_map.455 = (bf16[80,4352]{1,0:T(8,128)(2,1)}, f32[80,384]{1,0:T(8,128)}) custom-call(s32[1]{0:T(128)} %bitcast.8.refs_0_, f32[80,256]{1,0:T(8,128)} %fusion.33.refs_1_, f32[80,256]{1,0:T(8,128)} %get-tuple-element.96.refs_2_, f32[80,2048]{1,0:T(8,128)} %get-tuple-element.97.refs_3_, f32[80,2048]{1,0:T(8,128)} %get-tuple-element.98.refs_4_, ...), custom_call_target="tpu_custom_call" | custom-call | flops 100000000 | bytes 37000000 | tf_op jit(solution)/shard_map/pallas_call | solution.py:760
  349.5 13.8 %shard_map.456 = (f32[544,384]{1,0:T(8,128)}, f32[3,3168,128]{2,1,0:T(8,128)}, f32[8,384]{1,0:T(8,128)}, f32[1,2048]{1,0:T(1,128)}, f32[3,1280]{1,0:T(4,128)}) custom-call(s32[1]{0:T(128)} %bitcast.8.refs_0_, f32[544,384]{1,0:T(8,128)} %bitcast.339, f32[544,384]{1,0:T(8,128)} %get-tuple-element.91.refs_1_.refs_2_, ...), custom_call_target="tpu_custom_call", output_to_operand_aliasing={{3}: (8, {}), {4}: (9, {})} | custom-call | flops 100000000 | bytes 60000000 | tf_op jit(solution)/shard_map/pallas_call | solution.py:1046
  371.6 16.8 %shard_map.457 = (f32[544,384]{1,0:T(8,128)}, f32[3,1728,128]{2,1,0:T(8,128)}, f32[8,384]{1,0:T(8,128)}, f32[2,2048]{1,0:T(2,128)}, f32[3,1280]{1,0:T(4,128)}) custom-call(s32[1]{0:T(128)} %bitcast.8.refs_0_, f32[544,384]{1,0:T(8,128)} %get-tuple-element.105.refs_1_, ...), custom_call_target="tpu_custom_call", output_to_operand_aliasing={{3}: (7, {}), {4}: (8, {})} | custom-call | flops 100000000 | bytes 60000000 | tf_op jit(solution)/shard_map/pallas_call | solution.py:1046
  402.2 10.3 %shard_map.458 = (f32[96,2048]{1,0:T(8,128)}, bf16[96,2048]{1,0:T(8,128)(2,1)}, f32[3,6,144,128]{3,2,1,0:T(8,128)}, f32[4,2048]{1,0:T(4,128)}, f32[3,1280]{1,0:T(4,128)}) custom-call(s32[10]{0:T(128)} %fusion.78.refs_0_, bf16[1280,4608]{1,0:T(8,128)(2,1)} %all-gather.12.cloned.1.call-done.refs_1_, ...), custom_call_target="tpu_custom_call", output_to_operand_aliasing={{2}: (4, {}), {3}: (5, {}), {4}: (6, {})} | custom-call | flops 100000000 | bytes 37000000 | tf_op jit(solution)/shard_map/pallas_call | solution.py:1363
  424.5 8.5 %collective-permute-done.54 = f32[3,1280]{1,0:T(4,128)S(1)} collective-permute-done((f32[3,1280]{1,0:T(4,128)S(1)}, f32[3,1280]{1,0:T(4,128)S(1)}, u32[]{:S(2)}, u32[]{:S(2)}) %collective-permute-start.54) | collective-permute-done | bytes 15392 | tf_op jit(solution)/shard_map/ppermute | solution.py:1729
  433.0 13.6 %shard_map.459 = (f32[544,384]{1,0:T(8,128)}, f32[3,3168,128]{2,1,0:T(8,128)}, f32[8,384]{1,0:T(8,128)}, f32[8,2048]{1,0:T(8,128)}, f32[3,1280]{1,0:T(4,128)}, /*index=5*/bf16[96,2048]{1,0:T(8,128)(2,1)}) custom-call(s32[1]{0:T(128)} %bitcast.8.refs_0_, ...), custom_call_target="tpu_custom_call", output_to_operand_aliasing={{3}: (11, {}), {4}: (12, {}), {5}: (13, {})} | custom-call | flops 100000000 | bytes 60000000 | tf_op jit(solution)/shard_map/pallas_call | solution.py:1046
  461.9 16.5 %shard_map.460 = (f32[544,384]{1,0:T(8,128)}, f32[3,1728,128]{2,1,0:T(8,128)}, f32[8,384]{1,0:T(8,128)}, f32[16,2048]{1,0:T(8,128)}, f32[3,1280]{1,0:T(4,128)}, /*index=5*/f32[96,2048]{1,0:T(8,128)}) custom-call(s32[1]{0:T(128)} %bitcast.8.refs_0_, ...), custom_call_target="tpu_custom_call", output_to_operand_aliasing={{3}: (9, {}), {4}: (10, {}), {5}: (11, {})} | custom-call | flops 100000000 | bytes 60000000 | tf_op jit(solution)/shard_map/pallas_call | solution.py:1046
  501.1 10.4 %shard_map.462 = (f32[2048,256]{1,0:T(8,128)}, f32[8,128]{1,0:T(8,128)}, f32[3,2,72,128]{3,2,1,0:T(8,128)}, f32[3,2,72,128]{3,2,1,0:T(8,128)}, f32[3,2,2,2,88,12...) custom-call(bf16[1280,256]{1,0:T(8,128)(2,1)} %bitcast.343, ...), custom_call_target="tpu_custom_call", output_to_operand_aliasing={{2}: (6, {}), {3}: (7, {}), {4}: (8, {}), {5}: (9, {})} | custom-call | flops 100000000 | bytes 40000000 | tf_op jit(solution)/shard_map/pallas_call | solution.py:1259
  529.5 6.3 %collective-permute-done.68 = bf16[3,2,2,88,128]{4,3,0,1,2:T(8,128)(2,1)S(1)} collective-permute-done((bf16[3,2,2,88,128]{4,3,0,1,2:T(8,128)(2,1)S(1)}, bf16[3,2,2,88,128]{4,3,0,1,2:T(8,128)(2,1)S(1)}, u32[]{:S(2)}, u32[]{:S(2)}) %collective-permute-start.68) | collective-permute-done | bytes 270368 | tf_op jit(solution)/shard_map/ppermute | solution.py:462
  576.6 8.1 %shard_map.464 = (f32[2048,256]{1,0:T(8,128)}, f32[2048,256]{1,0:T(8,128)}, f32[2048,256]{1,0:T(8,128)}, bf16[2048,256]{1,0:T(8,128)(2,1)}, f32[2048,256]{1,0:T(8,128)}) custom-call(f32[1]{0:T(128)} %bitcast.163.factor_ref, f32[2048,256]{1,0:T(8,128)} %refs_0_.1, f32[2048,256]{1,0:T(8,128)} %refs_1_.1, f32[2048,256]{1,0:T(8,128)} %refs_2_.3, ...), custom_call_target="tpu_custom_call" | custom-call | flops 10000000 | bytes 20000000 | tf_op jit(solution)/shard_map/pallas_call | solution.py:1286
  (606 shorter events, 301.4 us)
Async XLA Ops:
  7.2 155.4 %all-gather.8.cloned.1.call-start = ((), (), s32[]{:S(2)}) async-start(), calls=%async_computation | async-start | bytes 15040512 | tf_op jit(solution)/shard_map/all_gather | solution.py:1475
  25.2 20.0 %collective-permute-start.21 = (bf16[4,144,384]{2,1,0:T(8,128)(2,1)S(1)}, bf16[4,144,384]{2,1,0:T(8,128)(2,1)S(1)}, u32[]{:S(2)}, u32[]{:S(2)}) collective-permute-start(bf16[4,144,384]{2,1,0:T(8,128)(2,1)S(1)} %get-tuple-element.90), channel_id=1, source_target_pairs={{0,24},{1,25},{2,26},{3,27},{4,28},{5,29},{6,30},{7,31},{8,16},{9,... | collective-permute-start | bytes 1327112 | tf_op jit(solution)/shard_map/ppermute | solution.py:1469
  46.3 185.3 %all-gather.10.cloned.1.call-start = ((), (), s32[]{:S(2)}) async-start(), calls=%async_computation.1 | async-start | bytes 13369344 | tf_op jit(solution)/shard_map/all_gather | solution.py:1517
  66.3 70.7 %collective-permute-start.3 = (f32[4,1,80]{2,0,1:T(4,128)S(1)}, f32[4,1,80]{2,0,1:T(4,128)S(1)}, u32[]{:S(2)}, u32[]{:S(2)}) collective-permute-start(f32[4,1,80]{2,0,1:T(4,128)S(1)} %maximum_select_fusion.30), channel_id=1, source_target_pairs={{0,8},{1,9},{2,10},{3,11},{4,12},{5,13},{6,14},{7,15},{8,0},{9,1},... | collective-permute-start | bytes 3848 | tf_op jit(solution)/shard_map/ppermute | solution.py:444
  79.7 19.3 %collective-permute-start.12 = (bf16[336,384]{1,0:T(8,128)(2,1)S(1)}, bf16[336,384]{1,0:T(8,128)(2,1)S(1)}, u32[]{:S(2)}, u32[]{:S(2)}) collective-permute-start(bf16[336,384]{1,0:T(8,128)(2,1)S(1)} %get-tuple-element.210), channel_id=1, source_target_pairs={{0,8},{1,9},{24,16},{25,17}} | collective-permute-start | bytes 774152 | tf_op jit(solution)/shard_map/ppermute | solution.py:1492
  81.7 27.5 %collective-permute-start.18 = (bf16[320,384]{1,0:T(8,128)(2,1)S(1)}, bf16[320,384]{1,0:T(8,128)(2,1)S(1)}, u32[]{:S(2)}, u32[]{:S(2)}) collective-permute-start(bf16[320,384]{1,0:T(8,128)(2,1)S(1)} %broadcast_select_fusion.12), channel_id=1, source_target_pairs={{0,8},{1,9},{4,12},{5,13},{24,16},{25,17},{28,20},{29,21}} | collective-permute-start | bytes 737288 | tf_op jit(solution)/shard_map/ppermute | solution.py:1492
  83.7 27.5 %collective-permute-start.9 = (bf16[336,384]{1,0:T(8,128)(2,1)S(1)}, bf16[336,384]{1,0:T(8,128)(2,1)S(1)}, u32[]{:S(2)}, u32[]{:S(2)}) collective-permute-start(bf16[336,384]{1,0:T(8,128)(2,1)S(1)} %broadcast_select_fusion.8), channel_id=1, source_target_pairs={{0,24},{1,25},{2,26},{3,27},{4,28},{5,29},{6,30},{7,31}} | collective-permute-start | bytes 774152 | tf_op jit(solution)/shard_map/ppermute | solution.py:1492
  133.5 22.2 %collective-permute-start.20 = (bf16[992,384]{1,0:T(8,128)(2,1)}, bf16[992,384]{1,0:T(8,128)(2,1)S(1)}, u32[]{:S(2)}, u32[]{:S(2)}) collective-permute-start(bf16[992,384]{1,0:T(8,128)(2,1)} %pad_maximum_fusion.6), channel_id=1, source_target_pairs={{0,1},{1,0},{2,3},{3,2},{4,5},{5,4},{6,7},{7,6},{8,9},{9,8},{10,11... | collective-permute-start | bytes 2285576 | tf_op jit(solution)/shard_map/ppermute | solution.py:1499
  133.5 21.2 %collective-permute-start.23 = (bf16[96,2048]{1,0:T(8,128)(2,1)S(1)}, bf16[96,2048]{1,0:T(8,128)(2,1)S(1)}, u32[]{:S(2)}, u32[]{:S(2)}) collective-permute-start(bf16[96,2048]{1,0:T(8,128)(2,1)S(1)} %get-tuple-element.201), channel_id=1, source_target_pairs={{0,24},{1,25},{2,26},{3,27},{4,28},{5,29},{6,30},{7,31},{8,16},{9,... | collective-permute-start | bytes 1179656 | tf_op jit(solution)/shard_map/ppermute | solution.py:1478
  164.8 237.4 %all-gather.12.cloned.1.call-start = ((), (), s32[]{:S(2)}) async-start(), calls=%async_computation.2 | async-start | bytes 12533760 | tf_op jit(solution)/shard_map/all_gather | solution.py:1586
  240.2 162.0 %all-gather.14.cloned.1.call-start = ((), (), s32[]{:S(2)}) async-start(), calls=%async_computation.3 | async-start | bytes 11837440 | tf_op jit(solution)/shard_map/all_gather | solution.py:1641
  366.6 31.4 %collective-permute-start.48 = (f32[3,11,144,128]{3,2,1,0:T(8,128)}, f32[3,11,144,128]{3,2,1,0:T(8,128)}, u32[]{:S(2)}, u32[]{:S(2)}) collective-permute-start(f32[3,11,144,128]{3,2,1,0:T(8,128)} %dynamic-slice_bitcast_fusion.1), channel_id=1, source_target_pairs={{0,1},{1,0},{2,3},{3,2},{4,5},{5,4},{6,7},{7,6},{8,9},{9,8},{10,11... | collective-permute-start | bytes 7299080 | tf_op jit(solution)/shard_map/ppermute | solution.py:462
  391.5 20.9 %collective-permute-start.47 = (f32[3,6,144,128]{3,2,1,0:T(8,128)S(1)}, f32[3,6,144,128]{3,2,1,0:T(8,128)}, u32[]{:S(2)}, u32[]{:S(2)}) collective-permute-start(f32[3,6,144,128]{3,2,1,0:T(8,128)S(1)} %get-tuple-element.193), channel_id=1, source_target_pairs={{0,1},{1,0},{2,3},{3,2},{4,5},{5,4},{6,7},{7,6},{8,9},{9,8},{10,11... | collective-permute-start | bytes 3981320 | tf_op jit(solution)/shard_map/ppermute | solution.py:462
  416.9 37.5 %collective-permute-start.52 = (bf16[3,2,2,2,72,128]{5,4,0,2,3,1:T(8,128)(2,1)S(1)}, bf16[3,2,2,2,72,128]{5,4,0,2,3,1:T(8,128)(2,1)S(1)}, u32[]{:S(2)}, u32[]{:S(2)}) collective-permute-start(bf16[3,2,2,2,72,128]{5,4,0,2,3,1:T(8,128)(2,1)S(1)} %fusion.16), channel_id=1, source_target_pairs={{0,24},{1,25},{2,26},{3,27},{4,28},{5,29},{6,30},{7,31},{8,16},{9,... | collective-permute-start | bytes 1327112 | tf_op jit(solution)/shard_map/ppermute | solution.py:462
  422.1 34.6 %collective-permute-start.51 = (bf16[3,2,2,2,72,128]{5,4,0,2,1,3:T(8,128)(2,1)S(1)}, bf16[3,2,2,2,72,128]{5,4,0,2,1,3:T(8,128)(2,1)S(1)}, u32[]{:S(2)}, u32[]{:S(2)}) collective-permute-start(bf16[3,2,2,2,72,128]{5,4,0,2,1,3:T(8,128)(2,1)S(1)} %fusion.15), channel_id=1, source_target_pairs={{0,2},{1,3},{2,0},{3,1},{4,6},{5,7},{6,4},{7,5},{8,10},{9,11},{10,... | collective-permute-start | bytes 1327112 | tf_op jit(solution)/shard_map/ppermute | solution.py:462
  454.3 38.9 %collective-permute-start.61 = (f32[3,11,144,128]{3,2,1,0:T(8,128)}, f32[3,11,144,128]{3,2,1,0:T(8,128)}, u32[]{:S(2)}, u32[]{:S(2)}) collective-permute-start(f32[3,11,144,128]{3,2,1,0:T(8,128)} %dynamic-slice_bitcast_fusion), channel_id=1, source_target_pairs={{0,1},{1,0},{2,3},{3,2},{4,5},{5,4},{6,7},{7,6},{8,9},{9,8},{10,11... | collective-permute-start | bytes 7299080 | tf_op jit(solution)/shard_map/ppermute | solution.py:462
  454.3 27.8 %collective-permute-start.56 = (bf16[96,2048]{1,0:T(8,128)(2,1)S(1)}, bf16[96,2048]{1,0:T(8,128)(2,1)S(1)}, u32[]{:S(2)}, u32[]{:S(2)}) collective-permute-start(bf16[96,2048]{1,0:T(8,128)(2,1)S(1)} %copy-done.25), channel_id=1, source_target_pairs={{16,8},{17,9},{18,10},{19,11},{20,12},{21,13},{22,14},{23,15},{24,... | collective-permute-start | bytes 1179656 | tf_op jit(solution)/shard_map/ppermute | solution.py:1757
  456.7 29.5 %collective-permute-start.59 = (bf16[3,2,2,72,128]{4,3,0,1,2:T(8,128)(2,1)S(1)}, bf16[3,2,2,72,128]{4,3,0,1,2:T(8,128)(2,1)S(1)}, u32[]{:S(2)}, u32[]{:S(2)}) collective-permute-start(bf16[3,2,2,72,128]{4,3,0,1,2:T(8,128)(2,1)S(1)} %fusion.23), channel_id=1, source_target_pairs={{0,8},{1,9},{2,10},{3,11},{4,12},{5,13},{6,14},{7,15},{8,0},{9,1},... | collective-permute-start | bytes 663560 | tf_op jit(solution)/shard_map/ppermute | solution.py:462
  460.5 23.0 %collective-permute-start.58 = (bf16[3,2,2,72,128]{4,3,0,2,1:T(8,128)(2,1)S(1)}, bf16[3,2,2,72,128]{4,3,0,2,1:T(8,128)(2,1)S(1)}, u32[]{:S(2)}, u32[]{:S(2)}) collective-permute-start(bf16[3,2,2,72,128]{4,3,0,2,1:T(8,128)(2,1)S(1)} %fusion.22), channel_id=1, source_target_pairs={{0,4},{1,5},{2,6},{3,7},{4,0},{5,1},{6,2},{7,3},{8,12},{9,13},{10,... | collective-permute-start | bytes 663560 | tf_op jit(solution)/shard_map/ppermute | solution.py:462
  483.5 80.6 %collective-permute-start.57 = (f32[16,2048]{1,0:T(8,128)S(1)}, f32[16,2048]{1,0:T(8,128)S(1)}, u32[]{:S(2)}, u32[]{:S(2)}) collective-permute-start(f32[16,2048]{1,0:T(8,128)S(1)} %constant_dynamic-slice_fusion.4), channel_id=1, source_target_pairs={{0,1},{1,2},{2,3},{3,4},{4,5},{5,6},{6,7},{7,8},{8,9},{9,10},{10,1... | collective-permute-start | bytes 393224 | tf_op jit(solution)/shard_map/ppermute | solution.py:1802
  486.1 25.4 %collective-permute-start.71 = (bf16[3,2,72,128]{3,2,0,1:T(8,128)(2,1)S(1)}, bf16[3,2,72,128]{3,2,0,1:T(8,128)(2,1)S(1)}, u32[]{:S(2)}, u32[]{:S(2)}) collective-permute-start(bf16[3,2,72,128]{3,2,0,1:T(8,128)(2,1)S(1)} %fusion.29), channel_id=1, source_target_pairs={{0,24},{1,25},{2,26},{3,27},{4,28},{5,29},{6,30},{7,31},{8,16},{9,... | collective-permute-start | bytes 331784 | tf_op jit(solution)/shard_map/ppermute | solution.py:462
  491.3 22.4 %collective-permute-start.73 = (bf16[3,2,72,128]{3,2,0,1:T(8,128)(2,1)S(1)}, bf16[3,2,72,128]{3,2,0,1:T(8,128)(2,1)S(1)}, u32[]{:S(2)}, u32[]{:S(2)}) collective-permute-start(bf16[3,2,72,128]{3,2,0,1:T(8,128)(2,1)S(1)} %fusion.30), channel_id=1, source_target_pairs={{0,2},{1,3},{2,0},{3,1},{4,6},{5,7},{6,4},{7,5},{8,10},{9,11},{10,... | collective-permute-start | bytes 331784 | tf_op jit(solution)/shard_map/ppermute | solution.py:462
  499.1 19.8 %collective-permute-start.63 = (bf16[3,2,2,2,88,128]{5,4,0,2,1,3:T(8,128)(2,1)S(1)}, bf16[3,2,2,2,88,128]{5,4,0,2,1,3:T(8,128)(2,1)S(1)}, u32[]{:S(2)}, u32[]{:S(2)}) collective-permute-start(bf16[3,2,2,2,88,128]{5,4,0,2,1,3:T(8,128)(2,1)S(1)} %fusion.6), channel_id=1, source_target_pairs={{0,2},{1,3},{2,0},{3,1},{4,6},{5,7},{6,4},{7,5},{8,10},{9,11},{10,... | collective-permute-start | bytes 1622024 | tf_op jit(solution)/shard_map/ppermute | solution.py:462
  500.1 26.1 %collective-permute-start.67 = (bf16[3,2,2,2,88,128]{5,4,0,2,3,1:T(8,128)(2,1)S(1)}, bf16[3,2,2,2,88,128]{5,4,0,2,3,1:T(8,128)(2,1)S(1)}, u32[]{:S(2)}, u32[]{:S(2)}) collective-permute-start(bf16[3,2,2,2,88,128]{5,4,0,2,3,1:T(8,128)(2,1)S(1)} %fusion.7), channel_id=1, source_target_pairs={{0,24},{1,25},{2,26},{3,27},{4,28},{5,29},{6,30},{7,31},{8,16},{9,... | collective-permute-start | bytes 1622024 | tf_op jit(solution)/shard_map/ppermute | solution.py:462
  (135 other events, 1092.5 us)
Sparse Core Ops, SparseCore 0:
  46.4 116.1 all-gather.7
  164.9 66.5 all-gather.9
  240.4 73.4 all-gather.11
  337.6 64.5 all-gather.13

commit v10 on v9

--- a/solution.py
+++ b/solution.py
@@ -509,6 +509,7 @@
     after_ref,
     layer_ref,
     before_ref,
+    last_ref,
     head_ref,
     block_ref,
     embed_ref,
@@ -544,7 +545,6 @@
             ).astype(narrow)
     tail_lines = tail // 128
     layer_lines = layer_ref.shape[1]
-    vector_at = tail + layer_piece - tail
     for part in range(layer_ref.shape[0]):
         flat_ref[pl.ds(0, tail_lines), :] = before_ref[part]
         flat_ref[pl.ds(tail_lines, layer_lines), :] = layer_ref[part]
@@ -552,12 +552,12 @@
             block_ref[part, :, pl.ds(chunk * 128, 128)] = shifted(
                 flat_ref, place_ref[4], place_ref[5], chunk, block_ref.shape[1], D // 128
             ).astype(narrow)
-            vector_ref[part, :, pl.ds(chunk * 128, 128)] = shifted(
-                flat_ref, vector_at // 128, vector_at % 128, chunk, 8, D // 128
-            ).astype(narrow)
-
-
-def own_blocks(place, stems, after, layer_rows, before, shape, slot, block_rows, embed_rows):
+            vector_ref[part, :, pl.ds(chunk * 128, 128)] = last_ref[
+                part, pl.ds(chunk, 8, stride=D // 128), :
+            ].astype(narrow)
+
+
+def own_blocks(place, stems, after, layer_rows, before, last_lines, shape, slot, block_rows, embed_rows):
     front, stem_piece, layer_piece, tail = shape
     lines = front + stem_piece // 128 + after.shape[1] + slot * ROW // 128
     flats = tail // 128 + layer_rows.shape[1] + 48
@@ -569,11 +569,11 @@
             jax.ShapeDtypeStruct((2, embed_rows, D), narrow),
             jax.ShapeDtypeStruct((2 * LAYERS, 8, D), narrow),
         ],
-        in_specs=[pl.BlockSpec(memory_space=pltpu.SMEM)] + [pl.BlockSpec(memory_space=pltpu.VMEM)] * 4,
+        in_specs=[pl.BlockSpec(memory_space=pltpu.SMEM)] + [pl.BlockSpec(memory_space=pltpu.VMEM)] * 5,
         out_specs=[pl.BlockSpec(memory_space=pltpu.VMEM)] * 4,
         scratch_shapes=[pltpu.VMEM((lines, 128), single), pltpu.VMEM((flats, 128), single)],
         compiler_params=pltpu.CompilerParams(vmem_limit_bytes=40 << 20),
-    )(place, stems, after, layer_rows, before)
+    )(place, stems, after, layer_rows, before, last_lines)
 
 
 def shards_kernel(held, place_ref, head_ref, previous_ref, block_ref, behind_ref, *refs):
@@ -1161,6 +1161,7 @@
     centre_ref,
     class_ref,
     mixed_ref,
+    mixed_teacher_ref,
     sums_ref,
     centre_sum_ref,
     student_mix_ref,
@@ -1189,10 +1190,10 @@
 
     @pl.when(step == pl.num_programs(0) - 1)
     def _():
-        mixed_ref[:, pl.ds(0, BOT)] = student_mix_ref[...].T
-        mixed_ref[:, pl.ds(BOT, BOT)] = teacher_mix_ref[...].T
+        mixed_ref[...] = student_mix_ref[...].T
+        mixed_teacher_ref[:, pl.ds(0, BOT)] = teacher_mix_ref[...].T
         lower = jnp.zeros((128 - totals_ref.shape[0], totals_ref.shape[1]), single)
-        mixed_ref[:, pl.ds(2 * BOT, 128)] = jnp.concatenate([totals_ref[...], lower]).T
+        mixed_teacher_ref[:, pl.ds(BOT, 128)] = jnp.concatenate([totals_ref[...], lower]).T
         sums_ref[...] = totals_ref[...]
 
 
@@ -1212,12 +1213,13 @@
         logits_kernel,
         grid=(4,),
         out_shape=[
-            jax.ShapeDtypeStruct((rows, 2 * BOT + 128), single),
+            jax.ShapeDtypeStruct((rows, BOT), single),
+            jax.ShapeDtypeStruct((rows, BOT + 128), single),
             jax.ShapeDtypeStruct((8, rows), single),
             jax.ShapeDtypeStruct((protos_here, 1), single),
         ],
         in_specs=[whole, whole, table, table, column, lines],
-        out_specs=[pl.BlockSpec((rows, 2 * BOT + 128), lambda i: (0, 0)), lines, column],
+        out_specs=[whole, pl.BlockSpec((rows, BOT + 128), lambda i: (0, 0)), lines, column],
         scratch_shapes=[
             pltpu.VMEM((BOT, rows), single),
             pltpu.VMEM((BOT, rows), single),
@@ -1439,6 +1441,9 @@
     own_layers = jnp.concatenate([layer_teacher, layers])
     own_tail = own_layers[:, layer_piece - tail :].reshape(2 * LAYERS, tail // 128, 128)
     before = lax.ppermute(own_tail, "dev", step_pairs(count, 1))
+    last_lines = lax.ppermute(
+        jnp.pad(own_tail, ((0, 0), (0, 24 - tail // 128), (0, 0))), "dev", [(count - 1, 0)]
+    )
     head_span = GROUP * ROW
     stems = jnp.stack([as_lanes(stem_teacher), as_lanes(stem)])
     stems_next = lax.ppermute(stems[:, : head_span // 128], "dev", step_pairs(count, -1))
@@ -1460,6 +1465,7 @@
         stems_next,
         as_lanes(own_layers),
         before,
+        last_lines,
         (front, stem_piece, layer_piece, tail),
         slot,
         block_rows,
@@ -1480,8 +1486,7 @@
         student_side, jnp.stack([head_got, head_keep]), jnp.stack([head_keep, head_got])
     )
 
-    vectors = lax.ppermute(vector_blocks, "dev", [(count - 1, 0)])
-    seed = jnp.concatenate([embed_blocks.reshape(2 * embed_rows, D), vectors.reshape(8 * 2 * LAYERS, D)])
+    seed = jnp.concatenate([embed_blocks.reshape(2 * embed_rows, D), vector_blocks.reshape(8 * 2 * LAYERS, D)])
     third = -(-seed.shape[0] // 48) * 16
     spread_parts = []
     for number, order in enumerate(("xyba", "baxy", "ybax")):
@@ -1509,12 +1514,7 @@
         )
         for m in range(2)
     ]
-    all_rows = half * pair_rows
-    kept_row = jnp.broadcast_to(kept[:, None], (images_here, 17)).reshape(1, rows_here)
-    kept_pair = cube_gather(kept_row, "b").reshape(1, 2 * rows_here)
-    kept_pair = jnp.pad(kept_pair, ((0, 0), (0, more_rows)))
-    all_kept = cube_gather(kept_pair, "xygc").reshape(all_rows)
-    gathered_head = lax.all_gather(after(both_head, gathered, even, odd, all_kept), "dev", axis=0, axis_index_groups=groups)
+    gathered_head = lax.all_gather(after(both_head, gathered, even, odd), "dev", axis=0, axis_index_groups=groups)
     vectors_all = even[2 * embed_rows :].reshape(2, LAYERS, 8, D)
 
     plan = []
@@ -1585,10 +1585,25 @@
     )
     inputs_all = lax.all_gather(acts, "dev", axis=0, axis_index_groups=groups).reshape(half * pair_rows, -1)
 
-    z_pair = cube_gather(unit_z, "b")
-    teacher_z_all = cube_gather(z_pair[0], "xygc").reshape(all_rows, BOT)
+    all_rows = half * pair_rows
+    flag_row = 2 * rows_here
+    kept_row = jnp.broadcast_to(kept[:, None] * (1.0 / 128.0), (images_here, 17)).reshape(1, rows_here)
+    kept_row = jnp.pad(kept_row.astype(narrow), ((0, 0), (0, BOT - rows_here)))
+    z_pair = cube_gather(jnp.concatenate([unit_z[:flag_row], kept_row, unit_z[flag_row + 1 :]]), "b")
+    teacher_z_all = cube_gather(z_pair[0], "xygc")
     student_z_all = cube_gather(z_pair[1], "gxyc").reshape((2,) * 4 + (pair_rows, BOT))
-    student_z_all = jnp.transpose(student_z_all, (0, 3, 1, 2, 4, 5)).reshape(all_rows, BOT)
+    student_z_all = jnp.transpose(student_z_all, (0, 3, 1, 2, 4, 5)).reshape(half, pair_rows, BOT)
+    all_kept = jnp.concatenate(
+        [
+            teacher_z_all[:, flag_row, :rows_here],
+            student_z_all[:, flag_row, :rows_here],
+            jnp.zeros((half, more_rows), narrow),
+        ],
+        axis=1,
+    )
+    all_kept = all_kept.astype(single).reshape(all_rows) * 128.0
+    teacher_z_all = teacher_z_all.reshape(all_rows, BOT)
+    student_z_all = student_z_all.reshape(all_rows, BOT)
     protos_here = protos.shape[0]
     own_centre = lax.dynamic_slice(centre, (me * protos_here,), (protos_here,))
     centre_column = own_centre.reshape(protos_here, 1)
@@ -1601,14 +1616,14 @@
     def lines(*values):
         return jnp.pad(jnp.stack(values), ((0, 8 - len(values)), (0, 0)))
 
-    mixed_rows, sums, centre_sum = logits_pass(
+    mixed_student, mixed_teacher, sums, centre_sum = logits_pass(
         teacher_z_all, student_z_all, proto_teacher, protos, centre_column, lines(class_kept)
     )
     by_pair = (2,) * 4 + (pair_rows, -1)
     mixed_own = jnp.concatenate(
         [
-            cube_scatter(mixed_rows[:, :BOT].reshape(by_pair), "cgyx", "cgyx"),
-            cube_scatter(mixed_rows[:, BOT:].reshape(by_pair), "cgyx", "cxyg"),
+            cube_scatter(mixed_student.reshape(by_pair), "cgyx", "cgyx"),
+            cube_scatter(mixed_teacher.reshape(by_pair), "cgyx", "cxyg"),
         ],
         axis=1,
     )
@@ -1637,6 +1652,22 @@
             jax.ShapeDtypeStruct((pair_rows, 2 * HID + BOT), narrow),
             jax.ShapeDtypeStruct((pair_rows, D), single),
         ],
+    )
+    carried = jnp.concatenate([own_new_centre, sums[:3].reshape(-1)])
+    carried_size = carried.shape[0]
+    width = grads.shape[1]
+    carried_rows = -(-3 * carried_size // width)
+    assert carried_rows <= more_rows
+    high = carried.astype(narrow)
+    middle = (carried - high.astype(single)).astype(narrow)
+    low = (carried - high.astype(single) - middle.astype(single)).astype(narrow)
+    carried = jnp.pad(jnp.concatenate([high, middle, low]), (0, carried_rows * width - 3 * carried_size))
+    grads = jnp.concatenate(
+        [
+            grads[: 2 * rows_here],
+            carried.reshape(carried_rows, width),
+            grads[2 * rows_here + carried_rows :],
+        ]
     )
     grads_all = lax.all_gather(grads, "dev", axis=0, axis_index_groups=groups).reshape(half * pair_rows, -1)
     normed_back = lax.ppermute(
@@ -1721,26 +1752,13 @@
             for i in range(count)
         ]
     )
-    slow = [own_new_centre.reshape(1, protos_here), sums[:3]]
-    slow_order = ["c", "x", "y", "a", "b"]
-
-    def slow_round(sent, stay):
-        name = slow_order.pop(0)
-        got = [lax.ppermute(array, "dev", pairs(count, MASKS[name])) for array in sent]
-        joined = jnp.where(
-            flags[name] == 1,
-            jnp.concatenate([got[0], stay[0]], axis=0),
-            jnp.concatenate([stay[0], got[0]], axis=0),
-        )
-        return [joined, stay[1] + got[1]]
-
     started = []
     held_block = None
     waits = ()
     for layer_index in reversed(range(LAYERS)):
         saved, vectors = saved_layers[layer_index], vectors_all[1, layer_index]
         part = LAYERS + layer_index
-        grad_stream, late_grad, late_vectors, stay_one, stay_two, *held_block = mlp_back(
+        grad_stream, late_grad, late_vectors, *held_block = mlp_back(
             side,
             grad_stream,
             saved,
@@ -1748,14 +1766,13 @@
             gathered,
             part,
             waits + sends(started),
-            slow + ([partner_block_grad] if started else []),
+            [partner_block_grad] if started else [],
         )
-        slow = slow_round(slow, [stay_one, stay_two])
         late = over_core(late_grad, block_rows)
         started = [advance(state) for state in started]
         if started:
             block_got = lax.ppermute(held_block[0], "dev", [(i, i ^ across) for i in range(half, count)])
-        grad_stream, early_grad, early_vectors, stay_one, stay_two, *held_block = attention_back(
+        grad_stream, early_grad, early_vectors, *held_block = attention_back(
             side,
             grad_stream,
             saved,
@@ -1763,23 +1780,32 @@
             gathered,
             part,
             sends(started),
-            slow + ([own_block_grad] if started else []),
+            [own_block_grad] if started else [],
         )
-        slow = slow_round(slow, [stay_one, stay_two])
         vector_grads[layer_index] = (late_vectors + early_vectors)[:6]
         if layer_index == LAYERS - 1:
             sent, stay = core_cut(early_grad, block_rows)
-            own_block_grad, partner_block_grad, stay, stay_one, stay_two = head_grads(
-                place, inputs_all, grads_all, slot, -min(bounds[1], 0), (early_vectors,), [stay] + slow
+            own_block_grad, partner_block_grad, stay = head_grads(
+                place, inputs_all, grads_all, slot, -min(bounds[1], 0), (early_vectors,), [stay]
             )
-            slow = slow_round(slow, [stay_one, stay_two])
             waits = (own_block_grad,)
         started = [advance(state) for state in started]
         if layer_index > 0:
             started.append(start(late, move(sent, stay, "c")))
     own_block_grad = held_block[0]
-    new_centre = slow[0].reshape(-1)
-    sums = slow[1]
+    rows = grads_all.reshape(half, pair_rows, width)[:, 2 * rows_here : 2 * rows_here + carried_rows]
+    rows = rows.reshape(half, -1)[:, : 3 * carried_size].reshape(half, 3, carried_size).astype(single)
+    rows = rows[:, 0] + rows[:, 1] + rows[:, 2]
+    half_centre = rows[:, :protos_here].reshape(-1)
+    half_sums = jnp.sum(rows[:, protos_here:], axis=0)
+    other = lax.ppermute(jnp.concatenate([half_centre, half_sums]), "dev", pairs(count, across))
+    other_centre, other_sums = other[: half * protos_here], other[half * protos_here :]
+    new_centre = jnp.where(
+        student_side,
+        jnp.concatenate([other_centre, half_centre]),
+        jnp.concatenate([half_centre, other_centre]),
+    )
+    sums = (half_sums + other_sums).reshape(3, all_rows)
     cross = jnp.log(sums[1]) - sums[2] / (sums[0] * tau_student)
     loss_total = jnp.sum(row_weight * cross)
     student_scale, teacher_scale = scale / sums[1], scale / sums[0]

time: 618 us -> 615 us (level)
  starting transfers between devices: 113 us -> 87.9 us
  local copies, waits for them, and re-layouts: 67.5 us -> 78.4 us
    ppermute x24 -> x19, starting transfers between devices: 39.5 us -> 19.8 us  [cube_gather(): got = lax.ppermute(held, 'dev', pairs(count, MASKS[name]))]
    all_gather x1, waiting for transfers between devices: 5.48 us -> 19.1 us  [close_local(): lax.all_gather(both_layers, 'dev', axis=0, axis_index_groups=groups)]
    ppermute x11 -> x2, waiting for transfers between devices: 11.4 us -> 0.01 us  [the longest x1 0.01 us: close_local(): lax.ppermute(jnp.pad(own_tail, ((0, 0), (0, 24 - tail // 128), (0, 0))),...]
    ppermute x11 -> x2, starting transfers between devices: 11 us -> 1.37 us  [the longest x1 0.71 us: close_local(): lax.ppermute(jnp.concatenate([half_centre, half_sums]), 'dev', pairs(coun...]
    all_gather x1, waiting for transfers between devices: 0.07 us -> 8.81 us  [close_local(): lax.all_gather(grads, 'dev', axis=0, axis_index_groups=groups)]
    ppermute x24 -> x19, waiting for transfers between devices: 24.2 us -> 21.4 us  [cube_gather(): got = lax.ppermute(held, 'dev', pairs(count, MASKS[name]))]
    unnamed x141 -> x115, local copies, waits for them, and re-layouts: 12.6 us -> 12.5 us
  transfers between devices with their start and end apart: 91 -> 77, of which waited for: 37 -> 33; matrix products, arithmetic and copies ran while one was open for 16% -> 18% of each run, Pallas kernels for 27% -> 27%
where the time goes in v10:
time: 615 us; the launch traced here: 603 us
  Pallas kernels  178 us (29%)
  waiting for transfers between devices  174 us (28%)
  starting transfers between devices  87.9 us (14%)
  local copies, waits for them, and re-layouts  78.4 us (13%)
  other arithmetic  60.5 us (10%)
  between operations  23.4 us (4%)
    pallas_call x4, Pallas kernels, layer_back(): pl.pallas_call(lambda *refs: kernel(part, *refs[:len(refs) - 6 - len(held...  60.6 us
    pallas_call x4, Pallas kernels, layer_forward(): pl.pallas_call(lambda *refs: forward_kernel(part, keep, *refs), out_shape...  47.9 us
    ppermute x12, waiting for transfers between devices, close_local(): got = lax.ppermute(spread, 'dev', moves)  37.3 us
    ppermute x29, waiting for transfers between devices, move(): lax.ppermute(sent, 'dev', pairs(1 << len(BITS), MASKS[name])).astype(single)  35.4 us
    ppermute x29, starting transfers between devices, move(): lax.ppermute(sent, 'dev', pairs(1 << len(BITS), MASKS[name])).astype(single)  32.9 us
    ppermute x19, waiting for transfers between devices, cube_gather(): got = lax.ppermute(held, 'dev', pairs(count, MASKS[name]))  21.4 us
    ppermute x19, starting transfers between devices, cube_gather(): got = lax.ppermute(held, 'dev', pairs(count, MASKS[name]))  19.8 us
    pallas_call x2, Pallas kernels, head_pass(): pl.pallas_call(lambda *refs: kernel(plan, *refs[:read], *refs[read + len(...  19.5 us
  transfers between devices with their start and end apart: 77, of which 33 were waited for; matrix products, arithmetic and copies ran while one was open for 18% of the time, Pallas kernels for 27%

profile of v10, /device:TPU:8, one launch (start us, length us, event | category | flops | bytes accessed | tf_op | source)
XLA Modules:
  0.0 603.1 jit_solution(3985511338291133471)
XLA Ops:
  26.6 18.6 %collective-permute-done.16 = bf16[4,144,384]{2,1,0:T(8,128)(2,1)S(1)} collective-permute-done((bf16[4,144,384]{2,1,0:T(8,128)(2,1)S(1)}, bf16[4,144,384]{2,1,0:T(8,128)(2,1)S(1)}, u32[]{:S(2)}, u32[]{:S(2)}) %collective-permute-start.16) | collective-permute-done | bytes 442400 | tf_op jit(solution)/shard_map/ppermute | solution.py:1475
  64.0 11.8 %collective-permute-done.8 = bf16[336,384]{1,0:T(8,128)(2,1)S(1)} collective-permute-done((bf16[336,384]{1,0:T(8,128)(2,1)S(1)}, bf16[336,384]{1,0:T(8,128)(2,1)S(1)}, u32[]{:S(2)}, u32[]{:S(2)}) %collective-permute-start.8) | collective-permute-done | bytes 258080 | tf_op jit(solution)/shard_map/ppermute | solution.py:1497
  77.8 8.5 %collective-permute-done.13 = bf16[320,384]{1,0:T(8,128)(2,1)S(1)} collective-permute-done((bf16[320,384]{1,0:T(8,128)(2,1)S(1)}, bf16[320,384]{1,0:T(8,128)(2,1)S(1)}, u32[]{:S(2)}, u32[]{:S(2)}) %collective-permute-start.13) | collective-permute-done | bytes 245792 | tf_op jit(solution)/shard_map/ppermute | solution.py:1497
  98.1 12.0 %collective-permute-done.6 = bf16[336,384]{1,0:T(8,128)(2,1)S(1)} collective-permute-done((bf16[336,384]{1,0:T(8,128)(2,1)S(1)}, bf16[336,384]{1,0:T(8,128)(2,1)S(1)}, u32[]{:S(2)}, u32[]{:S(2)}) %collective-permute-start.6) | collective-permute-done | bytes 258080 | tf_op jit(solution)/shard_map/ppermute | solution.py:1497
  115.9 17.7 %collective-permute-done.18 = bf16[96,2048]{1,0:T(8,128)(2,1)S(1)} collective-permute-done((bf16[96,2048]{1,0:T(8,128)(2,1)S(1)}, bf16[96,2048]{1,0:T(8,128)(2,1)S(1)}, u32[]{:S(2)}, u32[]{:S(2)}) %collective-permute-start.18) | collective-permute-done | bytes 393248 | tf_op jit(solution)/shard_map/ppermute | solution.py:1484
  136.0 19.1 %all-gather.8.cloned.1.call-done.refs_3_.refs_1_.refs_7_.refs_6_ = bf16[16,2,4,144,384]{4,3,2,1,0:T(8,128)(2,1)} async-done(((bf16[1,2,4,144,384]{4,3,2,1,0:T(8,128)(2,1)}), bf16[16,2,4,144,384]{4,3,2,1,0:T(8,128)(2,1)}) %all-gather.8.cloned.1.call-update) | async-done | bytes 14155792 | tf_op jit(solution)/shard_map/all_gather | solution.py:1481
  163.1 11.5 %shard_map.448.refs_1_ = f32[544,384]{1,0:T(8,128)} custom-call(s32[1]{0:T(128)} %bitcast.refs_0_, f32[544,384]{1,0:T(8,128)} %bitcast.355, bf16[8,384]{1,0:T(8,128)(2,1)} %get-tuple-element.208.refs_2_, bf16[16,2,4,144,384]{4,3,2,1,0:T(8,128)(2,1)} %all-gather.8.cloned.1.call-done.refs_3_.refs_1_.refs_7_.refs_6_), custom_call_target="tpu_custom_call" | custom-call | flops 100000000 | bytes 43000000 | tf_op jit(solution)/shard_map/pallas_call | solution.py:915
  174.6 11.8 %shard_map.449 = f32[544,384]{1,0:T(8,128)} custom-call(s32[1]{0:T(128)} %bitcast.refs_0_, f32[544,384]{1,0:T(8,128)} %shard_map.448.refs_1_, bf16[8,384]{1,0:T(8,128)(2,1)} %get-tuple-element.207.refs_2_, bf16[16,2,4,144,384]{4,3,2,1,0:T(8,128)(2,1)} %all-gather.8.cloned.1.call-done.refs_3_.refs_1_.refs_7_.refs_6_), custom_call_target="tpu_custom_call" | custom-call | flops 100000000 | bytes 43000000 | tf_op jit(solution)/shard_map/pallas_call | solution.py:915
  188.5 12.1 %shard_map.450 = (f32[544,384]{1,0:T(8,128)}, bf16[544,1152]{1,0:T(8,128)(2,1)}, bf16[544,384]{1,0:T(8,128)(2,1)}, f32[544,384]{1,0:T(8,128)}, f32[544,1536]{1,0:T(8,128)}, /*index=5*/f32[544,384]{1,0:T(8,128)}) custom-call(s32[1]{0:T(128)} %bitcast.refs_0_, f32[544,384]{1,0:T(8,128)} %bitcast.327, ...), custom_call_target="tpu_custom_call" | custom-call | flops 100000000 | bytes 43000000 | tf_op jit(solution)/shard_map/pallas_call | solution.py:915
  200.5 12.6 %shard_map.451 = (f32[544,384]{1,0:T(8,128)}, bf16[544,1152]{1,0:T(8,128)(2,1)}, bf16[544,384]{1,0:T(8,128)(2,1)}, f32[544,384]{1,0:T(8,128)}, f32[544,1536]{1,0:T(8,128)}, /*index=5*/f32[544,384]{1,0:T(8,128)}) custom-call(s32[1]{0:T(128)} %bitcast.refs_0_, f32[544,384]{1,0:T(8,128)} %get-tuple-element.82.refs_1_.refs_2_, ...), custom_call_target="tpu_custom_call" | custom-call | flops 100000000 | bytes 43000000 | tf_op jit(solution)/shard_map/pallas_call | solution.py:915
  224.1 8.7 %shard_map.453 = (bf16[80,256]{1,0:T(8,128)(2,1)}, bf16[80,4608]{1,0:T(8,128)(2,1)}, f32[80,256]{1,0:T(8,128)}, f32[80,2048]{1,0:T(8,128)}, f32[80,2048]{1,0:T(8,128)}) custom-call(s32[1]{0:T(128)} %bitcast.refs_0_, bf16[80,384]{1,0:T(8,128)(2,1)} %pad.53.refs_1_, bf16[16,2,96,2048]{3,2,1,0:T(8,128)(2,1)} %bitcast.324), custom_call_target="tpu_custom_call" | custom-call | flops 100000000 | bytes 37000000 | tf_op jit(solution)/shard_map/pallas_call | solution.py:760
  252.6 6.0 collective-permute-done.22
  265.0 14.0 %shard_map.454 = (f32[1280,256]{1,0:T(8,128)}, f32[1280,384]{1,0:T(8,128)}, f32[8,1280]{1,0:T(8,128)}, f32[2048,1]{1,0:T(8,128)}) custom-call(bf16[1280,256]{1,0:T(8,128)(2,1)} %bitcast.336, bf16[1280,256]{1,0:T(8,128)(2,1)} %bitcast.340, f32[2048,256]{1,0:T(8,128)} %refs_3_.3, f32[2048,256]{1,0:T(8,128)} %refs_0_.1, f32[2048,1]{1,0:T(8,128)} %copy.166.centre_ref.refs_4_, ...), custom_call_target="tpu_custom_call" | custom-call | flops 100000000 | bytes 52000000 | tf_op jit(solution)/shard_map/pallas_call | solution.py:1212
  320.8 10.8 %shard_map.455 = (bf16[80,4352]{1,0:T(8,128)(2,1)}, f32[80,384]{1,0:T(8,128)}) custom-call(s32[1]{0:T(128)} %bitcast.refs_0_, f32[80,256]{1,0:T(8,128)} %fusion.35.refs_1_, f32[80,256]{1,0:T(8,128)} %get-tuple-element.88.refs_2_, f32[80,2048]{1,0:T(8,128)} %get-tuple-element.89.refs_3_, f32[80,2048]{1,0:T(8,128)} %get-tuple-element.90.refs_4_, ...), custom_call_target="tpu_custom_call" | custom-call | flops 100000000 | bytes 37000000 | tf_op jit(solution)/shard_map/pallas_call | solution.py:760
  345.6 13.7 %shard_map.456 = (f32[544,384]{1,0:T(8,128)}, f32[3,3168,128]{2,1,0:T(8,128)}, f32[8,384]{1,0:T(8,128)}) custom-call(s32[1]{0:T(128)} %bitcast.refs_0_, f32[544,384]{1,0:T(8,128)} %bitcast.335, f32[544,384]{1,0:T(8,128)} %get-tuple-element.82.refs_1_.refs_2_, f32[544,384]{1,0:T(8,128)} %get-tuple-element.95.refs_3_, f32[544,1536]{1,0:T(8,128)} %get-tuple-element.96.refs_4_, ...), custom_call_target="tpu_custom_call" | custom-call | flops 100000000 | bytes 60000000 | tf_op jit(solution)/shard_map/pallas_call | solution.py:1046
  362.7 16.8 %shard_map.457 = (f32[544,384]{1,0:T(8,128)}, f32[3,1728,128]{2,1,0:T(8,128)}, f32[8,384]{1,0:T(8,128)}) custom-call(s32[1]{0:T(128)} %bitcast.refs_0_, f32[544,384]{1,0:T(8,128)} %get-tuple-element.98.refs_1_, f32[544,384]{1,0:T(8,128)} %get-tuple-element.82.refs_1_.refs_2_, bf16[544,1152]{1,0:T(8,128)(2,1)} %get-tuple-element.99.refs_3_, ...), custom_call_target="tpu_custom_call" | custom-call | flops 100000000 | bytes 60000000 | tf_op jit(solution)/shard_map/pallas_call | solution.py:1046
  391.5 8.8 %all-gather.12.cloned.1.call-done.refs_2_ = bf16[1280,4352]{1,0:T(8,128)(2,1)} async-done(((bf16[80,4352]{1,0:T(8,128)(2,1)}), bf16[1280,4352]{1,0:T(8,128)(2,1)}) %all-gather.12.cloned.1.call-update) | async-done | bytes 11141136 | tf_op jit(solution)/shard_map/all_gather | solution.py:1672
  400.4 10.3 %shard_map.458 = (f32[96,2048]{1,0:T(8,128)}, bf16[96,2048]{1,0:T(8,128)(2,1)}, f32[3,6,144,128]{3,2,1,0:T(8,128)}) custom-call(s32[10]{0:T(128)} %fusion.89.refs_0_, bf16[1280,4608]{1,0:T(8,128)(2,1)} %all-gather.14.cloned.1.call-done.refs_1_, bf16[1280,4352]{1,0:T(8,128)(2,1)} %all-gather.12.cloned.1.call-done.refs_2_, ...), custom_call_target="tpu_custom_call", output_to_operand_aliasing={{2}: (4, {})} | custom-call | flops 100000000 | bytes 37000000 | tf_op jit(solution)/shard_map/pallas_call | solution.py:1365
  432.0 13.7 %shard_map.459 = (f32[544,384]{1,0:T(8,128)}, f32[3,3168,128]{2,1,0:T(8,128)}, f32[8,384]{1,0:T(8,128)}, bf16[96,2048]{1,0:T(8,128)(2,1)}) custom-call(s32[1]{0:T(128)} %bitcast.refs_0_, f32[544,384]{1,0:T(8,128)} %get-tuple-element.101.refs_1_, f32[544,384]{1,0:T(8,128)} %bitcast.328, ...), custom_call_target="tpu_custom_call", output_to_operand_aliasing={{3}: (11, {})} | custom-call | flops 100000000 | bytes 60000000 | tf_op jit(solution)/shard_map/pallas_call | solution.py:1046
  458.3 16.4 %shard_map.460 = (f32[544,384]{1,0:T(8,128)}, f32[3,1728,128]{2,1,0:T(8,128)}, f32[8,384]{1,0:T(8,128)}, f32[96,2048]{1,0:T(8,128)}) custom-call(s32[1]{0:T(128)} %bitcast.refs_0_, f32[544,384]{1,0:T(8,128)} %get-tuple-element.112.refs_1_, f32[544,384]{1,0:T(8,128)} %bitcast.329, ...), custom_call_target="tpu_custom_call", output_to_operand_aliasing={{3}: (9, {})} | custom-call | flops 100000000 | bytes 60000000 | tf_op jit(solution)/shard_map/pallas_call | solution.py:1046
  497.8 10.4 %shard_map.462 = (f32[2048,256]{1,0:T(8,128)}, f32[8,128]{1,0:T(8,128)}, f32[3,2,72,128]{3,2,1,0:T(8,128)}, f32[3,2,72,128]{3,2,1,0:T(8,128)}, f32[3,2,2,2,88,12...) custom-call(bf16[1280,256]{1,0:T(8,128)(2,1)} %bitcast.337, ...), custom_call_target="tpu_custom_call", output_to_operand_aliasing={{2}: (6, {}), {3}: (7, {}), {4}: (8, {}), {5}: (9, {})} | custom-call | flops 100000000 | bytes 40000000 | tf_op jit(solution)/shard_map/pallas_call | solution.py:1261
  517.5 5.3 collective-permute-done.54
  527.0 5.6 collective-permute-done.55
  573.0 8.1 %shard_map.464 = (f32[2048,256]{1,0:T(8,128)}, f32[2048,256]{1,0:T(8,128)}, f32[2048,256]{1,0:T(8,128)}, bf16[2048,256]{1,0:T(8,128)(2,1)}, f32[2048,256]{1,0:T(8,128)}) custom-call(f32[1]{0:T(128)} %bitcast.155.factor_ref, f32[2048,256]{1,0:T(8,128)} %refs_0_.1, f32[2048,256]{1,0:T(8,128)} %refs_1_.1, f32[2048,256]{1,0:T(8,128)} %refs_2_.3, ...), custom_call_target="tpu_custom_call" | custom-call | flops 10000000 | bytes 20000000 | tf_op jit(solution)/shard_map/pallas_call | solution.py:1288
  (562 shorter events, 295.4 us)
Async XLA Ops:
  7.2 148.0 %all-gather.8.cloned.1.call-start = ((), (), s32[]{:S(2)}) async-start(), calls=%async_computation | async-start | bytes 15040512 | tf_op jit(solution)/shard_map/all_gather | solution.py:1481
  25.0 20.3 %collective-permute-start.16 = (bf16[4,144,384]{2,1,0:T(8,128)(2,1)S(1)}, bf16[4,144,384]{2,1,0:T(8,128)(2,1)S(1)}, u32[]{:S(2)}, u32[]{:S(2)}) collective-permute-start(bf16[4,144,384]{2,1,0:T(8,128)(2,1)S(1)} %get-tuple-element.81), channel_id=1, source_target_pairs={{0,24},{1,25},{2,26},{3,27},{4,28},{5,29},{6,30},{7,31},{8,16},{9,... | collective-permute-start | bytes 1327112 | tf_op jit(solution)/shard_map/ppermute | solution.py:1475
  46.4 177.7 %all-gather.10.cloned.1.call-start = ((), (), s32[]{:S(2)}) async-start(), calls=%async_computation.1 | async-start | bytes 13369344 | tf_op jit(solution)/shard_map/all_gather | solution.py:1517
  61.4 25.0 %collective-permute-start.13 = (bf16[320,384]{1,0:T(8,128)(2,1)S(1)}, bf16[320,384]{1,0:T(8,128)(2,1)S(1)}, u32[]{:S(2)}, u32[]{:S(2)}) collective-permute-start(bf16[320,384]{1,0:T(8,128)(2,1)S(1)} %broadcast_select_fusion.12), channel_id=1, source_target_pairs={{0,8},{1,9},{4,12},{5,13},{24,16},{25,17},{28,20},{29,21}} | collective-permute-start | bytes 737288 | tf_op jit(solution)/shard_map/ppermute | solution.py:1497
  63.4 25.0 %collective-permute-start.5 = (bf16[336,384]{1,0:T(8,128)(2,1)S(1)}, bf16[336,384]{1,0:T(8,128)(2,1)S(1)}, u32[]{:S(2)}, u32[]{:S(2)}) collective-permute-start(bf16[336,384]{1,0:T(8,128)(2,1)S(1)} %broadcast_select_fusion.8), channel_id=1, source_target_pairs={{0,24},{1,25},{2,26},{3,27},{4,28},{5,29},{6,30},{7,31}} | collective-permute-start | bytes 774152 | tf_op jit(solution)/shard_map/ppermute | solution.py:1497
  89.1 21.0 %collective-permute-start.6 = (bf16[336,384]{1,0:T(8,128)(2,1)S(1)}, bf16[336,384]{1,0:T(8,128)(2,1)S(1)}, u32[]{:S(2)}, u32[]{:S(2)}) collective-permute-start(bf16[336,384]{1,0:T(8,128)(2,1)S(1)} %broadcast_select_fusion.9), channel_id=1, source_target_pairs={{0,8},{1,9},{2,10},{3,11},{4,12},{5,13},{6,14},{7,15},{24,16},{25,... | collective-permute-start | bytes 774152 | tf_op jit(solution)/shard_map/ppermute | solution.py:1497
  91.1 19.7 %collective-permute-start.10 = (bf16[336,384]{1,0:T(8,128)(2,1)S(1)}, bf16[336,384]{1,0:T(8,128)(2,1)S(1)}, u32[]{:S(2)}, u32[]{:S(2)}) collective-permute-start(bf16[336,384]{1,0:T(8,128)(2,1)S(1)} %broadcast_select_fusion.5), channel_id=1, source_target_pairs={{0,4},{1,5},{24,28},{25,29},{8,12},{9,13},{16,20},{17,21},{2,6},{3... | collective-permute-start | bytes 774152 | tf_op jit(solution)/shard_map/ppermute | solution.py:1497
  112.4 22.3 %collective-permute-start.15 = (bf16[992,384]{1,0:T(8,128)(2,1)}, bf16[992,384]{1,0:T(8,128)(2,1)S(1)}, u32[]{:S(2)}, u32[]{:S(2)}) collective-permute-start(bf16[992,384]{1,0:T(8,128)(2,1)} %pad_maximum_fusion.6), channel_id=1, source_target_pairs={{0,1},{1,0},{2,3},{3,2},{4,5},{5,4},{6,7},{7,6},{8,9},{9,8},{10,11... | collective-permute-start | bytes 2285576 | tf_op jit(solution)/shard_map/ppermute | solution.py:1504
  112.4 21.2 %collective-permute-start.18 = (bf16[96,2048]{1,0:T(8,128)(2,1)S(1)}, bf16[96,2048]{1,0:T(8,128)(2,1)S(1)}, u32[]{:S(2)}, u32[]{:S(2)}) collective-permute-start(bf16[96,2048]{1,0:T(8,128)(2,1)S(1)} %get-tuple-element.185), channel_id=1, source_target_pairs={{0,24},{1,25},{2,26},{3,27},{4,28},{5,29},{6,30},{7,31},{8,16},{9,... | collective-permute-start | bytes 1179656 | tf_op jit(solution)/shard_map/ppermute | solution.py:1484
  157.3 234.2 %all-gather.14.cloned.1.call-start = ((), (), s32[]{:S(2)}) async-start(), calls=%async_computation.3 | async-start | bytes 12533760 | tf_op jit(solution)/shard_map/all_gather | solution.py:1586
  232.8 167.5 %all-gather.12.cloned.1.call-start = ((), (), s32[]{:S(2)}) async-start(), calls=%async_computation.2 | async-start | bytes 11837440 | tf_op jit(solution)/shard_map/all_gather | solution.py:1672
  362.7 24.7 %collective-permute-start.40 = (f32[3,11,144,128]{3,2,1,0:T(8,128)}, f32[3,11,144,128]{3,2,1,0:T(8,128)}, u32[]{:S(2)}, u32[]{:S(2)}) collective-permute-start(f32[3,11,144,128]{3,2,1,0:T(8,128)} %dynamic-slice_bitcast_fusion.1), channel_id=1, source_target_pairs={{0,1},{1,0},{2,3},{3,2},{4,5},{5,4},{6,7},{7,6},{8,9},{9,8},{10,11... | collective-permute-start | bytes 7299080 | tf_op jit(solution)/shard_map/ppermute | solution.py:462
  382.5 28.1 %collective-permute-start.39 = (f32[3,6,144,128]{3,2,1,0:T(8,128)S(1)}, f32[3,6,144,128]{3,2,1,0:T(8,128)}, u32[]{:S(2)}, u32[]{:S(2)}) collective-permute-start(f32[3,6,144,128]{3,2,1,0:T(8,128)S(1)} %get-tuple-element.177), channel_id=1, source_target_pairs={{0,1},{1,0},{2,3},{3,2},{4,5},{5,4},{6,7},{7,6},{8,9},{9,8},{10,11... | collective-permute-start | bytes 3981320 | tf_op jit(solution)/shard_map/ppermute | solution.py:462
  415.9 34.1 %collective-permute-start.42 = (bf16[3,2,2,2,72,128]{5,4,0,2,3,1:T(8,128)(2,1)}, bf16[3,2,2,2,72,128]{5,4,0,2,3,1:T(8,128)(2,1)}, u32[]{:S(2)}, u32[]{:S(2)}) collective-permute-start(bf16[3,2,2,2,72,128]{5,4,0,2,3,1:T(8,128)(2,1)} %fusion.16), channel_id=1, source_target_pairs={{0,24},{1,25},{2,26},{3,27},{4,28},{5,29},{6,30},{7,31},{8,16},{9,... | collective-permute-start | bytes 1327112 | tf_op jit(solution)/shard_map/ppermute | solution.py:462
  419.3 36.4 %collective-permute-start.41 = (bf16[3,2,2,2,72,128]{5,4,0,2,1,3:T(8,128)(2,1)S(1)}, bf16[3,2,2,2,72,128]{5,4,0,2,1,3:T(8,128)(2,1)}, u32[]{:S(2)}, u32[]{:S(2)}) collective-permute-start(bf16[3,2,2,2,72,128]{5,4,0,2,1,3:T(8,128)(2,1)S(1)} %fusion.15), channel_id=1, source_target_pairs={{0,2},{1,3},{2,0},{3,1},{4,6},{5,7},{6,4},{7,5},{8,10},{9,11},{10,... | collective-permute-start | bytes 1327112 | tf_op jit(solution)/shard_map/ppermute | solution.py:462
  447.6 41.6 %collective-permute-start.48 = (f32[3,11,144,128]{3,2,1,0:T(8,128)S(1)}, f32[3,11,144,128]{3,2,1,0:T(8,128)}, u32[]{:S(2)}, u32[]{:S(2)}) collective-permute-start(f32[3,11,144,128]{3,2,1,0:T(8,128)S(1)} %dynamic-slice_bitcast_fusion), channel_id=1, source_target_pairs={{0,1},{1,0},{2,3},{3,2},{4,5},{5,4},{6,7},{7,6},{8,9},{9,8},{10,11... | collective-permute-start | bytes 7299080 | tf_op jit(solution)/shard_map/ppermute | solution.py:462
  447.7 29.3 %collective-permute-start.43 = (bf16[96,2048]{1,0:T(8,128)(2,1)}, bf16[96,2048]{1,0:T(8,128)(2,1)S(1)}, u32[]{:S(2)}, u32[]{:S(2)}) collective-permute-start(bf16[96,2048]{1,0:T(8,128)(2,1)} %get-tuple-element.116), channel_id=1, source_target_pairs={{16,8},{17,9},{18,10},{19,11},{20,12},{21,13},{22,14},{23,15},{24,... | collective-permute-start | bytes 1179656 | tf_op jit(solution)/shard_map/ppermute | solution.py:1774
  453.4 27.8 %collective-permute-start.46 = (bf16[3,2,2,72,128]{4,3,0,1,2:T(8,128)(2,1)}, bf16[3,2,2,72,128]{4,3,0,1,2:T(8,128)(2,1)}, u32[]{:S(2)}, u32[]{:S(2)}) collective-permute-start(bf16[3,2,2,72,128]{4,3,0,1,2:T(8,128)(2,1)} %fusion.22), channel_id=1, source_target_pairs={{0,8},{1,9},{2,10},{3,11},{4,12},{5,13},{6,14},{7,15},{8,0},{9,1},... | collective-permute-start | bytes 663560 | tf_op jit(solution)/shard_map/ppermute | solution.py:462
  457.5 20.9 %collective-permute-start.45 = (bf16[3,2,2,72,128]{4,3,0,2,1:T(8,128)(2,1)S(1)}, bf16[3,2,2,72,128]{4,3,0,2,1:T(8,128)(2,1)S(1)}, u32[]{:S(2)}, u32[]{:S(2)}) collective-permute-start(bf16[3,2,2,72,128]{4,3,0,2,1:T(8,128)(2,1)S(1)} %fusion.21), channel_id=1, source_target_pairs={{0,4},{1,5},{2,6},{3,7},{4,0},{5,1},{6,2},{7,3},{8,12},{9,13},{10,... | collective-permute-start | bytes 663560 | tf_op jit(solution)/shard_map/ppermute | solution.py:462
  478.5 82.2 %collective-permute-start.44 = (f32[16,2048]{1,0:T(8,128)S(1)}, f32[16,2048]{1,0:T(8,128)S(1)}, u32[]{:S(2)}, u32[]{:S(2)}) collective-permute-start(f32[16,2048]{1,0:T(8,128)S(1)} %constant_dynamic-slice_fusion.4), channel_id=1, source_target_pairs={{0,1},{1,2},{2,3},{3,4},{4,5},{5,6},{6,7},{7,8},{8,9},{9,10},{10,1... | collective-permute-start | bytes 393224 | tf_op jit(solution)/shard_map/ppermute | solution.py:1828
  481.3 27.0 %collective-permute-start.58 = (bf16[3,2,72,128]{3,2,0,1:T(8,128)(2,1)S(1)}, bf16[3,2,72,128]{3,2,0,1:T(8,128)(2,1)S(1)}, u32[]{:S(2)}, u32[]{:S(2)}) collective-permute-start(bf16[3,2,72,128]{3,2,0,1:T(8,128)(2,1)S(1)} %fusion.28), channel_id=1, source_target_pairs={{0,24},{1,25},{2,26},{3,27},{4,28},{5,29},{6,30},{7,31},{8,16},{9,... | collective-permute-start | bytes 331784 | tf_op jit(solution)/shard_map/ppermute | solution.py:462
  487.3 23.0 %collective-permute-start.60 = (bf16[3,2,72,128]{3,2,0,1:T(8,128)(2,1)S(1)}, bf16[3,2,72,128]{3,2,0,1:T(8,128)(2,1)S(1)}, u32[]{:S(2)}, u32[]{:S(2)}) collective-permute-start(bf16[3,2,72,128]{3,2,0,1:T(8,128)(2,1)S(1)} %fusion.29), channel_id=1, source_target_pairs={{0,2},{1,3},{2,0},{3,1},{4,6},{5,7},{6,4},{7,5},{8,10},{9,11},{10,... | collective-permute-start | bytes 331784 | tf_op jit(solution)/shard_map/ppermute | solution.py:462
  495.4 20.9 %collective-permute-start.50 = (bf16[3,2,2,2,88,128]{5,4,0,2,1,3:T(8,128)(2,1)S(1)}, bf16[3,2,2,2,88,128]{5,4,0,2,1,3:T(8,128)(2,1)S(1)}, u32[]{:S(2)}, u32[]{:S(2)}) collective-permute-start(bf16[3,2,2,2,88,128]{5,4,0,2,1,3:T(8,128)(2,1)S(1)} %fusion.6), channel_id=1, source_target_pairs={{0,2},{1,3},{2,0},{3,1},{4,6},{5,7},{6,4},{7,5},{8,10},{9,11},{10,... | collective-permute-start | bytes 1622024 | tf_op jit(solution)/shard_map/ppermute | solution.py:462
  496.6 26.3 %collective-permute-start.54 = (bf16[3,2,2,2,88,128]{5,4,0,2,3,1:T(8,128)(2,1)S(1)}, bf16[3,2,2,2,88,128]{5,4,0,2,3,1:T(8,128)(2,1)S(1)}, u32[]{:S(2)}, u32[]{:S(2)}) collective-permute-start(bf16[3,2,2,2,88,128]{5,4,0,2,3,1:T(8,128)(2,1)S(1)} %fusion.7), channel_id=1, source_target_pairs={{0,24},{1,25},{2,26},{3,27},{4,28},{5,29},{6,30},{7,31},{8,16},{9,... | collective-permute-start | bytes 1622024 | tf_op jit(solution)/shard_map/ppermute | solution.py:462
  (107 other events, 614.6 us)
Sparse Core Ops, SparseCore 0:
  46.5 108.6 all-gather.7
  157.5 66.5 all-gather.9
  232.9 72.9 all-gather.13
  334.8 65.5 all-gather.11

commit v11 on v10

--- a/solution.py
+++ b/solution.py
@@ -777,7 +777,7 @@
     )(side, *inputs, gathered, *waits)
 
 
-def fetch_rows(side_ref, part, gathered_ref, flat_ref, sems):
+def fetch_rows(side_ref, part, gathered_ref, flat_ref, sems, first_row, last_row):
     quarter = flat_ref.shape[0] // 4
     side = side_ref[0]
     first, second = side * quarter, (1 - side) * quarter
@@ -788,11 +788,11 @@
             sems.at[spot],
         )
         for spot, (at, owner) in enumerate(((first, 0), (second, 0), (second, 1), (first, 1)))
+        if spot * quarter * flat_ref.shape[1] < last_row and first_row < (spot + 1) * quarter * flat_ref.shape[1]
     ]
     for copy in copies:
         copy.start()
-    for copy in copies:
-        copy.wait()
+    return copies
 
 
 def matrix_rows(flat_ref, first_row, length):
@@ -841,14 +841,15 @@
         flat_ref, wide_ref, qkv_ref, up_ref, hidden_ref, sems = refs[6:]
     else:
         flat_ref, wide_ref, qkv_ref, up_ref, hidden_ref, packed_ref, mixed_ref, sems = refs[1:]
-    fetch_rows(side_ref, part, gathered_ref, flat_ref, sems)
+    copies = fetch_rows(side_ref, part, gathered_ref, flat_ref, sems, 0, MATRIX_ROWS)
+    vectors = vector_ref[...].astype(single)
+    stream = stream_ref[...]
+    normed = (norm_parts(stream)[0] * vectors[0:1] + vectors[1:2]).astype(narrow)
+    wait_all(copies)
     spread_columns(flat_ref, 0, 3, wide_ref, qkv_ref)
     spread_columns(flat_ref, 4 * D, FF // D, wide_ref, up_ref)
     w_proj = matrix_rows(flat_ref, 3 * D, D)
     w_down = matrix_rows(flat_ref, 4 * D + FF, FF)
-    vectors = vector_ref[...].astype(single)
-    stream = stream_ref[...]
-    normed = (norm_parts(stream)[0] * vectors[0:1] + vectors[1:2]).astype(narrow)
     for group in range(3):
         packed_ref[:, pl.ds(group * D, D)] = product_plain(normed, qkv_ref[group]).astype(narrow)
     for image in range(stream.shape[0] // PAD_SEQ):
@@ -939,9 +940,7 @@
     flat_ref, wide_ref, up_ref, hidden_ref, grad_pre_ref, sems = refs[-6:]
     lead = weight_grad_ref.shape[1] - 2 * FF
     weight_grad_ref[:, pl.ds(0, lead), :] = jnp.zeros((D // 128, lead, 128), single)
-    fetch_rows(side_ref, part, gathered_ref, flat_ref, sems)
-    spread_columns(flat_ref, 4 * D, FF // D, wide_ref, up_ref)
-    w_down = matrix_rows(flat_ref, 4 * D + FF, FF)
+    copies = fetch_rows(side_ref, part, gathered_ref, flat_ref, sems, 4 * D, MATRIX_ROWS)
     vectors = vector_ref[...].astype(single)
     grad_out = grad_ref[...]
     vector_grad_ref[...] = jnp.zeros_like(vector_grad_ref)
@@ -951,6 +950,9 @@
     normed_two = (unit_two * vectors[3:4] + vectors[4:5]).astype(narrow)
     vector_grad_ref[pl.ds(5, 1), :] = jnp.sum(grad_out * mlp_ref[...], axis=0, keepdims=True)
     grad_mlp = (grad_out * vectors[5:6]).astype(narrow)
+    wait_all(copies)
+    spread_columns(flat_ref, 4 * D, FF // D, wide_ref, up_ref)
+    w_down = matrix_rows(flat_ref, 4 * D + FF, FF)
     grad_normed_two = jnp.zeros_like(grad_out)
     for group in range(FF // D):
         spot = pl.ds(group * D, D)
@@ -994,9 +996,7 @@
     flat_ref, wide_ref, qkv_ref, grad_mixed_ref, grad_packed_ref, sems = refs[-6:]
     rest = weight_grad_ref.shape[1] - 4 * D
     weight_grad_ref[:, pl.ds(4 * D, rest), :] = jnp.zeros((D // 128, rest, 128), single)
-    fetch_rows(side_ref, part, gathered_ref, flat_ref, sems)
-    spread_columns(flat_ref, 0, 3, wide_ref, qkv_ref)
-    w_proj = matrix_rows(flat_ref, 3 * D, D)
+    copies = fetch_rows(side_ref, part, gathered_ref, flat_ref, sems, 0, 4 * D)
     vectors = vector_ref[...].astype(single)
     vector_grad_ref[...] = jnp.zeros_like(vector_grad_ref)
     grad_mid = grad_ref[...]
@@ -1005,6 +1005,9 @@
     proj_grad = product_left(mixed_ref[...], grad_attn)
     for column in range(D // 128):
         weight_grad_ref[column, pl.ds(3 * D, D), :] = proj_grad[:, column * 128 : (column + 1) * 128]
+    wait_all(copies)
+    spread_columns(flat_ref, 0, 3, wide_ref, qkv_ref)
+    w_proj = matrix_rows(flat_ref, 3 * D, D)
     grad_mixed_ref[...] = product_right(grad_attn, w_proj).astype(narrow)
     for image in range(stream.shape[0] // PAD_SEQ):
         rows = pl.ds(image * PAD_SEQ, PAD_SEQ)
@@ -1653,22 +1656,18 @@
             jax.ShapeDtypeStruct((pair_rows, D), single),
         ],
     )
-    carried = jnp.concatenate([own_new_centre, sums[:3].reshape(-1)])
-    carried_size = carried.shape[0]
     width = grads.shape[1]
-    carried_rows = -(-3 * carried_size // width)
-    assert carried_rows <= more_rows
+    wide = max(protos_here, all_rows)
+    carried = jnp.stack(
+        [jnp.pad(row, (0, wide - row.shape[0])) for row in (own_new_centre, sums[0], sums[1], sums[2])]
+    )
+    carried_rows = 3 * carried.shape[0]
+    assert carried_rows <= more_rows and wide <= width
     high = carried.astype(narrow)
     middle = (carried - high.astype(single)).astype(narrow)
     low = (carried - high.astype(single) - middle.astype(single)).astype(narrow)
-    carried = jnp.pad(jnp.concatenate([high, middle, low]), (0, carried_rows * width - 3 * carried_size))
-    grads = jnp.concatenate(
-        [
-            grads[: 2 * rows_here],
-            carried.reshape(carried_rows, width),
-            grads[2 * rows_here + carried_rows :],
-        ]
-    )
+    carried = jnp.pad(jnp.concatenate([high, middle, low]), ((0, more_rows - carried_rows), (0, width - wide)))
+    grads = jnp.concatenate([grads[: 2 * rows_here], carried])
     grads_all = lax.all_gather(grads, "dev", axis=0, axis_index_groups=groups).reshape(half * pair_rows, -1)
     normed_back = lax.ppermute(
         grad_normed[:rows_here], "dev", [(i, i ^ across) for i in range(half, count)]
@@ -1793,19 +1792,18 @@
         if layer_index > 0:
             started.append(start(late, move(sent, stay, "c")))
     own_block_grad = held_block[0]
-    rows = grads_all.reshape(half, pair_rows, width)[:, 2 * rows_here : 2 * rows_here + carried_rows]
-    rows = rows.reshape(half, -1)[:, : 3 * carried_size].reshape(half, 3, carried_size).astype(single)
+    rows = grads_all.reshape(half, pair_rows, width)[:, 2 * rows_here : 2 * rows_here + carried_rows, :wide]
+    rows = rows.reshape(half, 3, carried_rows // 3, wide).astype(single)
     rows = rows[:, 0] + rows[:, 1] + rows[:, 2]
-    half_centre = rows[:, :protos_here].reshape(-1)
-    half_sums = jnp.sum(rows[:, protos_here:], axis=0)
-    other = lax.ppermute(jnp.concatenate([half_centre, half_sums]), "dev", pairs(count, across))
-    other_centre, other_sums = other[: half * protos_here], other[half * protos_here :]
+    half_centre = rows[:, 0, :protos_here]
+    half_sums = jnp.sum(rows[:, 1:, :all_rows], axis=0)
+    other_centre = lax.ppermute(half_centre, "dev", pairs(count, across))
+    sums = half_sums + lax.ppermute(half_sums, "dev", pairs(count, across))
     new_centre = jnp.where(
         student_side,
         jnp.concatenate([other_centre, half_centre]),
         jnp.concatenate([half_centre, other_centre]),
-    )
-    sums = (half_sums + other_sums).reshape(3, all_rows)
+    ).reshape(-1)
     cross = jnp.log(sums[1]) - sums[2] / (sums[0] * tau_student)
     loss_total = jnp.sum(row_weight * cross)
     student_scale, teacher_scale = scale / sums[1], scale / sums[0]

time: 615 us -> 609 us (level)
  waiting for transfers between devices: 174 us -> 182 us
    ppermute x1 -> x2, waiting for transfers between devices: 0.01 us -> 6.89 us  [the longest x1 6.89 us: close_local(): other_centre = lax.ppermute(half_centre, 'dev', pairs(count, across))]
    unnamed x115 -> x105, local copies, waits for them, and re-layouts: 12.5 us -> 12.8 us
  transfers between devices with their start and end apart: 77 -> 78, of which waited for: 33 -> 36; matrix products, arithmetic and copies ran while one was open for 18% -> 18% of each run, Pallas kernels for 27% -> 27%
where the time goes in v11:
time: 609 us; the launch traced here: 600 us
  waiting for transfers between devices  182 us (30%)
  Pallas kernels  175 us (29%)
  starting transfers between devices  85.5 us (14%)
  local copies, waits for them, and re-layouts  77 us (13%)
  other arithmetic  55.8 us (9%)
  between operations  23.3 us (4%)
    pallas_call x4, Pallas kernels, layer_back(): pl.pallas_call(lambda *refs: kernel(part, *refs[:len(refs) - 6 - len(held...  58.2 us
    pallas_call x4, Pallas kernels, layer_forward(): pl.pallas_call(lambda *refs: forward_kernel(part, keep, *refs), out_shape...  47 us
    ppermute x12, waiting for transfers between devices, close_local(): got = lax.ppermute(spread, 'dev', moves)  37.3 us
    ppermute x29, waiting for transfers between devices, move(): lax.ppermute(sent, 'dev', pairs(1 << len(BITS), MASKS[name])).astype(single)  34.5 us
    ppermute x29, starting transfers between devices, move(): lax.ppermute(sent, 'dev', pairs(1 << len(BITS), MASKS[name])).astype(single)  28.9 us
    ppermute x19, waiting for transfers between devices, cube_gather(): got = lax.ppermute(held, 'dev', pairs(count, MASKS[name]))  22.6 us
    ppermute x19, starting transfers between devices, cube_gather(): got = lax.ppermute(held, 'dev', pairs(count, MASKS[name]))  20.2 us
    pallas_call x2, Pallas kernels, head_pass(): pl.pallas_call(lambda *refs: kernel(plan, *refs[:read], *refs[read + len(...  19.5 us
  transfers between devices with their start and end apart: 78, of which 36 were waited for; matrix products, arithmetic and copies ran while one was open for 18% of the time, Pallas kernels for 27%

profile of v11, /device:TPU:8, one launch (start us, length us, event | category | flops | bytes accessed | tf_op | source)
XLA Modules:
  0.0 600.0 jit_solution(4580042126114330286)
XLA Ops:
  26.6 18.6 %collective-permute-done.16 = bf16[4,144,384]{2,1,0:T(8,128)(2,1)S(1)} collective-permute-done((bf16[4,144,384]{2,1,0:T(8,128)(2,1)S(1)}, bf16[4,144,384]{2,1,0:T(8,128)(2,1)S(1)}, u32[]{:S(2)}, u32[]{:S(2)}) %collective-permute-start.16) | collective-permute-done | bytes 442400 | tf_op jit(solution)/shard_map/ppermute | solution.py:1478
  64.0 11.8 %collective-permute-done.8 = bf16[336,384]{1,0:T(8,128)(2,1)S(1)} collective-permute-done((bf16[336,384]{1,0:T(8,128)(2,1)S(1)}, bf16[336,384]{1,0:T(8,128)(2,1)S(1)}, u32[]{:S(2)}, u32[]{:S(2)}) %collective-permute-start.8) | collective-permute-done | bytes 258080 | tf_op jit(solution)/shard_map/ppermute | solution.py:1500
  77.8 8.5 %collective-permute-done.13 = bf16[320,384]{1,0:T(8,128)(2,1)S(1)} collective-permute-done((bf16[320,384]{1,0:T(8,128)(2,1)S(1)}, bf16[320,384]{1,0:T(8,128)(2,1)S(1)}, u32[]{:S(2)}, u32[]{:S(2)}) %collective-permute-start.13) | collective-permute-done | bytes 245792 | tf_op jit(solution)/shard_map/ppermute | solution.py:1500
  98.1 12.0 %collective-permute-done.6 = bf16[336,384]{1,0:T(8,128)(2,1)S(1)} collective-permute-done((bf16[336,384]{1,0:T(8,128)(2,1)S(1)}, bf16[336,384]{1,0:T(8,128)(2,1)S(1)}, u32[]{:S(2)}, u32[]{:S(2)}) %collective-permute-start.6) | collective-permute-done | bytes 258080 | tf_op jit(solution)/shard_map/ppermute | solution.py:1500
  115.9 17.7 %collective-permute-done.18 = bf16[96,2048]{1,0:T(8,128)(2,1)S(1)} collective-permute-done((bf16[96,2048]{1,0:T(8,128)(2,1)S(1)}, bf16[96,2048]{1,0:T(8,128)(2,1)S(1)}, u32[]{:S(2)}, u32[]{:S(2)}) %collective-permute-start.18) | collective-permute-done | bytes 393248 | tf_op jit(solution)/shard_map/ppermute | solution.py:1487
  136.0 19.1 %all-gather.8.cloned.1.call-done.refs_3_.refs_1_.refs_7_.refs_6_ = bf16[16,2,4,144,384]{4,3,2,1,0:T(8,128)(2,1)} async-done(((bf16[1,2,4,144,384]{4,3,2,1,0:T(8,128)(2,1)}), bf16[16,2,4,144,384]{4,3,2,1,0:T(8,128)(2,1)}) %all-gather.8.cloned.1.call-update) | async-done | bytes 14155792 | tf_op jit(solution)/shard_map/all_gather | solution.py:1484
  163.1 11.2 %shard_map.448.refs_1_ = f32[544,384]{1,0:T(8,128)} custom-call(s32[1]{0:T(128)} %bitcast.refs_0_, f32[544,384]{1,0:T(8,128)} %bitcast.359, bf16[8,384]{1,0:T(8,128)(2,1)} %get-tuple-element.212.refs_2_, bf16[16,2,4,144,384]{4,3,2,1,0:T(8,128)(2,1)} %all-gather.8.cloned.1.call-done.refs_3_.refs_1_.refs_7_.refs_6_), custom_call_target="tpu_custom_call" | custom-call | flops 100000000 | bytes 43000000 | tf_op jit(solution)/shard_map/pallas_call | solution.py:916
  174.3 11.5 %shard_map.449 = f32[544,384]{1,0:T(8,128)} custom-call(s32[1]{0:T(128)} %bitcast.refs_0_, f32[544,384]{1,0:T(8,128)} %shard_map.448.refs_1_, bf16[8,384]{1,0:T(8,128)(2,1)} %get-tuple-element.211.refs_2_, bf16[16,2,4,144,384]{4,3,2,1,0:T(8,128)(2,1)} %all-gather.8.cloned.1.call-done.refs_3_.refs_1_.refs_7_.refs_6_), custom_call_target="tpu_custom_call" | custom-call | flops 100000000 | bytes 43000000 | tf_op jit(solution)/shard_map/pallas_call | solution.py:916
  187.7 11.9 %shard_map.450 = (f32[544,384]{1,0:T(8,128)}, bf16[544,1152]{1,0:T(8,128)(2,1)}, bf16[544,384]{1,0:T(8,128)(2,1)}, f32[544,384]{1,0:T(8,128)}, f32[544,1536]{1,0:T(8,128)}, /*index=5*/f32[544,384]{1,0:T(8,128)}) custom-call(s32[1]{0:T(128)} %bitcast.refs_0_, f32[544,384]{1,0:T(8,128)} %bitcast.331, ...), custom_call_target="tpu_custom_call" | custom-call | flops 100000000 | bytes 43000000 | tf_op jit(solution)/shard_map/pallas_call | solution.py:916
  199.7 12.4 %shard_map.451 = (f32[544,384]{1,0:T(8,128)}, bf16[544,1152]{1,0:T(8,128)(2,1)}, bf16[544,384]{1,0:T(8,128)(2,1)}, f32[544,384]{1,0:T(8,128)}, f32[544,1536]{1,0:T(8,128)}, /*index=5*/f32[544,384]{1,0:T(8,128)}) custom-call(s32[1]{0:T(128)} %bitcast.refs_0_, f32[544,384]{1,0:T(8,128)} %get-tuple-element.82.refs_1_.refs_2_, ...), custom_call_target="tpu_custom_call" | custom-call | flops 100000000 | bytes 43000000 | tf_op jit(solution)/shard_map/pallas_call | solution.py:916
  224.1 8.7 %shard_map.453 = (bf16[80,256]{1,0:T(8,128)(2,1)}, bf16[80,4608]{1,0:T(8,128)(2,1)}, f32[80,256]{1,0:T(8,128)}, f32[80,2048]{1,0:T(8,128)}, f32[80,2048]{1,0:T(8,128)}) custom-call(s32[1]{0:T(128)} %bitcast.refs_0_, bf16[80,384]{1,0:T(8,128)(2,1)} %pad.63.refs_1_, bf16[16,2,96,2048]{3,2,1,0:T(8,128)(2,1)} %bitcast.329), custom_call_target="tpu_custom_call" | custom-call | flops 100000000 | bytes 37000000 | tf_op jit(solution)/shard_map/pallas_call | solution.py:760
  270.3 14.1 %shard_map.454 = (f32[1280,256]{1,0:T(8,128)}, f32[1280,384]{1,0:T(8,128)}, f32[8,1280]{1,0:T(8,128)}, f32[2048,1]{1,0:T(8,128)}) custom-call(bf16[1280,256]{1,0:T(8,128)(2,1)} %bitcast.341, bf16[1280,256]{1,0:T(8,128)(2,1)} %bitcast.345, f32[2048,256]{1,0:T(8,128)} %refs_3_.3, f32[2048,256]{1,0:T(8,128)} %refs_0_.1, f32[2048,1]{1,0:T(8,128)} %copy.168.centre_ref.refs_4_, ...), custom_call_target="tpu_custom_call" | custom-call | flops 100000000 | bytes 52000000 | tf_op jit(solution)/shard_map/pallas_call | solution.py:1215
  297.2 6.4 %collective-permute-done.29 = bf16[2,2,80,256]{3,2,1,0:T(8,128)(2,1)S(1)} collective-permute-done((bf16[2,2,80,256]{3,2,1,0:T(8,128)(2,1)S(1)}, bf16[2,2,80,256]{3,2,1,0:T(8,128)(2,1)S(1)}, u32[]{:S(2)}, u32[]{:S(2)}) %collective-permute-start.29) | collective-permute-done | bytes 163872 | tf_op jit(solution)/shard_map/ppermute | solution.py:462
  322.5 10.8 %shard_map.455 = (bf16[80,4352]{1,0:T(8,128)(2,1)}, f32[80,384]{1,0:T(8,128)}) custom-call(s32[1]{0:T(128)} %bitcast.refs_0_, f32[80,256]{1,0:T(8,128)} %fusion.39.refs_1_, f32[80,256]{1,0:T(8,128)} %get-tuple-element.88.refs_2_, f32[80,2048]{1,0:T(8,128)} %get-tuple-element.89.refs_3_, f32[80,2048]{1,0:T(8,128)} %get-tuple-element.90.refs_4_, ...), custom_call_target="tpu_custom_call" | custom-call | flops 100000000 | bytes 37000000 | tf_op jit(solution)/shard_map/pallas_call | solution.py:760
  346.3 13.3 %shard_map.456 = (f32[544,384]{1,0:T(8,128)}, f32[3,3168,128]{2,1,0:T(8,128)}, f32[8,384]{1,0:T(8,128)}) custom-call(s32[1]{0:T(128)} %bitcast.refs_0_, f32[544,384]{1,0:T(8,128)} %bitcast.340, f32[544,384]{1,0:T(8,128)} %get-tuple-element.82.refs_1_.refs_2_, f32[544,384]{1,0:T(8,128)} %get-tuple-element.95.refs_3_, f32[544,1536]{1,0:T(8,128)} %get-tuple-element.96.refs_4_, ...), custom_call_target="tpu_custom_call" | custom-call | flops 100000000 | bytes 60000000 | tf_op jit(solution)/shard_map/pallas_call | solution.py:1049
  363.0 16.1 %shard_map.457 = (f32[544,384]{1,0:T(8,128)}, f32[3,1728,128]{2,1,0:T(8,128)}, f32[8,384]{1,0:T(8,128)}) custom-call(s32[1]{0:T(128)} %bitcast.refs_0_, f32[544,384]{1,0:T(8,128)} %get-tuple-element.98.refs_1_, f32[544,384]{1,0:T(8,128)} %get-tuple-element.82.refs_1_.refs_2_, bf16[544,1152]{1,0:T(8,128)(2,1)} %get-tuple-element.99.refs_3_, ...), custom_call_target="tpu_custom_call" | custom-call | flops 100000000 | bytes 60000000 | tf_op jit(solution)/shard_map/pallas_call | solution.py:1049
  391.1 9.2 %all-gather.12.cloned.1.call-done.refs_2_ = bf16[1280,4352]{1,0:T(8,128)(2,1)} async-done(((bf16[80,4352]{1,0:T(8,128)(2,1)}), bf16[1280,4352]{1,0:T(8,128)(2,1)}) %all-gather.12.cloned.1.call-update) | async-done | bytes 11141136 | tf_op jit(solution)/shard_map/all_gather | solution.py:1671
  400.2 10.3 %shard_map.458 = (f32[96,2048]{1,0:T(8,128)}, bf16[96,2048]{1,0:T(8,128)(2,1)}, f32[3,6,144,128]{3,2,1,0:T(8,128)}) custom-call(s32[10]{0:T(128)} %fusion.82.refs_0_, bf16[1280,4608]{1,0:T(8,128)(2,1)} %all-gather.14.cloned.1.call-done.refs_1_, bf16[1280,4352]{1,0:T(8,128)(2,1)} %all-gather.12.cloned.1.call-done.refs_2_, ...), custom_call_target="tpu_custom_call", output_to_operand_aliasing={{2}: (4, {})} | custom-call | flops 100000000 | bytes 37000000 | tf_op jit(solution)/shard_map/pallas_call | solution.py:1368
  424.3 13.3 %shard_map.459 = (f32[544,384]{1,0:T(8,128)}, f32[3,3168,128]{2,1,0:T(8,128)}, f32[8,384]{1,0:T(8,128)}, bf16[96,2048]{1,0:T(8,128)(2,1)}) custom-call(s32[1]{0:T(128)} %bitcast.refs_0_, f32[544,384]{1,0:T(8,128)} %get-tuple-element.101.refs_1_, f32[544,384]{1,0:T(8,128)} %bitcast.332, ...), custom_call_target="tpu_custom_call", output_to_operand_aliasing={{3}: (11, {})} | custom-call | flops 100000000 | bytes 60000000 | tf_op jit(solution)/shard_map/pallas_call | solution.py:1049
  450.3 15.6 %shard_map.460 = (f32[544,384]{1,0:T(8,128)}, f32[3,1728,128]{2,1,0:T(8,128)}, f32[8,384]{1,0:T(8,128)}, f32[96,2048]{1,0:T(8,128)}) custom-call(s32[1]{0:T(128)} %bitcast.refs_0_, f32[544,384]{1,0:T(8,128)} %get-tuple-element.112.refs_1_, f32[544,384]{1,0:T(8,128)} %bitcast.333, ...), custom_call_target="tpu_custom_call", output_to_operand_aliasing={{3}: (9, {})} | custom-call | flops 100000000 | bytes 60000000 | tf_op jit(solution)/shard_map/pallas_call | solution.py:1049
  488.0 10.4 %shard_map.462 = (f32[2048,256]{1,0:T(8,128)}, f32[8,128]{1,0:T(8,128)}, f32[3,2,72,128]{3,2,1,0:T(8,128)}, f32[3,2,72,128]{3,2,1,0:T(8,128)}, f32[3,2,2,2,88,12...) custom-call(bf16[1280,256]{1,0:T(8,128)(2,1)} %bitcast.342, ...), custom_call_target="tpu_custom_call", output_to_operand_aliasing={{2}: (6, {}), {3}: (7, {}), {4}: (8, {}), {5}: (9, {})} | custom-call | flops 100000000 | bytes 40000000 | tf_op jit(solution)/shard_map/pallas_call | solution.py:1264
  516.5 6.3 %collective-permute-done.55 = bf16[3,2,2,88,128]{4,3,0,1,2:T(8,128)(2,1)S(1)} collective-permute-done((bf16[3,2,2,88,128]{4,3,0,1,2:T(8,128)(2,1)S(1)}, bf16[3,2,2,88,128]{4,3,0,1,2:T(8,128)(2,1)S(1)}, u32[]{:S(2)}, u32[]{:S(2)}) %collective-permute-start.55) | collective-permute-done | bytes 270368 | tf_op jit(solution)/shard_map/ppermute | solution.py:462
  557.5 6.9 %collective-permute-done.71 = f32[16,2048]{1,0:T(8,128)S(1)} collective-permute-done((f32[16,2048]{1,0:T(8,128)S(1)}, f32[16,2048]{1,0:T(8,128)S(1)}, u32[]{:S(2)}, u32[]{:S(2)}) %collective-permute-start.71) | collective-permute-done | bytes 131104 | tf_op jit(solution)/shard_map/ppermute | solution.py:1800
  569.9 8.1 %shard_map.464 = (f32[2048,256]{1,0:T(8,128)}, f32[2048,256]{1,0:T(8,128)}, f32[2048,256]{1,0:T(8,128)}, bf16[2048,256]{1,0:T(8,128)(2,1)}, f32[2048,256]{1,0:T(8,128)}) custom-call(f32[1]{0:T(128)} %bitcast.163.factor_ref, f32[2048,256]{1,0:T(8,128)} %refs_0_.1, f32[2048,256]{1,0:T(8,128)} %refs_1_.1, f32[2048,256]{1,0:T(8,128)} %refs_2_.3, ...), custom_call_target="tpu_custom_call" | custom-call | flops 10000000 | bytes 20000000 | tf_op jit(solution)/shard_map/pallas_call | solution.py:1291
  (550 shorter events, 292.4 us)
Async XLA Ops:
  7.2 148.0 %all-gather.8.cloned.1.call-start = ((), (), s32[]{:S(2)}) async-start(), calls=%async_computation | async-start | bytes 15040512 | tf_op jit(solution)/shard_map/all_gather | solution.py:1484
  25.0 20.3 %collective-permute-start.16 = (bf16[4,144,384]{2,1,0:T(8,128)(2,1)S(1)}, bf16[4,144,384]{2,1,0:T(8,128)(2,1)S(1)}, u32[]{:S(2)}, u32[]{:S(2)}) collective-permute-start(bf16[4,144,384]{2,1,0:T(8,128)(2,1)S(1)} %get-tuple-element.81), channel_id=1, source_target_pairs={{0,24},{1,25},{2,26},{3,27},{4,28},{5,29},{6,30},{7,31},{8,16},{9,... | collective-permute-start | bytes 1327112 | tf_op jit(solution)/shard_map/ppermute | solution.py:1478
  46.4 177.7 %all-gather.10.cloned.1.call-start = ((), (), s32[]{:S(2)}) async-start(), calls=%async_computation.1 | async-start | bytes 13369344 | tf_op jit(solution)/shard_map/all_gather | solution.py:1520
  61.4 25.0 %collective-permute-start.13 = (bf16[320,384]{1,0:T(8,128)(2,1)S(1)}, bf16[320,384]{1,0:T(8,128)(2,1)S(1)}, u32[]{:S(2)}, u32[]{:S(2)}) collective-permute-start(bf16[320,384]{1,0:T(8,128)(2,1)S(1)} %broadcast_select_fusion.12), channel_id=1, source_target_pairs={{0,8},{1,9},{4,12},{5,13},{24,16},{25,17},{28,20},{29,21}} | collective-permute-start | bytes 737288 | tf_op jit(solution)/shard_map/ppermute | solution.py:1500
  63.4 25.0 %collective-permute-start.5 = (bf16[336,384]{1,0:T(8,128)(2,1)S(1)}, bf16[336,384]{1,0:T(8,128)(2,1)S(1)}, u32[]{:S(2)}, u32[]{:S(2)}) collective-permute-start(bf16[336,384]{1,0:T(8,128)(2,1)S(1)} %broadcast_select_fusion.8), channel_id=1, source_target_pairs={{0,24},{1,25},{2,26},{3,27},{4,28},{5,29},{6,30},{7,31}} | collective-permute-start | bytes 774152 | tf_op jit(solution)/shard_map/ppermute | solution.py:1500
  89.1 21.0 %collective-permute-start.6 = (bf16[336,384]{1,0:T(8,128)(2,1)S(1)}, bf16[336,384]{1,0:T(8,128)(2,1)S(1)}, u32[]{:S(2)}, u32[]{:S(2)}) collective-permute-start(bf16[336,384]{1,0:T(8,128)(2,1)S(1)} %broadcast_select_fusion.9), channel_id=1, source_target_pairs={{0,8},{1,9},{2,10},{3,11},{4,12},{5,13},{6,14},{7,15},{24,16},{25,... | collective-permute-start | bytes 774152 | tf_op jit(solution)/shard_map/ppermute | solution.py:1500
  91.1 19.7 %collective-permute-start.10 = (bf16[336,384]{1,0:T(8,128)(2,1)S(1)}, bf16[336,384]{1,0:T(8,128)(2,1)S(1)}, u32[]{:S(2)}, u32[]{:S(2)}) collective-permute-start(bf16[336,384]{1,0:T(8,128)(2,1)S(1)} %broadcast_select_fusion.5), channel_id=1, source_target_pairs={{0,4},{1,5},{24,28},{25,29},{8,12},{9,13},{16,20},{17,21},{2,6},{3... | collective-permute-start | bytes 774152 | tf_op jit(solution)/shard_map/ppermute | solution.py:1500
  112.4 22.3 %collective-permute-start.15 = (bf16[992,384]{1,0:T(8,128)(2,1)}, bf16[992,384]{1,0:T(8,128)(2,1)S(1)}, u32[]{:S(2)}, u32[]{:S(2)}) collective-permute-start(bf16[992,384]{1,0:T(8,128)(2,1)} %pad_maximum_fusion.6), channel_id=1, source_target_pairs={{0,1},{1,0},{2,3},{3,2},{4,5},{5,4},{6,7},{7,6},{8,9},{9,8},{10,11... | collective-permute-start | bytes 2285576 | tf_op jit(solution)/shard_map/ppermute | solution.py:1507
  112.4 21.2 %collective-permute-start.18 = (bf16[96,2048]{1,0:T(8,128)(2,1)S(1)}, bf16[96,2048]{1,0:T(8,128)(2,1)S(1)}, u32[]{:S(2)}, u32[]{:S(2)}) collective-permute-start(bf16[96,2048]{1,0:T(8,128)(2,1)S(1)} %get-tuple-element.188), channel_id=1, source_target_pairs={{0,24},{1,25},{2,26},{3,27},{4,28},{5,29},{6,30},{7,31},{8,16},{9,... | collective-permute-start | bytes 1179656 | tf_op jit(solution)/shard_map/ppermute | solution.py:1487
  157.3 233.7 %all-gather.14.cloned.1.call-start = ((), (), s32[]{:S(2)}) async-start(), calls=%async_computation.3 | async-start | bytes 12533760 | tf_op jit(solution)/shard_map/all_gather | solution.py:1589
  232.8 167.4 %all-gather.12.cloned.1.call-start = ((), (), s32[]{:S(2)}) async-start(), calls=%async_computation.2 | async-start | bytes 11837440 | tf_op jit(solution)/shard_map/all_gather | solution.py:1671
  362.9 23.9 %collective-permute-start.40 = (f32[3,11,144,128]{3,2,1,0:T(8,128)}, f32[3,11,144,128]{3,2,1,0:T(8,128)}, u32[]{:S(2)}, u32[]{:S(2)}) collective-permute-start(f32[3,11,144,128]{3,2,1,0:T(8,128)} %dynamic-slice_bitcast_fusion.1), channel_id=1, source_target_pairs={{0,1},{1,0},{2,3},{3,2},{4,5},{5,4},{6,7},{7,6},{8,9},{9,8},{10,11... | collective-permute-start | bytes 7299080 | tf_op jit(solution)/shard_map/ppermute | solution.py:462
  382.1 28.4 %collective-permute-start.39 = (f32[3,6,144,128]{3,2,1,0:T(8,128)S(1)}, f32[3,6,144,128]{3,2,1,0:T(8,128)}, u32[]{:S(2)}, u32[]{:S(2)}) collective-permute-start(f32[3,6,144,128]{3,2,1,0:T(8,128)S(1)} %get-tuple-element.180), channel_id=1, source_target_pairs={{0,1},{1,0},{2,3},{3,2},{4,5},{5,4},{6,7},{7,6},{8,9},{9,8},{10,11... | collective-permute-start | bytes 3981320 | tf_op jit(solution)/shard_map/ppermute | solution.py:462
  415.6 28.1 %collective-permute-start.42 = (bf16[3,2,2,2,72,128]{5,4,0,2,3,1:T(8,128)(2,1)}, bf16[3,2,2,2,72,128]{5,4,0,2,3,1:T(8,128)(2,1)}, u32[]{:S(2)}, u32[]{:S(2)}) collective-permute-start(bf16[3,2,2,2,72,128]{5,4,0,2,3,1:T(8,128)(2,1)} %fusion.17), channel_id=1, source_target_pairs={{0,24},{1,25},{2,26},{3,27},{4,28},{5,29},{6,30},{7,31},{8,16},{9,... | collective-permute-start | bytes 1327112 | tf_op jit(solution)/shard_map/ppermute | solution.py:462
  419.0 28.7 %collective-permute-start.41 = (bf16[3,2,2,2,72,128]{5,4,0,2,1,3:T(8,128)(2,1)S(1)}, bf16[3,2,2,2,72,128]{5,4,0,2,1,3:T(8,128)(2,1)}, u32[]{:S(2)}, u32[]{:S(2)}) collective-permute-start(bf16[3,2,2,2,72,128]{5,4,0,2,1,3:T(8,128)(2,1)S(1)} %fusion.16), channel_id=1, source_target_pairs={{0,2},{1,3},{2,0},{3,1},{4,6},{5,7},{6,4},{7,5},{8,10},{9,11},{10,... | collective-permute-start | bytes 1327112 | tf_op jit(solution)/shard_map/ppermute | solution.py:462
  440.9 38.6 %collective-permute-start.48 = (f32[3,11,144,128]{3,2,1,0:T(8,128)}, f32[3,11,144,128]{3,2,1,0:T(8,128)}, u32[]{:S(2)}, u32[]{:S(2)}) collective-permute-start(f32[3,11,144,128]{3,2,1,0:T(8,128)} %dynamic-slice_bitcast_fusion), channel_id=1, source_target_pairs={{0,1},{1,0},{2,3},{3,2},{4,5},{5,4},{6,7},{7,6},{8,9},{9,8},{10,11... | collective-permute-start | bytes 7299080 | tf_op jit(solution)/shard_map/ppermute | solution.py:462
  440.9 27.4 %collective-permute-start.43 = (bf16[96,2048]{1,0:T(8,128)(2,1)}, bf16[96,2048]{1,0:T(8,128)(2,1)S(1)}, u32[]{:S(2)}, u32[]{:S(2)}) collective-permute-start(bf16[96,2048]{1,0:T(8,128)(2,1)} %get-tuple-element.116), channel_id=1, source_target_pairs={{16,8},{17,9},{18,10},{19,11},{20,12},{21,13},{22,14},{23,15},{24,... | collective-permute-start | bytes 1179656 | tf_op jit(solution)/shard_map/ppermute | solution.py:1773
  445.6 26.9 %collective-permute-start.46 = (bf16[3,2,2,72,128]{4,3,0,1,2:T(8,128)(2,1)S(1)}, bf16[3,2,2,72,128]{4,3,0,1,2:T(8,128)(2,1)S(1)}, u32[]{:S(2)}, u32[]{:S(2)}) collective-permute-start(bf16[3,2,2,72,128]{4,3,0,1,2:T(8,128)(2,1)S(1)} %fusion.27), channel_id=1, source_target_pairs={{0,8},{1,9},{2,10},{3,11},{4,12},{5,13},{6,14},{7,15},{8,0},{9,1},... | collective-permute-start | bytes 663560 | tf_op jit(solution)/shard_map/ppermute | solution.py:462
  449.6 20.0 %collective-permute-start.45 = (bf16[3,2,2,72,128]{4,3,0,2,1:T(8,128)(2,1)S(1)}, bf16[3,2,2,72,128]{4,3,0,2,1:T(8,128)(2,1)S(1)}, u32[]{:S(2)}, u32[]{:S(2)}) collective-permute-start(bf16[3,2,2,72,128]{4,3,0,2,1:T(8,128)(2,1)S(1)} %fusion.26), channel_id=1, source_target_pairs={{0,4},{1,5},{2,6},{3,7},{4,0},{5,1},{6,2},{7,3},{8,12},{9,13},{10,... | collective-permute-start | bytes 663560 | tf_op jit(solution)/shard_map/ppermute | solution.py:462
  469.6 81.3 %collective-permute-start.44 = (f32[16,2048]{1,0:T(8,128)S(1)}, f32[16,2048]{1,0:T(8,128)S(1)}, u32[]{:S(2)}, u32[]{:S(2)}) collective-permute-start(f32[16,2048]{1,0:T(8,128)S(1)} %constant_dynamic-slice_fusion.4), channel_id=1, source_target_pairs={{0,1},{1,2},{2,3},{3,4},{4,5},{5,6},{6,7},{7,8},{8,9},{9,10},{10,1... | collective-permute-start | bytes 393224 | tf_op jit(solution)/shard_map/ppermute | solution.py:1826
  472.4 26.0 %collective-permute-start.58 = (bf16[3,2,72,128]{3,2,0,1:T(8,128)(2,1)S(1)}, bf16[3,2,72,128]{3,2,0,1:T(8,128)(2,1)S(1)}, u32[]{:S(2)}, u32[]{:S(2)}) collective-permute-start(bf16[3,2,72,128]{3,2,0,1:T(8,128)(2,1)S(1)} %fusion.35), channel_id=1, source_target_pairs={{0,24},{1,25},{2,26},{3,27},{4,28},{5,29},{6,30},{7,31},{8,16},{9,... | collective-permute-start | bytes 331784 | tf_op jit(solution)/shard_map/ppermute | solution.py:462
  477.6 23.0 %collective-permute-start.60 = (bf16[3,2,72,128]{3,2,0,1:T(8,128)(2,1)S(1)}, bf16[3,2,72,128]{3,2,0,1:T(8,128)(2,1)S(1)}, u32[]{:S(2)}, u32[]{:S(2)}) collective-permute-start(bf16[3,2,72,128]{3,2,0,1:T(8,128)(2,1)S(1)} %fusion.36), channel_id=1, source_target_pairs={{0,2},{1,3},{2,0},{3,1},{4,6},{5,7},{6,4},{7,5},{8,10},{9,11},{10,... | collective-permute-start | bytes 331784 | tf_op jit(solution)/shard_map/ppermute | solution.py:462
  485.8 20.0 %collective-permute-start.50 = (bf16[3,2,2,2,88,128]{5,4,0,2,1,3:T(8,128)(2,1)S(1)}, bf16[3,2,2,2,88,128]{5,4,0,2,1,3:T(8,128)(2,1)S(1)}, u32[]{:S(2)}, u32[]{:S(2)}) collective-permute-start(bf16[3,2,2,2,88,128]{5,4,0,2,1,3:T(8,128)(2,1)S(1)} %fusion.6), channel_id=1, source_target_pairs={{0,2},{1,3},{2,0},{3,1},{4,6},{5,7},{6,4},{7,5},{8,10},{9,11},{10,... | collective-permute-start | bytes 1622024 | tf_op jit(solution)/shard_map/ppermute | solution.py:462
  487.0 26.2 %collective-permute-start.54 = (bf16[3,2,2,2,88,128]{5,4,0,2,3,1:T(8,128)(2,1)S(1)}, bf16[3,2,2,2,88,128]{5,4,0,2,3,1:T(8,128)(2,1)S(1)}, u32[]{:S(2)}, u32[]{:S(2)}) collective-permute-start(bf16[3,2,2,2,88,128]{5,4,0,2,3,1:T(8,128)(2,1)S(1)} %fusion.7), channel_id=1, source_target_pairs={{0,24},{1,25},{2,26},{3,27},{4,28},{5,29},{6,30},{7,31},{8,16},{9,... | collective-permute-start | bytes 1622024 | tf_op jit(solution)/shard_map/ppermute | solution.py:462
  (103 other events, 613.3 us)
Sparse Core Ops, SparseCore 0:
  46.5 108.6 all-gather.7
  157.5 66.5 all-gather.9
  232.9 71.7 all-gather.13
  335.5 64.7 all-gather.11

commit v12 on v11

--- a/solution.py
+++ b/solution.py
@@ -1752,25 +1752,30 @@
         ]
     )
     started = []
-    held_block = None
-    waits = ()
     for layer_index in reversed(range(LAYERS)):
         saved, vectors = saved_layers[layer_index], vectors_all[1, layer_index]
         part = LAYERS + layer_index
-        grad_stream, late_grad, late_vectors, *held_block = mlp_back(
-            side,
-            grad_stream,
-            saved,
-            vectors,
-            gathered,
-            part,
-            waits + sends(started),
-            [partner_block_grad] if started else [],
+        grad_stream, late_grad, late_vectors = mlp_back(
+            side, grad_stream, saved, vectors, gathered, part, sends(started), []
         )
         late = over_core(late_grad, block_rows)
         started = [advance(state) for state in started]
-        if started:
-            block_got = lax.ppermute(held_block[0], "dev", [(i, i ^ across) for i in range(half, count)])
+        if layer_index == 0:
+            own_block_grad, partner_block_grad, *held = head_grads(
+                place,
+                inputs_all,
+                grads_all,
+                slot,
+                -min(bounds[1], 0),
+                (late_vectors,),
+                [stay for pieces, stage in started for sent, stay, left in pieces],
+            )
+            held = iter(held)
+            started = [
+                ([(sent, next(held), left) for sent, _, left in pieces], stage) for pieces, stage in started
+            ]
+            started = [advance(state) for state in started]
+            block_got = lax.ppermute(partner_block_grad, "dev", [(i, i ^ across) for i in range(half, count)])
         grad_stream, early_grad, early_vectors, *held_block = attention_back(
             side,
             grad_stream,
@@ -1779,18 +1784,12 @@
             gathered,
             part,
             sends(started),
-            [own_block_grad] if started else [],
+            [own_block_grad] if layer_index == 0 else [],
         )
         vector_grads[layer_index] = (late_vectors + early_vectors)[:6]
-        if layer_index == LAYERS - 1:
-            sent, stay = core_cut(early_grad, block_rows)
-            own_block_grad, partner_block_grad, stay = head_grads(
-                place, inputs_all, grads_all, slot, -min(bounds[1], 0), (early_vectors,), [stay]
-            )
-            waits = (own_block_grad,)
         started = [advance(state) for state in started]
         if layer_index > 0:
-            started.append(start(late, move(sent, stay, "c")))
+            started.append(start(late, over_core(early_grad, block_rows)))
     own_block_grad = held_block[0]
     rows = grads_all.reshape(half, pair_rows, width)[:, 2 * rows_here : 2 * rows_here + carried_rows, :wide]
     rows = rows.reshape(half, 3, carried_rows // 3, wide).astype(single)

time: 609 us -> 632 us (1.038)
  waiting for transfers between devices: 182 us -> 213 us
    ppermute x29, waiting for transfers between devices: 34.5 us -> 61.7 us  [move(): lax.ppermute(sent, 'dev', pairs(1 << len(BITS), MASKS[name])).astype(single)]
    ppermute x1, waiting for transfers between devices: 0.01 us -> 11 us  [close_local(): lax.ppermute(partner_block_grad, 'dev', [(i, i ^ across) for i in range(h...]
    all_gather x1, waiting for transfers between devices: 9.18 us -> 0.01 us  [close_local(): lax.all_gather(grads, 'dev', axis=0, axis_index_groups=groups)]
    unnamed x105 -> x111, local copies, waits for them, and re-layouts: 12.8 us -> 15 us
  transfers between devices with their start and end apart: 78 -> 78, of which waited for: 36 -> 38; matrix products, arithmetic and copies ran while one was open for 18% -> 17% of each run, Pallas kernels for 27% -> 26%
where the time goes in v12:
time: 632 us; the launch traced here: 624 us
  waiting for transfers between devices  213 us (34%)
  Pallas kernels  175 us (28%)
  starting transfers between devices  80.9 us (13%)
  local copies, waits for them, and re-layouts  76.1 us (12%)
  other arithmetic  54.7 us (9%)
  between operations  23.3 us (4%)
    ppermute x29, waiting for transfers between devices, move(): lax.ppermute(sent, 'dev', pairs(1 << len(BITS), MASKS[name])).astype(single)  61.7 us
    pallas_call x4, Pallas kernels, layer_back(): pl.pallas_call(lambda *refs: kernel(part, *refs[:len(refs) - 6 - len(held...  58.3 us
    pallas_call x4, Pallas kernels, layer_forward(): pl.pallas_call(lambda *refs: forward_kernel(part, keep, *refs), out_shape...  47 us
    ppermute x12, waiting for transfers between devices, close_local(): got = lax.ppermute(spread, 'dev', moves)  37.3 us
    ppermute x29, starting transfers between devices, move(): lax.ppermute(sent, 'dev', pairs(1 << len(BITS), MASKS[name])).astype(single)  22.7 us
    ppermute x19, starting transfers between devices, cube_gather(): got = lax.ppermute(held, 'dev', pairs(count, MASKS[name]))  22.2 us
    ppermute x19, waiting for transfers between devices, cube_gather(): got = lax.ppermute(held, 'dev', pairs(count, MASKS[name]))  21.9 us
    pallas_call x2, Pallas kernels, head_pass(): pl.pallas_call(lambda *refs: kernel(plan, *refs[:read], *refs[read + len(...  19.5 us
  transfers between devices with their start and end apart: 78, of which 38 were waited for; matrix products, arithmetic and copies ran while one was open for 17% of the time, Pallas kernels for 26%

profile of v12, /device:TPU:8, one launch (start us, length us, event | category | flops | bytes accessed | tf_op | source)
XLA Modules:
  0.0 623.6 jit_solution(4585606440264661422)
XLA Ops:
  26.9 18.6 %collective-permute-done.16 = bf16[4,144,384]{2,1,0:T(8,128)(2,1)S(1)} collective-permute-done((bf16[4,144,384]{2,1,0:T(8,128)(2,1)S(1)}, bf16[4,144,384]{2,1,0:T(8,128)(2,1)S(1)}, u32[]{:S(2)}, u32[]{:S(2)}) %collective-permute-start.16) | collective-permute-done | bytes 442400 | tf_op jit(solution)/shard_map/ppermute | solution.py:1478
  64.4 11.8 %collective-permute-done.8 = bf16[336,384]{1,0:T(8,128)(2,1)S(1)} collective-permute-done((bf16[336,384]{1,0:T(8,128)(2,1)S(1)}, bf16[336,384]{1,0:T(8,128)(2,1)S(1)}, u32[]{:S(2)}, u32[]{:S(2)}) %collective-permute-start.8) | collective-permute-done | bytes 258080 | tf_op jit(solution)/shard_map/ppermute | solution.py:1500
  78.2 8.5 %collective-permute-done.13 = bf16[320,384]{1,0:T(8,128)(2,1)S(1)} collective-permute-done((bf16[320,384]{1,0:T(8,128)(2,1)S(1)}, bf16[320,384]{1,0:T(8,128)(2,1)S(1)}, u32[]{:S(2)}, u32[]{:S(2)}) %collective-permute-start.13) | collective-permute-done | bytes 245792 | tf_op jit(solution)/shard_map/ppermute | solution.py:1500
  98.9 11.4 %collective-permute-done.6 = bf16[336,384]{1,0:T(8,128)(2,1)S(1)} collective-permute-done((bf16[336,384]{1,0:T(8,128)(2,1)S(1)}, bf16[336,384]{1,0:T(8,128)(2,1)S(1)}, u32[]{:S(2)}, u32[]{:S(2)}) %collective-permute-start.6) | collective-permute-done | bytes 258080 | tf_op jit(solution)/shard_map/ppermute | solution.py:1500
  116.1 17.9 %collective-permute-done.18 = bf16[96,2048]{1,0:T(8,128)(2,1)S(1)} collective-permute-done((bf16[96,2048]{1,0:T(8,128)(2,1)}, bf16[96,2048]{1,0:T(8,128)(2,1)S(1)}, u32[]{:S(2)}, u32[]{:S(2)}) %collective-permute-start.18) | collective-permute-done | bytes 393248 | tf_op jit(solution)/shard_map/ppermute | solution.py:1487
  136.4 19.3 %all-gather.8.cloned.1.call-done.refs_3_.refs_1_.refs_7_.refs_6_ = bf16[16,2,4,144,384]{4,3,2,1,0:T(8,128)(2,1)} async-done(((bf16[1,2,4,144,384]{4,3,2,1,0:T(8,128)(2,1)}), bf16[16,2,4,144,384]{4,3,2,1,0:T(8,128)(2,1)}) %all-gather.8.cloned.1.call-update) | async-done | bytes 14155792 | tf_op jit(solution)/shard_map/all_gather | solution.py:1484
  163.7 11.2 %shard_map.448.refs_1_ = f32[544,384]{1,0:T(8,128)} custom-call(s32[1]{0:T(128)} %bitcast.refs_0_, f32[544,384]{1,0:T(8,128)} %bitcast.349, bf16[8,384]{1,0:T(8,128)(2,1)} %get-tuple-element.210.refs_2_, bf16[16,2,4,144,384]{4,3,2,1,0:T(8,128)(2,1)} %all-gather.8.cloned.1.call-done.refs_3_.refs_1_.refs_7_.refs_6_), custom_call_target="tpu_custom_call" | custom-call | flops 100000000 | bytes 43000000 | tf_op jit(solution)/shard_map/pallas_call | solution.py:916
  174.9 11.7 %shard_map.449 = f32[544,384]{1,0:T(8,128)} custom-call(s32[1]{0:T(128)} %bitcast.refs_0_, f32[544,384]{1,0:T(8,128)} %shard_map.448.refs_1_, bf16[8,384]{1,0:T(8,128)(2,1)} %get-tuple-element.209.refs_2_, bf16[16,2,4,144,384]{4,3,2,1,0:T(8,128)(2,1)} %all-gather.8.cloned.1.call-done.refs_3_.refs_1_.refs_7_.refs_6_), custom_call_target="tpu_custom_call" | custom-call | flops 100000000 | bytes 43000000 | tf_op jit(solution)/shard_map/pallas_call | solution.py:916
  188.6 12.0 %shard_map.450 = (f32[544,384]{1,0:T(8,128)}, bf16[544,1152]{1,0:T(8,128)(2,1)}, bf16[544,384]{1,0:T(8,128)(2,1)}, f32[544,384]{1,0:T(8,128)}, f32[544,1536]{1,0:T(8,128)}, /*index=5*/f32[544,384]{1,0:T(8,128)}) custom-call(s32[1]{0:T(128)} %bitcast.refs_0_, f32[544,384]{1,0:T(8,128)} %bitcast.323, ...), custom_call_target="tpu_custom_call" | custom-call | flops 100000000 | bytes 43000000 | tf_op jit(solution)/shard_map/pallas_call | solution.py:916
  200.6 12.1 %shard_map.451 = (f32[544,384]{1,0:T(8,128)}, bf16[544,1152]{1,0:T(8,128)(2,1)}, bf16[544,384]{1,0:T(8,128)(2,1)}, f32[544,384]{1,0:T(8,128)}, f32[544,1536]{1,0:T(8,128)}, /*index=5*/f32[544,384]{1,0:T(8,128)}) custom-call(s32[1]{0:T(128)} %bitcast.refs_0_, f32[544,384]{1,0:T(8,128)} %get-tuple-element.82.refs_1_.refs_2_, ...), custom_call_target="tpu_custom_call" | custom-call | flops 100000000 | bytes 43000000 | tf_op jit(solution)/shard_map/pallas_call | solution.py:916
  224.7 8.7 %shard_map.453 = (bf16[80,256]{1,0:T(8,128)(2,1)}, bf16[80,4608]{1,0:T(8,128)(2,1)}, f32[80,256]{1,0:T(8,128)}, f32[80,2048]{1,0:T(8,128)}, f32[80,2048]{1,0:T(8,128)}) custom-call(s32[1]{0:T(128)} %bitcast.refs_0_, bf16[80,384]{1,0:T(8,128)(2,1)} %pad.63.refs_1_, bf16[16,2,96,2048]{3,2,1,0:T(8,128)(2,1)} %bitcast.321), custom_call_target="tpu_custom_call" | custom-call | flops 100000000 | bytes 37000000 | tf_op jit(solution)/shard_map/pallas_call | solution.py:760
  269.9 14.1 %shard_map.454 = (f32[1280,256]{1,0:T(8,128)}, f32[1280,384]{1,0:T(8,128)}, f32[8,1280]{1,0:T(8,128)}, f32[2048,1]{1,0:T(8,128)}) custom-call(bf16[1280,256]{1,0:T(8,128)(2,1)} %bitcast.333, bf16[1280,256]{1,0:T(8,128)(2,1)} %bitcast.335, f32[2048,256]{1,0:T(8,128)} %refs_3_.3, f32[2048,256]{1,0:T(8,128)} %refs_0_.1, f32[2048,1]{1,0:T(8,128)} %copy.156.centre_ref.refs_4_, ...), custom_call_target="tpu_custom_call" | custom-call | flops 100000000 | bytes 52000000 | tf_op jit(solution)/shard_map/pallas_call | solution.py:1215
  322.5 10.8 %shard_map.455 = (bf16[80,4352]{1,0:T(8,128)(2,1)}, f32[80,384]{1,0:T(8,128)}) custom-call(s32[1]{0:T(128)} %bitcast.refs_0_, f32[80,256]{1,0:T(8,128)} %fusion.39.refs_1_, f32[80,256]{1,0:T(8,128)} %get-tuple-element.88.refs_2_, f32[80,2048]{1,0:T(8,128)} %get-tuple-element.89.refs_3_, f32[80,2048]{1,0:T(8,128)} %get-tuple-element.90.refs_4_, ...), custom_call_target="tpu_custom_call" | custom-call | flops 100000000 | bytes 37000000 | tf_op jit(solution)/shard_map/pallas_call | solution.py:760
  346.5 13.2 %shard_map.456 = (f32[544,384]{1,0:T(8,128)}, f32[3,3168,128]{2,1,0:T(8,128)}, f32[8,384]{1,0:T(8,128)}) custom-call(s32[1]{0:T(128)} %bitcast.refs_0_, f32[544,384]{1,0:T(8,128)} %bitcast.332, f32[544,384]{1,0:T(8,128)} %get-tuple-element.82.refs_1_.refs_2_, f32[544,384]{1,0:T(8,128)} %get-tuple-element.95.refs_3_, f32[544,1536]{1,0:T(8,128)} %get-tuple-element.96.refs_4_, ...), custom_call_target="tpu_custom_call" | custom-call | flops 100000000 | bytes 60000000 | tf_op jit(solution)/shard_map/pallas_call | solution.py:1049
  363.2 15.9 %shard_map.457 = (f32[544,384]{1,0:T(8,128)}, f32[3,1728,128]{2,1,0:T(8,128)}, f32[8,384]{1,0:T(8,128)}) custom-call(s32[1]{0:T(128)} %bitcast.refs_0_, f32[544,384]{1,0:T(8,128)} %get-tuple-element.98.refs_1_, f32[544,384]{1,0:T(8,128)} %get-tuple-element.82.refs_1_.refs_2_, bf16[544,1152]{1,0:T(8,128)(2,1)} %get-tuple-element.99.refs_3_, ...), custom_call_target="tpu_custom_call" | custom-call | flops 100000000 | bytes 60000000 | tf_op jit(solution)/shard_map/pallas_call | solution.py:1049
  392.9 13.5 %shard_map.458 = (f32[544,384]{1,0:T(8,128)}, f32[3,3168,128]{2,1,0:T(8,128)}, f32[8,384]{1,0:T(8,128)}) custom-call(s32[1]{0:T(128)} %bitcast.refs_0_, f32[544,384]{1,0:T(8,128)} %get-tuple-element.101.refs_1_, f32[544,384]{1,0:T(8,128)} %bitcast.324, f32[544,384]{1,0:T(8,128)} %get-tuple-element.102.refs_3_, f32[544,1536]{1,0:T(8,128)} %get-tuple-element.103.refs_4_, ...), custom_call_target="tpu_custom_call" | custom-call | flops 100000000 | bytes 60000000 | tf_op jit(solution)/shard_map/pallas_call | solution.py:1049
  414.9 20.6 %collective-permute-done.42 = bf16[3,2,2,2,72,128]{5,4,0,2,3,1:T(8,128)(2,1)} collective-permute-done((bf16[3,2,2,2,72,128]{5,4,0,2,3,1:T(8,128)(2,1)}, bf16[3,2,2,2,72,128]{5,4,0,2,3,1:T(8,128)(2,1)}, u32[]{:S(2)}, u32[]{:S(2)}) %collective-permute-start.42) | collective-permute-done | bytes 442400 | tf_op jit(solution)/shard_map/ppermute | solution.py:462
  443.7 10.1 %shard_map.459 = (f32[96,2048]{1,0:T(8,128)}, bf16[96,2048]{1,0:T(8,128)(2,1)}, f32[3,2,2,72,128]{4,3,2,1,0:T(8,128)}, f32[3,2,2,72,128]{4,3,2,1,0:T(8,128)}) custom-call(s32[10]{0:T(128)} %fusion.82.refs_0_, bf16[1280,4608]{1,0:T(8,128)(2,1)} %all-gather.14.cloned.1.call-done.refs_1_, ...), custom_call_target="tpu_custom_call", output_to_operand_aliasing={{2}: (4, {}), {3}: (5, {})} | custom-call | flops 100000000 | bytes 37000000 | tf_op jit(solution)/shard_map/pallas_call | solution.py:1368
  456.7 15.6 %shard_map.460 = (f32[544,384]{1,0:T(8,128)}, f32[3,1728,128]{2,1,0:T(8,128)}, f32[8,384]{1,0:T(8,128)}, f32[96,2048]{1,0:T(8,128)}) custom-call(s32[1]{0:T(128)} %bitcast.refs_0_, f32[544,384]{1,0:T(8,128)} %get-tuple-element.107.refs_1_, f32[544,384]{1,0:T(8,128)} %bitcast.325, ...), custom_call_target="tpu_custom_call", output_to_operand_aliasing={{3}: (9, {})} | custom-call | flops 100000000 | bytes 60000000 | tf_op jit(solution)/shard_map/pallas_call | solution.py:1049
  490.0 11.0 %collective-permute-done.45 = bf16[96,2048]{1,0:T(8,128)(2,1)S(1)} collective-permute-done((bf16[96,2048]{1,0:T(8,128)(2,1)S(1)}, bf16[96,2048]{1,0:T(8,128)(2,1)S(1)}, u32[]{:S(2)}, u32[]{:S(2)}) %collective-permute-start.45) | collective-permute-done | bytes 393248 | tf_op jit(solution)/shard_map/ppermute | solution.py:1778
  512.0 10.4 %shard_map.462 = (f32[2048,256]{1,0:T(8,128)}, f32[8,128]{1,0:T(8,128)}, f32[3,72,128]{2,1,0:T(8,128)}, f32[3,72,128]{2,1,0:T(8,128)}, f32[3,2,2,2,88,128]{5,4,3...) custom-call(bf16[1280,256]{1,0:T(8,128)(2,1)} %bitcast.334, ...), custom_call_target="tpu_custom_call", output_to_operand_aliasing={{2}: (6, {}), {3}: (7, {}), {4}: (8, {}), {5}: (9, {})} | custom-call | flops 100000000 | bytes 40000000 | tf_op jit(solution)/shard_map/pallas_call | solution.py:1264
  527.8 9.3 %collective-permute-done.56 = bf16[3,2,2,2,88,128]{5,4,0,2,3,1:T(8,128)(2,1)S(1)} collective-permute-done((bf16[3,2,2,2,88,128]{5,4,0,2,3,1:T(8,128)(2,1)S(1)}, bf16[3,2,2,2,88,128]{5,4,0,2,3,1:T(8,128)(2,1)S(1)}, u32[]{:S(2)}, u32[]{:S(2)}) %collective-permute-start.56) | collective-permute-done | bytes 540704 | tf_op jit(solution)/shard_map/ppermute | solution.py:462
  537.8 8.8 %collective-permute-done.57 = bf16[3,2,2,88,128]{4,3,0,1,2:T(8,128)(2,1)S(1)} collective-permute-done((bf16[3,2,2,88,128]{4,3,0,1,2:T(8,128)(2,1)S(1)}, bf16[3,2,2,88,128]{4,3,0,1,2:T(8,128)(2,1)S(1)}, u32[]{:S(2)}, u32[]{:S(2)}) %collective-permute-start.57) | collective-permute-done | bytes 270368 | tf_op jit(solution)/shard_map/ppermute | solution.py:462
  594.0 8.1 %shard_map.464 = (f32[2048,256]{1,0:T(8,128)}, f32[2048,256]{1,0:T(8,128)}, f32[2048,256]{1,0:T(8,128)}, bf16[2048,256]{1,0:T(8,128)(2,1)}, f32[2048,256]{1,0:T(8,128)}) custom-call(f32[1]{0:T(128)} %bitcast.163.factor_ref, f32[2048,256]{1,0:T(8,128)} %refs_0_.1, f32[2048,256]{1,0:T(8,128)} %refs_1_.1, f32[2048,256]{1,0:T(8,128)} %refs_2_.3, ...), custom_call_target="tpu_custom_call" | custom-call | flops 10000000 | bytes 20000000 | tf_op jit(solution)/shard_map/pallas_call | solution.py:1291
  (556 shorter events, 295.3 us)
Async XLA Ops:
  7.2 148.6 %all-gather.8.cloned.1.call-start = ((), (), s32[]{:S(2)}) async-start(), calls=%async_computation | async-start | bytes 15040512 | tf_op jit(solution)/shard_map/all_gather | solution.py:1484
  25.3 20.3 %collective-permute-start.16 = (bf16[4,144,384]{2,1,0:T(8,128)(2,1)S(1)}, bf16[4,144,384]{2,1,0:T(8,128)(2,1)S(1)}, u32[]{:S(2)}, u32[]{:S(2)}) collective-permute-start(bf16[4,144,384]{2,1,0:T(8,128)(2,1)S(1)} %get-tuple-element.81), channel_id=1, source_target_pairs={{0,24},{1,25},{2,26},{3,27},{4,28},{5,29},{6,30},{7,31},{8,16},{9,... | collective-permute-start | bytes 1327112 | tf_op jit(solution)/shard_map/ppermute | solution.py:1478
  46.7 178.0 %all-gather.10.cloned.1.call-start = ((), (), s32[]{:S(2)}) async-start(), calls=%async_computation.1 | async-start | bytes 13369344 | tf_op jit(solution)/shard_map/all_gather | solution.py:1520
  61.7 25.0 %collective-permute-start.13 = (bf16[320,384]{1,0:T(8,128)(2,1)S(1)}, bf16[320,384]{1,0:T(8,128)(2,1)S(1)}, u32[]{:S(2)}, u32[]{:S(2)}) collective-permute-start(bf16[320,384]{1,0:T(8,128)(2,1)S(1)} %broadcast_select_fusion.12), channel_id=1, source_target_pairs={{0,8},{1,9},{4,12},{5,13},{24,16},{25,17},{28,20},{29,21}} | collective-permute-start | bytes 737288 | tf_op jit(solution)/shard_map/ppermute | solution.py:1500
  63.7 25.0 %collective-permute-start.5 = (bf16[336,384]{1,0:T(8,128)(2,1)S(1)}, bf16[336,384]{1,0:T(8,128)(2,1)S(1)}, u32[]{:S(2)}, u32[]{:S(2)}) collective-permute-start(bf16[336,384]{1,0:T(8,128)(2,1)S(1)} %broadcast_select_fusion.8), channel_id=1, source_target_pairs={{0,24},{1,25},{2,26},{3,27},{4,28},{5,29},{6,30},{7,31}} | collective-permute-start | bytes 774152 | tf_op jit(solution)/shard_map/ppermute | solution.py:1500
  89.4 21.0 %collective-permute-start.6 = (bf16[336,384]{1,0:T(8,128)(2,1)S(1)}, bf16[336,384]{1,0:T(8,128)(2,1)S(1)}, u32[]{:S(2)}, u32[]{:S(2)}) collective-permute-start(bf16[336,384]{1,0:T(8,128)(2,1)S(1)} %broadcast_select_fusion.9), channel_id=1, source_target_pairs={{0,8},{1,9},{2,10},{3,11},{4,12},{5,13},{6,14},{7,15},{24,16},{25,... | collective-permute-start | bytes 774152 | tf_op jit(solution)/shard_map/ppermute | solution.py:1500
  91.4 19.7 %collective-permute-start.10 = (bf16[336,384]{1,0:T(8,128)(2,1)S(1)}, bf16[336,384]{1,0:T(8,128)(2,1)S(1)}, u32[]{:S(2)}, u32[]{:S(2)}) collective-permute-start(bf16[336,384]{1,0:T(8,128)(2,1)S(1)} %broadcast_select_fusion.5), channel_id=1, source_target_pairs={{0,4},{1,5},{24,28},{25,29},{8,12},{9,13},{16,20},{17,21},{2,6},{3... | collective-permute-start | bytes 774152 | tf_op jit(solution)/shard_map/ppermute | solution.py:1500
  111.8 23.2 %collective-permute-start.15 = (bf16[992,384]{1,0:T(8,128)(2,1)S(1)}, bf16[992,384]{1,0:T(8,128)(2,1)S(1)}, u32[]{:S(2)}, u32[]{:S(2)}) collective-permute-start(bf16[992,384]{1,0:T(8,128)(2,1)S(1)} %pad_maximum_fusion.6), channel_id=1, source_target_pairs={{0,1},{1,0},{2,3},{3,2},{4,5},{5,4},{6,7},{7,6},{8,9},{9,8},{10,11... | collective-permute-start | bytes 2285576 | tf_op jit(solution)/shard_map/ppermute | solution.py:1507
  112.7 21.3 %collective-permute-start.18 = (bf16[96,2048]{1,0:T(8,128)(2,1)}, bf16[96,2048]{1,0:T(8,128)(2,1)S(1)}, u32[]{:S(2)}, u32[]{:S(2)}) collective-permute-start(bf16[96,2048]{1,0:T(8,128)(2,1)} %get-tuple-element.186), channel_id=1, source_target_pairs={{0,24},{1,25},{2,26},{3,27},{4,28},{5,29},{6,30},{7,31},{8,16},{9,... | collective-permute-start | bytes 1179656 | tf_op jit(solution)/shard_map/ppermute | solution.py:1487
  157.9 285.8 %all-gather.14.cloned.1.call-start = ((), (), s32[]{:S(2)}) async-start(), calls=%async_computation.3 | async-start | bytes 12533760 | tf_op jit(solution)/shard_map/all_gather | solution.py:1589
  233.5 210.2 %all-gather.12.cloned.1.call-start = ((), (), s32[]{:S(2)}) async-start(), calls=%async_computation.2 | async-start | bytes 11837440 | tf_op jit(solution)/shard_map/all_gather | solution.py:1671
  363.2 23.8 %collective-permute-start.40 = (f32[3,11,144,128]{3,2,1,0:T(8,128)}, f32[3,11,144,128]{3,2,1,0:T(8,128)}, u32[]{:S(2)}, u32[]{:S(2)}) collective-permute-start(f32[3,11,144,128]{3,2,1,0:T(8,128)} %dynamic-slice_bitcast_fusion.1), channel_id=1, source_target_pairs={{0,1},{1,0},{2,3},{3,2},{4,5},{5,4},{6,7},{7,6},{8,9},{9,8},{10,11... | collective-permute-start | bytes 7299080 | tf_op jit(solution)/shard_map/ppermute | solution.py:462
  409.7 30.4 %collective-permute-start.50 = (f32[3,11,144,128]{3,2,1,0:T(8,128)}, f32[3,11,144,128]{3,2,1,0:T(8,128)}, u32[]{:S(2)}, u32[]{:S(2)}) collective-permute-start(f32[3,11,144,128]{3,2,1,0:T(8,128)} %dynamic-slice_bitcast_fusion), channel_id=1, source_target_pairs={{0,1},{1,0},{2,3},{3,2},{4,5},{5,4},{6,7},{7,6},{8,9},{9,8},{10,11... | collective-permute-start | bytes 7299080 | tf_op jit(solution)/shard_map/ppermute | solution.py:462
  413.5 22.0 %collective-permute-start.42 = (bf16[3,2,2,2,72,128]{5,4,0,2,3,1:T(8,128)(2,1)}, bf16[3,2,2,2,72,128]{5,4,0,2,3,1:T(8,128)(2,1)}, u32[]{:S(2)}, u32[]{:S(2)}) collective-permute-start(bf16[3,2,2,2,72,128]{5,4,0,2,3,1:T(8,128)(2,1)} %copy-done.25), channel_id=1, source_target_pairs={{0,24},{1,25},{2,26},{3,27},{4,28},{5,29},{6,30},{7,31},{8,16},{9,... | collective-permute-start | bytes 1327112 | tf_op jit(solution)/shard_map/ppermute | solution.py:462
  414.3 22.7 %collective-permute-start.41 = (bf16[3,2,2,2,72,128]{5,4,0,2,1,3:T(8,128)(2,1)S(1)}, bf16[3,2,2,2,72,128]{5,4,0,2,1,3:T(8,128)(2,1)S(1)}, u32[]{:S(2)}, u32[]{:S(2)}) collective-permute-start(bf16[3,2,2,2,72,128]{5,4,0,2,1,3:T(8,128)(2,1)S(1)} %fusion.16), channel_id=1, source_target_pairs={{0,2},{1,3},{2,0},{3,1},{4,6},{5,7},{6,4},{7,5},{8,10},{9,11},{10,... | collective-permute-start | bytes 1327112 | tf_op jit(solution)/shard_map/ppermute | solution.py:462
  455.7 32.2 %collective-permute-start.48 = (bf16[3,2,72,128]{3,2,0,1:T(8,128)(2,1)S(1)}, bf16[3,2,72,128]{3,2,0,1:T(8,128)(2,1)S(1)}, u32[]{:S(2)}, u32[]{:S(2)}) collective-permute-start(bf16[3,2,72,128]{3,2,0,1:T(8,128)(2,1)S(1)} %fusion.36), channel_id=1, source_target_pairs={{0,2},{1,3},{2,0},{3,1},{4,6},{5,7},{6,4},{7,5},{8,10},{9,11},{10,... | collective-permute-start | bytes 331784 | tf_op jit(solution)/shard_map/ppermute | solution.py:462
  456.4 26.6 %collective-permute-start.47 = (bf16[3,2,72,128]{3,2,0,1:T(8,128)(2,1)S(1)}, bf16[3,2,72,128]{3,2,0,1:T(8,128)(2,1)S(1)}, u32[]{:S(2)}, u32[]{:S(2)}) collective-permute-start(bf16[3,2,72,128]{3,2,0,1:T(8,128)(2,1)S(1)} %fusion.35), channel_id=1, source_target_pairs={{0,24},{1,25},{2,26},{3,27},{4,28},{5,29},{6,30},{7,31},{8,16},{9,... | collective-permute-start | bytes 331784 | tf_op jit(solution)/shard_map/ppermute | solution.py:462
  473.7 30.6 %collective-permute-start.49 = (f32[3,6,144,128]{3,2,1,0:T(8,128)S(1)}, f32[3,6,144,128]{3,2,1,0:T(8,128)S(1)}, u32[]{:S(2)}, u32[]{:S(2)}) collective-permute-start(f32[3,6,144,128]{3,2,1,0:T(8,128)S(1)} %dynamic-slice_bitcast_fusion.2), channel_id=1, source_target_pairs={{0,1},{1,0},{2,3},{3,2},{4,5},{5,4},{6,7},{7,6},{8,9},{9,8},{10,11... | collective-permute-start | bytes 3981320 | tf_op jit(solution)/shard_map/ppermute | solution.py:462
  479.1 25.0 %collective-permute-start.51 = (f32[3,16,32,128]{3,2,1,0:T(8,128)S(1)}, f32[3,16,32,128]{3,2,1,0:T(8,128)S(1)}, u32[]{:S(2)}, u32[]{:S(2)}) collective-permute-start(f32[3,16,32,128]{3,2,1,0:T(8,128)S(1)} %dynamic-slice_bitcast_fusion.6), channel_id=1, source_target_pairs={{0,1},{1,0},{2,3},{3,2},{4,5},{5,4},{6,7},{7,6},{8,9},{9,8},{10,11... | collective-permute-start | bytes 2359304 | tf_op jit(solution)/shard_map/ppermute | solution.py:462
  480.4 20.7 %collective-permute-start.45 = (bf16[96,2048]{1,0:T(8,128)(2,1)S(1)}, bf16[96,2048]{1,0:T(8,128)(2,1)S(1)}, u32[]{:S(2)}, u32[]{:S(2)}) collective-permute-start(bf16[96,2048]{1,0:T(8,128)(2,1)S(1)} %copy-done.35), channel_id=1, source_target_pairs={{16,8},{17,9},{18,10},{19,11},{20,12},{21,13},{22,14},{23,15},{24,... | collective-permute-start | bytes 1179656 | tf_op jit(solution)/shard_map/ppermute | solution.py:1778
  483.1 39.3 %collective-permute-start.60 = (bf16[3,72,128]{2,1,0:T(8,128)(2,1)S(1)}, bf16[3,72,128]{2,1,0:T(8,128)(2,1)S(1)}, u32[]{:S(2)}, u32[]{:S(2)}) collective-permute-start(bf16[3,72,128]{2,1,0:T(8,128)(2,1)S(1)} %fusion.45), channel_id=1, source_target_pairs={{0,8},{1,9},{2,10},{3,11},{4,12},{5,13},{6,14},{7,15},{8,0},{9,1},... | collective-permute-start | bytes 165896 | tf_op jit(solution)/shard_map/ppermute | solution.py:462
  487.9 35.4 %collective-permute-start.61 = (bf16[3,72,128]{2,1,0:T(8,128)(2,1)S(1)}, bf16[3,72,128]{2,1,0:T(8,128)(2,1)S(1)}, u32[]{:S(2)}, u32[]{:S(2)}) collective-permute-start(bf16[3,72,128]{2,1,0:T(8,128)(2,1)S(1)} %fusion.46), channel_id=1, source_target_pairs={{0,4},{1,5},{2,6},{3,7},{4,0},{5,1},{6,2},{7,3},{8,12},{9,13},{10,... | collective-permute-start | bytes 165896 | tf_op jit(solution)/shard_map/ppermute | solution.py:462
  501.9 72.8 %collective-permute-start.46 = (f32[16,2048]{1,0:T(8,128)S(1)}, f32[16,2048]{1,0:T(8,128)S(1)}, u32[]{:S(2)}, u32[]{:S(2)}) collective-permute-start(f32[16,2048]{1,0:T(8,128)S(1)} %constant_dynamic-slice_fusion.2), channel_id=1, source_target_pairs={{0,1},{1,2},{2,3},{3,4},{4,5},{5,6},{6,7},{7,8},{8,9},{9,10},{10,1... | collective-permute-start | bytes 393224 | tf_op jit(solution)/shard_map/ppermute | solution.py:1825
  512.0 25.1 %collective-permute-start.56 = (bf16[3,2,2,2,88,128]{5,4,0,2,3,1:T(8,128)(2,1)S(1)}, bf16[3,2,2,2,88,128]{5,4,0,2,3,1:T(8,128)(2,1)S(1)}, u32[]{:S(2)}, u32[]{:S(2)}) collective-permute-start(bf16[3,2,2,2,88,128]{5,4,0,2,3,1:T(8,128)(2,1)S(1)} %fusion.7), channel_id=1, source_target_pairs={{0,24},{1,25},{2,26},{3,27},{4,28},{5,29},{6,30},{7,31},{8,16},{9,... | collective-permute-start | bytes 1622024 | tf_op jit(solution)/shard_map/ppermute | solution.py:462
  (105 other events, 645.1 us)
Sparse Core Ops, SparseCore 0:
  46.8 108.9 all-gather.7
  158.0 66.6 all-gather.9
  233.6 72.3 all-gather.13
  335.5 64.7 all-gather.11

commit v13 on v11

--- a/solution.py
+++ b/solution.py
@@ -455,7 +455,7 @@
     place = names.index(name) + lead
     sent = lax.dynamic_index_in_dim(array, 1 - mine, place, keepdims=False)
     kept = lax.dynamic_index_in_dim(array, mine, place, keepdims=False)
-    return (sent if name == "c" else sent.astype(narrow)), kept, names.replace(name, "")
+    return sent.astype(narrow), kept, names.replace(name, "")
 
 
 def move(sent, kept, name):

time: 609 us -> 608 us (level)
    squeeze x6 -> x0, local copies, waits for them, and re-layouts: 13.2 us -> none  [cut(): sent = lax.dynamic_index_in_dim(array, 1 - mine, place, keepdims=False)]
    convert_element_type x26 -> x33, local copies, waits for them, and re-layouts: 5.58 us -> 18.5 us  [cut(): return (sent.astype(narrow), kept, names.replace(name, ''))]
    unnamed x105 -> x102, local copies, waits for them, and re-layouts: 12.8 us -> 11.1 us
  transfers between devices with their start and end apart: 78 -> 78, of which waited for: 36 -> 37; matrix products, arithmetic and copies ran while one was open for 18% -> 18% of each run, Pallas kernels for 27% -> 27%
where the time goes in v13:
time: 608 us; the launch traced here: 599 us
  waiting for transfers between devices  183 us (30%)
  Pallas kernels  175 us (29%)
  starting transfers between devices  85.4 us (14%)
  local copies, waits for them, and re-layouts  76 us (12%)
  other arithmetic  55.1 us (9%)
  between operations  23.3 us (4%)
    pallas_call x4, Pallas kernels, layer_back(): pl.pallas_call(lambda *refs: kernel(part, *refs[:len(refs) - 6 - len(held...  58.2 us
    pallas_call x4, Pallas kernels, layer_forward(): pl.pallas_call(lambda *refs: forward_kernel(part, keep, *refs), out_shape...  47 us
    ppermute x12, waiting for transfers between devices, close_local(): got = lax.ppermute(spread, 'dev', moves)  37.3 us
    ppermute x29, waiting for transfers between devices, move(): lax.ppermute(sent, 'dev', pairs(1 << len(BITS), MASKS[name])).astype(single)  35.9 us
    ppermute x29, starting transfers between devices, move(): lax.ppermute(sent, 'dev', pairs(1 << len(BITS), MASKS[name])).astype(single)  28.8 us
    ppermute x19, waiting for transfers between devices, cube_gather(): got = lax.ppermute(held, 'dev', pairs(count, MASKS[name]))  22.3 us
    ppermute x19, starting transfers between devices, cube_gather(): got = lax.ppermute(held, 'dev', pairs(count, MASKS[name]))  20.7 us
    pallas_call x2, Pallas kernels, head_pass(): pl.pallas_call(lambda *refs: kernel(plan, *refs[:read], *refs[read + len(...  19.5 us
  transfers between devices with their start and end apart: 78, of which 37 were waited for; matrix products, arithmetic and copies ran while one was open for 18% of the time, Pallas kernels for 27%

profile of v13, /device:TPU:8, one launch (start us, length us, event | category | flops | bytes accessed | tf_op | source)
XLA Modules:
  0.0 598.9 jit_solution(14866103856254355513)
XLA Ops:
  26.6 18.6 %collective-permute-done.16 = bf16[4,144,384]{2,1,0:T(8,128)(2,1)S(1)} collective-permute-done((bf16[4,144,384]{2,1,0:T(8,128)(2,1)S(1)}, bf16[4,144,384]{2,1,0:T(8,128)(2,1)S(1)}, u32[]{:S(2)}, u32[]{:S(2)}) %collective-permute-start.16) | collective-permute-done | bytes 442400 | tf_op jit(solution)/shard_map/ppermute | solution.py:1478
  64.0 11.8 %collective-permute-done.8 = bf16[336,384]{1,0:T(8,128)(2,1)S(1)} collective-permute-done((bf16[336,384]{1,0:T(8,128)(2,1)S(1)}, bf16[336,384]{1,0:T(8,128)(2,1)S(1)}, u32[]{:S(2)}, u32[]{:S(2)}) %collective-permute-start.8) | collective-permute-done | bytes 258080 | tf_op jit(solution)/shard_map/ppermute | solution.py:1500
  77.8 8.5 %collective-permute-done.13 = bf16[320,384]{1,0:T(8,128)(2,1)S(1)} collective-permute-done((bf16[320,384]{1,0:T(8,128)(2,1)S(1)}, bf16[320,384]{1,0:T(8,128)(2,1)S(1)}, u32[]{:S(2)}, u32[]{:S(2)}) %collective-permute-start.13) | collective-permute-done | bytes 245792 | tf_op jit(solution)/shard_map/ppermute | solution.py:1500
  98.1 12.0 %collective-permute-done.6 = bf16[336,384]{1,0:T(8,128)(2,1)S(1)} collective-permute-done((bf16[336,384]{1,0:T(8,128)(2,1)S(1)}, bf16[336,384]{1,0:T(8,128)(2,1)S(1)}, u32[]{:S(2)}, u32[]{:S(2)}) %collective-permute-start.6) | collective-permute-done | bytes 258080 | tf_op jit(solution)/shard_map/ppermute | solution.py:1500
  115.9 17.7 %collective-permute-done.18 = bf16[96,2048]{1,0:T(8,128)(2,1)S(1)} collective-permute-done((bf16[96,2048]{1,0:T(8,128)(2,1)S(1)}, bf16[96,2048]{1,0:T(8,128)(2,1)S(1)}, u32[]{:S(2)}, u32[]{:S(2)}) %collective-permute-start.18) | collective-permute-done | bytes 393248 | tf_op jit(solution)/shard_map/ppermute | solution.py:1487
  136.0 19.1 %all-gather.8.cloned.1.call-done.refs_3_.refs_1_.refs_7_.refs_6_ = bf16[16,2,4,144,384]{4,3,2,1,0:T(8,128)(2,1)} async-done(((bf16[1,2,4,144,384]{4,3,2,1,0:T(8,128)(2,1)}), bf16[16,2,4,144,384]{4,3,2,1,0:T(8,128)(2,1)}) %all-gather.8.cloned.1.call-update) | async-done | bytes 14155792 | tf_op jit(solution)/shard_map/all_gather | solution.py:1484
  163.1 11.2 %shard_map.448.refs_1_ = f32[544,384]{1,0:T(8,128)} custom-call(s32[1]{0:T(128)} %bitcast.refs_0_, f32[544,384]{1,0:T(8,128)} %bitcast.362, bf16[8,384]{1,0:T(8,128)(2,1)} %get-tuple-element.208.refs_2_, bf16[16,2,4,144,384]{4,3,2,1,0:T(8,128)(2,1)} %all-gather.8.cloned.1.call-done.refs_3_.refs_1_.refs_7_.refs_6_), custom_call_target="tpu_custom_call" | custom-call | flops 100000000 | bytes 43000000 | tf_op jit(solution)/shard_map/pallas_call | solution.py:916
  174.3 11.5 %shard_map.449 = f32[544,384]{1,0:T(8,128)} custom-call(s32[1]{0:T(128)} %bitcast.refs_0_, f32[544,384]{1,0:T(8,128)} %shard_map.448.refs_1_, bf16[8,384]{1,0:T(8,128)(2,1)} %get-tuple-element.207.refs_2_, bf16[16,2,4,144,384]{4,3,2,1,0:T(8,128)(2,1)} %all-gather.8.cloned.1.call-done.refs_3_.refs_1_.refs_7_.refs_6_), custom_call_target="tpu_custom_call" | custom-call | flops 100000000 | bytes 43000000 | tf_op jit(solution)/shard_map/pallas_call | solution.py:916
  187.8 11.9 %shard_map.450 = (f32[544,384]{1,0:T(8,128)}, bf16[544,1152]{1,0:T(8,128)(2,1)}, bf16[544,384]{1,0:T(8,128)(2,1)}, f32[544,384]{1,0:T(8,128)}, f32[544,1536]{1,0:T(8,128)}, /*index=5*/f32[544,384]{1,0:T(8,128)}) custom-call(s32[1]{0:T(128)} %bitcast.refs_0_, f32[544,384]{1,0:T(8,128)} %bitcast.340, ...), custom_call_target="tpu_custom_call" | custom-call | flops 100000000 | bytes 43000000 | tf_op jit(solution)/shard_map/pallas_call | solution.py:916
  199.7 12.4 %shard_map.451 = (f32[544,384]{1,0:T(8,128)}, bf16[544,1152]{1,0:T(8,128)(2,1)}, bf16[544,384]{1,0:T(8,128)(2,1)}, f32[544,384]{1,0:T(8,128)}, f32[544,1536]{1,0:T(8,128)}, /*index=5*/f32[544,384]{1,0:T(8,128)}) custom-call(s32[1]{0:T(128)} %bitcast.refs_0_, f32[544,384]{1,0:T(8,128)} %get-tuple-element.82.refs_1_.refs_2_, ...), custom_call_target="tpu_custom_call" | custom-call | flops 100000000 | bytes 43000000 | tf_op jit(solution)/shard_map/pallas_call | solution.py:916
  224.1 8.7 %shard_map.453 = (bf16[80,256]{1,0:T(8,128)(2,1)}, bf16[80,4608]{1,0:T(8,128)(2,1)}, f32[80,256]{1,0:T(8,128)}, f32[80,2048]{1,0:T(8,128)}, f32[80,2048]{1,0:T(8,128)}) custom-call(s32[1]{0:T(128)} %bitcast.refs_0_, bf16[80,384]{1,0:T(8,128)(2,1)} %pad.63.refs_1_, bf16[16,2,96,2048]{3,2,1,0:T(8,128)(2,1)} %bitcast.338), custom_call_target="tpu_custom_call" | custom-call | flops 100000000 | bytes 37000000 | tf_op jit(solution)/shard_map/pallas_call | solution.py:760
  270.4 14.1 %shard_map.454 = (f32[1280,256]{1,0:T(8,128)}, f32[1280,384]{1,0:T(8,128)}, f32[8,1280]{1,0:T(8,128)}, f32[2048,1]{1,0:T(8,128)}) custom-call(bf16[1280,256]{1,0:T(8,128)(2,1)} %bitcast.350, bf16[1280,256]{1,0:T(8,128)(2,1)} %bitcast.354, f32[2048,256]{1,0:T(8,128)} %refs_3_.3, f32[2048,256]{1,0:T(8,128)} %refs_0_.1, f32[2048,1]{1,0:T(8,128)} %copy.165.centre_ref.refs_4_, ...), custom_call_target="tpu_custom_call" | custom-call | flops 100000000 | bytes 52000000 | tf_op jit(solution)/shard_map/pallas_call | solution.py:1215
  295.7 7.4 %collective-permute-done.29 = bf16[2,2,80,256]{3,2,1,0:T(8,128)(2,1)S(1)} collective-permute-done((bf16[2,2,80,256]{3,2,1,0:T(8,128)(2,1)S(1)}, bf16[2,2,80,256]{3,2,1,0:T(8,128)(2,1)S(1)}, u32[]{:S(2)}, u32[]{:S(2)}) %collective-permute-start.29) | collective-permute-done | bytes 163872 | tf_op jit(solution)/shard_map/ppermute | solution.py:462
  321.9 10.8 %shard_map.455 = (bf16[80,4352]{1,0:T(8,128)(2,1)}, f32[80,384]{1,0:T(8,128)}) custom-call(s32[1]{0:T(128)} %bitcast.refs_0_, f32[80,256]{1,0:T(8,128)} %fusion.45.refs_1_, f32[80,256]{1,0:T(8,128)} %get-tuple-element.88.refs_2_, f32[80,2048]{1,0:T(8,128)} %get-tuple-element.89.refs_3_, f32[80,2048]{1,0:T(8,128)} %get-tuple-element.90.refs_4_, ...), custom_call_target="tpu_custom_call" | custom-call | flops 100000000 | bytes 37000000 | tf_op jit(solution)/shard_map/pallas_call | solution.py:760
  345.8 13.3 %shard_map.456 = (f32[544,384]{1,0:T(8,128)}, f32[3,3168,128]{2,1,0:T(8,128)}, f32[8,384]{1,0:T(8,128)}) custom-call(s32[1]{0:T(128)} %bitcast.refs_0_, f32[544,384]{1,0:T(8,128)} %bitcast.349, f32[544,384]{1,0:T(8,128)} %get-tuple-element.82.refs_1_.refs_2_, f32[544,384]{1,0:T(8,128)} %get-tuple-element.95.refs_3_, f32[544,1536]{1,0:T(8,128)} %get-tuple-element.96.refs_4_, ...), custom_call_target="tpu_custom_call" | custom-call | flops 100000000 | bytes 60000000 | tf_op jit(solution)/shard_map/pallas_call | solution.py:1049
  366.2 16.1 %shard_map.457 = (f32[544,384]{1,0:T(8,128)}, f32[3,1728,128]{2,1,0:T(8,128)}, f32[8,384]{1,0:T(8,128)}) custom-call(s32[1]{0:T(128)} %bitcast.refs_0_, f32[544,384]{1,0:T(8,128)} %get-tuple-element.98.refs_1_, f32[544,384]{1,0:T(8,128)} %get-tuple-element.82.refs_1_.refs_2_, bf16[544,1152]{1,0:T(8,128)(2,1)} %get-tuple-element.99.refs_3_, ...), custom_call_target="tpu_custom_call" | custom-call | flops 100000000 | bytes 60000000 | tf_op jit(solution)/shard_map/pallas_call | solution.py:1049
  391.0 8.6 %all-gather.12.cloned.1.call-done.refs_2_ = bf16[1280,4352]{1,0:T(8,128)(2,1)} async-done(((bf16[80,4352]{1,0:T(8,128)(2,1)}), bf16[1280,4352]{1,0:T(8,128)(2,1)}) %all-gather.12.cloned.1.call-update) | async-done | bytes 11141136 | tf_op jit(solution)/shard_map/all_gather | solution.py:1671
  399.6 10.3 %shard_map.458 = (f32[96,2048]{1,0:T(8,128)}, bf16[96,2048]{1,0:T(8,128)(2,1)}, f32[3,6,144,128]{3,2,1,0:T(8,128)}) custom-call(s32[10]{0:T(128)} %fusion.88.refs_0_, bf16[1280,4608]{1,0:T(8,128)(2,1)} %all-gather.14.cloned.1.call-done.refs_1_, bf16[1280,4352]{1,0:T(8,128)(2,1)} %all-gather.12.cloned.1.call-done.refs_2_, ...), custom_call_target="tpu_custom_call", output_to_operand_aliasing={{2}: (4, {})} | custom-call | flops 100000000 | bytes 37000000 | tf_op jit(solution)/shard_map/pallas_call | solution.py:1368
  423.2 13.2 %shard_map.459 = (f32[544,384]{1,0:T(8,128)}, f32[3,3168,128]{2,1,0:T(8,128)}, f32[8,384]{1,0:T(8,128)}, bf16[96,2048]{1,0:T(8,128)(2,1)}) custom-call(s32[1]{0:T(128)} %bitcast.refs_0_, f32[544,384]{1,0:T(8,128)} %get-tuple-element.101.refs_1_, f32[544,384]{1,0:T(8,128)} %bitcast.341, ...), custom_call_target="tpu_custom_call", output_to_operand_aliasing={{3}: (11, {})} | custom-call | flops 100000000 | bytes 60000000 | tf_op jit(solution)/shard_map/pallas_call | solution.py:1049
  448.8 15.6 %shard_map.460 = (f32[544,384]{1,0:T(8,128)}, f32[3,1728,128]{2,1,0:T(8,128)}, f32[8,384]{1,0:T(8,128)}, f32[96,2048]{1,0:T(8,128)}) custom-call(s32[1]{0:T(128)} %bitcast.refs_0_, f32[544,384]{1,0:T(8,128)} %get-tuple-element.112.refs_1_, f32[544,384]{1,0:T(8,128)} %bitcast.342, ...), custom_call_target="tpu_custom_call", output_to_operand_aliasing={{3}: (9, {})} | custom-call | flops 100000000 | bytes 60000000 | tf_op jit(solution)/shard_map/pallas_call | solution.py:1049
  486.8 10.4 %shard_map.462 = (f32[2048,256]{1,0:T(8,128)}, f32[8,128]{1,0:T(8,128)}, f32[3,2,72,128]{3,2,1,0:T(8,128)}, f32[3,2,72,128]{3,2,1,0:T(8,128)}, f32[3,2,2,2,88,12...) custom-call(bf16[1280,256]{1,0:T(8,128)(2,1)} %bitcast.351, ...), custom_call_target="tpu_custom_call", output_to_operand_aliasing={{2}: (6, {}), {3}: (7, {}), {4}: (8, {}), {5}: (9, {})} | custom-call | flops 100000000 | bytes 40000000 | tf_op jit(solution)/shard_map/pallas_call | solution.py:1264
  515.4 6.3 %collective-permute-done.55 = bf16[3,2,2,88,128]{4,3,0,1,2:T(8,128)(2,1)S(1)} collective-permute-done((bf16[3,2,2,88,128]{4,3,0,1,2:T(8,128)(2,1)S(1)}, bf16[3,2,2,88,128]{4,3,0,1,2:T(8,128)(2,1)S(1)}, u32[]{:S(2)}, u32[]{:S(2)}) %collective-permute-start.55) | collective-permute-done | bytes 270368 | tf_op jit(solution)/shard_map/ppermute | solution.py:462
  556.3 7.0 %collective-permute-done.71 = f32[16,2048]{1,0:T(8,128)S(1)} collective-permute-done((f32[16,2048]{1,0:T(8,128)S(1)}, f32[16,2048]{1,0:T(8,128)S(1)}, u32[]{:S(2)}, u32[]{:S(2)}) %collective-permute-start.71) | collective-permute-done | bytes 131104 | tf_op jit(solution)/shard_map/ppermute | solution.py:1800
  568.8 8.1 %shard_map.464 = (f32[2048,256]{1,0:T(8,128)}, f32[2048,256]{1,0:T(8,128)}, f32[2048,256]{1,0:T(8,128)}, bf16[2048,256]{1,0:T(8,128)(2,1)}, f32[2048,256]{1,0:T(8,128)}) custom-call(f32[1]{0:T(128)} %bitcast.163.factor_ref, f32[2048,256]{1,0:T(8,128)} %refs_0_.1, f32[2048,256]{1,0:T(8,128)} %refs_1_.1, f32[2048,256]{1,0:T(8,128)} %refs_2_.3, ...), custom_call_target="tpu_custom_call" | custom-call | flops 10000000 | bytes 20000000 | tf_op jit(solution)/shard_map/pallas_call | solution.py:1291
  (548 shorter events, 290.9 us)
Async XLA Ops:
  7.2 148.0 %all-gather.8.cloned.1.call-start = ((), (), s32[]{:S(2)}) async-start(), calls=%async_computation | async-start | bytes 15040512 | tf_op jit(solution)/shard_map/all_gather | solution.py:1484
  25.0 20.3 %collective-permute-start.16 = (bf16[4,144,384]{2,1,0:T(8,128)(2,1)S(1)}, bf16[4,144,384]{2,1,0:T(8,128)(2,1)S(1)}, u32[]{:S(2)}, u32[]{:S(2)}) collective-permute-start(bf16[4,144,384]{2,1,0:T(8,128)(2,1)S(1)} %get-tuple-element.81), channel_id=1, source_target_pairs={{0,24},{1,25},{2,26},{3,27},{4,28},{5,29},{6,30},{7,31},{8,16},{9,... | collective-permute-start | bytes 1327112 | tf_op jit(solution)/shard_map/ppermute | solution.py:1478
  46.4 177.7 %all-gather.10.cloned.1.call-start = ((), (), s32[]{:S(2)}) async-start(), calls=%async_computation.1 | async-start | bytes 13369344 | tf_op jit(solution)/shard_map/all_gather | solution.py:1520
  61.4 25.0 %collective-permute-start.13 = (bf16[320,384]{1,0:T(8,128)(2,1)S(1)}, bf16[320,384]{1,0:T(8,128)(2,1)S(1)}, u32[]{:S(2)}, u32[]{:S(2)}) collective-permute-start(bf16[320,384]{1,0:T(8,128)(2,1)S(1)} %broadcast_select_fusion.12), channel_id=1, source_target_pairs={{0,8},{1,9},{4,12},{5,13},{24,16},{25,17},{28,20},{29,21}} | collective-permute-start | bytes 737288 | tf_op jit(solution)/shard_map/ppermute | solution.py:1500
  63.4 25.0 %collective-permute-start.5 = (bf16[336,384]{1,0:T(8,128)(2,1)S(1)}, bf16[336,384]{1,0:T(8,128)(2,1)S(1)}, u32[]{:S(2)}, u32[]{:S(2)}) collective-permute-start(bf16[336,384]{1,0:T(8,128)(2,1)S(1)} %broadcast_select_fusion.8), channel_id=1, source_target_pairs={{0,24},{1,25},{2,26},{3,27},{4,28},{5,29},{6,30},{7,31}} | collective-permute-start | bytes 774152 | tf_op jit(solution)/shard_map/ppermute | solution.py:1500
  89.1 21.0 %collective-permute-start.6 = (bf16[336,384]{1,0:T(8,128)(2,1)S(1)}, bf16[336,384]{1,0:T(8,128)(2,1)S(1)}, u32[]{:S(2)}, u32[]{:S(2)}) collective-permute-start(bf16[336,384]{1,0:T(8,128)(2,1)S(1)} %broadcast_select_fusion.9), channel_id=1, source_target_pairs={{0,8},{1,9},{2,10},{3,11},{4,12},{5,13},{6,14},{7,15},{24,16},{25,... | collective-permute-start | bytes 774152 | tf_op jit(solution)/shard_map/ppermute | solution.py:1500
  91.1 19.7 %collective-permute-start.10 = (bf16[336,384]{1,0:T(8,128)(2,1)S(1)}, bf16[336,384]{1,0:T(8,128)(2,1)S(1)}, u32[]{:S(2)}, u32[]{:S(2)}) collective-permute-start(bf16[336,384]{1,0:T(8,128)(2,1)S(1)} %broadcast_select_fusion.5), channel_id=1, source_target_pairs={{0,4},{1,5},{24,28},{25,29},{8,12},{9,13},{16,20},{17,21},{2,6},{3... | collective-permute-start | bytes 774152 | tf_op jit(solution)/shard_map/ppermute | solution.py:1500
  112.4 22.3 %collective-permute-start.15 = (bf16[992,384]{1,0:T(8,128)(2,1)}, bf16[992,384]{1,0:T(8,128)(2,1)S(1)}, u32[]{:S(2)}, u32[]{:S(2)}) collective-permute-start(bf16[992,384]{1,0:T(8,128)(2,1)} %pad_maximum_fusion.6), channel_id=1, source_target_pairs={{0,1},{1,0},{2,3},{3,2},{4,5},{5,4},{6,7},{7,6},{8,9},{9,8},{10,11... | collective-permute-start | bytes 2285576 | tf_op jit(solution)/shard_map/ppermute | solution.py:1507
  112.4 21.2 %collective-permute-start.18 = (bf16[96,2048]{1,0:T(8,128)(2,1)S(1)}, bf16[96,2048]{1,0:T(8,128)(2,1)S(1)}, u32[]{:S(2)}, u32[]{:S(2)}) collective-permute-start(bf16[96,2048]{1,0:T(8,128)(2,1)S(1)} %get-tuple-element.184), channel_id=1, source_target_pairs={{0,24},{1,25},{2,26},{3,27},{4,28},{5,29},{6,30},{7,31},{8,16},{9,... | collective-permute-start | bytes 1179656 | tf_op jit(solution)/shard_map/ppermute | solution.py:1487
  157.3 233.7 %all-gather.14.cloned.1.call-start = ((), (), s32[]{:S(2)}) async-start(), calls=%async_computation.3 | async-start | bytes 12533760 | tf_op jit(solution)/shard_map/all_gather | solution.py:1589
  232.8 166.8 %all-gather.12.cloned.1.call-start = ((), (), s32[]{:S(2)}) async-start(), calls=%async_computation.2 | async-start | bytes 11837440 | tf_op jit(solution)/shard_map/all_gather | solution.py:1671
  362.0 25.6 %collective-permute-start.40 = (bf16[3,11,144,128]{3,2,1,0:T(8,128)(2,1)}, bf16[3,11,144,128]{3,2,1,0:T(8,128)(2,1)S(1)}, u32[]{:S(2)}, u32[]{:S(2)}) collective-permute-start(bf16[3,11,144,128]{3,2,1,0:T(8,128)(2,1)} %fusion.1), channel_id=1, source_target_pairs={{0,1},{1,0},{2,3},{3,2},{4,5},{5,4},{6,7},{7,6},{8,9},{9,8},{10,11... | collective-permute-start | bytes 3649544 | tf_op jit(solution)/shard_map/ppermute | solution.py:462
  384.6 25.3 %collective-permute-start.39 = (bf16[3,6,144,128]{3,2,1,0:T(8,128)(2,1)}, bf16[3,6,144,128]{3,2,1,0:T(8,128)(2,1)S(1)}, u32[]{:S(2)}, u32[]{:S(2)}) collective-permute-start(bf16[3,6,144,128]{3,2,1,0:T(8,128)(2,1)} %fusion.7), channel_id=1, source_target_pairs={{0,1},{1,0},{2,3},{3,2},{4,5},{5,4},{6,7},{7,6},{8,9},{9,8},{10,11... | collective-permute-start | bytes 1990664 | tf_op jit(solution)/shard_map/ppermute | solution.py:462
  414.6 27.6 %collective-permute-start.42 = (bf16[3,2,2,2,72,128]{5,4,0,2,3,1:T(8,128)(2,1)}, bf16[3,2,2,2,72,128]{5,4,0,2,3,1:T(8,128)(2,1)}, u32[]{:S(2)}, u32[]{:S(2)}) collective-permute-start(bf16[3,2,2,2,72,128]{5,4,0,2,3,1:T(8,128)(2,1)} %fusion.21), channel_id=1, source_target_pairs={{0,24},{1,25},{2,26},{3,27},{4,28},{5,29},{6,30},{7,31},{8,16},{9,... | collective-permute-start | bytes 1327112 | tf_op jit(solution)/shard_map/ppermute | solution.py:462
  418.0 28.3 %collective-permute-start.41 = (bf16[3,2,2,2,72,128]{5,4,0,2,1,3:T(8,128)(2,1)S(1)}, bf16[3,2,2,2,72,128]{5,4,0,2,1,3:T(8,128)(2,1)}, u32[]{:S(2)}, u32[]{:S(2)}) collective-permute-start(bf16[3,2,2,2,72,128]{5,4,0,2,1,3:T(8,128)(2,1)S(1)} %fusion.20), channel_id=1, source_target_pairs={{0,2},{1,3},{2,0},{3,1},{4,6},{5,7},{6,4},{7,5},{8,10},{9,11},{10,... | collective-permute-start | bytes 1327112 | tf_op jit(solution)/shard_map/ppermute | solution.py:462
  439.4 39.4 %collective-permute-start.48 = (bf16[3,11,144,128]{3,2,1,0:T(8,128)(2,1)}, bf16[3,11,144,128]{3,2,1,0:T(8,128)(2,1)}, u32[]{:S(2)}, u32[]{:S(2)}) collective-permute-start(bf16[3,11,144,128]{3,2,1,0:T(8,128)(2,1)} %fusion.2), channel_id=1, source_target_pairs={{0,1},{1,0},{2,3},{3,2},{4,5},{5,4},{6,7},{7,6},{8,9},{9,8},{10,11... | collective-permute-start | bytes 3649544 | tf_op jit(solution)/shard_map/ppermute | solution.py:462
  439.4 28.1 %collective-permute-start.43 = (bf16[96,2048]{1,0:T(8,128)(2,1)}, bf16[96,2048]{1,0:T(8,128)(2,1)S(1)}, u32[]{:S(2)}, u32[]{:S(2)}) collective-permute-start(bf16[96,2048]{1,0:T(8,128)(2,1)} %get-tuple-element.116), channel_id=1, source_target_pairs={{16,8},{17,9},{18,10},{19,11},{20,12},{21,13},{22,14},{23,15},{24,... | collective-permute-start | bytes 1179656 | tf_op jit(solution)/shard_map/ppermute | solution.py:1773
  444.1 27.7 %collective-permute-start.46 = (bf16[3,2,2,72,128]{4,3,0,1,2:T(8,128)(2,1)S(1)}, bf16[3,2,2,72,128]{4,3,0,1,2:T(8,128)(2,1)S(1)}, u32[]{:S(2)}, u32[]{:S(2)}) collective-permute-start(bf16[3,2,2,72,128]{4,3,0,1,2:T(8,128)(2,1)S(1)} %fusion.33), channel_id=1, source_target_pairs={{0,8},{1,9},{2,10},{3,11},{4,12},{5,13},{6,14},{7,15},{8,0},{9,1},... | collective-permute-start | bytes 663560 | tf_op jit(solution)/shard_map/ppermute | solution.py:462
  448.2 20.7 %collective-permute-start.45 = (bf16[3,2,2,72,128]{4,3,0,2,1:T(8,128)(2,1)S(1)}, bf16[3,2,2,72,128]{4,3,0,2,1:T(8,128)(2,1)S(1)}, u32[]{:S(2)}, u32[]{:S(2)}) collective-permute-start(bf16[3,2,2,72,128]{4,3,0,2,1:T(8,128)(2,1)S(1)} %fusion.32), channel_id=1, source_target_pairs={{0,4},{1,5},{2,6},{3,7},{4,0},{5,1},{6,2},{7,3},{8,12},{9,13},{10,... | collective-permute-start | bytes 663560 | tf_op jit(solution)/shard_map/ppermute | solution.py:462
  468.9 80.9 %collective-permute-start.44 = (f32[16,2048]{1,0:T(8,128)S(1)}, f32[16,2048]{1,0:T(8,128)S(1)}, u32[]{:S(2)}, u32[]{:S(2)}) collective-permute-start(f32[16,2048]{1,0:T(8,128)S(1)} %constant_dynamic-slice_fusion.4), channel_id=1, source_target_pairs={{0,1},{1,2},{2,3},{3,4},{4,5},{5,6},{6,7},{7,8},{8,9},{9,10},{10,1... | collective-permute-start | bytes 393224 | tf_op jit(solution)/shard_map/ppermute | solution.py:1826
  472.6 24.7 %collective-permute-start.58 = (bf16[3,2,72,128]{3,2,0,1:T(8,128)(2,1)S(1)}, bf16[3,2,72,128]{3,2,0,1:T(8,128)(2,1)S(1)}, u32[]{:S(2)}, u32[]{:S(2)}) collective-permute-start(bf16[3,2,72,128]{3,2,0,1:T(8,128)(2,1)S(1)} %fusion.41), channel_id=1, source_target_pairs={{0,24},{1,25},{2,26},{3,27},{4,28},{5,29},{6,30},{7,31},{8,16},{9,... | collective-permute-start | bytes 331784 | tf_op jit(solution)/shard_map/ppermute | solution.py:462
  476.9 22.4 %collective-permute-start.60 = (bf16[3,2,72,128]{3,2,0,1:T(8,128)(2,1)S(1)}, bf16[3,2,72,128]{3,2,0,1:T(8,128)(2,1)S(1)}, u32[]{:S(2)}, u32[]{:S(2)}) collective-permute-start(bf16[3,2,72,128]{3,2,0,1:T(8,128)(2,1)S(1)} %fusion.42), channel_id=1, source_target_pairs={{0,2},{1,3},{2,0},{3,1},{4,6},{5,7},{6,4},{7,5},{8,10},{9,11},{10,... | collective-permute-start | bytes 331784 | tf_op jit(solution)/shard_map/ppermute | solution.py:462
  484.2 20.4 %collective-permute-start.50 = (bf16[3,2,2,2,88,128]{5,4,0,2,1,3:T(8,128)(2,1)S(1)}, bf16[3,2,2,2,88,128]{5,4,0,2,1,3:T(8,128)(2,1)S(1)}, u32[]{:S(2)}, u32[]{:S(2)}) collective-permute-start(bf16[3,2,2,2,88,128]{5,4,0,2,1,3:T(8,128)(2,1)S(1)} %fusion.9), channel_id=1, source_target_pairs={{0,2},{1,3},{2,0},{3,1},{4,6},{5,7},{6,4},{7,5},{8,10},{9,11},{10,... | collective-permute-start | bytes 1622024 | tf_op jit(solution)/shard_map/ppermute | solution.py:462
  485.8 26.3 %collective-permute-start.54 = (bf16[3,2,2,2,88,128]{5,4,0,2,3,1:T(8,128)(2,1)S(1)}, bf16[3,2,2,2,88,128]{5,4,0,2,3,1:T(8,128)(2,1)S(1)}, u32[]{:S(2)}, u32[]{:S(2)}) collective-permute-start(bf16[3,2,2,2,88,128]{5,4,0,2,3,1:T(8,128)(2,1)S(1)} %fusion.10), channel_id=1, source_target_pairs={{0,24},{1,25},{2,26},{3,27},{4,28},{5,29},{6,30},{7,31},{8,16},{9,... | collective-permute-start | bytes 1622024 | tf_op jit(solution)/shard_map/ppermute | solution.py:462
  (102 other events, 629.8 us)
Sparse Core Ops, SparseCore 0:
  46.5 108.6 all-gather.7
  157.5 66.5 all-gather.9
  232.9 72.4 all-gather.13
  334.9 64.6 all-gather.11
